TPU v7x, 32 devices: a whole 2x2x4 slice. The times are simulated.
32 devices in a mesh: ctx: 8 (over z, x), fsdp: 4 (over y, core).
Axes of the slice: x: 2, y: 2, z: 4, core: 2. Of those that a mesh axis runs over, the one named last changes fastest.
Arguments:
- tokens: bfloat16 [12, 8, 2, 128, 1024], P('fsdp', 'ctx'), may hold values from -6 to 6
- cotangent: bfloat16 [12, 8, 2, 128, 1024], P('fsdp', 'ctx'), may hold values from -6 to 6
- query_weight: bfloat16 [1024, 1024], P('fsdp'), may hold values from -0.1875 to 0.1875
- key_weight: bfloat16 [1024, 1024], P('fsdp'), may hold values from -0.1875 to 0.1875
- value_weight: bfloat16 [1024, 1024], P('fsdp'), may hold values from -0.1875 to 0.1875
- output_weight: bfloat16 [1024, 1024], P('fsdp'), may hold values from -3 to 3
- gate_weight: bfloat16 [1024, 2816], P('fsdp'), may hold values from -0.1875 to 0.1875
- up_weight: bfloat16 [1024, 2816], P('fsdp'), may hold values from -0.1875 to 0.1875
- down_weight: bfloat16 [2816, 1024], P('fsdp'), may hold values from -0.109375 to 0.109375
- first_gain: bfloat16 [1024], P('fsdp'), may hold values from 0.099609375 to 1.8984375
- second_gain: bfloat16 [1024], P('fsdp'), may hold values from 0.099609375 to 1.8984375
- cache_keys: bfloat16 [12, 16384, 1024], P('fsdp', 'ctx'), may hold values from -6 to 6
- cache_values: bfloat16 [12, 16384, 1024], P('fsdp', 'ctx'), may hold values from -6 to 6
- block_indices: int32 [12, 8, 2, 2, 8, 4], P('fsdp', 'ctx'), may hold values from 0 to 511, as said below
- partner: int32 [12], P('fsdp'), may hold values from 0 to 2
Outputs:
- layer_output: bfloat16 [12, 8, 2, 128, 1024], P('fsdp', 'ctx')
- input_gradient: float32 [12, 8, 2, 128, 1024], P('fsdp', 'ctx')
- gradient_query: float32 [1024, 1024], P('fsdp')
- gradient_key: float32 [1024, 1024], P('fsdp')
- gradient_value: float32 [1024, 1024], P('fsdp')
- gradient_output: float32 [1024, 1024], P('fsdp')
- gradient_gate: float32 [1024, 2816], P('fsdp')
- gradient_up: float32 [1024, 2816], P('fsdp')
- gradient_down: float32 [2816, 1024], P('fsdp')
- gradient_first: float32 [1024], P('fsdp')
- gradient_second: float32 [1024], P('fsdp')
Inputs may be any that keep to these rules, and one draw needn't show every extreme that they name: `block_indices`: entry [s, i, c, n, h, k] is the k-th cache block read by query block n of the piece stored at [s, i, c], head h. A value b below 256 names block b of sequence s's own cache, b - 256 block b - 256 of its partner's; block m of a cache lies on ctx device m // 32. The 128 values of one [s, i] name at most 32 blocks that lie on any one ctx device; in each sequence one ctx device is named exactly 32 times by the values of every [s, i]. Values may repeat. `partner`: index, within the 3 sequences of the same fsdp group, of the sequence whose cache the partner blocks read; it may be the sequence itself.
All inputs are finite; a program needn't handle non-finite values.
Results may differ from a plain program's by a relative error of at most 0.023.
Values may be sent and summed in bfloat16 or wider, within the bound.
A program may use at most 512 MiB of HBM per device.

v0:
```python
import jax
import jax.numpy as jnp
from jax import lax
from jax.sharding import PartitionSpec as P

D = 1024
HEADS = 8
HEAD_DIM = 128
HALF = 128
MICRO = 3
BLOCK = 64
TOPK = 4


EPS = 1e-05


def normed(value):
    return value * lax.rsqrt(jnp.mean(value * value, axis=-1, keepdims=True) + EPS)


def scaled_norm(value, gain):
    return normed(value) * gain


def gated(gate, upper):
    return jax.nn.silu(gate) * upper


def rotary(value, cosine, sine):
    half = value.shape[-1] // 2
    first = value[..., :half]
    second = value[..., half:]
    return jnp.concatenate(
        [first * cosine - second * sine, second * cosine + first * sine], axis=-1
    )


def angles(positions):
    inverse = 10000.0 ** (-jnp.arange(HEAD_DIM // 2, dtype=jnp.float32) * 2.0 / HEAD_DIM)
    phase = positions.astype(jnp.float32)[:, None] * inverse[None, :]
    return (jnp.cos(phase)[:, None, :], jnp.sin(phase)[:, None, :])


def piece_positions(count, context_count):
    slots = jnp.arange(count, dtype=jnp.int32)
    device = slots // 2
    segment_at = jnp.where(slots % 2 == 0, device, 2 * context_count - 1 - device)
    return (segment_at[:, None] * HALF + jnp.arange(HALF, dtype=jnp.int32)[None, :]).reshape(-1)


def split_pairs(piece):
    count = piece.shape[0]
    flat = piece.reshape(count * HALF, 2 * D)
    return (flat[:, :D].reshape(-1, HEADS, HEAD_DIM), flat[:, D:].reshape(-1, HEADS, HEAD_DIM))


def attend_piece(query, positions, piece, context_count):
    scale = HEAD_DIM ** (-0.5)
    keys, values = split_pairs(piece)
    visible = positions[:, None] >= piece_positions(piece.shape[0], context_count)[None, :]
    scores = jnp.einsum("qhd,khd->hqk", query, keys, preferred_element_type=jnp.float32) * scale
    weights = jnp.where(visible[None], jnp.exp(scores), 0.0).astype(jnp.bfloat16)
    total = jnp.sum(weights, axis=-1, dtype=jnp.float32)
    weighted = jnp.einsum("hqk,khd->qhd", weights, values, preferred_element_type=jnp.float32)
    return (weighted, total)


def back_piece(query, positions, back_weighted, back_total, carry, piece, context_count):
    scale = HEAD_DIM ** (-0.5)
    count = piece.shape[0]
    keys, values = split_pairs(piece)
    visible = positions[:, None] >= piece_positions(count, context_count)[None, :]
    scores = jnp.einsum("qhd,khd->hqk", query, keys, preferred_element_type=jnp.float32) * scale
    raised = jnp.where(visible[None], jnp.exp(scores), 0.0)
    back_weights = (
        jnp.einsum("qhd,khd->hqk", back_weighted, values, preferred_element_type=jnp.float32)
        + back_total[:, :, None]
    )
    back_scores = (raised * back_weights).astype(jnp.bfloat16)
    back_query = (
        carry[0]
        + jnp.einsum("hqk,khd->qhd", back_scores, keys, preferred_element_type=jnp.float32) * scale
    )
    back_keys = (
        jnp.einsum("hqk,qhd->khd", back_scores, query, preferred_element_type=jnp.float32) * scale
    )
    back_values = jnp.einsum(
        "hqk,qhd->khd",
        raised.astype(jnp.bfloat16),
        back_weighted,
        preferred_element_type=jnp.float32,
    )
    update = jnp.concatenate(
        [back_keys.reshape(-1, D), back_values.reshape(-1, D)], axis=1
    ).reshape(count, HALF, 2 * D)
    return (back_query, update)


def memory_forward(query, memory_keys, memory_values):
    scale = HEAD_DIM ** (-0.5)
    groups = query.reshape(-1, BLOCK, HEADS, HEAD_DIM)
    scores = (
        jnp.einsum("nqhd,nhmd->nhqm", groups, memory_keys, preferred_element_type=jnp.float32)
        * scale
    )
    weights = jnp.exp(scores).astype(jnp.bfloat16)
    total = jnp.transpose(jnp.sum(weights, axis=-1, dtype=jnp.float32), (1, 0, 2)).reshape(
        HEADS, -1
    )
    weighted = jnp.einsum(
        "nhqm,nhmd->nqhd", weights, memory_values, preferred_element_type=jnp.float32
    )
    return (weighted.reshape(-1, HEADS, HEAD_DIM), total)


def memory_backward(query, memory_keys, memory_values, back_weighted, back_total):
    scale = HEAD_DIM ** (-0.5)
    groups = query.reshape(-1, BLOCK, HEADS, HEAD_DIM)
    count = groups.shape[0]
    scores = (
        jnp.einsum("nqhd,nhmd->nhqm", groups, memory_keys, preferred_element_type=jnp.float32)
        * scale
    )
    raised = jnp.exp(scores)
    back_groups = back_weighted.reshape(count, BLOCK, HEADS, HEAD_DIM)
    shift = jnp.transpose(back_total.reshape(HEADS, count, BLOCK), (1, 0, 2))[..., None]
    back_weights = (
        jnp.einsum(
            "nqhd,nhmd->nhqm", back_groups, memory_values, preferred_element_type=jnp.float32
        )
        + shift
    )
    back_scores = (raised * back_weights).astype(jnp.bfloat16)
    back_query = (
        jnp.einsum("nhqm,nhmd->nqhd", back_scores, memory_keys, preferred_element_type=jnp.float32)
        * scale
    )
    return back_query.reshape(-1, HEADS, HEAD_DIM)


def fetch(cache_keys, cache_values, indices, partner, micro, context_count):
    per_device = cache_keys.shape[1] // BLOCK
    all_blocks = per_device * context_count
    flat = indices.reshape(-1)
    count = flat.shape[0]
    capacity = 2 * count // context_count
    side = flat // all_blocks
    number = flat % all_blocks
    owner = number // per_device
    document = jnp.where(side == 0, micro, partner[micro])
    heads = jnp.arange(count, dtype=jnp.int32) // TOPK % HEADS
    code = (document * per_device + number % per_device) * HEADS + heads
    owner_table = (owner[:, None] == jnp.arange(context_count, dtype=jnp.int32)[None, :]).astype(
        jnp.int32
    )
    rank = jnp.sum(jnp.cumsum(owner_table, axis=0) * owner_table, axis=1) - 1
    slot = owner * capacity + rank
    requests = jnp.zeros((context_count * capacity,), jnp.int32).at[slot].set(code)
    asked = lax.all_to_all(
        requests.reshape(context_count, capacity), "ctx", split_axis=0, concat_axis=0, tiled=True
    )
    table_keys = cache_keys.reshape(-1, BLOCK, HEADS, HEAD_DIM)
    table_values = cache_values.reshape(-1, BLOCK, HEADS, HEAD_DIM)
    picked = asked // HEADS
    chosen_head = asked % HEADS
    sent_keys = table_keys[picked, :, chosen_head, :]
    sent_values = table_values[picked, :, chosen_head, :]
    got_keys, got_values = (
        lax.all_to_all(sent_keys, "ctx", split_axis=0, concat_axis=0, tiled=True),
        lax.all_to_all(sent_values, "ctx", split_axis=0, concat_axis=0, tiled=True),
    )
    shape = (-1, HEADS, TOPK * BLOCK, HEAD_DIM)
    memory_keys = got_keys.reshape(-1, BLOCK, HEAD_DIM)[slot].reshape(shape)
    memory_values = got_values.reshape(-1, BLOCK, HEAD_DIM)[slot].reshape(shape)
    return (memory_keys, memory_values)


def body(
    tokens,
    cotangent,
    query_weight,
    key_weight,
    value_weight,
    output_weight,
    gate_weight,
    up_weight,
    down_weight,
    first_gain,
    second_gain,
    cache_keys,
    cache_values,
    block_indices,
    partner,
):
    context_count = lax.axis_size("ctx")
    context_index = lax.axis_index("ctx")
    rows = 2 * HALF
    pieces_at = jnp.stack([context_index, 2 * context_count - 1 - context_index])
    positions = (pieces_at[:, None] * HALF + jnp.arange(HALF, dtype=jnp.int32)[None, :]).reshape(
        rows
    )
    cosine, sine = angles(positions)

    def rotate(value):
        return rotary(value.reshape(rows, HEADS, HEAD_DIM), cosine, sine)

    totals = None
    outputs = []
    input_parts = []
    for micro in range(MICRO):
        gathered = (
            lax.all_gather(query_weight, "fsdp", axis=0, tiled=True),
            lax.all_gather(key_weight, "fsdp", axis=0, tiled=True),
            lax.all_gather(value_weight, "fsdp", axis=0, tiled=True),
            lax.all_gather(output_weight, "fsdp", axis=0, tiled=True),
            lax.all_gather(gate_weight, "fsdp", axis=0, tiled=True),
            lax.all_gather(up_weight, "fsdp", axis=0, tiled=True),
            lax.all_gather(down_weight, "fsdp", axis=0, tiled=True),
            lax.all_gather(first_gain, "fsdp", axis=0, tiled=True),
            lax.all_gather(second_gain, "fsdp", axis=0, tiled=True),
        )
        (
            full_query,
            full_key,
            full_value,
            full_output,
            full_gate,
            full_up,
            full_down,
            gain_one,
            gain_two,
        ) = gathered
        inputs = tokens[micro].reshape(rows, D).astype(jnp.float32)
        normed_one, norm_back_one = jax.vjp(scaled_norm, inputs, gain_one.astype(jnp.float32))
        normed_low = normed_one.astype(jnp.bfloat16)
        query_rot, query_back = jax.vjp(
            rotate, jnp.dot(normed_low, full_query, preferred_element_type=jnp.float32)
        )
        key_rot, key_back = jax.vjp(
            rotate, jnp.dot(normed_low, full_key, preferred_element_type=jnp.float32)
        )
        value_low = jnp.dot(normed_low, full_value, preferred_element_type=jnp.float32).astype(
            jnp.bfloat16
        )
        query = query_rot.astype(jnp.bfloat16)
        key_low = key_rot.astype(jnp.bfloat16)
        pairs = jnp.concatenate([key_low.reshape(rows, D), value_low], axis=1).reshape(
            2, HALF, 2 * D
        )
        memory_keys, memory_values = fetch(
            cache_keys, cache_values, block_indices[micro, 0], partner, micro, context_count
        )
        weighted, total = attend_piece(
            query, positions, lax.all_gather(pairs, "ctx", axis=0, tiled=True), context_count
        )
        memory_weighted, memory_total = memory_forward(query, memory_keys, memory_values)
        weighted = weighted + memory_weighted
        total = total + memory_total
        per_row = jnp.transpose(total)
        mixed_full = weighted / per_row[:, :, None]
        mixed_low = mixed_full.astype(jnp.bfloat16).reshape(rows, D)
        middle = inputs + jnp.dot(mixed_low, full_output, preferred_element_type=jnp.float32)
        normed_two, norm_back_two = jax.vjp(scaled_norm, middle, gain_two.astype(jnp.float32))
        middle_low = normed_two.astype(jnp.bfloat16)
        gate = jnp.dot(middle_low, full_gate, preferred_element_type=jnp.float32)
        upper = jnp.dot(middle_low, full_up, preferred_element_type=jnp.float32)
        hidden_full, hidden_back = jax.vjp(gated, gate, upper)
        hidden = hidden_full.astype(jnp.bfloat16)
        result = middle + jnp.dot(hidden, full_down, preferred_element_type=jnp.float32)
        outputs.append(result.astype(jnp.bfloat16))
        incoming = cotangent[micro].reshape(rows, D)
        gradient_down = jnp.einsum(
            "tf,td->fd", hidden, incoming, preferred_element_type=jnp.float32
        )
        back_hidden = jnp.einsum(
            "td,fd->tf", incoming, full_down, preferred_element_type=jnp.float32
        )
        back_gate, back_upper = hidden_back(back_hidden)
        back_gate = back_gate.astype(jnp.bfloat16)
        back_upper = back_upper.astype(jnp.bfloat16)
        gradient_gate = jnp.einsum(
            "td,tf->df", middle_low, back_gate, preferred_element_type=jnp.float32
        )
        gradient_up = jnp.einsum(
            "td,tf->df", middle_low, back_upper, preferred_element_type=jnp.float32
        )
        back_mid_normed = jnp.einsum(
            "tf,df->td", back_gate, full_gate, preferred_element_type=jnp.float32
        ) + jnp.einsum("tf,df->td", back_upper, full_up, preferred_element_type=jnp.float32)
        back_mid_part, gradient_second = norm_back_two(back_mid_normed)
        back_middle = incoming.astype(jnp.float32) + back_mid_part
        back_attn = back_middle.astype(jnp.bfloat16)
        gradient_output = jnp.einsum(
            "tc,td->cd", mixed_low, back_attn, preferred_element_type=jnp.float32
        )
        back_mixed = jnp.einsum(
            "td,cd->tc", back_attn, full_output, preferred_element_type=jnp.float32
        ).reshape(rows, HEADS, HEAD_DIM)
        back_weighted = (back_mixed / per_row[:, :, None]).astype(jnp.bfloat16)
        back_total = jnp.transpose(-jnp.sum(back_mixed * mixed_full, axis=-1) / per_row)
        memory_back = memory_backward(query, memory_keys, memory_values, back_weighted, back_total)
        first_carry = (memory_back, jnp.zeros((2 * context_count, HALF, 2 * D), jnp.float32))
        folded = back_piece(
            query,
            positions,
            back_weighted,
            back_total,
            first_carry,
            lax.all_gather(pairs, "ctx", axis=0, tiled=True),
            context_count,
        )
        mine = (
            lax.psum_scatter(folded[1].astype(jnp.bfloat16), "ctx", scatter_dimension=0, tiled=True)
            .astype(jnp.float32)
            .reshape(rows, 2 * D)
        )
        back_query = query_back(folded[0])[0].astype(jnp.bfloat16)
        back_key = key_back(mine[:, :D].reshape(rows, HEADS, HEAD_DIM))[0].astype(jnp.bfloat16)
        back_value = mine[:, D:].astype(jnp.bfloat16)
        gradient_query = jnp.einsum(
            "tc,td->cd", normed_low, back_query, preferred_element_type=jnp.float32
        )
        gradient_key = jnp.einsum(
            "tc,td->cd", normed_low, back_key, preferred_element_type=jnp.float32
        )
        gradient_value = jnp.einsum(
            "tc,td->cd", normed_low, back_value, preferred_element_type=jnp.float32
        )
        back_in_normed = jnp.einsum(
            "td,cd->tc", back_query, full_query, preferred_element_type=jnp.float32
        )
        back_in_normed = back_in_normed + jnp.einsum(
            "td,cd->tc", back_key, full_key, preferred_element_type=jnp.float32
        )
        back_in_normed = back_in_normed + jnp.einsum(
            "td,cd->tc", back_value, full_value, preferred_element_type=jnp.float32
        )
        back_in_part, gradient_first = norm_back_one(back_in_normed)
        input_parts.append(back_middle + back_in_part)
        changes = (
            gradient_query,
            gradient_key,
            gradient_value,
            gradient_output,
            gradient_gate,
            gradient_up,
            gradient_down,
            gradient_first,
            gradient_second,
        )
        totals = changes if totals is None else jax.tree.map(jnp.add, totals, changes)
    shards = (
        lax.psum_scatter(
            totals[0].astype(jnp.bfloat16), "fsdp", scatter_dimension=0, tiled=True
        ).astype(jnp.float32),
        lax.psum_scatter(
            totals[1].astype(jnp.bfloat16), "fsdp", scatter_dimension=0, tiled=True
        ).astype(jnp.float32),
        lax.psum_scatter(
            totals[2].astype(jnp.bfloat16), "fsdp", scatter_dimension=0, tiled=True
        ).astype(jnp.float32),
        lax.psum_scatter(
            totals[3].astype(jnp.bfloat16), "fsdp", scatter_dimension=0, tiled=True
        ).astype(jnp.float32),
        lax.psum_scatter(
            totals[4].astype(jnp.bfloat16), "fsdp", scatter_dimension=0, tiled=True
        ).astype(jnp.float32),
        lax.psum_scatter(
            totals[5].astype(jnp.bfloat16), "fsdp", scatter_dimension=0, tiled=True
        ).astype(jnp.float32),
        lax.psum_scatter(
            totals[6].astype(jnp.bfloat16), "fsdp", scatter_dimension=0, tiled=True
        ).astype(jnp.float32),
        lax.psum_scatter(
            totals[7].astype(jnp.bfloat16), "fsdp", scatter_dimension=0, tiled=True
        ).astype(jnp.float32),
        lax.psum_scatter(
            totals[8].astype(jnp.bfloat16), "fsdp", scatter_dimension=0, tiled=True
        ).astype(jnp.float32),
    )
    final = (
        lax.psum(shards[0].astype(jnp.bfloat16), "ctx").astype(jnp.float32),
        lax.psum(shards[1].astype(jnp.bfloat16), "ctx").astype(jnp.float32),
        lax.psum(shards[2].astype(jnp.bfloat16), "ctx").astype(jnp.float32),
        lax.psum(shards[3].astype(jnp.bfloat16), "ctx").astype(jnp.float32),
        lax.psum(shards[4].astype(jnp.bfloat16), "ctx").astype(jnp.float32),
        lax.psum(shards[5].astype(jnp.bfloat16), "ctx").astype(jnp.float32),
        lax.psum(shards[6].astype(jnp.bfloat16), "ctx").astype(jnp.float32),
        lax.psum(shards[7].astype(jnp.bfloat16), "ctx").astype(jnp.float32),
        lax.psum(shards[8].astype(jnp.bfloat16), "ctx").astype(jnp.float32),
    )
    layer_output = jnp.stack(outputs).reshape(tokens.shape)
    input_gradient = jnp.stack(input_parts).reshape(tokens.shape)
    return (
        layer_output,
        input_gradient,
        final[0],
        final[1],
        final[2],
        final[3],
        final[4],
        final[5],
        final[6],
        final[7],
        final[8],
    )


def solution(mesh):
    return jax.shard_map(
        body,
        mesh=mesh,
        in_specs=(
            P("fsdp", "ctx", None, None, None),
            P("fsdp", "ctx", None, None, None),
            P("fsdp", None),
            P("fsdp", None),
            P("fsdp", None),
            P("fsdp", None),
            P("fsdp", None),
            P("fsdp", None),
            P("fsdp", None),
            P("fsdp"),
            P("fsdp"),
            P("fsdp", "ctx", None),
            P("fsdp", "ctx", None),
            P("fsdp", "ctx", None, None, None, None),
            P("fsdp"),
        ),
        out_specs=(
            P("fsdp", "ctx", None, None, None),
            P("fsdp", "ctx", None, None, None),
            P("fsdp", None),
            P("fsdp", None),
            P("fsdp", None),
            P("fsdp", None),
            P("fsdp", None),
            P("fsdp", None),
            P("fsdp", None),
            P("fsdp"),
            P("fsdp"),
        ),
        check_vma=False,
    )
```

profile of v0, /device:TPU:0, one launch (start us, length us, event | category | flops | bytes accessed | tf_op | source)
XLA Modules:
  0.0 2214.8 jit_solution(5079850321460189181)
XLA Ops:
  20.6 14.3 all-gather.13.cloned.1.call-done
  38.9 20.2 all-gather.19.cloned.1.call-done
  73.0 10.3 all-gather.15.cloned.1.call-done
  180.2 135.0 %all-to-all-done.8 = bf16[8,32,64,128]{3,2,1,0:T(8,128)(2,1)} async-done(((bf16[8,32,64,128]{3,2,1,0:T(8,128)(2,1)}), bf16[8,32,64,128]{3,2,1,0:T(8,128)(2,1)}, u32[]{:S(2)}, u32[]{:S(2)}) %all-to-all-start.8) | async-done | bytes 4194336 | tf_op jit(solution)/shard_map/all_to_all | solution.py:170
  328.1 154.6 %all-to-all-done.5 = bf16[8,32,64,128]{3,2,1,0:T(8,128)(2,1)} async-done(((bf16[8,32,64,128]{3,2,1,0:T(8,128)(2,1)}), bf16[8,32,64,128]{3,2,1,0:T(8,128)(2,1)}, u32[]{:S(2)}, u32[]{:S(2)}) %all-to-all-start.5) | async-done | bytes 4194336 | tf_op jit(solution)/shard_map/all_to_all | solution.py:170
  482.6 12.2 all-to-all-start.2
  518.4 148.2 %all-to-all-done.2 = bf16[8,32,64,128]{3,2,1,0:T(8,128)(2,1)} async-done(((bf16[8,32,64,128]{3,2,1,0:T(8,128)(2,1)}), bf16[8,32,64,128]{3,2,1,0:T(8,128)(2,1)}, u32[]{:S(2)}, u32[]{:S(2)}) %all-to-all-start.2) | async-done | bytes 4194336 | tf_op jit(solution)/shard_map/all_to_all | solution.py:170
  679.9 99.5 %all-to-all-done.7 = bf16[8,32,64,128]{3,2,1,0:T(8,128)(2,1)} async-done(((bf16[8,32,64,128]{3,2,1,0:T(8,128)(2,1)}), bf16[8,32,64,128]{3,2,1,0:T(8,128)(2,1)}, u32[]{:S(2)}, u32[]{:S(2)}) %all-to-all-start.7) | async-done | bytes 4194336 | tf_op jit(solution)/shard_map/all_to_all | solution.py:171
  793.0 82.6 %all-to-all-done.4 = bf16[8,32,64,128]{3,2,1,0:T(8,128)(2,1)} async-done(((bf16[8,32,64,128]{3,2,1,0:T(8,128)(2,1)}), bf16[8,32,64,128]{3,2,1,0:T(8,128)(2,1)}, u32[]{:S(2)}, u32[]{:S(2)}) %all-to-all-start.4) | async-done | bytes 4194336 | tf_op jit(solution)/shard_map/all_to_all | solution.py:171
  938.0 34.7 %all-to-all-done.1 = bf16[8,32,64,128]{3,2,1,0:T(8,128)(2,1)} async-done(((bf16[8,32,64,128]{3,2,1,0:T(8,128)(2,1)}), bf16[8,32,64,128]{3,2,1,0:T(8,128)(2,1)}, u32[]{:S(2)}, u32[]{:S(2)}) %all-to-all-start.1) | async-done | bytes 4194336 | tf_op jit(solution)/shard_map/all_to_all | solution.py:171
  1019.6 10.5 fusion.114
  1064.4 26.4 %convert_reduce_fusion.2 = (f32[8,256]{1,0:T(8,128)S(1)}, bf16[8,256,2048]{2,1,0:T(8,128)(2,1)}, f32[8,256]{1,0:T(8,128)S(1)}, bf16[8,256,2048]{2,1,0:T(8,128)(2...) fusion(pred[256,2048]{1,0:T(8,128)(4,1)S(1)} %copy-done.92, ...), kind=kOutput, calls=%fused_computation.22 | convolution fusion | flops 1137698816 | bytes 80764928 | tf_op jit(solution)/shard_map/qhd,khd->hqk/dot_general | solution.py:62
  1104.2 8.3 fusion.212
  1135.3 8.9 multiply_convert_fusion.8
  1173.7 11.1 multiply_convert_fusion.2
  1273.0 11.2 multiply_convert_fusion.1
  1327.0 10.7 multiply_convert_fusion
  1375.0 9.0 add_convert_fusion.1
  1394.3 9.4 add_convert_fusion.2
  1414.0 9.0 add_convert_fusion
  1447.8 8.6 fusion.33
  1460.3 46.7 %reduce-scatter.13.cloned.1.call-done = bf16[2,128,2048]{2,1,0:T(8,128)(2,1)} async-done(((bf16[16,128,2048]{2,1,0:T(8,128)(2,1)}), bf16[2,128,2048]{2,1,0:T(8,128)(2,1)}) %reduce-scatter.13.cloned.1.call-update) | async-done | bytes 1048592 | tf_op jit(solution)/shard_map/reduce_scatter | solution.py:314
  1510.9 147.9 %reduce-scatter.15.cloned.1.call-done = bf16[2,128,2048]{2,1,0:T(8,128)(2,1)} async-done(((bf16[16,128,2048]{2,1,0:T(8,128)(2,1)}), bf16[2,128,2048]{2,1,0:T(8,128)(2,1)}) %reduce-scatter.15.cloned.1.call-update) | async-done | bytes 1048592 | tf_op jit(solution)/shard_map/reduce_scatter | solution.py:314
  1674.6 9.1 fusion.34
  1723.9 25.1 %reduce-scatter.27.cloned.1.call-done = bf16[256,2816]{1,0:T(8,128)(2,1)} async-done(((bf16[1024,2816]{1,0:T(8,128)(2,1)}), bf16[256,2816]{1,0:T(8,128)(2,1)}) %reduce-scatter.27.cloned.1.call-update) | async-done | bytes 1441808 | tf_op jit(solution)/shard_map/reduce_scatter | solution.py:369
  1749.0 57.4 %reduce-scatter.25.cloned.1.call-done = bf16[256,2816]{1,0:T(8,128)(2,1)} async-done(((bf16[1024,2816]{1,0:T(8,128)(2,1)}), bf16[256,2816]{1,0:T(8,128)(2,1)}) %reduce-scatter.25.cloned.1.call-update) | async-done | bytes 1441808 | tf_op jit(solution)/shard_map/reduce_scatter | solution.py:366
  1806.5 57.3 %reduce-scatter.29.cloned.1.call-done = bf16[704,1024]{1,0:T(8,128)(2,1)} async-done(((bf16[2816,1024]{1,0:T(8,128)(2,1)}), bf16[704,1024]{1,0:T(8,128)(2,1)}) %reduce-scatter.29.cloned.1.call-update) | async-done | bytes 1441808 | tf_op jit(solution)/shard_map/reduce_scatter | solution.py:372
  1863.7 34.6 %reduce-scatter.21.cloned.1.call-done = bf16[256,1024]{1,0:T(8,128)(2,1)} async-done(((bf16[1024,1024]{1,0:T(8,128)(2,1)}), bf16[256,1024]{1,0:T(8,128)(2,1)}) %reduce-scatter.21.cloned.1.call-update) | async-done | bytes 524304 | tf_op jit(solution)/shard_map/reduce_scatter | solution.py:360
  1898.3 34.6 %reduce-scatter.19.cloned.1.call-done = bf16[256,1024]{1,0:T(8,128)(2,1)} async-done(((bf16[1024,1024]{1,0:T(8,128)(2,1)}), bf16[256,1024]{1,0:T(8,128)(2,1)}) %reduce-scatter.19.cloned.1.call-update) | async-done | bytes 524304 | tf_op jit(solution)/shard_map/reduce_scatter | solution.py:357
  1932.9 34.6 %reduce-scatter.17.cloned.1.call-done = bf16[256,1024]{1,0:T(8,128)(2,1)} async-done(((bf16[1024,1024]{1,0:T(8,128)(2,1)}), bf16[256,1024]{1,0:T(8,128)(2,1)}) %reduce-scatter.17.cloned.1.call-update) | async-done | bytes 524304 | tf_op jit(solution)/shard_map/reduce_scatter | solution.py:354
  1995.9 22.8 %all-reduce.14 = (bf16[256]{0:T(256)(128)(2,1)S(1)}, bf16[256]{0:T(256)(128)(2,1)S(1)}) all-reduce(bf16[256]{0:T(256)(128)(2,1)S(1)} %dynamic-slice.1, bf16[256]{0:T(256)(128)(2,1)S(1)} %dynamic-slice.3), channel_id=1, replica_groups=mesh['ctx'=8,'fsdp'=4] {'ctx'}, use_global_device_ids=true, to_apply=%region_51.52 | all-reduce | flops 512 | bytes 2048 | tf_op jit(solution)/shard_map/psum | solution.py:390
  2025.1 169.3 %all-reduce.19.cloned.1.call-done = (bf16[256,1024]{1,0:T(8,128)(2,1)}, bf16[256,1024]{1,0:T(8,128)(2,1)}, bf16[256,1024]{1,0:T(8,128)(2,1)}, bf16[256,1024]{1,0...) async-done(((bf16[256,1024]{1,0:T(8,128)(2,1)}, bf16[256,1024]{1,0:T(8,128)(2,1)}, bf16[256,1024]{1,0:T(8,128)(2,1)}, ...) | async-done | bytes 6422544 | tf_op jit(solution)/shard_map/psum | solution.py:383
  (681 shorter events, 723.1 us)
Async XLA Ops:
  7.2 27.7 %all-gather.13.cloned.1.call-start = ((), (), s32[]{:S(2)}) async-start(), calls=%async_computation.19 | async-start | bytes 2621440 | tf_op jit(solution)/shard_map/all_gather | solution.py:214
  7.9 51.2 %all-gather.19.cloned.1.call-start = ((), (), s32[]{:S(2)}) async-start(), calls=%async_computation.22 | async-start | bytes 2621440 | tf_op jit(solution)/shard_map/all_gather | solution.py:213
  8.7 74.6 %all-gather.15.cloned.1.call-start = ((), (), s32[]{:S(2)}) async-start(), calls=%async_computation.20 | async-start | bytes 2621440 | tf_op jit(solution)/shard_map/all_gather | solution.py:215
  9.4 979.1 %all-gather.31.cloned.1.call-start = ((), (), s32[]{:S(2)}) async-start(), calls=%async_computation.28 | async-start | bytes 9437184 | tf_op jit(solution)/shard_map/all_gather | solution.py:255
  87.9 913.1 %all-gather.17.cloned.1.call-start = ((), (), s32[]{:S(2)}) async-start(), calls=%async_computation.21 | async-start | bytes 9437184 | tf_op jit(solution)/shard_map/all_gather | solution.py:255
  96.0 968.4 %copy-start.74 = (bf16[256,8,64]{0,2,1:T(8,128)(2,1)}, bf16[256,8,64]{0,2,1:T(8,128)(2,1)S(1)}, u32[]{:S(2)}) copy-start(bf16[256,8,64]{0,2,1:T(8,128)(2,1)S(1)} %get-tuple-element.122) | copy-start | bytes 786436
  96.0 968.4 %copy-start.76 = (bf16[256,8,64]{0,2,1:T(8,128)(2,1)}, bf16[256,8,64]{0,2,1:T(8,128)(2,1)S(1)}, u32[]{:S(2)}) copy-start(bf16[256,8,64]{0,2,1:T(8,128)(2,1)S(1)} %get-tuple-element.123) | copy-start | bytes 786436
  109.3 12.0 all-to-all-start.3
  121.2 20.4 all-to-all-start.6
  141.6 14.1 all-to-all-start
  155.8 159.5 %all-to-all-start.8 = ((bf16[8,32,64,128]{3,2,1,0:T(8,128)(2,1)}), bf16[8,32,64,128]{3,2,1,0:T(8,128)(2,1)}, u32[]{:S(2)}, u32[]{:S(2)}) async-start(bf16[8,32,64,128]{3,2,1,0:T(8,128)(2,1)} %bitcast.534), calls=%async_computation.8 | async-start | bytes 8388608 | tf_op jit(solution)/shard_map/all_to_all | solution.py:170
  161.7 845.4 %all-gather.29.cloned.1.call-start = ((), (), s32[]{:S(2)}) async-start(), calls=%async_computation.27 | async-start | bytes 9437184 | tf_op jit(solution)/shard_map/all_gather | solution.py:255
  315.2 167.4 %all-to-all-start.5 = ((bf16[8,32,64,128]{3,2,1,0:T(8,128)(2,1)}), bf16[8,32,64,128]{3,2,1,0:T(8,128)(2,1)}, u32[]{:S(2)}, u32[]{:S(2)}) async-start(bf16[8,32,64,128]{3,2,1,0:T(8,128)(2,1)} %bitcast.538), calls=%async_computation.5 | async-start | bytes 8388608 | tf_op jit(solution)/shard_map/all_to_all | solution.py:170
  482.6 183.9 %all-to-all-start.2 = ((bf16[8,32,64,128]{3,2,1,0:T(8,128)(2,1)}), bf16[8,32,64,128]{3,2,1,0:T(8,128)(2,1)}, u32[]{:S(2)}, u32[]{:S(2)}) async-start(bf16[8,32,64,128]{3,2,1,0:T(8,128)(2,1)} %bitcast.535), calls=%async_computation.2 | async-start | bytes 8388608 | tf_op jit(solution)/shard_map/all_to_all | solution.py:170
  494.9 606.0 %all-gather.21.cloned.1.call-start = ((), (), s32[]{:S(2)}) async-start(), calls=%async_computation.23 | async-start | bytes 2621440 | tf_op jit(solution)/shard_map/all_gather | solution.py:216
  666.6 112.9 %all-to-all-start.7 = ((bf16[8,32,64,128]{3,2,1,0:T(8,128)(2,1)}), bf16[8,32,64,128]{3,2,1,0:T(8,128)(2,1)}, u32[]{:S(2)}, u32[]{:S(2)}) async-start(bf16[8,32,64,128]{3,2,1,0:T(8,128)(2,1)} %bitcast.537), calls=%async_computation.7 | async-start | bytes 8388608 | tf_op jit(solution)/shard_map/all_to_all | solution.py:171
  671.1 452.0 %all-gather.25.cloned.1.call-start = ((), (), s32[]{:S(2)}) async-start(), calls=%async_computation.25 | async-start | bytes 7208960 | tf_op jit(solution)/shard_map/all_gather | solution.py:218
  779.4 96.1 %all-to-all-start.4 = ((bf16[8,32,64,128]{3,2,1,0:T(8,128)(2,1)}), bf16[8,32,64,128]{3,2,1,0:T(8,128)(2,1)}, u32[]{:S(2)}, u32[]{:S(2)}) async-start(bf16[8,32,64,128]{3,2,1,0:T(8,128)(2,1)} %bitcast.536), calls=%async_computation.4 | async-start | bytes 8388608 | tf_op jit(solution)/shard_map/all_to_all | solution.py:171
  784.1 345.2 %all-gather.23.cloned.1.call-start = ((), (), s32[]{:S(2)}) async-start(), calls=%async_computation.24 | async-start | bytes 7208960 | tf_op jit(solution)/shard_map/all_gather | solution.py:217
  875.5 97.2 %all-to-all-start.1 = ((bf16[8,32,64,128]{3,2,1,0:T(8,128)(2,1)}), bf16[8,32,64,128]{3,2,1,0:T(8,128)(2,1)}, u32[]{:S(2)}, u32[]{:S(2)}) async-start(bf16[8,32,64,128]{3,2,1,0:T(8,128)(2,1)} %bitcast.533), calls=%async_computation.1 | async-start | bytes 8388608 | tf_op jit(solution)/shard_map/all_to_all | solution.py:171
  880.2 255.1 %all-gather.27.cloned.1.call-start = ((), (), s32[]{:S(2)}) async-start(), calls=%async_computation.26 | async-start | bytes 7208960 | tf_op jit(solution)/shard_map/all_gather | solution.py:219
  880.8 575.6 %reduce-scatter.11.cloned.1.call-start = ((), (), s32[]{:S(2)}) async-start(), calls=%async_computation.29 | async-start | bytes 9437184 | tf_op jit(solution)/shard_map/reduce_scatter | solution.py:314
  1206.7 300.4 %reduce-scatter.13.cloned.1.call-start = ((), (), s32[]{:S(2)}) async-start(), calls=%async_computation.30 | async-start | bytes 9437184 | tf_op jit(solution)/shard_map/reduce_scatter | solution.py:314
  1306.1 352.6 %reduce-scatter.15.cloned.1.call-start = ((), (), s32[]{:S(2)}) async-start(), calls=%async_computation.31 | async-start | bytes 9437184 | tf_op jit(solution)/shard_map/reduce_scatter | solution.py:314
  1359.6 364.3 %reduce-scatter.23.cloned.1.call-start = ((), (), s32[]{:S(2)}) async-start(), calls=%async_computation.35 | async-start | bytes 2621440 | tf_op jit(solution)/shard_map/reduce_scatter | solution.py:363
  1365.7 383.3 %reduce-scatter.27.cloned.1.call-start = ((), (), s32[]{:S(2)}) async-start(), calls=%async_computation.37 | async-start | bytes 7208960 | tf_op jit(solution)/shard_map/reduce_scatter | solution.py:369
  1384.0 422.4 %reduce-scatter.25.cloned.1.call-start = ((), (), s32[]{:S(2)}) async-start(), calls=%async_computation.36 | async-start | bytes 7208960 | tf_op jit(solution)/shard_map/reduce_scatter | solution.py:366
  1403.7 460.1 %reduce-scatter.29.cloned.1.call-start = ((), (), s32[]{:S(2)}) async-start(), calls=%async_computation.38 | async-start | bytes 7208960 | tf_op jit(solution)/shard_map/reduce_scatter | solution.py:372
  1423.0 475.3 %reduce-scatter.21.cloned.1.call-start = ((), (), s32[]{:S(2)}) async-start(), calls=%async_computation.34 | async-start | bytes 2621440 | tf_op jit(solution)/shard_map/reduce_scatter | solution.py:360
  1664.7 268.1 %reduce-scatter.19.cloned.1.call-start = ((), (), s32[]{:S(2)}) async-start(), calls=%async_computation.33 | async-start | bytes 2621440 | tf_op jit(solution)/shard_map/reduce_scatter | solution.py:357
  1714.0 253.4 %reduce-scatter.17.cloned.1.call-start = ((), (), s32[]{:S(2)}) async-start(), calls=%async_computation.32 | async-start | bytes 2621440 | tf_op jit(solution)/shard_map/reduce_scatter | solution.py:354
  1722.3 472.1 %all-reduce.19.cloned.1.call-start = ((), (), s32[]{:S(2)}) async-start(), calls=%async_computation.39 | async-start | bytes 12845056 | tf_op jit(solution)/shard_map/psum | solution.py:383
  (153 other events, 5338.7 us)
Sparse Core Ops, SparseCore 0:
  9.6 25.2 all-gather.12
  36.5 22.5 all-gather.18
  60.7 22.5 all-gather.14
  88.0 193.8 all-gather.30
  284.4 207.3 all-gather.16
  494.4 255.9 all-gather.28
  751.9 21.2 all-gather.20
  774.7 43.3 all-gather.24
  819.7 43.3 all-gather.22
  882.3 44.8 all-gather.26
  1206.8 148.2 reduce-scatter.10
  1359.0 147.9 reduce-scatter.12
  1510.7 148.0 reduce-scatter.14
  1661.3 30.4 reduce-scatter.22
  1694.1 54.8 reduce-scatter.26
  1751.6 54.8 reduce-scatter.24
  1808.8 54.8 reduce-scatter.28
  1866.9 31.4 reduce-scatter.20
  1901.4 31.4 reduce-scatter.18
  1936.0 31.4 reduce-scatter.16
  1972.9 221.4 all-reduce.18
where the time goes:
time: 2230 us; the launch traced here: 2210 us
  waiting for transfers between devices  1310 us (59%)
  matrix products  379 us (17%)
  local copies, waits for them, and re-layouts  319 us (14%)
  other arithmetic  90.3 us (4%)
  starting transfers between devices  54.5 us (2%)
  blocking collectives  40.4 us (2%)
    all_to_all x3, waiting for transfers between devices, fetch(): lax.all_to_all(sent_keys, 'ctx', split_axis=0, concat_axis=0, tiled=True)  438 us
    all_to_all x3, waiting for transfers between devices, fetch(): lax.all_to_all(sent_values, 'ctx', split_axis=0, concat_axis=0, tiled=True)  217 us
    reduce_scatter x3, waiting for transfers between devices, body(): lax.psum_scatter(folded[1].astype(jnp.bfloat16), 'ctx', scatter_dimension...  195 us
    psum x1, waiting for transfers between devices, body(): lax.psum(shards[0].astype(jnp.bfloat16), 'ctx').astype(jnp.float32)  169 us
    unnamed x335, local copies, waits for them, and re-layouts  106 us
    reduce_scatter x1, waiting for transfers between devices, body(): lax.psum_scatter(totals[4].astype(jnp.bfloat16), 'fsdp', scatter_dimensio...  57.4 us
    reduce_scatter x1, waiting for transfers between devices, body(): lax.psum_scatter(totals[6].astype(jnp.bfloat16), 'fsdp', scatter_dimensio...  57.3 us
    dot_general x3, matrix products, attend_piece(): jnp.einsum('qhd,khd->hqk', query, keys, preferred_element_type=jnp.float32)  45.1 us
  transfers between devices with their start and end apart: 30, of which 19 were waited for; matrix products, arithmetic and copies ran while one was open for 31% of the time, Pallas kernels for 0%

commit v1 on v0

v1 whole, which is shorter than its diff:
```python
import functools

import jax
import jax.numpy as jnp
from jax import lax
from jax.experimental import pallas as pl
from jax.experimental.pallas import tpu as pltpu
from jax.sharding import PartitionSpec as P

D = 1024
HEADS = 8
HEAD_DIM = 128
HALF = 128
ROWS = 2 * HALF
BLOCK = 64
TOPK = 4
SIDE = HEADS // 2
SW = SIDE * HEAD_DIM
GROUP = 4
EPS = 1e-05
SCALE = HEAD_DIM**-0.5
LOG2E = 1.4426950408889634
F32 = jnp.float32
BF16 = jnp.bfloat16
EXTRA = 16
SENT = ROWS + EXTRA
VMEM_LIMIT = 56 * 2**20


def nn(a, b):
    return lax.dot_general(a, b, (((1,), (0,)), ((), ())), preferred_element_type=F32)


def nt(a, b):
    return lax.dot_general(a, b, (((1,), (1,)), ((), ())), preferred_element_type=F32)


def tn(a, b):
    return lax.dot_general(a, b, (((0,), (0,)), ((), ())), preferred_element_type=F32)


def params(**more):
    return pltpu.CompilerParams(vmem_limit_bytes=VMEM_LIMIT, **more)


def ring_order(count):
    if count == 8:
        return [0, 2, 4, 6, 7, 5, 3, 1]
    half = count // 2
    return list(range(half)) + [count - 1 - i for i in range(count - half)]


def list_base(count):
    return 1 + 2 * count


def list_at(owner, micro, side, micros, cap):
    return ((owner * micros + micro) * 2 + side) * (cap + 1)


def make_meta(indices, partner, cb_dev, count):
    micros = indices.shape[0]
    here = lax.axis_index("ctx")
    order = ring_order(count)
    place = sum(jnp.where(here == d, p, 0) for p, d in enumerate(order))
    steps = jnp.arange(count, dtype=jnp.int32)
    at = jnp.stack([(place - steps) % count, (place + steps) % count], axis=1)
    owners = sum(jnp.where(at == p, d, 0) for p, d in enumerate(order))
    blocks = cb_dev * count
    cap = 2 * 128 // count
    side_shape = (micros, count, 2 * ROWS // (2 * BLOCK), 2, SIDE, TOPK)
    index = indices.reshape(side_shape).transpose(1, 0, 3, 2, 4, 5)
    index = index.reshape(count, micros, 2, -1)
    number = index % blocks
    mine = (number // cb_dev) == here
    own = jnp.arange(micros, dtype=jnp.int32)[None, :, None, None]
    document = jnp.where(index < blocks, own, partner[None, :, None, None])
    entries = index.shape[-1]
    entry = jnp.arange(entries, dtype=jnp.int32)
    query_block = entry // (SIDE * TOPK)
    head = entry // TOPK % SIDE
    code = ((document * cb_dev + number % cb_dev) * 4 + query_block) * SIDE + head
    before = (entry[:, None] < entry[None, :]).astype(F32)
    flags = mine.astype(F32)
    rank = jnp.dot(flags.reshape(-1, entries), before, preferred_element_type=F32).reshape(flags.shape)
    rank = rank.astype(jnp.int32)
    slot = jnp.arange(cap, dtype=jnp.int32)
    hit = mine[..., None, :] & (rank[..., None, :] == slot[:, None])
    codes = jnp.sum(jnp.where(hit, code[..., None, :], 0), axis=-1)
    length = jnp.sum(mine.astype(jnp.int32), axis=-1, keepdims=True)
    lists = jnp.concatenate([length, codes], axis=-1).reshape(-1)
    return jnp.concatenate([here.reshape(1), owners.reshape(-1), lists]).astype(jnp.int32), cap


def collect_kernel(meta, ck, cv, mk, mv, sem_k, sem_v, *, micros, count, cap):
    owner = pl.program_id(0)

    def groups(i):
        base = list_base(count) + (owner * 2 * micros + i) * (cap + 1)
        return base, (meta[base] + GROUP - 1) // GROUP

    def start(i, carry):
        base, rounds = groups(i)

        def one(g, c):
            for u in range(GROUP):
                j = g * GROUP + u
                code = meta[base + 1 + j]
                head = (i & 1) * SIDE + (code & (SIDE - 1))
                rows = pl.ds(pl.multiple_of((code >> 4) << 6, BLOCK), BLOCK)
                cols = pl.ds(pl.multiple_of(head << 7, HEAD_DIM), HEAD_DIM)
                pltpu.make_async_copy(ck.at[rows, cols], mk.at[i >> 1, 0, i & 1, j], sem_k).start()
                pltpu.make_async_copy(cv.at[rows, cols], mv.at[i >> 1, 0, i & 1, j], sem_v).start()
            return c

        return lax.fori_loop(0, rounds, one, carry)

    def finish(i, carry):
        _, rounds = groups(i)

        def one(g, c):
            some = pl.ds(g * GROUP, GROUP)
            for place, sem in ((mk, sem_k), (mv, sem_v)):
                whole = place.at[i >> 1, 0, i & 1, some]
                pltpu.make_async_copy(whole, whole, sem).wait()
            return c

        return lax.fori_loop(0, rounds, one, carry)

    lax.fori_loop(0, 2 * micros, start, 0)
    lax.fori_loop(0, 2 * micros, finish, 0)


def collect(meta, cache_keys, cache_values, count, cap):
    micros = cache_keys.shape[0]
    shape = jax.ShapeDtypeStruct((micros, count, 2, cap, BLOCK, HEAD_DIM), BF16)
    anywhere = pl.BlockSpec(memory_space=pl.ANY)
    block = pl.BlockSpec((micros, 1, 2, cap, BLOCK, HEAD_DIM), lambda o, meta: (0, o, 0, 0, 0, 0))
    return pl.pallas_call(
        functools.partial(collect_kernel, micros=micros, count=count, cap=cap),
        grid_spec=pltpu.PrefetchScalarGridSpec(
            num_scalar_prefetch=1,
            grid=(count,),
            in_specs=[anywhere, anywhere],
            out_specs=[block, block],
            scratch_shapes=[pltpu.SemaphoreType.DMA, pltpu.SemaphoreType.DMA],
        ),
        out_shape=[shape, shape],
        compiler_params=params(),
        name="collect",
        cost_estimate=pl.CostEstimate(flops=0, bytes_accessed=90_000_000, transcendentals=0),
    )(meta, cache_keys.reshape(-1, D), cache_values.reshape(-1, D))


def turn(value, cosine, sine):
    return value * cosine + pltpu.roll(value, HEAD_DIM // 2, 1) * sine


def first_kernel(x, gain, weight, cosine, sine, normed, qa, qb):
    value = x[0].astype(F32)
    scale = lax.rsqrt(jnp.mean(value * value, axis=-1, keepdims=True) + EPS)
    low = (value * scale * gain[...]).astype(BF16)
    normed[0] = low
    product = nn(low, weight[...])
    for h in range(HEADS):
        cols = slice(h * HEAD_DIM, (h + 1) * HEAD_DIM)
        out = qa if h < SIDE else qb
        place = slice((h % SIDE) * HEAD_DIM, (h % SIDE + 1) * HEAD_DIM)
        out[0, :, place] = turn(product[:, cols], cosine[...], sine[...]).astype(BF16)


def second_kernel(normed, key_weight, value_weight, cosine, sine, keys, values):
    low = normed[0]
    product = nn(low, key_weight[...])
    for h in range(HEADS):
        cols = slice(h * HEAD_DIM, (h + 1) * HEAD_DIM)
        keys[0, :, cols] = turn(product[:, cols], cosine[...], sine[...]).astype(BF16)
    values[0] = nn(low, value_weight[...]).astype(BF16)


def seq_spec(*shape):
    return pl.BlockSpec((1,) + shape, lambda m, *_: (m,) + (0,) * len(shape))


def full_spec(*shape):
    return pl.BlockSpec(shape, lambda m, *_: (0,) * len(shape))


def seq_shape(micros, *shape, dtype=BF16):
    return jax.ShapeDtypeStruct((micros,) + shape, dtype)


def project_query(x, gain, weight, cosine, sine):
    micros = x.shape[0]
    return pl.pallas_call(
        first_kernel,
        grid=(micros,),
        in_specs=[
            seq_spec(ROWS, D),
            full_spec(1, D),
            full_spec(D, D),
            full_spec(ROWS, HEAD_DIM),
            full_spec(ROWS, HEAD_DIM),
        ],
        out_specs=[seq_spec(ROWS, D), seq_spec(ROWS, SW), seq_spec(ROWS, SW)],
        out_shape=[seq_shape(micros, ROWS, D), seq_shape(micros, ROWS, SW), seq_shape(micros, ROWS, SW)],
        compiler_params=params(),
        name="project_query",
        cost_estimate=pl.CostEstimate(flops=2 * micros * ROWS * D * D, bytes_accessed=8_000_000, transcendentals=0),
    )(x, gain, weight, cosine, sine)


def project_pairs(normed, key_weight, value_weight, cosine, sine):
    micros = normed.shape[0]
    return pl.pallas_call(
        second_kernel,
        grid=(micros,),
        in_specs=[
            seq_spec(ROWS, D),
            full_spec(D, D),
            full_spec(D, D),
            full_spec(ROWS, HEAD_DIM),
            full_spec(ROWS, HEAD_DIM),
        ],
        out_specs=[seq_spec(ROWS, D), seq_spec(ROWS, D)],
        out_shape=[seq_shape(micros, ROWS, D), seq_shape(micros, ROWS, D)],
        compiler_params=params(),
        name="project_pairs",
        cost_estimate=pl.CostEstimate(flops=4 * micros * ROWS * D * D, bytes_accessed=10_000_000, transcendentals=0),
    )(normed, key_weight, value_weight, cosine, sine)


def causal_mask():
    row = lax.broadcasted_iota(jnp.int32, (ROWS, ROWS), 0)
    col = lax.broadcasted_iota(jnp.int32, (ROWS, ROWS), 1)
    return row >= col


def to_lanes(wide):
    lane = lax.broadcasted_iota(jnp.int32, (ROWS, HEAD_DIM), 1)
    packed = jnp.zeros((ROWS, HEAD_DIM), F32)
    for h in range(SIDE):
        packed = jnp.where(lane == h, wide[:, h * HEAD_DIM : (h + 1) * HEAD_DIM], packed)
    return packed.T[:8]


def to_columns(lanes):
    return jnp.concatenate([lanes, jnp.zeros((HEAD_DIM - 8, ROWS), F32)], axis=0).T


def split3(value):
    high = value.astype(BF16).astype(F32)
    middle = (value - high).astype(BF16).astype(F32)
    return high, middle, value - high - middle


def pack_lanes(lanes):
    high, middle, low = split3(lanes)
    rows = jnp.concatenate(
        [jnp.concatenate([high, middle], axis=1), jnp.concatenate([low, jnp.zeros_like(low)], axis=1)],
        axis=0,
    )
    return rows.astype(BF16)


def unpack_lanes(rows):
    value = rows.astype(F32)
    return value[:8, :ROWS] + value[:8, ROWS:] + value[8:, :ROWS]


def forward_kernel(meta, qa, qb, k, v, mka, mkb, mva, mvb, pa, pb, ta, tb, wide, *, step, count, cap, micros):
    micro = pl.program_id(0)
    here = meta[0]
    for side, (q, mk, mv, part, total) in enumerate(
        ((qa, mka, mva, pa, ta), (qb, mkb, mvb, pb, tb))
    ):
        owner = meta[1 + 2 * step + side]

        def local(qrows, krows, masked):
            for h in range(SIDE):
                cols = slice(h * HEAD_DIM, (h + 1) * HEAD_DIM)
                kcols = slice((side * SIDE + h) * HEAD_DIM, (side * SIDE + h + 1) * HEAD_DIM)
                keys = k[0, krows, kcols]
                values = v[0, krows, kcols]
                score = nt(q[0, qrows, cols], keys)
                weight = jnp.exp2(score * (SCALE * LOG2E))
                if masked:
                    weight = jnp.where(causal_mask(), weight, 0.0)
                more = jnp.concatenate([values, jnp.ones_like(values)], axis=1)
                out = nn(weight.astype(BF16), more)
                part[0, qrows, cols] = out[:, :HEAD_DIM]
                wide[qrows, cols] = out[:, HEAD_DIM:]

        everything = slice(0, ROWS)
        low = slice(0, HALF)
        high = slice(HALF, ROWS)
        if step == 0:
            local(everything, everything, True)
        else:

            @pl.when(owner < here)
            def _():
                part[0, low, :] = jnp.zeros((HALF, SW), F32)
                wide[low, :] = jnp.zeros((HALF, SW), F32)
                local(high, everything, False)

            @pl.when(owner > here)
            def _():
                local(everything, low, False)

        base = list_base(count) + list_at(owner, micro, side, micros, cap)
        length = meta[base]

        def group(i, carry):
            for j in range(GROUP):
                slot = i * GROUP + j
                code = meta[base + 1 + slot]
                rows = pl.ds(pl.multiple_of(code // SIDE % 4 * BLOCK, BLOCK), BLOCK)
                cols = pl.ds(pl.multiple_of(code % SIDE * HEAD_DIM, HEAD_DIM), HEAD_DIM)
                keys = mk[0, 0, 0, slot]
                values = mv[0, 0, 0, slot]
                score = nt(q[0, rows, cols], keys)
                weight = jnp.exp2(score * (SCALE * LOG2E))
                weight = jnp.where(slot < length, weight, 0.0).astype(BF16)
                more = jnp.concatenate([values, jnp.ones_like(values)], axis=1)
                out = nn(weight, more)
                part[0, rows, cols] += out[:, :HEAD_DIM]
                wide[rows, cols] += out[:, HEAD_DIM:]
            return carry

        lax.fori_loop(0, (length + GROUP - 1) // GROUP, group, 0)
        total[0] = to_lanes(wide[...])


def memory_specs(step, cap):
    def spec(side):
        return pl.BlockSpec(
            (1, 1, 1, cap, BLOCK, HEAD_DIM),
            lambda m, meta: (m, meta[1 + 2 * step + side], side, 0, 0, 0),
        )

    return [spec(0), spec(1), spec(0), spec(1)]


def attend(meta, qa, qb, keys, values, memory_keys, memory_values, step, count, cap):
    micros = qa.shape[0]
    return pl.pallas_call(
        functools.partial(forward_kernel, step=step, count=count, cap=cap, micros=micros),
        grid_spec=pltpu.PrefetchScalarGridSpec(
            num_scalar_prefetch=1,
            grid=(micros,),
            in_specs=[seq_spec(ROWS, SW), seq_spec(ROWS, SW), seq_spec(ROWS, D), seq_spec(ROWS, D)]
            + memory_specs(step, cap),
            out_specs=[seq_spec(ROWS, SW), seq_spec(ROWS, SW), seq_spec(8, ROWS), seq_spec(8, ROWS)],
            scratch_shapes=[pltpu.VMEM((ROWS, SW), F32)],
        ),
        out_shape=[
            seq_shape(micros, ROWS, SW, dtype=F32),
            seq_shape(micros, ROWS, SW, dtype=F32),
            seq_shape(micros, 8, ROWS, dtype=F32),
            seq_shape(micros, 8, ROWS, dtype=F32),
        ],
        compiler_params=params(),
        name="attend",
        cost_estimate=pl.CostEstimate(flops=8_000_000_000, bytes_accessed=14_000_000, transcendentals=0),
    )(meta, qa, qb, keys, values, memory_keys, memory_keys, memory_values, memory_values)


def combine_kernel(*refs, carried, sums):
    refs = list(refs)
    received = [refs.pop(0), refs.pop(0)] if carried else [None, None]
    parts = [refs.pop(0), refs.pop(0)]
    totals = [refs.pop(0), refs.pop(0)] if sums else [None, None]
    for got, part, total, out in zip(received, parts, totals, refs):
        value = part[0]
        if carried:
            value = value + got[0, :ROWS].astype(F32)
        out[0, :ROWS] = value.astype(BF16)
        if sums:
            lanes = total[0]
            if carried:
                lanes = lanes + unpack_lanes(got[0, ROWS:])
            out[0, ROWS:] = pack_lanes(lanes)


def combine(received, parts, totals=()):
    micros = parts[0].shape[0]
    sent = SENT if totals else ROWS
    half, lanes, packed = seq_spec(ROWS, SW), seq_spec(8, ROWS), seq_spec(sent, SW)
    return pl.pallas_call(
        functools.partial(combine_kernel, carried=bool(received), sums=bool(totals)),
        grid=(micros,),
        in_specs=[packed] * len(received) + [half] * 2 + [lanes] * len(totals),
        out_specs=[packed, packed],
        out_shape=[seq_shape(micros, sent, SW)] * 2,
        compiler_params=params(),
        name="combine",
        cost_estimate=pl.CostEstimate(flops=2_000_000, bytes_accessed=7_000_000, transcendentals=0),
    )(*received, *parts, *totals)


def finish_kernel(acc_a, acc_b, pa, pb, ta, tb, mixed, low, total):
    for side, (acc, part, own) in enumerate(((acc_a, pa, ta), (acc_b, pb, tb))):
        lanes = unpack_lanes(acc[0, ROWS:]) + own[0]
        total[0, side] = lanes
        columns = to_columns(lanes)
        for h in range(SIDE):
            cols = slice(h * HEAD_DIM, (h + 1) * HEAD_DIM)
            place = slice((side * SIDE + h) * HEAD_DIM, (side * SIDE + h + 1) * HEAD_DIM)
            weighted = acc[0, :ROWS, cols].astype(F32) + part[0, :, cols]
            value = weighted / columns[:, h : h + 1]
            mixed[0, :, place] = value
            low[0, :, place] = value.astype(BF16)


def finish(acc_a, acc_b, pa, pb, ta, tb):
    micros = acc_a.shape[0]
    packed, half, lanes = seq_spec(SENT, SW), seq_spec(ROWS, SW), seq_spec(8, ROWS)
    return pl.pallas_call(
        finish_kernel,
        grid=(micros,),
        in_specs=[packed, packed, half, half, lanes, lanes],
        out_specs=[seq_spec(ROWS, D), seq_spec(ROWS, D), seq_spec(2, 8, ROWS)],
        out_shape=[
            seq_shape(micros, ROWS, D, dtype=F32),
            seq_shape(micros, ROWS, D),
            seq_shape(micros, 2, 8, ROWS, dtype=F32),
        ],
        compiler_params=params(),
        name="finish",
        cost_estimate=pl.CostEstimate(flops=3_000_000, bytes_accessed=10_000_000, transcendentals=0),
    )(acc_a, acc_b, pa, pb, ta, tb)


def prepare_kernel(back_attn, weight, mixed, total, da, db):
    lane = lax.broadcasted_iota(jnp.int32, (ROWS, HEAD_DIM), 1)
    for side, out in enumerate((da, db)):
        columns = to_columns(total[0, side])
        packed = jnp.zeros((ROWS, HEAD_DIM), F32)
        back = nt(back_attn[0], weight[side * SW : (side + 1) * SW, :])
        for h in range(SIDE):
            cols = slice(h * HEAD_DIM, (h + 1) * HEAD_DIM)
            place = slice((side * SIDE + h) * HEAD_DIM, (side * SIDE + h + 1) * HEAD_DIM)
            part = back[:, cols]
            divisor = columns[:, h : h + 1]
            out[0, :ROWS, cols] = (part / divisor).astype(BF16)
            product = jnp.sum(part * mixed[0, :, place], axis=1, keepdims=True)
            packed = jnp.where(lane == h, -product / divisor, packed)
        out[0, ROWS:] = pack_lanes(packed.T[:8])


def prepare(back_attn, weight, mixed, total):
    micros = back_attn.shape[0]
    return pl.pallas_call(
        prepare_kernel,
        grid=(micros,),
        in_specs=[seq_spec(ROWS, D), full_spec(D, D), seq_spec(ROWS, D), seq_spec(2, 8, ROWS)],
        out_specs=[seq_spec(SENT, SW), seq_spec(SENT, SW)],
        out_shape=[seq_shape(micros, SENT, SW)] * 2,
        compiler_params=params(),
        name="prepare",
        cost_estimate=pl.CostEstimate(flops=2 * micros * ROWS * D * D, bytes_accessed=10_000_000, transcendentals=0),
    )(back_attn, weight, mixed, total)


def backward_kernel(
    meta, qa, qb, da, db, k, v, mka, mkb, mva, mvb, *rest, step, count, cap, micros
):
    if step == 0:
        dqa, dqb, dk, dv, wide = rest
    else:
        dk_in, dv_in, dqa, dqb, dk, dv, wide = rest
    micro = pl.program_id(0)
    here = meta[0]
    if step == 0:
        dk[...] = jnp.zeros_like(dk)
        dv[...] = jnp.zeros_like(dv)
    else:
        dk[...] = dk_in[...]
        dv[...] = dv_in[...]
    for side, (q, d, mk, mv, dq) in enumerate(
        ((qa, da, mka, mva, dqa), (qb, db, mkb, mvb, dqb))
    ):
        owner = meta[1 + 2 * step + side]
        columns = to_columns(unpack_lanes(d[0, ROWS:]))
        for h in range(SIDE):
            cols = slice(h * HEAD_DIM, (h + 1) * HEAD_DIM)
            wide[:, cols] = jnp.broadcast_to(columns[:, h : h + 1], (ROWS, HEAD_DIM))

        def local(qrows, krows, masked):
            for h in range(SIDE):
                cols = slice(h * HEAD_DIM, (h + 1) * HEAD_DIM)
                kcols = slice((side * SIDE + h) * HEAD_DIM, (side * SIDE + h + 1) * HEAD_DIM)
                keys = k[0, krows, kcols]
                values = v[0, krows, kcols]
                query = q[0, qrows, cols]
                back = d[0, qrows, cols]
                score = nt(query, keys)
                weight = jnp.exp2(score * (SCALE * LOG2E))
                if masked:
                    weight = jnp.where(causal_mask(), weight, 0.0)
                slope = nt(back, values) + wide[qrows, cols][:, :1]
                slope = (weight * slope).astype(BF16)
                dq[0, qrows, cols] = nn(slope, keys)
                dk[0, krows, kcols] += tn(slope, query)
                dv[0, krows, kcols] += tn(weight.astype(BF16), back)

        everything = slice(0, ROWS)
        low = slice(0, HALF)
        high = slice(HALF, ROWS)
        if step == 0:
            local(everything, everything, True)
        else:

            @pl.when(owner < here)
            def _():
                dq[0, low, :] = jnp.zeros((HALF, SW), F32)
                local(high, everything, False)

            @pl.when(owner > here)
            def _():
                local(everything, low, False)

        base = list_base(count) + list_at(owner, micro, side, micros, cap)
        length = meta[base]

        def group(i, carry):
            for j in range(GROUP):
                slot = i * GROUP + j
                code = meta[base + 1 + slot]
                rows = pl.ds(pl.multiple_of(code // SIDE % 4 * BLOCK, BLOCK), BLOCK)
                cols = pl.ds(pl.multiple_of(code % SIDE * HEAD_DIM, HEAD_DIM), HEAD_DIM)
                keys = mk[0, 0, 0, slot]
                values = mv[0, 0, 0, slot]
                score = nt(q[0, rows, cols], keys)
                weight = jnp.exp2(score * (SCALE * LOG2E))
                slope = nt(d[0, rows, cols], values) + wide[rows, cols][:, :BLOCK]
                slope = jnp.where(slot < length, weight * slope, 0.0).astype(BF16)
                dq[0, rows, cols] += nn(slope, keys)
            return carry

        lax.fori_loop(0, (length + GROUP - 1) // GROUP, group, 0)


def unattend(meta, qa, qb, da, db, keys, values, memory_keys, memory_values, sums, step, count, cap):
    micros = qa.shape[0]
    half, packed, whole = seq_spec(ROWS, SW), seq_spec(SENT, SW), seq_spec(ROWS, D)
    carried = [] if sums is None else list(sums)
    first = 11
    return pl.pallas_call(
        functools.partial(backward_kernel, step=step, count=count, cap=cap, micros=micros),
        grid_spec=pltpu.PrefetchScalarGridSpec(
            num_scalar_prefetch=1,
            grid=(micros,),
            in_specs=[half, half, packed, packed, whole, whole]
            + memory_specs(step, cap)
            + [whole] * len(carried),
            out_specs=[half, half, whole, whole],
            scratch_shapes=[pltpu.VMEM((ROWS, SW), F32)],
        ),
        out_shape=[
            seq_shape(micros, ROWS, SW, dtype=F32),
            seq_shape(micros, ROWS, SW, dtype=F32),
            seq_shape(micros, ROWS, D, dtype=F32),
            seq_shape(micros, ROWS, D, dtype=F32),
        ],
        input_output_aliases={first: 2, first + 1: 3} if carried else {},
        compiler_params=params(),
        name="unattend",
        cost_estimate=pl.CostEstimate(flops=16_000_000_000, bytes_accessed=30_000_000, transcendentals=0),
    )(
        meta,
        qa,
        qb,
        da,
        db,
        keys,
        values,
        memory_keys,
        memory_keys,
        memory_values,
        memory_values,
        *carried,
    )


def unturn_kernel(acc_a, acc_b, pa, pb, dk, dv, cosine, sine, back):
    for h in range(HEADS):
        acc, part = (acc_a, pa) if h < SIDE else (acc_b, pb)
        cols = slice(h % SIDE * HEAD_DIM, (h % SIDE + 1) * HEAD_DIM)
        place = slice(h * HEAD_DIM, (h + 1) * HEAD_DIM)
        value = (acc[0, :, cols].astype(F32) + part[0, :, cols]) * SCALE
        key_place = slice(D + h * HEAD_DIM, D + (h + 1) * HEAD_DIM)
        back[0, :, place] = turn(value, cosine[...], -sine[...]).astype(BF16)
        back[0, :, key_place] = turn(dk[0, :, place] * SCALE, cosine[...], -sine[...]).astype(BF16)
    back[0, :, 2 * D :] = dv[0].astype(BF16)


def unturn(acc_a, acc_b, pa, pb, dk, dv, cosine, sine):
    micros = acc_a.shape[0]
    half, whole, angle = seq_spec(ROWS, SW), seq_spec(ROWS, D), full_spec(ROWS, HEAD_DIM)
    return pl.pallas_call(
        unturn_kernel,
        grid=(micros,),
        in_specs=[half, half, half, half, whole, whole, angle, angle],
        out_specs=seq_spec(ROWS, 3 * D),
        out_shape=seq_shape(micros, ROWS, 3 * D),
        compiler_params=params(),
        name="unturn",
        cost_estimate=pl.CostEstimate(flops=10_000_000, bytes_accessed=16_000_000, transcendentals=0),
    )(acc_a, acc_b, pa, pb, dk, dv, cosine, sine)


def norm_parts(value):
    scale = lax.rsqrt(jnp.mean(value * value, axis=-1, keepdims=True) + EPS)
    return value * scale, scale


def norm_back(hat, scale, back, gain):
    slope = back * gain
    return scale * (slope - hat * jnp.mean(slope * hat, axis=-1, keepdims=True))


def body(
    tokens,
    cotangent,
    query_weight,
    key_weight,
    value_weight,
    output_weight,
    gate_weight,
    up_weight,
    down_weight,
    first_gain,
    second_gain,
    cache_keys,
    cache_values,
    block_indices,
    partner,
):
    count = lax.axis_size("ctx")
    here = lax.axis_index("ctx")
    micros = tokens.shape[0]
    rows = micros * ROWS
    order = ring_order(count)
    onward = [(order[i], order[(i + 1) % count]) for i in range(count)]
    backward = [(b, a) for a, b in onward]

    def gather(value):
        return lax.all_gather(value, "fsdp", axis=0, tiled=True)

    indices = lax.all_gather(block_indices, "ctx", axis=1, tiled=True)
    gains = lax.all_gather(jnp.stack([first_gain, second_gain]), "fsdp", axis=1, tiled=True)
    full_query = gather(query_weight)
    full_key = gather(key_weight)
    full_value = gather(value_weight)
    full_output = gather(output_weight)
    full_gate = gather(gate_weight)
    full_up = gather(up_weight)
    full_down = gather(down_weight)
    gain_one = gains[0:1].astype(F32)
    gain_two = gains[1:2].astype(F32)

    pieces_at = jnp.stack([here, 2 * count - 1 - here])
    positions = (pieces_at[:, None] * HALF + jnp.arange(HALF, dtype=jnp.int32)[None, :]).reshape(ROWS)
    inverse = 10000.0 ** (-jnp.arange(HEAD_DIM // 2, dtype=F32) * 2.0 / HEAD_DIM)
    phase = positions.astype(F32)[:, None] * inverse[None, :]
    cosine = jnp.tile(jnp.cos(phase), (1, 2))
    sine = jnp.sin(phase)
    sine = jnp.concatenate([-sine, sine], axis=1)

    meta, cap = make_meta(indices, partner, cache_keys.shape[1] // BLOCK, count)
    memory_keys, memory_values = collect(meta, cache_keys, cache_values, count, cap)

    x = tokens.reshape(micros, ROWS, D)
    normed_low, qa, qb = project_query(x, gain_one, full_query, cosine, sine)
    keys, values = project_pairs(normed_low, full_key, full_value, cosine, sine)

    queries = [(qa, qb)]
    for _ in range(count - 1):
        qa, qb = lax.ppermute(qa, "ctx", onward), lax.ppermute(qb, "ctx", backward)
        queries.append((qa, qb))

    acc = ()
    for step in list(range(1, count)) + [0]:
        pa, pb, ta, tb = attend(
            meta, *queries[step], keys, values, memory_keys, memory_values, step, count, cap
        )
        if acc:
            acc = (lax.ppermute(acc[0], "ctx", onward), lax.ppermute(acc[1], "ctx", backward))
        if step == 0:
            mixed, mixed_low, total = finish(*acc, pa, pb, ta, tb)
        else:
            acc = combine(acc, (pa, pb), (ta, tb))

    inputs = tokens.reshape(rows, D).astype(F32)
    mixed_low = mixed_low.reshape(rows, D)
    middle = inputs + jnp.dot(mixed_low, full_output, preferred_element_type=F32)
    mid_hat, mid_scale = norm_parts(middle)
    middle_low = (mid_hat * gain_two).astype(BF16)
    gate = jnp.dot(middle_low, full_gate, preferred_element_type=F32)
    upper = jnp.dot(middle_low, full_up, preferred_element_type=F32)
    sigma = jax.nn.sigmoid(gate)
    silu = gate * sigma
    hidden = (silu * upper).astype(BF16)
    layer_output = (middle + jnp.dot(hidden, full_down, preferred_element_type=F32)).astype(BF16)
    incoming = cotangent.reshape(rows, D)
    gradient_down = jnp.einsum("tf,td->fd", hidden, incoming, preferred_element_type=F32).astype(BF16)
    back_hidden = jnp.einsum("td,fd->tf", incoming, full_down, preferred_element_type=F32)
    back_gate = (back_hidden * upper * (sigma * (1.0 + gate * (1.0 - sigma)))).astype(BF16)
    back_upper = (back_hidden * silu).astype(BF16)
    gradient_gate = jnp.einsum("td,tf->df", middle_low, back_gate, preferred_element_type=F32).astype(BF16)
    gradient_up = jnp.einsum("td,tf->df", middle_low, back_upper, preferred_element_type=F32).astype(BF16)
    back_mid_normed = jnp.einsum(
        "tf,df->td", back_gate, full_gate, preferred_element_type=F32
    ) + jnp.einsum("tf,df->td", back_upper, full_up, preferred_element_type=F32)
    gradient_second = jnp.sum(back_mid_normed * mid_hat, axis=0)
    back_middle = incoming.astype(F32) + norm_back(mid_hat, mid_scale, back_mid_normed, gain_two)
    back_attn = back_middle.astype(BF16)
    gradient_output = jnp.einsum("tc,td->cd", mixed_low, back_attn, preferred_element_type=F32).astype(BF16)

    slopes = [prepare(back_attn.reshape(micros, ROWS, D), full_output, mixed, total)]
    for _ in range(count - 1):
        da, db = slopes[-1]
        slopes.append((lax.ppermute(da, "ctx", onward), lax.ppermute(db, "ctx", backward)))
    slopes[1], (gradient_down, gradient_gate, gradient_up, gradient_output) = lax.optimization_barrier(
        (slopes[1], (gradient_down, gradient_gate, gradient_up, gradient_output))
    )

    sums = None
    acc = ()
    for step in range(count):
        dqa, dqb, dk, dv = unattend(
            meta,
            *queries[step],
            *slopes[step],
            keys,
            values,
            memory_keys,
            memory_values,
            sums,
            step,
            count,
            cap,
        )
        sums = (dk, dv)
        if step == 0:
            own = (dqa, dqb)
            continue
        if acc:
            acc = (lax.ppermute(acc[0], "ctx", onward), lax.ppermute(acc[1], "ctx", backward))
        acc = combine(acc, (dqa, dqb))
    ra, rb = lax.ppermute(acc[0], "ctx", onward), lax.ppermute(acc[1], "ctx", backward)
    back = unturn(ra, rb, *own, *sums, cosine, sine).reshape(rows, 3 * D)
    normed_low = normed_low.reshape(rows, D)
    gradient_three = jnp.einsum("tc,td->cd", normed_low, back, preferred_element_type=F32).astype(BF16)
    back_in_normed = (
        jnp.einsum("td,cd->tc", back[:, :D], full_query, preferred_element_type=F32)
        + jnp.einsum("td,cd->tc", back[:, D : 2 * D], full_key, preferred_element_type=F32)
        + jnp.einsum("td,cd->tc", back[:, 2 * D :], full_value, preferred_element_type=F32)
    )
    in_hat, in_scale = norm_parts(inputs)
    gradient_first = jnp.sum(back_in_normed * in_hat, axis=0)
    input_gradient = back_middle + norm_back(in_hat, in_scale, back_in_normed, gain_one)

    def scatter(part):
        return lax.psum_scatter(part, "fsdp", scatter_dimension=0, tiled=True)

    early = [
        scatter(part) for part in (gradient_down, gradient_gate, gradient_up, gradient_output)
    ]
    early, three = lax.optimization_barrier((lax.psum(early, "ctx"), scatter(gradient_three)))
    early = [part.astype(F32) for part in early]
    three = lax.psum(three, "ctx").astype(F32)
    gain_changes = lax.psum(jnp.stack([gradient_first, gradient_second]), ("ctx", "fsdp"))
    own_rows = D // lax.axis_size("fsdp")
    gain_changes = lax.dynamic_slice_in_dim(
        gain_changes, lax.axis_index("fsdp") * own_rows, own_rows, axis=1
    )
    return (
        layer_output.reshape(tokens.shape),
        input_gradient.reshape(tokens.shape),
        three[:, :D],
        three[:, D : 2 * D],
        three[:, 2 * D :],
        early[3],
        early[1],
        early[2],
        early[0],
        gain_changes[0],
        gain_changes[1],
    )


def solution(mesh):
    split = P("fsdp", "ctx", None, None, None)
    shard = P("fsdp", None)
    return jax.shard_map(
        body,
        mesh=mesh,
        in_specs=(
            split,
            split,
            *([shard] * 7),
            P("fsdp"),
            P("fsdp"),
            P("fsdp", "ctx", None),
            P("fsdp", "ctx", None),
            P("fsdp", "ctx", None, None, None, None),
            P("fsdp"),
        ),
        out_specs=(split, split, *([shard] * 7), P("fsdp"), P("fsdp")),
        check_vma=False,
    )
```

time: 2230 us -> 1100 us (0.49)
  waiting for transfers between devices: 1310 us -> 223 us
  Pallas kernels: 0 us -> 444 us
  local copies, waits for them, and re-layouts: 319 us -> 24.5 us
  matrix products: 379 us -> 130 us
  starting transfers between devices: 54.5 us -> 151 us
  other arithmetic: 90.3 us -> 22 us
  blocking collectives: 40.4 us -> 77.8 us
    all_to_all x9 -> x0, waiting for transfers between devices: 656 us -> none  [the longest x3 438 us: fetch(): lax.all_to_all(sent_keys, 'ctx', split_axis=0, concat_axis=0, tiled=True)]
    pallas_call x0 -> x36, Pallas kernels: none -> 444 us  [the longest x8 193 us: unattend(): pl.pallas_call(functools.partial(backward_kernel, step=step, count=count,...]
    reduce_scatter x10 -> x5, waiting for transfers between devices: 438 us -> 60 us  [scatter(): return lax.psum_scatter(part, 'fsdp', scatter_dimension=0, tiled=True)]
    dot_general x90 -> x16, matrix products: 379 us -> 130 us  [the longest x1 17.1 us: body(): jnp.einsum('td,fd->tf', incoming, full_down, preferred_element_type=F32)]
    ppermute x0 -> x56, starting transfers between devices: none -> 150 us  [the longest x14 54 us: body(): lax.ppermute(acc[1], 'ctx', backward)]
    unnamed x335 -> x158, local copies, waits for them, and re-layouts: 106 us -> 18.5 us
    psum x1 -> x2, waiting for transfers between devices: 169 us -> 86.7 us  [the longest x1 57.3 us: body(): lax.psum(early, 'ctx')]
    gather x12 -> x0, local copies, waits for them, and re-layouts: 73.2 us -> none  [the longest x3 24.1 us: fetch(): sent_values = table_values[picked, :, chosen_head, :]]
  transfers between devices with their start and end apart: 30 -> 70, of which waited for: 19 -> 19; matrix products, arithmetic and copies ran while one was open for 31% -> 9% of each run, Pallas kernels for 0% -> 40%
where the time goes in v1:
time: 1100 us; the launch traced here: 1090 us
  Pallas kernels  444 us (40%)
  waiting for transfers between devices  223 us (20%)
  starting transfers between devices  151 us (14%)
  matrix products  130 us (12%)
  blocking collectives  77.8 us (7%)
  local copies, waits for them, and re-layouts  24.5 us (2%)
  other arithmetic  22 us (2%)
  between operations  15.2 us (1%)
    pallas_call x8, Pallas kernels, unattend(): pl.pallas_call(functools.partial(backward_kernel, step=step, count=count,...  193 us
    pallas_call x8, Pallas kernels, attend(): pl.pallas_call(functools.partial(forward_kernel, step=step, count=count,...  133 us
    reduce_scatter x5, waiting for transfers between devices, scatter(): return lax.psum_scatter(part, 'fsdp', scatter_dimension=0, tiled=True)  60 us
    pallas_call x14, Pallas kernels, combine(): pl.pallas_call(functools.partial(combine_kernel, carried=bool(received),...  57.9 us
    psum x1, waiting for transfers between devices, body(): lax.psum(early, 'ctx')  57.3 us
    ppermute x14, starting transfers between devices, body(): lax.ppermute(acc[1], 'ctx', backward)  54 us
    ppermute x7, starting transfers between devices, body(): lax.ppermute(db, 'ctx', backward)  45.4 us
    psum x1, blocking collectives, body(): lax.psum(jnp.stack([gradient_first, gradient_second]), ('ctx', 'fsdp'))  40.4 us
  transfers between devices with their start and end apart: 70, of which 19 were waited for; matrix products, arithmetic and copies ran while one was open for 9% of the time, Pallas kernels for 40%

profile of v1, /device:TPU:0, one launch (start us, length us, event | category | flops | bytes accessed | tf_op | source)
XLA Modules:
  0.0 1087.0 jit_solution(5821380949619287598)
XLA Ops:
  11.3 32.4 %all_gather.27 = s32[3,8,2,2,8,4]{4,5,3,2,0,1:T(4,128)S(1)} all-gather(s32[3,1,2,2,8,4]{4,5,3,2,0,1:T(4,128)S(1)} %bitcast.109), channel_id=1, replica_groups=mesh['ctx'=8,'fsdp'=4] {'ctx'}, dimensions={1}, use_global_device_ids=true | all-gather | bytes 13824 | tf_op jit(solution)/shard_map/all_gather | solution.py:652
  62.8 25.6 %collect.1 = (bf16[3,8,2,32,64,128]{5,4,3,2,1,0:T(8,128)(2,1)}, bf16[3,8,2,32,64,128]{5,4,3,2,1,0:T(8,128)(2,1)}) custom-call(s32[1601]{0:T(1024)} %concatenate.14.meta, bf16[6144,1024]{1,0:T(8,128)(2,1)} %bitcast.91, bf16[6144,1024]{1,0:T(8,128)(2,1)} %bitcast.92), custom_call_target="tpu_custom_call" | custom-call | bytes 90000000 | tf_op jit(solution)/shard_map/collect/pallas_call | solution.py:139
  101.4 17.0 %attend.8 = (f32[3,256,512]{2,1,0:T(8,128)}, f32[3,256,512]{2,1,0:T(8,128)}, f32[3,8,256]{2,1,0:T(8,128)}, f32[3,8,256]{2,1,0:T(8,128)}) custom-call(s32[1601]{0:T(1024)} %concatenate.14.meta, bf16[3,256,512]{2,1,0:T(8,128)(2,1)} %copy-done.10, bf16[3,256,512]{2,1,0:T(8,128)(2,1)} %copy-done.11, bf16[3,256,1024]{2,1,0:T(8,128)(2,1)} %get-tuple-element.129.k, ...), custom_call_target="tpu_custom_call" | custom-call | flops 8000000000 | bytes 14000000 | tf_op jit(solution)/shard_map/attend/pallas_call | solution.py:347
  134.3 14.3 %attend.9 = (f32[3,256,512]{2,1,0:T(8,128)}, f32[3,256,512]{2,1,0:T(8,128)}, f32[3,8,256]{2,1,0:T(8,128)}, f32[3,8,256]{2,1,0:T(8,128)}) custom-call(s32[1601]{0:T(1024)} %concatenate.14.meta, bf16[3,256,512]{2,1,0:T(8,128)(2,1)} %copy-done.17, bf16[3,256,512]{2,1,0:T(8,128)(2,1)} %copy-done.19, bf16[3,256,1024]{2,1,0:T(8,128)(2,1)} %get-tuple-element.129.k, ...), custom_call_target="tpu_custom_call" | custom-call | flops 8000000000 | bytes 14000000 | tf_op jit(solution)/shard_map/attend/pallas_call | solution.py:347
  170.6 16.3 %attend.10 = (f32[3,256,512]{2,1,0:T(8,128)}, f32[3,256,512]{2,1,0:T(8,128)}, f32[3,8,256]{2,1,0:T(8,128)}, f32[3,8,256]{2,1,0:T(8,128)}) custom-call(s32[1601]{0:T(1024)} %concatenate.14.meta, bf16[3,256,512]{2,1,0:T(8,128)(2,1)} %copy-done.15, bf16[3,256,512]{2,1,0:T(8,128)(2,1)} %copy-done.18, bf16[3,256,1024]{2,1,0:T(8,128)(2,1)} %get-tuple-element.129.k, ...), custom_call_target="tpu_custom_call" | custom-call | flops 8000000000 | bytes 14000000 | tf_op jit(solution)/shard_map/attend/pallas_call | solution.py:347
  205.0 16.8 %attend.11 = (f32[3,256,512]{2,1,0:T(8,128)}, f32[3,256,512]{2,1,0:T(8,128)}, f32[3,8,256]{2,1,0:T(8,128)}, f32[3,8,256]{2,1,0:T(8,128)}) custom-call(s32[1601]{0:T(1024)} %concatenate.14.meta, bf16[3,256,512]{2,1,0:T(8,128)(2,1)} %copy-done.13, bf16[3,256,512]{2,1,0:T(8,128)(2,1)} %copy-done.16, bf16[3,256,1024]{2,1,0:T(8,128)(2,1)} %get-tuple-element.129.k, ...), custom_call_target="tpu_custom_call" | custom-call | flops 8000000000 | bytes 14000000 | tf_op jit(solution)/shard_map/attend/pallas_call | solution.py:347
  237.8 17.0 %attend.12 = (f32[3,256,512]{2,1,0:T(8,128)}, f32[3,256,512]{2,1,0:T(8,128)}, f32[3,8,256]{2,1,0:T(8,128)}, f32[3,8,256]{2,1,0:T(8,128)}) custom-call(s32[1601]{0:T(1024)} %concatenate.14.meta, bf16[3,256,512]{2,1,0:T(8,128)(2,1)} %copy-done.12, bf16[3,256,512]{2,1,0:T(8,128)(2,1)} %copy-done.14, bf16[3,256,1024]{2,1,0:T(8,128)(2,1)} %get-tuple-element.129.k, ...), custom_call_target="tpu_custom_call" | custom-call | flops 8000000000 | bytes 14000000 | tf_op jit(solution)/shard_map/attend/pallas_call | solution.py:347
  272.8 17.7 %attend.13 = (f32[3,256,512]{2,1,0:T(8,128)}, f32[3,256,512]{2,1,0:T(8,128)}, f32[3,8,256]{2,1,0:T(8,128)}, f32[3,8,256]{2,1,0:T(8,128)}) custom-call(s32[1601]{0:T(1024)} %concatenate.14.meta, bf16[3,256,512]{2,1,0:T(8,128)(2,1)} %copy-done.7, bf16[3,256,512]{2,1,0:T(8,128)(2,1)} %copy-done.9, bf16[3,256,1024]{2,1,0:T(8,128)(2,1)} %get-tuple-element.129.k, ...), custom_call_target="tpu_custom_call" | custom-call | flops 8000000000 | bytes 14000000 | tf_op jit(solution)/shard_map/attend/pallas_call | solution.py:347
  303.4 17.7 %attend.14 = (f32[3,256,512]{2,1,0:T(8,128)}, f32[3,256,512]{2,1,0:T(8,128)}, f32[3,8,256]{2,1,0:T(8,128)}, f32[3,8,256]{2,1,0:T(8,128)}) custom-call(s32[1601]{0:T(1024)} %concatenate.14.meta, bf16[3,256,512]{2,1,0:T(8,128)(2,1)} %copy-done.6, bf16[3,256,512]{2,1,0:T(8,128)(2,1)} %copy-done.8, bf16[3,256,1024]{2,1,0:T(8,128)(2,1)} %get-tuple-element.129.k, ...), custom_call_target="tpu_custom_call" | custom-call | flops 8000000000 | bytes 14000000 | tf_op jit(solution)/shard_map/attend/pallas_call | solution.py:347
  330.5 16.3 %attend.15 = (f32[3,256,512]{2,1,0:T(8,128)}, f32[3,256,512]{2,1,0:T(8,128)}, f32[3,8,256]{2,1,0:T(8,128)}, f32[3,8,256]{2,1,0:T(8,128)}) custom-call(s32[1601]{0:T(1024)} %concatenate.14.meta, bf16[3,256,512]{2,1,0:T(8,128)(2,1)} %get-tuple-element.126.qa, bf16[3,256,512]{2,1,0:T(8,128)(2,1)} %get-tuple-element.127.qb, ...), custom_call_target="tpu_custom_call" | custom-call | flops 8000000000 | bytes 14000000 | tf_op jit(solution)/shard_map/attend/pallas_call | solution.py:347
  361.8 11.1 %fusion.47 = f32[768,2816]{1,0:T(8,128)} fusion(bf16[768,1024]{1,0:T(8,128)(2,1)} %multiply_convert_fusion.3, bf16[1024,2816]{1,0:T(8,128)(2,1)} %all-gather.16.cloned.1.call-done), kind=kOutput, calls=%fused_computation.125 | convolution fusion | flops 4429185024 | bytes 15990784 | tf_op jit(solution)/shard_map/dot_general | solution.py:701
  373.0 11.1 %fusion.48 = f32[768,2816]{1,0:T(8,128)} fusion(bf16[768,1024]{1,0:T(8,128)(2,1)} %multiply_convert_fusion.3, bf16[1024,2816]{1,0:T(8,128)(2,1)} %all-gather.18.cloned.1.call-done), kind=kOutput, calls=%fused_computation.126 | convolution fusion | flops 4429185024 | bytes 15990784 | tf_op jit(solution)/shard_map/dot_general | solution.py:702
  384.1 17.1 %multiply_convert_fusion = (bf16[768,2816]{1,0:T(8,128)(2,1)}, bf16[768,2816]{1,0:T(8,128)(2,1)}, bf16[768,2816]{1,0:T(8,128)(2,1)}) fusion(f32[768,2816]{1,0:T(8,128)} %fusion.47, f32[768,2816]{1,0:T(8,128)} %fusion.48, bf16[768,1024]{1,0:T(8,128)(2,1)} %bitcast.93, bf16[2816,1024]{1,0:T(8,128)(2,1)} %all-gather.20.cloned.1.call-done), kind=kOutput, calls=%fused_computation.1 | convolution fusion | flops 4461625344 | bytes 37617664 | tf_op jit(solution)/shard_map/td,fd->tf/dot_general | solution.py:709
  410.0 10.0 convolution_convert_fusion
  477.3 23.3 %unattend.8 = (f32[3,256,512]{2,1,0:T(8,128)}, f32[3,256,512]{2,1,0:T(8,128)}, f32[3,256,1024]{2,1,0:T(8,128)}, f32[3,256,1024]{2,1,0:T(8,128)}) custom-call(s32[1601]{0:T(1024)} %concatenate.14.meta, bf16[3,256,512]{2,1,0:T(8,128)(2,1)} %get-tuple-element.126.qa, bf16[3,256,512]{2,1,0:T(8,128)(2,1)} %get-tuple-element.127.qb, ...), custom_call_target="tpu_custom_call" | custom-call | flops 16000000000 | bytes 30000000 | tf_op jit(solution)/shard_map/unattend/pallas_call | solution.py:550
  504.3 24.3 %unattend.9 = (f32[3,256,512]{2,1,0:T(8,128)}, f32[3,256,512]{2,1,0:T(8,128)}, f32[3,256,1024]{2,1,0:T(8,128)}, f32[3,256,1024]{2,1,0:T(8,128)}) custom-call(s32[1601]{0:T(1024)} %concatenate.14.meta, bf16[3,256,512]{2,1,0:T(8,128)(2,1)} %copy-done.10, bf16[3,256,512]{2,1,0:T(8,128)(2,1)} %copy-done.11, ...), custom_call_target="tpu_custom_call", output_to_operand_aliasing={{2}: (11, {}), {3}: (12, {})} | custom-call | flops 16000000000 | bytes 30000000 | tf_op jit(solution)/shard_map/unattend/pallas_call | solution.py:550
  549.2 21.5 %unattend.10 = (f32[3,256,512]{2,1,0:T(8,128)}, f32[3,256,512]{2,1,0:T(8,128)}, f32[3,256,1024]{2,1,0:T(8,128)}, f32[3,256,1024]{2,1,0:T(8,128)}) custom-call(s32[1601]{0:T(1024)} %concatenate.14.meta, bf16[3,256,512]{2,1,0:T(8,128)(2,1)} %copy-done.17, bf16[3,256,512]{2,1,0:T(8,128)(2,1)} %copy-done.19, ...), custom_call_target="tpu_custom_call", output_to_operand_aliasing={{2}: (11, {}), {3}: (12, {})} | custom-call | flops 16000000000 | bytes 30000000 | tf_op jit(solution)/shard_map/unattend/pallas_call | solution.py:550
  587.1 24.6 %unattend.11 = (f32[3,256,512]{2,1,0:T(8,128)}, f32[3,256,512]{2,1,0:T(8,128)}, f32[3,256,1024]{2,1,0:T(8,128)}, f32[3,256,1024]{2,1,0:T(8,128)}) custom-call(s32[1601]{0:T(1024)} %concatenate.14.meta, bf16[3,256,512]{2,1,0:T(8,128)(2,1)} %copy-done.15, bf16[3,256,512]{2,1,0:T(8,128)(2,1)} %copy-done.18, ...), custom_call_target="tpu_custom_call", output_to_operand_aliasing={{2}: (11, {}), {3}: (12, {})} | custom-call | flops 16000000000 | bytes 30000000 | tf_op jit(solution)/shard_map/unattend/pallas_call | solution.py:550
  619.8 9.9 collective-permute-start.45
  629.7 24.4 %unattend.12 = (f32[3,256,512]{2,1,0:T(8,128)}, f32[3,256,512]{2,1,0:T(8,128)}, f32[3,256,1024]{2,1,0:T(8,128)}, f32[3,256,1024]{2,1,0:T(8,128)}) custom-call(s32[1601]{0:T(1024)} %concatenate.14.meta, bf16[3,256,512]{2,1,0:T(8,128)(2,1)} %copy-done.13, bf16[3,256,512]{2,1,0:T(8,128)(2,1)} %copy-done.16, ...), custom_call_target="tpu_custom_call", output_to_operand_aliasing={{2}: (11, {}), {3}: (12, {})} | custom-call | flops 16000000000 | bytes 30000000 | tf_op jit(solution)/shard_map/unattend/pallas_call | solution.py:550
  668.9 24.4 %unattend.13 = (f32[3,256,512]{2,1,0:T(8,128)}, f32[3,256,512]{2,1,0:T(8,128)}, f32[3,256,1024]{2,1,0:T(8,128)}, f32[3,256,1024]{2,1,0:T(8,128)}) custom-call(s32[1601]{0:T(1024)} %concatenate.14.meta, bf16[3,256,512]{2,1,0:T(8,128)(2,1)} %copy-done.12, bf16[3,256,512]{2,1,0:T(8,128)(2,1)} %copy-done.14, ...), custom_call_target="tpu_custom_call", output_to_operand_aliasing={{2}: (11, {}), {3}: (12, {})} | custom-call | flops 16000000000 | bytes 30000000 | tf_op jit(solution)/shard_map/unattend/pallas_call | solution.py:550
  707.4 24.8 %unattend.14 = (f32[3,256,512]{2,1,0:T(8,128)}, f32[3,256,512]{2,1,0:T(8,128)}, f32[3,256,1024]{2,1,0:T(8,128)}, f32[3,256,1024]{2,1,0:T(8,128)}) custom-call(s32[1601]{0:T(1024)} %concatenate.14.meta, bf16[3,256,512]{2,1,0:T(8,128)(2,1)} %copy-done.7, bf16[3,256,512]{2,1,0:T(8,128)(2,1)} %copy-done.9, ...), custom_call_target="tpu_custom_call", output_to_operand_aliasing={{2}: (11, {}), {3}: (12, {})} | custom-call | flops 16000000000 | bytes 30000000 | tf_op jit(solution)/shard_map/unattend/pallas_call | solution.py:550
  738.4 10.9 %collective-permute-done.53.db = bf16[3,272,512]{2,1,0:T(8,128)(2,1)S(1)} collective-permute-done((bf16[3,272,512]{2,1,0:T(8,128)(2,1)S(1)}, bf16[3,272,512]{2,1,0:T(8,128)(2,1)S(1)}, u32[]{:S(2)}, u32[]{:S(2)}) %collective-permute-start.53) | collective-permute-done | bytes 835616 | tf_op jit(solution)/shard_map/ppermute | solution.py:725
  750.2 25.4 %unattend.15 = (f32[3,256,512]{2,1,0:T(8,128)}, f32[3,256,512]{2,1,0:T(8,128)}, f32[3,256,1024]{2,1,0:T(8,128)}, f32[3,256,1024]{2,1,0:T(8,128)}) custom-call(s32[1601]{0:T(1024)} %concatenate.14.meta, bf16[3,256,512]{2,1,0:T(8,128)(2,1)} %copy-done.6, bf16[3,256,512]{2,1,0:T(8,128)(2,1)} %copy-done.8, ...), custom_call_target="tpu_custom_call", output_to_operand_aliasing={{2}: (11, {}), {3}: (12, {})} | custom-call | flops 16000000000 | bytes 30000000 | tf_op jit(solution)/shard_map/unattend/pallas_call | solution.py:550
  775.6 16.6 %collective-permute-done.51.refs_1_ = bf16[3,256,512]{2,1,0:T(8,128)(2,1)S(1)} collective-permute-done((bf16[3,256,512]{2,1,0:T(8,128)(2,1)}, bf16[3,256,512]{2,1,0:T(8,128)(2,1)S(1)}, u32[]{:S(2)}, u32[]{:S(2)}) %collective-permute-start.51) | collective-permute-done | bytes 786464 | tf_op jit(solution)/shard_map/ppermute | solution.py:751
  797.2 12.8 %collective-permute-start.55 = (bf16[3,256,512]{2,1,0:T(8,128)(2,1)}, bf16[3,256,512]{2,1,0:T(8,128)(2,1)S(1)}, u32[]{:S(2)}, u32[]{:S(2)}) collective-permute-start(bf16[3,256,512]{2,1,0:T(8,128)(2,1)} %get-tuple-element.227), channel_id=1, source_target_pairs={{8,0},{16,8},{24,16},{28,24},{20,28},{12,20},{4,12},{0,4},{9,1},{1... | collective-permute-start | bytes 2359304 | tf_op jit(solution)/shard_map/ppermute | solution.py:753
  810.1 16.0 %collective-permute-done.54.acc_a = bf16[3,256,512]{2,1,0:T(8,128)(2,1)S(1)} collective-permute-done((bf16[3,256,512]{2,1,0:T(8,128)(2,1)}, bf16[3,256,512]{2,1,0:T(8,128)(2,1)S(1)}, u32[]{:S(2)}, u32[]{:S(2)}) %collective-permute-start.54) | collective-permute-done | bytes 786464 | tf_op jit(solution)/shard_map/ppermute | solution.py:753
  847.3 9.9 add_convert_fusion
  867.1 57.3 %all-reduce.6.cloned.1.call-done = (bf16[704,1024]{1,0:T(8,128)(2,1)}, bf16[256,2816]{1,0:T(8,128)(2,1)}, bf16[256,2816]{1,0:T(8,128)(2,1)}, bf16[256,1024]{1,0:T(8,128)(2,1)}) async-done(((bf16[704,1024]{1,0:T(8,128)(2,1)}, bf16[256,2816]{1,0:T(8,128)(2,1)}, bf16[256,2816]{1,0:T(8,128)(2,1)}, bf16[256,1024]{1,0:T(8,128)(2,1)}), (bf16[704,1024]{1,0:T(8,128)(2,1)}, bf16[256,2816]{1,0:T(8,128)(2,1)}, ...) | async-done | bytes 4849680 | tf_op jit(solution)/shard_map/psum | solution.py:772
  924.4 60.0 %reduce-scatter.14.cloned.1.call-done = bf16[256,3072]{1,0:T(8,128)(2,1)} async-done(((bf16[1024,3072]{1,0:T(8,128)(2,1)}), bf16[256,3072]{1,0:T(8,128)(2,1)}) %reduce-scatter.14.cloned.1.call-update) | async-done | bytes 1572880 | tf_op jit(solution)/shard_map/reduce_scatter | solution.py:767
  992.9 40.4 %psum.47 = f32[2,1024]{1,0:T(2,128)S(1)} all-reduce(f32[2,1024]{1,0:T(2,128)S(1)} %pad_maximum_fusion.1), channel_id=1, replica_groups=mesh['ctx'=8,'fsdp'=4] {'ctx','fsdp'}, use_global_device_ids=true, to_apply=%region_18.19 | all-reduce | flops 2048 | bytes 16384 | tf_op jit(solution)/shard_map/psum | solution.py:775
  1047.8 29.4 %all-reduce.4.cloned.1.call-done = bf16[256,3072]{1,0:T(8,128)(2,1)} async-done(((bf16[256,3072]{1,0:T(8,128)(2,1)}), bf16[256,3072]{1,0:T(8,128)(2,1)}) %all-reduce.4.cloned.1.call-update) | async-done | bytes 1572880 | tf_op jit(solution)/shard_map/psum | solution.py:774
  (382 shorter events, 375.8 us)
Async XLA Ops:
  7.2 45.1 %all-gather.8.cloned.1.call-start = ((), (), s32[]{:S(2)}) async-start(), calls=%async_computation.5 | async-start | bytes 2621440 | tf_op jit(solution)/shard_map/all_gather | solution.py:650
  7.9 80.5 %all-gather.10.cloned.1.call-start = ((), (), s32[]{:S(2)}) async-start(), calls=%async_computation.6 | async-start | bytes 2621440 | tf_op jit(solution)/shard_map/all_gather | solution.py:650
  8.7 79.8 %all-gather.12.cloned.1.call-start = ((), (), s32[]{:S(2)}) async-start(), calls=%async_computation.7 | async-start | bytes 2621440 | tf_op jit(solution)/shard_map/all_gather | solution.py:650
  9.4 346.2 %all-gather.14.cloned.1.call-start = ((), (), s32[]{:S(2)}) async-start(), calls=%async_computation.8 | async-start | bytes 2621440 | tf_op jit(solution)/shard_map/all_gather | solution.py:650
  10.0 351.8 %all-gather.16.cloned.1.call-start = ((), (), s32[]{:S(2)}) async-start(), calls=%async_computation.9 | async-start | bytes 7208960 | tf_op jit(solution)/shard_map/all_gather | solution.py:650
  10.6 362.4 %all-gather.18.cloned.1.call-start = ((), (), s32[]{:S(2)}) async-start(), calls=%async_computation.10 | async-start | bytes 7208960 | tf_op jit(solution)/shard_map/all_gather | solution.py:650
  11.2 372.9 %all-gather.20.cloned.1.call-start = ((), (), s32[]{:S(2)}) async-start(), calls=%async_computation.11 | async-start | bytes 7208960 | tf_op jit(solution)/shard_map/all_gather | solution.py:650
  58.2 37.5 %collective-permute-start = (bf16[3,256,512]{2,1,0:T(8,128)(2,1)}, bf16[3,256,512]{2,1,0:T(8,128)(2,1)S(1)}, u32[]{:S(2)}, u32[]{:S(2)}) collective-permute-start(bf16[3,256,512]{2,1,0:T(8,128)(2,1)} %get-tuple-element.126.qa), channel_id=1, source_target_pairs={{0,8},{8,16},{16,24},{24,28},{28,20},{20,12},{12,4},{4,0},{1,9},{9... | collective-permute-start | bytes 2359304 | tf_op jit(solution)/shard_map/ppermute | solution.py:681
  58.2 42.3 %collective-permute-start.1 = (bf16[3,256,512]{2,1,0:T(8,128)(2,1)}, bf16[3,256,512]{2,1,0:T(8,128)(2,1)S(1)}, u32[]{:S(2)}, u32[]{:S(2)}) collective-permute-start(bf16[3,256,512]{2,1,0:T(8,128)(2,1)} %get-tuple-element.127.qb), channel_id=1, source_target_pairs={{8,0},{16,8},{24,16},{28,24},{20,28},{12,20},{4,12},{0,4},{9,1},{1... | collective-permute-start | bytes 2359304 | tf_op jit(solution)/shard_map/ppermute | solution.py:681
  127.2 580.1 %reduce-scatter.12.cloned.1.call-start = ((), (), s32[]{:S(2)}) async-start(), calls=%async_computation.15 | async-start | bytes 2621440 | tf_op jit(solution)/shard_map/reduce_scatter | solution.py:767
  475.2 232.1 %reduce-scatter.6.cloned.1.call-start = ((), (), s32[]{:S(2)}) async-start(), calls=%async_computation.12 | async-start | bytes 7208960 | tf_op jit(solution)/shard_map/reduce_scatter | solution.py:767
  475.9 231.4 %reduce-scatter.8.cloned.1.call-start = ((), (), s32[]{:S(2)}) async-start(), calls=%async_computation.13 | async-start | bytes 7208960 | tf_op jit(solution)/shard_map/reduce_scatter | solution.py:767
  476.5 230.8 %reduce-scatter.10.cloned.1.call-start = ((), (), s32[]{:S(2)}) async-start(), calls=%async_computation.14 | async-start | bytes 7208960 | tf_op jit(solution)/shard_map/reduce_scatter | solution.py:767
  477.3 447.2 %all-reduce.6.cloned.1.call-start = ((), (), s32[]{:S(2)}) async-start(), calls=%async_computation.18 | async-start | bytes 9699328 | tf_op jit(solution)/shard_map/psum | solution.py:772
  500.7 41.8 %collective-permute-start.32 = (bf16[3,272,512]{2,1,0:T(8,128)(2,1)S(1)}, bf16[3,272,512]{2,1,0:T(8,128)(2,1)S(1)}, u32[]{:S(2)}, u32[]{:S(2)}) collective-permute-start(bf16[3,272,512]{2,1,0:T(8,128)(2,1)S(1)} %collective-permute-done.28.da), channel_id=1, source_target_pairs={{0,8},{8,16},{16,24},{24,28},{28,20},{20,12},{12,4},{4,0},{1,9},{9... | collective-permute-start | bytes 2506760 | tf_op jit(solution)/shard_map/ppermute | solution.py:725
  501.8 40.7 %collective-permute-start.33 = (bf16[3,272,512]{2,1,0:T(8,128)(2,1)S(1)}, bf16[3,272,512]{2,1,0:T(8,128)(2,1)S(1)}, u32[]{:S(2)}, u32[]{:S(2)}) collective-permute-start(bf16[3,272,512]{2,1,0:T(8,128)(2,1)S(1)} %collective-permute-done.29.db), channel_id=1, source_target_pairs={{8,0},{16,8},{24,16},{28,24},{20,28},{12,20},{4,12},{0,4},{9,1},{1... | collective-permute-start | bytes 2506760 | tf_op jit(solution)/shard_map/ppermute | solution.py:725
  532.4 38.4 %collective-permute-start.30 = (bf16[3,256,512]{2,1,0:T(8,128)(2,1)}, bf16[3,256,512]{2,1,0:T(8,128)(2,1)S(1)}, u32[]{:S(2)}, u32[]{:S(2)}) collective-permute-start(bf16[3,256,512]{2,1,0:T(8,128)(2,1)} %get-tuple-element.190), channel_id=1, source_target_pairs={{0,8},{8,16},{16,24},{24,28},{28,20},{20,12},{12,4},{4,0},{1,9},{9... | collective-permute-start | bytes 2359304 | tf_op jit(solution)/shard_map/ppermute | solution.py:751
  542.4 38.4 %collective-permute-start.36 = (bf16[3,272,512]{2,1,0:T(8,128)(2,1)S(1)}, bf16[3,272,512]{2,1,0:T(8,128)(2,1)S(1)}, u32[]{:S(2)}, u32[]{:S(2)}) collective-permute-start(bf16[3,272,512]{2,1,0:T(8,128)(2,1)S(1)} %collective-permute-done.32.da), channel_id=1, source_target_pairs={{0,8},{8,16},{16,24},{24,28},{28,20},{20,12},{12,4},{4,0},{1,9},{9... | collective-permute-start | bytes 2506760 | tf_op jit(solution)/shard_map/ppermute | solution.py:725
  542.4 38.4 %collective-permute-start.37 = (bf16[3,272,512]{2,1,0:T(8,128)(2,1)S(1)}, bf16[3,272,512]{2,1,0:T(8,128)(2,1)S(1)}, u32[]{:S(2)}, u32[]{:S(2)}) collective-permute-start(bf16[3,272,512]{2,1,0:T(8,128)(2,1)S(1)} %collective-permute-done.33.db), channel_id=1, source_target_pairs={{8,0},{16,8},{24,16},{28,24},{20,28},{12,20},{4,12},{0,4},{9,1},{1... | collective-permute-start | bytes 2506760 | tf_op jit(solution)/shard_map/ppermute | solution.py:725
  580.8 39.0 %collective-permute-start.40 = (bf16[3,272,512]{2,1,0:T(8,128)(2,1)S(1)}, bf16[3,272,512]{2,1,0:T(8,128)(2,1)S(1)}, u32[]{:S(2)}, u32[]{:S(2)}) collective-permute-start(bf16[3,272,512]{2,1,0:T(8,128)(2,1)S(1)} %collective-permute-done.36.da), channel_id=1, source_target_pairs={{0,8},{8,16},{16,24},{24,28},{28,20},{20,12},{12,4},{4,0},{1,9},{9... | collective-permute-start | bytes 2506760 | tf_op jit(solution)/shard_map/ppermute | solution.py:725
  580.8 39.0 %collective-permute-start.41 = (bf16[3,272,512]{2,1,0:T(8,128)(2,1)S(1)}, bf16[3,272,512]{2,1,0:T(8,128)(2,1)S(1)}, u32[]{:S(2)}, u32[]{:S(2)}) collective-permute-start(bf16[3,272,512]{2,1,0:T(8,128)(2,1)S(1)} %collective-permute-done.37.db), channel_id=1, source_target_pairs={{8,0},{16,8},{24,16},{28,24},{20,28},{12,20},{4,12},{0,4},{9,1},{1... | collective-permute-start | bytes 2506760 | tf_op jit(solution)/shard_map/ppermute | solution.py:725
  617.0 37.1 %collective-permute-start.39 = (bf16[3,256,512]{2,1,0:T(8,128)(2,1)}, bf16[3,256,512]{2,1,0:T(8,128)(2,1)S(1)}, u32[]{:S(2)}, u32[]{:S(2)}) collective-permute-start(bf16[3,256,512]{2,1,0:T(8,128)(2,1)} %get-tuple-element.203), channel_id=1, source_target_pairs={{8,0},{16,8},{24,16},{28,24},{20,28},{12,20},{4,12},{0,4},{9,1},{1... | collective-permute-start | bytes 2359304 | tf_op jit(solution)/shard_map/ppermute | solution.py:751
  619.8 42.4 %collective-permute-start.44 = (bf16[3,272,512]{2,1,0:T(8,128)(2,1)S(1)}, bf16[3,272,512]{2,1,0:T(8,128)(2,1)S(1)}, u32[]{:S(2)}, u32[]{:S(2)}) collective-permute-start(bf16[3,272,512]{2,1,0:T(8,128)(2,1)S(1)} %collective-permute-done.40.da), channel_id=1, source_target_pairs={{0,8},{8,16},{16,24},{24,28},{28,20},{20,12},{12,4},{4,0},{1,9},{9... | collective-permute-start | bytes 2506760 | tf_op jit(solution)/shard_map/ppermute | solution.py:725
  619.8 42.3 %collective-permute-start.45 = (bf16[3,272,512]{2,1,0:T(8,128)(2,1)S(1)}, bf16[3,272,512]{2,1,0:T(8,128)(2,1)S(1)}, u32[]{:S(2)}, u32[]{:S(2)}) collective-permute-start(bf16[3,272,512]{2,1,0:T(8,128)(2,1)S(1)} %collective-permute-done.41.db), channel_id=1, source_target_pairs={{8,0},{16,8},{24,16},{28,24},{20,28},{12,20},{4,12},{0,4},{9,1},{1... | collective-permute-start | bytes 2506760 | tf_op jit(solution)/shard_map/ppermute | solution.py:725
  662.1 38.5 %collective-permute-start.48 = (bf16[3,272,512]{2,1,0:T(8,128)(2,1)S(1)}, bf16[3,272,512]{2,1,0:T(8,128)(2,1)S(1)}, u32[]{:S(2)}, u32[]{:S(2)}) collective-permute-start(bf16[3,272,512]{2,1,0:T(8,128)(2,1)S(1)} %collective-permute-done.44.da), channel_id=1, source_target_pairs={{0,8},{8,16},{16,24},{24,28},{28,20},{20,12},{12,4},{4,0},{1,9},{9... | collective-permute-start | bytes 2506760 | tf_op jit(solution)/shard_map/ppermute | solution.py:725
  662.2 38.5 %collective-permute-start.49 = (bf16[3,272,512]{2,1,0:T(8,128)(2,1)S(1)}, bf16[3,272,512]{2,1,0:T(8,128)(2,1)S(1)}, u32[]{:S(2)}, u32[]{:S(2)}) collective-permute-start(bf16[3,272,512]{2,1,0:T(8,128)(2,1)S(1)} %collective-permute-done.45.db), channel_id=1, source_target_pairs={{8,0},{16,8},{24,16},{28,24},{20,28},{12,20},{4,12},{0,4},{9,1},{1... | collective-permute-start | bytes 2506760 | tf_op jit(solution)/shard_map/ppermute | solution.py:725
  700.6 37.8 %collective-permute-start.52 = (bf16[3,272,512]{2,1,0:T(8,128)(2,1)S(1)}, bf16[3,272,512]{2,1,0:T(8,128)(2,1)S(1)}, u32[]{:S(2)}, u32[]{:S(2)}) collective-permute-start(bf16[3,272,512]{2,1,0:T(8,128)(2,1)S(1)} %collective-permute-done.48.da), channel_id=1, source_target_pairs={{0,8},{8,16},{16,24},{24,28},{28,20},{20,12},{12,4},{4,0},{1,9},{9... | collective-permute-start | bytes 2506760 | tf_op jit(solution)/shard_map/ppermute | solution.py:725
  700.7 48.7 %collective-permute-start.53 = (bf16[3,272,512]{2,1,0:T(8,128)(2,1)S(1)}, bf16[3,272,512]{2,1,0:T(8,128)(2,1)S(1)}, u32[]{:S(2)}, u32[]{:S(2)}) collective-permute-start(bf16[3,272,512]{2,1,0:T(8,128)(2,1)S(1)} %collective-permute-done.49.db), channel_id=1, source_target_pairs={{8,0},{16,8},{24,16},{28,24},{20,28},{12,20},{4,12},{0,4},{9,1},{1... | collective-permute-start | bytes 2506760 | tf_op jit(solution)/shard_map/ppermute | solution.py:725
  707.3 277.1 %reduce-scatter.14.cloned.1.call-start = ((), (), s32[]{:S(2)}) async-start(), calls=%async_computation.16 | async-start | bytes 7864320 | tf_op jit(solution)/shard_map/reduce_scatter | solution.py:767
  736.4 39.2 %collective-permute-start.50 = (bf16[3,256,512]{2,1,0:T(8,128)(2,1)}, bf16[3,256,512]{2,1,0:T(8,128)(2,1)S(1)}, u32[]{:S(2)}, u32[]{:S(2)}) collective-permute-start(bf16[3,256,512]{2,1,0:T(8,128)(2,1)} %get-tuple-element.220), channel_id=1, source_target_pairs={{0,8},{8,16},{16,24},{24,28},{28,20},{20,12},{12,4},{4,0},{1,9},{9... | collective-permute-start | bytes 2359304 | tf_op jit(solution)/shard_map/ppermute | solution.py:751
  736.4 55.8 %collective-permute-start.51 = (bf16[3,256,512]{2,1,0:T(8,128)(2,1)}, bf16[3,256,512]{2,1,0:T(8,128)(2,1)S(1)}, u32[]{:S(2)}, u32[]{:S(2)}) collective-permute-start(bf16[3,256,512]{2,1,0:T(8,128)(2,1)} %get-tuple-element.221), channel_id=1, source_target_pairs={{8,0},{16,8},{24,16},{28,24},{20,28},{12,20},{4,12},{0,4},{9,1},{1... | collective-permute-start | bytes 2359304 | tf_op jit(solution)/shard_map/ppermute | solution.py:751
  844.9 232.3 %all-reduce.4.cloned.1.call-start = ((), (), s32[]{:S(2)}) async-start(), calls=%async_computation.17 | async-start | bytes 3145728 | tf_op jit(solution)/shard_map/psum | solution.py:774
  (117 other events, 2080.6 us)
Sparse Core Ops, SparseCore 0:
  9.6 25.2 all-gather.7
  36.5 22.6 all-gather.9
  60.7 22.5 all-gather.11
  84.7 22.6 all-gather.13
  108.8 43.4 all-gather.15
  153.7 43.5 all-gather.17
  198.9 43.4 all-gather.19
  475.3 33.7 reduce-scatter.11
  511.8 55.0 reduce-scatter.5
  569.3 54.8 reduce-scatter.7
  626.9 54.9 reduce-scatter.9
  707.5 216.9 all-reduce.5
  927.1 57.2 reduce-scatter.13
  987.8 89.3 all-reduce.3

commit v2 on v1

v2 whole, which is shorter than its diff:
```python
import functools

import jax
import jax.numpy as jnp
from jax import lax
from jax.experimental import pallas as pl
from jax.experimental.pallas import tpu as pltpu
from jax.sharding import PartitionSpec as P

D = 1024
HEADS = 8
HEAD_DIM = 128
HALF = 128
ROWS = 2 * HALF
BLOCK = 64
TOPK = 4
SIDE = HEADS // 2
SW = SIDE * HEAD_DIM
GROUP = 8
EPS = 1e-05
SCALE = HEAD_DIM**-0.5
LOG2E = 1.4426950408889634
F32 = jnp.float32
BF16 = jnp.bfloat16
EXTRA = 16
SENT = ROWS + EXTRA


def nn(a, b):
    return lax.dot_general(a, b, (((1,), (0,)), ((), ())), preferred_element_type=F32)


def nt(a, b):
    return lax.dot_general(a, b, (((1,), (1,)), ((), ())), preferred_element_type=F32)


def tn(a, b):
    return lax.dot_general(a, b, (((0,), (0,)), ((), ())), preferred_element_type=F32)


def params(mib=56):
    return pltpu.CompilerParams(vmem_limit_bytes=mib * 2**20)


def ring_order(count):
    if count == 8:
        return [0, 2, 4, 6, 7, 5, 3, 1]
    half = count // 2
    return list(range(half)) + [count - 1 - i for i in range(count - half)]


def ring_place(count):
    here = lax.axis_index("ctx")
    half = count // 2
    if count == 8:
        turned = here % 2
        return (1 - turned) * (here // 2) + turned * (count - 1 - here // 2)
    turned = here // half
    return (1 - turned) * here + turned * (count - 1 + half - here)


def ring_index(place, count):
    half = count // 2
    place = place % count
    turned = place // half
    if count == 8:
        return (1 - turned) * 2 * place + turned * (2 * count - 1 - 2 * place)
    return (1 - turned) * place + turned * (count - 1 + half - place)


def ring_pairs(count):
    order = ring_order(count)
    onward = [(order[i], order[(i + 1) % count]) for i in range(count)]
    return onward, [(b, a) for a, b in onward]


def list_base(count):
    return 1 + 2 * count


def list_at(owner, micro, side, micros, cap):
    return ((owner * micros + micro) * 2 + side) * (cap + 1)


def make_meta(indices, partner, cb_dev, count):
    micros = indices.shape[0]
    here = lax.axis_index("ctx")
    order = ring_order(count)
    place = ring_place(count)
    steps = jnp.arange(count, dtype=jnp.int32)
    at = jnp.stack([(place - steps) % count, (place + steps) % count], axis=1)
    owners = sum(jnp.where(at == p, d, 0) for p, d in enumerate(order))
    blocks = cb_dev * count
    cap = 2 * 128 // count
    side_shape = (micros, count, 2 * ROWS // (2 * BLOCK), 2, SIDE, TOPK)
    index = indices.reshape(side_shape).transpose(1, 0, 3, 2, 4, 5)
    index = index.reshape(count, micros, 2, -1)
    number = index % blocks
    mine = (number // cb_dev) == here
    own = jnp.arange(micros, dtype=jnp.int32)[None, :, None, None]
    document = jnp.where(index < blocks, own, partner[None, :, None, None])
    entries = index.shape[-1]
    entry = jnp.arange(entries, dtype=jnp.int32)
    query_block = entry // (SIDE * TOPK)
    head = entry // TOPK % SIDE
    code = ((document * cb_dev + number % cb_dev) * 4 + query_block) * SIDE + head
    before = (entry[:, None] < entry[None, :]).astype(F32)
    flags = mine.astype(F32)
    rank = jnp.dot(flags.reshape(-1, entries), before, preferred_element_type=F32).reshape(flags.shape)
    rank = rank.astype(jnp.int32)
    slot = jnp.arange(cap, dtype=jnp.int32)
    hit = mine[..., None, :] & (rank[..., None, :] == slot[:, None])
    codes = jnp.sum(jnp.where(hit, code[..., None, :], 0), axis=-1)
    length = jnp.sum(mine.astype(jnp.int32), axis=-1, keepdims=True)
    lists = jnp.concatenate([length, codes], axis=-1).reshape(-1)
    return jnp.concatenate([here.reshape(1), owners.reshape(-1), lists]).astype(jnp.int32), cap


def collect_kernel(meta, ck, cv, mk, mv, sem_k, sem_v, *, micros, count, cap):
    owner = pl.program_id(0)

    def list_of(i):
        base = list_base(count) + (owner * 2 * micros + i) * (cap + 1)
        return base, meta[base]

    def start(i, carry):
        base, length = list_of(i)

        def one(j, c):
            code = meta[base + 1 + j]
            head = (i & 1) * SIDE + (code & (SIDE - 1))
            rows = pl.ds(pl.multiple_of((code >> 4) << 6, BLOCK), BLOCK)
            cols = pl.ds(pl.multiple_of(head << 7, HEAD_DIM), HEAD_DIM)
            pltpu.make_async_copy(ck.at[rows, cols], mk.at[i >> 1, 0, i & 1, j], sem_k).start()
            pltpu.make_async_copy(cv.at[rows, cols], mv.at[i >> 1, 0, i & 1, j], sem_v).start()
            return c

        def clear(j, c):
            mk[i >> 1, 0, i & 1, j] = jnp.zeros((BLOCK, HEAD_DIM), BF16)
            mv[i >> 1, 0, i & 1, j] = jnp.zeros((BLOCK, HEAD_DIM), BF16)
            return c

        lax.fori_loop(0, length, one, carry)
        return lax.fori_loop(length, (length + GROUP - 1) // GROUP * GROUP, clear, carry)

    def finish(i, carry):
        _, length = list_of(i)
        rounds = length // GROUP

        def many(g, c):
            some = pl.ds(g * GROUP, GROUP)
            for place, sem in ((mk, sem_k), (mv, sem_v)):
                whole = place.at[i >> 1, 0, i & 1, some]
                pltpu.make_async_copy(whole, whole, sem).wait()
            return c

        def one(j, c):
            for place, sem in ((mk, sem_k), (mv, sem_v)):
                whole = place.at[i >> 1, 0, i & 1, j]
                pltpu.make_async_copy(whole, whole, sem).wait()
            return c

        lax.fori_loop(0, rounds, many, carry)
        return lax.fori_loop(rounds * GROUP, length, one, carry)

    lax.fori_loop(0, 2 * micros, start, 0)
    lax.fori_loop(0, 2 * micros, finish, 0)


def collect(meta, cache_keys, cache_values, count, cap):
    micros = cache_keys.shape[0]
    shape = jax.ShapeDtypeStruct((micros, count, 2, cap, BLOCK, HEAD_DIM), BF16)
    anywhere = pl.BlockSpec(memory_space=pl.ANY)
    block = pl.BlockSpec((micros, 1, 2, cap, BLOCK, HEAD_DIM), lambda o, meta: (0, o, 0, 0, 0, 0))
    return pl.pallas_call(
        functools.partial(collect_kernel, micros=micros, count=count, cap=cap),
        grid_spec=pltpu.PrefetchScalarGridSpec(
            num_scalar_prefetch=1,
            grid=(count,),
            in_specs=[anywhere, anywhere],
            out_specs=[block, block],
            scratch_shapes=[pltpu.SemaphoreType.DMA, pltpu.SemaphoreType.DMA],
        ),
        out_shape=[shape, shape],
        compiler_params=params(),
        name="collect",
        cost_estimate=pl.CostEstimate(flops=0, bytes_accessed=90_000_000, transcendentals=0),
    )(meta, cache_keys.reshape(-1, D), cache_values.reshape(-1, D))


def turn(value, cosine, sine):
    return value * cosine + pltpu.roll(value, HEAD_DIM // 2, 1) * sine


def first_kernel(x, gain, weight, cosine, sine, normed, qa, qb):
    value = x[0].astype(F32)
    scale = lax.rsqrt(jnp.mean(value * value, axis=-1, keepdims=True) + EPS)
    low = (value * scale * gain[...]).astype(BF16)
    normed[0] = low
    product = nn(low, weight[...])
    for h in range(HEADS):
        cols = slice(h * HEAD_DIM, (h + 1) * HEAD_DIM)
        out = qa if h < SIDE else qb
        place = slice((h % SIDE) * HEAD_DIM, (h % SIDE + 1) * HEAD_DIM)
        out[0, :, place] = turn(product[:, cols], cosine[...], sine[...]).astype(BF16)


def second_kernel(normed, key_weight, value_weight, cosine, sine, keys, values):
    low = normed[0]
    product = nn(low, key_weight[...])
    for h in range(HEADS):
        cols = slice(h * HEAD_DIM, (h + 1) * HEAD_DIM)
        keys[0, :, cols] = turn(product[:, cols], cosine[...], sine[...]).astype(BF16)
    values[0] = nn(low, value_weight[...]).astype(BF16)


def seq_spec(*shape):
    return pl.BlockSpec((1,) + shape, lambda m, *_: (m,) + (0,) * len(shape))


def full_spec(*shape):
    return pl.BlockSpec(shape, lambda m, *_: (0,) * len(shape))


def seq_shape(micros, *shape, dtype=BF16):
    return jax.ShapeDtypeStruct((micros,) + shape, dtype)


def project_query(x, gain, weight, cosine, sine):
    micros = x.shape[0]
    return pl.pallas_call(
        first_kernel,
        grid=(micros,),
        in_specs=[
            seq_spec(ROWS, D),
            full_spec(1, D),
            full_spec(D, D),
            full_spec(ROWS, HEAD_DIM),
            full_spec(ROWS, HEAD_DIM),
        ],
        out_specs=[seq_spec(ROWS, D), seq_spec(ROWS, SW), seq_spec(ROWS, SW)],
        out_shape=[seq_shape(micros, ROWS, D), seq_shape(micros, ROWS, SW), seq_shape(micros, ROWS, SW)],
        compiler_params=params(),
        name="project_query",
        cost_estimate=pl.CostEstimate(flops=2 * micros * ROWS * D * D, bytes_accessed=8_000_000, transcendentals=0),
    )(x, gain, weight, cosine, sine)


def project_pairs(normed, key_weight, value_weight, cosine, sine):
    micros = normed.shape[0]
    return pl.pallas_call(
        second_kernel,
        grid=(micros,),
        in_specs=[
            seq_spec(ROWS, D),
            full_spec(D, D),
            full_spec(D, D),
            full_spec(ROWS, HEAD_DIM),
            full_spec(ROWS, HEAD_DIM),
        ],
        out_specs=[seq_spec(ROWS, D), seq_spec(ROWS, D)],
        out_shape=[seq_shape(micros, ROWS, D), seq_shape(micros, ROWS, D)],
        compiler_params=params(),
        name="project_pairs",
        cost_estimate=pl.CostEstimate(flops=4 * micros * ROWS * D * D, bytes_accessed=10_000_000, transcendentals=0),
    )(normed, key_weight, value_weight, cosine, sine)


def causal_mask(turned=False):
    row = lax.broadcasted_iota(jnp.int32, (ROWS, ROWS), 0)
    col = lax.broadcasted_iota(jnp.int32, (ROWS, ROWS), 1)
    return row <= col if turned else row >= col


def to_lanes(wide):
    lane = lax.broadcasted_iota(jnp.int32, (ROWS, HEAD_DIM), 1)
    packed = jnp.zeros((ROWS, HEAD_DIM), F32)
    for h in range(SIDE):
        packed = jnp.where(lane == h, wide[:, h * HEAD_DIM : (h + 1) * HEAD_DIM], packed)
    return packed.T[:8]


def to_columns(lanes):
    return jnp.concatenate([lanes, jnp.zeros((HEAD_DIM - 8, ROWS), F32)], axis=0).T


def split3(value):
    high = value.astype(BF16).astype(F32)
    middle = (value - high).astype(BF16).astype(F32)
    return high, middle, value - high - middle


def pack_lanes(lanes):
    high, middle, low = split3(lanes)
    rows = jnp.concatenate(
        [jnp.concatenate([high, middle], axis=1), jnp.concatenate([low, jnp.zeros_like(low)], axis=1)],
        axis=0,
    )
    return rows.astype(BF16)


def unpack_lanes(rows):
    value = rows.astype(F32)
    return value[:8, :ROWS] + value[:8, ROWS:] + value[8:, :ROWS]


def requests(meta, mk, mv, kbuf, vbuf, sem, micro, act, *, step, count, cap, micros):
    slot = micro % 2
    for side in range(2):
        owner = meta[1 + 2 * step + side]
        length = meta[list_base(count) + list_at(owner, micro, side, micros, cap)]

        def one(g, carry):
            some = pl.ds(g * GROUP, GROUP)
            for source, place in ((mk, kbuf), (mv, vbuf)):
                copy = pltpu.make_async_copy(
                    source.at[micro, owner, side, some], place.at[slot, side, some], sem.at[slot]
                )
                if act == "start":
                    copy.start()
                else:
                    copy.wait()
            return carry

        lax.fori_loop(0, (length + GROUP - 1) // GROUP, one, 0)


def request_ahead(fetch, micro, micros):
    @pl.when(micro == 0)
    def _():
        fetch(micro, "start")

    @pl.when(micro + 1 < micros)
    def _():
        fetch(micro + 1, "start")


def request_scratch(cap):
    return [
        pltpu.VMEM((2, 2, cap, BLOCK, HEAD_DIM), BF16),
        pltpu.VMEM((2, 2, cap, BLOCK, HEAD_DIM), BF16),
        pltpu.SemaphoreType.DMA((2,)),
    ]


EVERYTHING, LOW, HIGH = slice(0, ROWS), slice(0, HALF), slice(HALF, ROWS)


def tiles(side):
    return [
        (
            slice(h * HEAD_DIM, (h + 1) * HEAD_DIM),
            slice((side * SIDE + h) * HEAD_DIM, (side * SIDE + h + 1) * HEAD_DIM),
        )
        for h in range(SIDE)
    ]


def forward_kernel(
    meta, qa, qb, k, v, mk, mv, pa, pb, ta, tb, part, wide, kbuf, vbuf, sem, *, step, count, cap, micros
):
    micro = pl.program_id(0)
    here = meta[0]
    fetch = functools.partial(
        requests, meta, mk, mv, kbuf, vbuf, sem, step=step, count=count, cap=cap, micros=micros
    )
    request_ahead(fetch, micro, micros)
    for side, q in enumerate((qa, qb)):
        owner = meta[1 + 2 * step + side]

        def local(qrows, krows, masked):
            spots = tiles(side)
            scores = [nt(q[0, qrows, cols], k[0, krows, kcols]) for cols, kcols in spots]
            weights = [jnp.exp2(score * (SCALE * LOG2E)) for score in scores]
            if masked:
                weights = [jnp.where(causal_mask(), weight, 0.0) for weight in weights]
            for weight, (cols, kcols) in zip(weights, spots):
                values = v[0, krows, kcols]
                more = jnp.concatenate([values, jnp.ones_like(values)], axis=1)
                out = nn(weight.astype(BF16), more)
                part[qrows, kcols] = out[:, :HEAD_DIM]
                wide[qrows, kcols] = out[:, HEAD_DIM:]

        if step == 0:
            local(EVERYTHING, EVERYTHING, True)
        else:

            @pl.when(owner < here)
            def _():
                zeros = jnp.zeros((HALF, SW), F32)
                part[LOW, side * SW : (side + 1) * SW] = zeros
                wide[LOW, side * SW : (side + 1) * SW] = zeros
                local(HIGH, EVERYTHING, False)

            @pl.when(owner > here)
            def _():
                local(EVERYTHING, LOW, False)

    fetch(micro, "wait")
    slot = micro % 2
    for side, (q, out, total) in enumerate(((qa, pa, ta), (qb, pb, tb))):
        owner = meta[1 + 2 * step + side]
        base = list_base(count) + list_at(owner, micro, side, micros, cap)
        length = meta[base]

        def group(i, carry):
            numbers = [i * GROUP + j for j in range(GROUP)]
            places = [request_place(meta[base + 1 + number]) for number in numbers]
            scores = [
                nt(q[0, rows, cols], kbuf[slot, side, number])
                for number, (rows, cols) in zip(numbers, places)
            ]
            weights = [
                jnp.where(number < length, jnp.exp2(score * (SCALE * LOG2E)), 0.0).astype(BF16)
                for number, score in zip(numbers, scores)
            ]
            outs = []
            for number, weight in zip(numbers, weights):
                values = vbuf[slot, side, number]
                outs.append(nn(weight, jnp.concatenate([values, jnp.ones_like(values)], axis=1)))
            for o, (rows, cols) in zip(outs, places):
                cols = pl.ds(pl.multiple_of(cols.start + side * SW, HEAD_DIM), HEAD_DIM)
                part[rows, cols] += o[:, :HEAD_DIM]
                wide[rows, cols] += o[:, HEAD_DIM:]
            return carry

        lax.fori_loop(0, (length + GROUP - 1) // GROUP, group, 0)
        out[0] = part[:, side * SW : (side + 1) * SW].astype(BF16)
        total[0] = to_lanes(wide[:, side * SW : (side + 1) * SW])


def request_place(code):
    return (
        pl.ds(pl.multiple_of(((code >> 2) & 3) << 6, BLOCK), BLOCK),
        pl.ds(pl.multiple_of((code & 3) << 7, HEAD_DIM), HEAD_DIM),
    )


def attend(meta, qa, qb, keys, values, memory_keys, memory_values, step, count, cap):
    micros = qa.shape[0]
    half, whole, lanes = seq_spec(ROWS, SW), seq_spec(ROWS, D), seq_spec(8, ROWS)
    anywhere = pl.BlockSpec(memory_space=pl.ANY)
    return pl.pallas_call(
        functools.partial(forward_kernel, step=step, count=count, cap=cap, micros=micros),
        grid_spec=pltpu.PrefetchScalarGridSpec(
            num_scalar_prefetch=1,
            grid=(micros,),
            in_specs=[half, half, whole, whole, anywhere, anywhere],
            out_specs=[half, half, lanes, lanes],
            scratch_shapes=[pltpu.VMEM((ROWS, D), F32), pltpu.VMEM((ROWS, D), F32)]
            + request_scratch(cap),
        ),
        out_shape=[
            seq_shape(micros, ROWS, SW),
            seq_shape(micros, ROWS, SW),
            seq_shape(micros, 8, ROWS, dtype=F32),
            seq_shape(micros, 8, ROWS, dtype=F32),
        ],
        compiler_params=params(24),
        name="attend",
        cost_estimate=pl.CostEstimate(flops=6_000_000_000, bytes_accessed=10_000_000, transcendentals=0),
    )(meta, qa, qb, keys, values, memory_keys, memory_values)


def combine_kernel(*refs, carried, sums):
    refs = list(refs)
    received = [refs.pop(0), refs.pop(0)] if carried else [None, None]
    parts = [refs.pop(0), refs.pop(0)]
    totals = [refs.pop(0), refs.pop(0)] if sums else [None, None]
    for got, part, total, out in zip(received, parts, totals, refs):
        value = part[0].astype(F32)
        if carried:
            value = value + got[0, :ROWS].astype(F32)
        out[0, :ROWS] = value.astype(BF16)
        if sums:
            lanes = total[0]
            if carried:
                lanes = lanes + unpack_lanes(got[0, ROWS:])
            out[0, ROWS:] = pack_lanes(lanes)


def combine(received, parts, totals=()):
    micros = parts[0].shape[0]
    sent = SENT if totals else ROWS
    half, lanes, packed = seq_spec(ROWS, SW), seq_spec(8, ROWS), seq_spec(sent, SW)
    return pl.pallas_call(
        functools.partial(combine_kernel, carried=bool(received), sums=bool(totals)),
        grid=(micros,),
        in_specs=[packed] * len(received) + [half] * 2 + [lanes] * len(totals),
        out_specs=[packed, packed],
        out_shape=[seq_shape(micros, sent, SW)] * 2,
        compiler_params=params(16),
        name="combine",
        cost_estimate=pl.CostEstimate(flops=2_000_000, bytes_accessed=7_000_000, transcendentals=0),
    )(*received, *parts, *totals)


def finish_kernel(acc_a, acc_b, pa, pb, ta, tb, x, weight, gain, mixed, low, total, middle, normed):
    for side, (acc, part, own) in enumerate(((acc_a, pa, ta), (acc_b, pb, tb))):
        lanes = unpack_lanes(acc[0, ROWS:]) + own[0]
        total[0, side] = lanes
        columns = to_columns(lanes)
        for h in range(SIDE):
            cols = slice(h * HEAD_DIM, (h + 1) * HEAD_DIM)
            place = slice((side * SIDE + h) * HEAD_DIM, (side * SIDE + h + 1) * HEAD_DIM)
            weighted = acc[0, :ROWS, cols].astype(F32) + part[0, :, cols].astype(F32)
            value = weighted / columns[:, h : h + 1]
            mixed[0, :, place] = value
            low[0, :, place] = value.astype(BF16)
    value = x[0].astype(F32) + nn(low[0], weight[...])
    middle[0] = value
    scale = lax.rsqrt(jnp.mean(value * value, axis=-1, keepdims=True) + EPS)
    normed[0] = (value * scale * gain[...]).astype(BF16)


def finish(acc_a, acc_b, pa, pb, ta, tb, x, weight, gain):
    micros = acc_a.shape[0]
    packed, half, lanes = seq_spec(SENT, SW), seq_spec(ROWS, SW), seq_spec(8, ROWS)
    whole = seq_spec(ROWS, D)
    return pl.pallas_call(
        finish_kernel,
        grid=(micros,),
        in_specs=[packed, packed, half, half, lanes, lanes, whole, full_spec(D, D), full_spec(1, D)],
        out_specs=[whole, whole, seq_spec(2, 8, ROWS), whole, whole],
        out_shape=[
            seq_shape(micros, ROWS, D, dtype=F32),
            seq_shape(micros, ROWS, D),
            seq_shape(micros, 2, 8, ROWS, dtype=F32),
            seq_shape(micros, ROWS, D, dtype=F32),
            seq_shape(micros, ROWS, D),
        ],
        compiler_params=params(),
        name="finish",
        cost_estimate=pl.CostEstimate(flops=2 * micros * ROWS * D * D, bytes_accessed=16_000_000, transcendentals=0),
    )(acc_a, acc_b, pa, pb, ta, tb, x, weight, gain)


TILE = 256


def feed_kernel(
    normed, incoming, middle, gate_weight, up_weight, down_weight, out, back, dg, du, dd, turned, acc, hid, bg, bu
):
    step = pl.program_id(0)
    micros = normed.shape[0]

    @pl.when(step == 0)
    def _():
        for m in range(micros):
            turned[:, m * ROWS : (m + 1) * ROWS] = normed[m].T
            acc[m] = middle[m]
            back[m] = jnp.zeros((ROWS, D), F32)

    wg, wu, wd = gate_weight[...], up_weight[...], down_weight[...]
    for m in range(micros):
        rows = slice(m * ROWS, (m + 1) * ROWS)
        gate = nn(normed[m], wg)
        upper = nn(normed[m], wu)
        slope = nt(incoming[m], wd)
        sigma = 1.0 / (1.0 + jnp.exp(-gate))
        silu = gate * sigma
        hid[rows] = (silu * upper).astype(BF16)
        bg[rows] = (slope * upper * (sigma * (1.0 + gate * (1.0 - sigma)))).astype(BF16)
        bu[rows] = (slope * silu).astype(BF16)
        acc[m] += nn(hid[rows], wd)
        back[m] += nt(bg[rows], wg) + nt(bu[rows], wu)
    dg[...] = nn(turned[...], bg[...]).astype(BF16)
    du[...] = nn(turned[...], bu[...]).astype(BF16)
    dd[...] = tn(hid[...], incoming[...].reshape(micros * ROWS, D)).astype(BF16)

    @pl.when(step == pl.num_programs(0) - 1)
    def _():
        out[...] = acc[...].astype(BF16)


def feed(normed, incoming, middle, gate_weight, up_weight, down_weight):
    micros = normed.shape[0]
    units = gate_weight.shape[1]
    whole = full_spec(micros, ROWS, D)
    wide = pl.BlockSpec((D, TILE), lambda f: (0, f))
    tall = pl.BlockSpec((TILE, D), lambda f: (f, 0))
    return pl.pallas_call(
        feed_kernel,
        grid=(units // TILE,),
        in_specs=[whole, whole, whole, wide, wide, tall],
        out_specs=[whole, whole, wide, wide, tall],
        out_shape=[
            seq_shape(micros, ROWS, D),
            seq_shape(micros, ROWS, D, dtype=F32),
            jax.ShapeDtypeStruct((D, units), BF16),
            jax.ShapeDtypeStruct((D, units), BF16),
            jax.ShapeDtypeStruct((units, D), BF16),
        ],
        scratch_shapes=[
            pltpu.VMEM((D, micros * ROWS), BF16),
            pltpu.VMEM((micros, ROWS, D), F32),
            pltpu.VMEM((micros * ROWS, TILE), BF16),
            pltpu.VMEM((micros * ROWS, TILE), BF16),
            pltpu.VMEM((micros * ROWS, TILE), BF16),
        ],
        compiler_params=params(),
        name="feed",
        cost_estimate=pl.CostEstimate(
            flops=18 * micros * ROWS * D * units, bytes_accessed=50_000_000, transcendentals=0
        ),
    )(normed, incoming, middle, gate_weight, up_weight, down_weight)


def prepare_kernel(back_normed, middle, incoming, gain, weight, mixed, total, da, db, back_middle, back_attn, dgain):
    value = middle[0]
    scale = lax.rsqrt(jnp.mean(value * value, axis=-1, keepdims=True) + EPS)
    hat = value * scale
    slope = back_normed[0] * gain[...]
    slope = incoming[0].astype(F32) + scale * (
        slope - hat * jnp.mean(slope * hat, axis=-1, keepdims=True)
    )
    back_middle[0] = slope
    back_attn[0] = slope.astype(BF16)
    dgain[0] = jnp.sum((back_normed[0] * hat).reshape(ROWS // 8, 8, D), axis=0)
    lane = lax.broadcasted_iota(jnp.int32, (ROWS, HEAD_DIM), 1)
    for side, out in enumerate((da, db)):
        columns = to_columns(total[0, side])
        packed = jnp.zeros((ROWS, HEAD_DIM), F32)
        back = nt(back_attn[0], weight[side * SW : (side + 1) * SW, :])
        for h in range(SIDE):
            cols = slice(h * HEAD_DIM, (h + 1) * HEAD_DIM)
            place = slice((side * SIDE + h) * HEAD_DIM, (side * SIDE + h + 1) * HEAD_DIM)
            part = back[:, cols]
            divisor = columns[:, h : h + 1]
            out[0, :ROWS, cols] = (part / divisor).astype(BF16)
            product = jnp.sum(part * mixed[0, :, place], axis=1, keepdims=True)
            packed = jnp.where(lane == h, -product / divisor, packed)
        out[0, ROWS:] = pack_lanes(packed.T[:8])


def prepare(back_normed, middle, incoming, gain, weight, mixed, total):
    micros = middle.shape[0]
    whole = seq_spec(ROWS, D)
    return pl.pallas_call(
        prepare_kernel,
        grid=(micros,),
        in_specs=[whole, whole, whole, full_spec(1, D), full_spec(D, D), whole, seq_spec(2, 8, ROWS)],
        out_specs=[seq_spec(SENT, SW), seq_spec(SENT, SW), whole, whole, seq_spec(8, D)],
        out_shape=[
            seq_shape(micros, SENT, SW),
            seq_shape(micros, SENT, SW),
            seq_shape(micros, ROWS, D, dtype=F32),
            seq_shape(micros, ROWS, D),
            seq_shape(micros, 8, D, dtype=F32),
        ],
        compiler_params=params(),
        name="prepare",
        cost_estimate=pl.CostEstimate(flops=2 * micros * ROWS * D * D, bytes_accessed=22_000_000, transcendentals=0),
    )(back_normed, middle, incoming, gain, weight, mixed, total)


def backward_kernel(
    meta, qa, qb, da, db, k, v, mk, mv, dqa, dqb, part, wide, kbuf, vbuf, sem, *, step, count, cap, micros
):
    micro = pl.program_id(0)
    here = meta[0]
    fetch = functools.partial(
        requests, meta, mk, mv, kbuf, vbuf, sem, step=step, count=count, cap=cap, micros=micros
    )
    request_ahead(fetch, micro, micros)
    for side, (q, d) in enumerate(((qa, da), (qb, db))):
        owner = meta[1 + 2 * step + side]
        columns = to_columns(unpack_lanes(d[0, ROWS:]))
        for h, (_, place) in enumerate(tiles(side)):
            wide[:, place] = jnp.broadcast_to(columns[:, h : h + 1], (ROWS, HEAD_DIM))

        def local(qrows, krows, masked):
            spots = tiles(side)
            scores = [nt(q[0, qrows, cols], k[0, krows, kcols]) for cols, kcols in spots]
            slopes = [nt(d[0, qrows, cols], v[0, krows, kcols]) for cols, kcols in spots]
            weights = [jnp.exp2(score * (SCALE * LOG2E)) for score in scores]
            if masked:
                weights = [jnp.where(causal_mask(), weight, 0.0) for weight in weights]
            slopes = [
                (weight * (slope + wide[qrows, kcols][:, :1])).astype(BF16)
                for weight, slope, (_, kcols) in zip(weights, slopes, spots)
            ]
            for slope, (_, kcols) in zip(slopes, spots):
                part[qrows, kcols] = nn(slope, k[0, krows, kcols])

        if step == 0:
            local(EVERYTHING, EVERYTHING, True)
        else:

            @pl.when(owner < here)
            def _():
                part[LOW, side * SW : (side + 1) * SW] = jnp.zeros((HALF, SW), F32)
                local(HIGH, EVERYTHING, False)

            @pl.when(owner > here)
            def _():
                local(EVERYTHING, LOW, False)

    fetch(micro, "wait")
    slot = micro % 2
    for side, (q, d, out) in enumerate(((qa, da, dqa), (qb, db, dqb))):
        owner = meta[1 + 2 * step + side]
        base = list_base(count) + list_at(owner, micro, side, micros, cap)
        length = meta[base]

        def group(i, carry):
            numbers = [i * GROUP + j for j in range(GROUP)]
            places = [request_place(meta[base + 1 + number]) for number in numbers]
            shifted = [
                (rows, pl.ds(pl.multiple_of(cols.start + side * SW, HEAD_DIM), HEAD_DIM))
                for rows, cols in places
            ]
            scores = [
                nt(q[0, rows, cols], kbuf[slot, side, number])
                for number, (rows, cols) in zip(numbers, places)
            ]
            slopes = [
                nt(d[0, rows, cols], vbuf[slot, side, number])
                for number, (rows, cols) in zip(numbers, places)
            ]
            weights = [jnp.exp2(score * (SCALE * LOG2E)) for score in scores]
            slopes = [
                jnp.where(
                    number < length, weight * (slope + wide[rows, cols][:, :BLOCK]), 0.0
                ).astype(BF16)
                for number, weight, slope, (rows, cols) in zip(numbers, weights, slopes, shifted)
            ]
            outs = [nn(slope, kbuf[slot, side, number]) for number, slope in zip(numbers, slopes)]
            for o, (rows, cols) in zip(outs, shifted):
                part[rows, cols] += o
            return carry

        lax.fori_loop(0, (length + GROUP - 1) // GROUP, group, 0)
        out[0] = part[:, side * SW : (side + 1) * SW].astype(BF16)


def unattend(meta, qa, qb, da, db, keys, values, memory_keys, memory_values, step, count, cap):
    micros = qa.shape[0]
    half, packed, whole = seq_spec(ROWS, SW), seq_spec(SENT, SW), seq_spec(ROWS, D)
    anywhere = pl.BlockSpec(memory_space=pl.ANY)
    return pl.pallas_call(
        functools.partial(backward_kernel, step=step, count=count, cap=cap, micros=micros),
        grid_spec=pltpu.PrefetchScalarGridSpec(
            num_scalar_prefetch=1,
            grid=(micros,),
            in_specs=[half, half, packed, packed, whole, whole, anywhere, anywhere],
            out_specs=[half, half],
            scratch_shapes=[pltpu.VMEM((ROWS, D), F32), pltpu.VMEM((ROWS, D), F32)]
            + request_scratch(cap),
        ),
        out_shape=[seq_shape(micros, ROWS, SW), seq_shape(micros, ROWS, SW)],
        compiler_params=params(24),
        name="unattend",
        cost_estimate=pl.CostEstimate(flops=8_000_000_000, bytes_accessed=12_000_000, transcendentals=0),
    )(meta, qa, qb, da, db, keys, values, memory_keys, memory_values)


def key_kernel(meta, k, v, *refs, steps, micros):
    number = len(steps)
    sources, (dk, dv, qbuf, dbuf, sem) = refs[: 4 * number], refs[4 * number :]
    micro = pl.program_id(0)
    here = meta[0]

    def fetch(m, act):
        slot = m % 2
        for i in range(number):
            for side in range(2):
                for source, place in (
                    (sources[4 * i + side], qbuf.at[slot, side, i]),
                    (sources[4 * i + 2 + side], dbuf.at[slot, side, i]),
                ):
                    copy = pltpu.make_async_copy(source.at[m], place, sem.at[slot])
                    if act == "start":
                        copy.start()
                    else:
                        copy.wait()

    request_ahead(fetch, micro, micros)
    fetch(micro, "wait")
    dk[0] = jnp.zeros((ROWS, D), F32)
    dv[0] = jnp.zeros((ROWS, D), F32)
    slot = micro % 2
    for side in range(2):
        spots = tiles(side)

        def one(i, step, own):
            q, d = qbuf.at[slot, side, i], dbuf.at[slot, side, i]
            shift = unpack_lanes(d[ROWS:, :])

            def local(qrows, krows, masked):
                scores = [nt(k[0, krows, kcols], q[qrows, cols]) for cols, kcols in spots]
                slopes = [nt(v[0, krows, kcols], d[qrows, cols]) for cols, kcols in spots]
                weights = [jnp.exp2(score * (SCALE * LOG2E)) for score in scores]
                if masked:
                    weights = [jnp.where(causal_mask(True), weight, 0.0) for weight in weights]
                slopes = [
                    (weight * (slope + shift[h : h + 1, qrows])).astype(BF16)
                    for h, (weight, slope) in enumerate(zip(weights, slopes))
                ]
                for weight, slope, (cols, kcols) in zip(weights, slopes, spots):
                    dk[0, krows, kcols] += nn(slope, q[qrows, cols])
                    dv[0, krows, kcols] += nn(weight.astype(BF16), d[qrows, cols])

            if own:
                local(EVERYTHING, EVERYTHING, True)
                return
            owner = meta[1 + 2 * step + side]

            @pl.when(owner < here)
            def _():
                local(HIGH, EVERYTHING, False)

            @pl.when(owner > here)
            def _():
                local(EVERYTHING, LOW, False)

        first = 0
        if steps[0] == 0:
            one(0, 0, True)
            first = 1

        def loop(i, carry):
            one(i, steps[0] + i, False)
            return carry

        lax.fori_loop(first, number, loop, 0)


def key_gradients(meta, keys, values, queries, slopes, steps):
    micros = keys.shape[0]
    whole = seq_spec(ROWS, D)
    anywhere = pl.BlockSpec(memory_space=pl.ANY)
    sources = []
    for step in steps:
        sources += [*queries[step], *slopes[step]]
    return pl.pallas_call(
        functools.partial(key_kernel, steps=steps, micros=micros),
        grid_spec=pltpu.PrefetchScalarGridSpec(
            num_scalar_prefetch=1,
            grid=(micros,),
            in_specs=[whole, whole] + [anywhere] * len(sources),
            out_specs=[whole, whole],
            scratch_shapes=[
                pltpu.VMEM((2, 2, len(steps), ROWS, SW), BF16),
                pltpu.VMEM((2, 2, len(steps), SENT, SW), BF16),
                pltpu.SemaphoreType.DMA((2,)),
            ],
        ),
        out_shape=[
            seq_shape(micros, ROWS, D, dtype=F32),
            seq_shape(micros, ROWS, D, dtype=F32),
        ],
        compiler_params=params(40),
        name="key_gradients",
        cost_estimate=pl.CostEstimate(
            flops=3_000_000_000 * len(steps), bytes_accessed=20_000_000, transcendentals=0
        ),
    )(meta, keys, values, *sources)


def unturn_kernel(acc_a, acc_b, pa, pb, dk, dv, dk_more, dv_more, cosine, sine, back):
    for h in range(HEADS):
        acc, part = (acc_a, pa) if h < SIDE else (acc_b, pb)
        cols = slice(h % SIDE * HEAD_DIM, (h % SIDE + 1) * HEAD_DIM)
        place = slice(h * HEAD_DIM, (h + 1) * HEAD_DIM)
        value = (acc[0, :, cols].astype(F32) + part[0, :, cols].astype(F32)) * SCALE
        key_place = slice(D + h * HEAD_DIM, D + (h + 1) * HEAD_DIM)
        back[0, :, place] = turn(value, cosine[...], -sine[...]).astype(BF16)
        back[0, :, key_place] = turn((dk[0, :, place] + dk_more[0, :, place]) * SCALE, cosine[...], -sine[...]).astype(BF16)
    back[0, :, 2 * D :] = (dv[0] + dv_more[0]).astype(BF16)


def unturn(acc_a, acc_b, pa, pb, key_parts, cosine, sine):
    micros = acc_a.shape[0]
    half, whole, angle = seq_spec(ROWS, SW), seq_spec(ROWS, D), full_spec(ROWS, HEAD_DIM)
    return pl.pallas_call(
        unturn_kernel,
        grid=(micros,),
        in_specs=[half, half, half, half, whole, whole, whole, whole, angle, angle],
        out_specs=seq_spec(ROWS, 3 * D),
        out_shape=seq_shape(micros, ROWS, 3 * D),
        compiler_params=params(),
        name="unturn",
        cost_estimate=pl.CostEstimate(flops=10_000_000, bytes_accessed=16_000_000, transcendentals=0),
    )(acc_a, acc_b, pa, pb, *key_parts, cosine, sine)


def bits(size):
    return [1 << i for i in range(size.bit_length() - 1)]


def sums_kernel(
    early,
    late,
    gains,
    early_out,
    late_out,
    gains_out,
    *scratch,
    count,
    shards,
):
    scratch = list(scratch)
    halves = [scratch.pop(0) for _ in bits(shards)]
    early_slots, late_slots, gain_in, gain_sum = (scratch.pop(0) for _ in range(4))
    ring_send, ring_recv, half_send, half_recv, gain_send, gain_recv = scratch
    here, shard = lax.axis_index("ctx"), lax.axis_index("fsdp")
    place = ring_place(count)
    neighbour = (ring_index(place + 1, count), ring_index(place + count - 1, count))
    partners = [("fsdp", shard, bit) for bit in bits(shards)] + [("ctx", here, bit) for bit in bits(count)]

    def partner(axis, index, bit):
        return {axis: index + bit * (1 - 2 * ((index // bit) % 2))}

    barrier = pltpu.get_barrier_semaphore()
    known = [{"ctx": neighbour[0]}, {"ctx": neighbour[1]}] + [partner(*p) for p in partners]
    for device in known:
        pl.semaphore_signal(barrier, inc=1, device_id=device, device_id_type=pl.DeviceIdType.MESH)
    pl.semaphore_wait(barrier, len(known))

    sent = []

    def send(source, target, send_sem, recv_sem, device):
        copy = pltpu.make_async_remote_copy(
            source, target, send_sem, recv_sem, device_id=device, device_id_type=pl.DeviceIdType.MESH
        )
        copy.start()
        sent.append(copy)
        return copy

    def halve_start(i):
        held = late if i == 0 else halves[i - 1]
        bit = (shard // (1 << i)) % 2
        return [
            send(
                held.at[2 * j + 1 - bit],
                halves[i].at[j],
                half_send.at[i, j],
                half_recv.at[i, j],
                partner("fsdp", shard, 1 << i),
            )
            for j in range(shards >> (i + 1))
        ]

    def halve_finish(i, copies):
        held = late if i == 0 else halves[i - 1]
        bit = (shard // (1 << i)) % 2
        for j, copy in enumerate(copies):
            copy.wait_recv()

            def add(c, carry):
                halves[i][j, c] = (
                    halves[i][j, c].astype(F32) + held[2 * j + bit, c].astype(F32)
                ).astype(BF16)
                return carry

            lax.fori_loop(0, 2 * count, add, 0)

    def gain_start(i):
        return send(gain_sum.at[i], gain_in.at[i], gain_send.at[i], gain_recv.at[i], partner(*partners[i]))

    def gain_finish(i, copy):
        copy.wait_recv()
        gain_sum[i + 1] = gain_sum[i] + gain_in[i]

    def flow(number, source, slots, out):
        def home(side, hop):
            sign = 1 - 2 * side
            return side * count + (place - sign * hop + 2 * count) % count

        def sum_start(hop):
            copies = []
            for side in range(2):
                held = source.at[home(side, 1)] if hop == 1 else slots.at[side, hop - 2]
                copies.append(
                    send(
                        held,
                        slots.at[side, hop - 1],
                        ring_send.at[number, side, hop - 1],
                        ring_recv.at[number, side, hop - 1],
                        {"ctx": neighbour[side]},
                    )
                )
            return copies

        def sum_finish(hop, copies):
            for side in range(2):
                copies[side].wait_recv()
                total = slots[side, hop - 1].astype(F32) + source[home(side, 1 + hop)].astype(F32)
                if hop == count - 1:
                    out[home(side, 0)] = total.astype(BF16)
                else:
                    slots[side, hop - 1] = total.astype(BF16)

        def copy_start(hop):
            copies = []
            for side in range(2):
                chunk = home(side, hop - 1)
                copies.append(
                    send(
                        out.at[chunk],
                        out.at[chunk],
                        ring_send.at[number, side, count - 2 + hop],
                        ring_recv.at[number, side, count - 2 + hop],
                        {"ctx": neighbour[side]},
                    )
                )
            return copies

        def copy_finish(copies):
            for copy in copies:
                copy.wait_recv()

        return sum_start, sum_finish, copy_start, copy_finish

    early_flow = flow(0, early, early_slots, early_out)
    late_flow = flow(1, halves[-1].at[0], late_slots, late_out)
    gain_sum[0] = gains[...]
    stages, exchanges = len(halves), len(partners)
    half = halve_start(0)
    gain = gain_start(0)
    stage, exchange = 0, 0
    ring = early_flow[0](1)
    for hop in range(1, count):
        early_flow[1](hop, ring)
        if hop < count - 1:
            ring = early_flow[0](hop + 1)
        if stage < stages - 1:
            halve_finish(stage, half)
            stage += 1
            half = halve_start(stage)
        if exchange < exchanges:
            gain_finish(exchange, gain)
            exchange += 1
            if exchange < exchanges:
                gain = gain_start(exchange)
    ring = early_flow[2](1)
    halve_finish(stage, half)
    late_ring = late_flow[0](1)
    for hop in range(1, count):
        early_flow[3](ring)
        if hop < count - 1:
            ring = early_flow[2](hop + 1)
        late_flow[1](hop, late_ring)
        if hop < count - 1:
            late_ring = late_flow[0](hop + 1)
        if exchange < exchanges:
            gain_finish(exchange, gain)
            exchange += 1
            if exchange < exchanges:
                gain = gain_start(exchange)
    for hop in range(1, count):
        late_flow[3](late_flow[2](hop))
    gains_out[...] = gain_sum[exchanges]
    for copy in sent:
        copy.wait_send()


def sums(early, late, gains):
    shards, chunks, rows, width = late.shape
    count = chunks // 2
    more = early.shape[-1]
    exchanges = len(bits(shards)) + len(bits(count))
    vmem = pl.BlockSpec(memory_space=pltpu.VMEM)
    return pl.pallas_call(
        functools.partial(sums_kernel, count=count, shards=shards),
        in_specs=[vmem] * 3,
        out_specs=[vmem] * 3,
        out_shape=[
            jax.ShapeDtypeStruct(early.shape, BF16),
            jax.ShapeDtypeStruct(late.shape[1:], BF16),
            jax.ShapeDtypeStruct(gains.shape, F32),
        ],
        scratch_shapes=[pltpu.VMEM((bit and shards // (2 * bit), chunks, rows, width), BF16) for bit in bits(shards)]
        + [
            pltpu.VMEM((2, count - 1, early.shape[1], more), BF16),
            pltpu.VMEM((2, count - 1, rows, width), BF16),
            pltpu.VMEM((exchanges,) + gains.shape, F32),
            pltpu.VMEM((exchanges + 1,) + gains.shape, F32),
            pltpu.SemaphoreType.DMA((2, 2, 2 * count - 2)),
            pltpu.SemaphoreType.DMA((2, 2, 2 * count - 2)),
            pltpu.SemaphoreType.DMA((len(bits(shards)), shards // 2)),
            pltpu.SemaphoreType.DMA((len(bits(shards)), shards // 2)),
            pltpu.SemaphoreType.DMA((exchanges,)),
            pltpu.SemaphoreType.DMA((exchanges,)),
        ],
        compiler_params=pltpu.CompilerParams(
            vmem_limit_bytes=48 * 2**20, collective_id=0, has_side_effects=True
        ),
        name="sums",
        cost_estimate=pl.CostEstimate(flops=50_000_000, bytes_accessed=400_000_000, transcendentals=0),
    )(early, late, gains)


def to_chunks(value, count):
    rows, width = value.shape[-2:]
    lead = value.shape[:-2]
    chunks = 2 * count
    if rows % (16 * chunks) == 0:
        return value.reshape(lead + (chunks, rows // chunks, width))
    step = -(-width // (chunks * HEAD_DIM)) * HEAD_DIM
    value = jnp.pad(value, [(0, 0)] * len(lead) + [(0, 0), (0, step * chunks - width)])
    return jnp.moveaxis(value.reshape(lead + (rows, chunks, step)), -2, -3)


def from_chunks(value, rows, width):
    if value.shape[0] * value.shape[1] == rows:
        return value.reshape(rows, width)
    return jnp.moveaxis(value, 0, 1).reshape(rows, -1)[:, :width]


def norm_parts(value):
    scale = lax.rsqrt(jnp.mean(value * value, axis=-1, keepdims=True) + EPS)
    return value * scale, scale


def norm_back(hat, scale, back, gain):
    slope = back * gain
    return scale * (slope - hat * jnp.mean(slope * hat, axis=-1, keepdims=True))


def body(
    tokens,
    cotangent,
    query_weight,
    key_weight,
    value_weight,
    output_weight,
    gate_weight,
    up_weight,
    down_weight,
    first_gain,
    second_gain,
    cache_keys,
    cache_values,
    block_indices,
    partner,
):
    count = lax.axis_size("ctx")
    here = lax.axis_index("ctx")
    micros = tokens.shape[0]
    rows = micros * ROWS
    onward, backward = ring_pairs(count)

    def gather(value):
        return lax.all_gather(value, "fsdp", axis=0, tiled=True)

    indices = lax.all_gather(block_indices, "ctx", axis=1, tiled=True)
    gains = lax.all_gather(jnp.stack([first_gain, second_gain]), "fsdp", axis=1, tiled=True)
    full_query = gather(query_weight)
    full_key = gather(key_weight)
    full_value = gather(value_weight)
    full_output = gather(output_weight)
    full_gate = gather(gate_weight)
    full_up = gather(up_weight)
    full_down = gather(down_weight)
    gain_one = gains[0:1].astype(F32)
    gain_two = gains[1:2].astype(F32)

    pieces_at = jnp.stack([here, 2 * count - 1 - here])
    positions = (pieces_at[:, None] * HALF + jnp.arange(HALF, dtype=jnp.int32)[None, :]).reshape(ROWS)
    inverse = 10000.0 ** (-jnp.arange(HEAD_DIM // 2, dtype=F32) * 2.0 / HEAD_DIM)
    phase = positions.astype(F32)[:, None] * inverse[None, :]
    cosine = jnp.tile(jnp.cos(phase), (1, 2))
    sine = jnp.sin(phase)
    sine = jnp.concatenate([-sine, sine], axis=1)

    meta, cap = make_meta(indices, partner, cache_keys.shape[1] // BLOCK, count)
    memory_keys, memory_values = collect(meta, cache_keys, cache_values, count, cap)

    x = tokens.reshape(micros, ROWS, D)
    normed_low, qa, qb = project_query(x, gain_one, full_query, cosine, sine)
    keys, values = project_pairs(normed_low, full_key, full_value, cosine, sine)

    queries = [(qa, qb)]
    for _ in range(count - 1):
        qa, qb = lax.ppermute(qa, "ctx", onward), lax.ppermute(qb, "ctx", backward)
        queries.append((qa, qb))

    acc = ()
    for step in list(range(1, count)) + [0]:
        pa, pb, ta, tb = attend(
            meta, *queries[step], keys, values, memory_keys, memory_values, step, count, cap
        )
        if acc:
            acc = (lax.ppermute(acc[0], "ctx", onward), lax.ppermute(acc[1], "ctx", backward))
        if step == 0:
            mixed, mixed_low, total, middle, middle_low = finish(
                *acc, pa, pb, ta, tb, x, full_output, gain_two
            )
        else:
            acc = combine(acc, (pa, pb), (ta, tb))

    incoming = cotangent.reshape(micros, ROWS, D)
    layer_output, back_mid_normed, gradient_gate, gradient_up, gradient_down = feed(
        middle_low, incoming, middle, full_gate, full_up, full_down
    )
    da, db, back_middle, back_attn, gain_part = prepare(
        back_mid_normed, middle, incoming, gain_two, full_output, mixed, total
    )
    gradient_second = jnp.sum(gain_part, axis=(0, 1))
    gradient_output = jnp.einsum(
        "tc,td->cd", mixed_low.reshape(rows, D), back_attn.reshape(rows, D), preferred_element_type=F32
    ).astype(BF16)
    back_middle = back_middle.reshape(rows, D)
    inputs = tokens.reshape(rows, D).astype(F32)

    slopes = [(da, db)]
    for _ in range(count - 1):
        da, db = slopes[-1]
        slopes.append((lax.ppermute(da, "ctx", onward), lax.ppermute(db, "ctx", backward)))
    slopes[1], gradient_output = lax.optimization_barrier((slopes[1], gradient_output))

    acc = ()
    for step in range(count):
        part = unattend(
            meta, *queries[step], *slopes[step], keys, values, memory_keys, memory_values, step, count, cap
        )
        if step == 0:
            own = part
            continue
        if acc:
            acc = (lax.ppermute(acc[0], "ctx", onward), lax.ppermute(acc[1], "ctx", backward))
        acc = combine(acc, part)
    key_parts = [
        part
        for steps in (range(count // 2), range(count // 2, count))
        for part in key_gradients(meta, keys, values, queries, slopes, steps)
    ]
    ra, rb = lax.ppermute(acc[0], "ctx", onward), lax.ppermute(acc[1], "ctx", backward)
    back = unturn(ra, rb, *own, key_parts, cosine, sine).reshape(rows, 3 * D)
    normed_low = normed_low.reshape(rows, D)
    late = jnp.einsum("tc,td->cd", normed_low, back, preferred_element_type=F32).astype(BF16)
    back_in_normed = (
        jnp.einsum("td,cd->tc", back[:, :D], full_query, preferred_element_type=F32)
        + jnp.einsum("td,cd->tc", back[:, D : 2 * D], full_key, preferred_element_type=F32)
        + jnp.einsum("td,cd->tc", back[:, 2 * D :], full_value, preferred_element_type=F32)
    )
    in_hat, in_scale = norm_parts(inputs)
    gradient_first = jnp.sum(back_in_normed * in_hat, axis=0)
    input_gradient = back_middle + norm_back(in_hat, in_scale, back_in_normed, gain_one)

    def scatter(part):
        return lax.psum_scatter(part, "fsdp", scatter_dimension=0, tiled=True)

    early = jnp.concatenate(
        [
            scatter(part).reshape(D // lax.axis_size("fsdp"), -1)
            for part in (gradient_down, gradient_gate, gradient_up, gradient_output)
        ],
        axis=1,
    )
    shards = lax.axis_size("fsdp")
    late = late.reshape(shards, D // shards, 3 * D)
    gains_part = jnp.concatenate(
        [gradient_first[None], gradient_second[None], jnp.zeros((6, D), F32)], axis=0
    )
    early_sum, late_sum, gain_changes = sums(to_chunks(early, count), to_chunks(late, count), gains_part)
    early = from_chunks(early_sum, *early.shape).astype(F32)
    three = from_chunks(late_sum, *late.shape[1:]).astype(F32)
    units = gate_weight.shape[1]
    own_rows = D // lax.axis_size("fsdp")
    gain_changes = lax.dynamic_slice_in_dim(
        gain_changes, lax.axis_index("fsdp") * own_rows, own_rows, axis=1
    )
    return (
        layer_output.reshape(tokens.shape),
        input_gradient.reshape(tokens.shape),
        three[:, :D],
        three[:, D : 2 * D],
        three[:, 2 * D :],
        early[:, 3 * units :],
        early[:, units : 2 * units],
        early[:, 2 * units : 3 * units],
        early[:, :units].reshape(down_weight.shape),
        gain_changes[0],
        gain_changes[1],
    )


def solution(mesh):
    split = P("fsdp", "ctx", None, None, None)
    shard = P("fsdp", None)
    return jax.shard_map(
        body,
        mesh=mesh,
        in_specs=(
            split,
            split,
            *([shard] * 7),
            P("fsdp"),
            P("fsdp"),
            P("fsdp", "ctx", None),
            P("fsdp", "ctx", None),
            P("fsdp", "ctx", None, None, None, None),
            P("fsdp"),
        ),
        out_specs=(split, split, *([shard] * 7), P("fsdp"), P("fsdp")),
        check_vma=False,
    )
```

time: 1100 us -> 919 us (0.84)
  matrix products: 130 us -> 19.6 us
  starting transfers between devices: 151 us -> 70.9 us
  Pallas kernels: 444 us -> 488 us
  blocking collectives: 77.8 us -> 37.5 us
  local copies, waits for them, and re-layouts: 24.5 us -> 36.4 us
    pallas_call x1 -> x5, Pallas kernels: 7.73 us -> 275 us  [the longest x1 175 us: sums(): pl.pallas_call(functools.partial(sums_kernel, count=count, shards=shards)...]
    pallas_call x8, Pallas kernels: 193 us -> 82.2 us  [unattend(): pl.pallas_call(functools.partial(backward_kernel, step=step, count=count,...]
    dot_general x11 -> x1, matrix products: 102 us -> 4.59 us  [body(): jnp.einsum('tc,td->cd', mixed_low.reshape(rows, D), back_attn.reshape(row...]
    psum x2 -> x0, waiting for transfers between devices: 86.7 us -> none  [the longest x1 57.3 us: body(): lax.psum(early, 'ctx')]
    pallas_call x8, Pallas kernels: 133 us -> 59.4 us  [attend(): pl.pallas_call(functools.partial(forward_kernel, step=step, count=count,...]
    ppermute x7, waiting for transfers between devices: 7.24 us -> 74.4 us  [body(): lax.ppermute(da, 'ctx', onward)]
    reduce_scatter x5 -> x4, waiting for transfers between devices: 60 us -> 0.06 us  [scatter(): return lax.psum_scatter(part, 'fsdp', scatter_dimension=0, tiled=True)]
    ppermute x14, waiting for transfers between devices: 17.4 us -> 65.4 us  [body(): lax.ppermute(acc[0], 'ctx', onward)]
  transfers between devices with their start and end apart: 70 -> 67, of which waited for: 19 -> 39; matrix products, arithmetic and copies ran while one was open for 9% -> 4% of each run, Pallas kernels for 40% -> 29%
where the time goes in v2:
time: 919 us; the launch traced here: 910 us
  Pallas kernels  488 us (53%)
  waiting for transfers between devices  228 us (25%)
  starting transfers between devices  70.9 us (8%)
  blocking collectives  37.5 us (4%)
  local copies, waits for them, and re-layouts  36.4 us (4%)
  matrix products  19.6 us (2%)
  between operations  15.4 us (2%)
  other arithmetic  13.9 us (2%)
    pallas_call x1, Pallas kernels, sums(): pl.pallas_call(functools.partial(sums_kernel, count=count, shards=shards)...  175 us
    pallas_call x8, Pallas kernels, unattend(): pl.pallas_call(functools.partial(backward_kernel, step=step, count=count,...  82.2 us
    ppermute x7, waiting for transfers between devices, body(): lax.ppermute(da, 'ctx', onward)  74.4 us
    ppermute x14, waiting for transfers between devices, body(): lax.ppermute(acc[0], 'ctx', onward)  65.4 us
    ppermute x7, waiting for transfers between devices, body(): lax.ppermute(qa, 'ctx', onward)  60.8 us
    pallas_call x8, Pallas kernels, attend(): pl.pallas_call(functools.partial(forward_kernel, step=step, count=count,...  59.4 us
    pallas_call x1, Pallas kernels, feed(): pl.pallas_call(feed_kernel, grid=(units // TILE,), in_specs=[whole, whole...  52.6 us
    pallas_call x2, Pallas kernels, key_gradients(): pl.pallas_call(functools.partial(key_kernel, steps=steps, micros=micros),...  36 us
  transfers between devices with their start and end apart: 67, of which 39 were waited for; matrix products, arithmetic and copies ran while one was open for 4% of the time, Pallas kernels for 29%

profile of v2, /device:TPU:0, one launch (start us, length us, event | category | flops | bytes accessed | tf_op | source)
XLA Modules:
  0.0 910.1 jit_solution(14761047174416913152)
XLA Ops:
  12.8 32.4 %all_gather.27 = s32[3,8,2,2,8,4]{4,5,3,2,0,1:T(4,128)S(1)} all-gather(s32[3,1,2,2,8,4]{4,5,3,2,0,1:T(4,128)S(1)} %bitcast.84), channel_id=1, replica_groups=mesh['ctx'=8,'fsdp'=4] {'ctx'}, dimensions={1}, use_global_device_ids=true | all-gather | bytes 13824 | tf_op jit(solution)/shard_map/all_gather | solution.py:1148
  63.6 24.7 %collect.1 = (bf16[3,8,2,32,64,128]{5,4,3,2,1,0:T(8,128)(2,1)}, bf16[3,8,2,32,64,128]{5,4,3,2,1,0:T(8,128)(2,1)}) custom-call(s32[1601]{0:T(1024)} %concatenate.29.meta, bf16[6144,1024]{1,0:T(8,128)(2,1)} %bitcast.68, bf16[6144,1024]{1,0:T(8,128)(2,1)} %bitcast.69), custom_call_target="tpu_custom_call" | custom-call | bytes 90000000 | tf_op jit(solution)/shard_map/collect/pallas_call | solution.py:175
  102.3 7.9 attend.8
  117.3 7.7 attend.9
  136.9 11.9 %collective-permute-done.8.qa.refs_12_ = bf16[3,256,512]{2,1,0:T(8,128)(2,1)S(1)} collective-permute-done((bf16[3,256,512]{2,1,0:T(8,128)(2,1)S(1)}, bf16[3,256,512]{2,1,0:T(8,128)(2,1)S(1)}, u32[]{:S(2)}, u32[]{:S(2)}) %collective-permute-start.8) | collective-permute-done | bytes 786464 | tf_op jit(solution)/shard_map/ppermute | solution.py:1177
  171.7 11.9 %collective-permute-done.12.qa.refs_0_ = bf16[3,256,512]{2,1,0:T(8,128)(2,1)S(1)} collective-permute-done((bf16[3,256,512]{2,1,0:T(8,128)(2,1)S(1)}, bf16[3,256,512]{2,1,0:T(8,128)(2,1)S(1)}, u32[]{:S(2)}, u32[]{:S(2)}) %collective-permute-start.12) | collective-permute-done | bytes 786464 | tf_op jit(solution)/shard_map/ppermute | solution.py:1177
  206.4 11.9 %collective-permute-done.16.qa.refs_4_ = bf16[3,256,512]{2,1,0:T(8,128)(2,1)S(1)} collective-permute-done((bf16[3,256,512]{2,1,0:T(8,128)(2,1)S(1)}, bf16[3,256,512]{2,1,0:T(8,128)(2,1)S(1)}, u32[]{:S(2)}, u32[]{:S(2)}) %collective-permute-start.16) | collective-permute-done | bytes 786464 | tf_op jit(solution)/shard_map/ppermute | solution.py:1177
  221.6 7.4 attend.12
  241.2 11.9 %collective-permute-done.20.qa.refs_8_ = bf16[3,256,512]{2,1,0:T(8,128)(2,1)S(1)} collective-permute-done((bf16[3,256,512]{2,1,0:T(8,128)(2,1)S(1)}, bf16[3,256,512]{2,1,0:T(8,128)(2,1)S(1)}, u32[]{:S(2)}, u32[]{:S(2)}) %collective-permute-start.20) | collective-permute-done | bytes 786464 | tf_op jit(solution)/shard_map/ppermute | solution.py:1177
  256.3 7.4 attend.13
  275.9 11.9 %collective-permute-done.24.qa.refs_12_ = bf16[3,256,512]{2,1,0:T(8,128)(2,1)S(1)} collective-permute-done((bf16[3,256,512]{2,1,0:T(8,128)(2,1)S(1)}, bf16[3,256,512]{2,1,0:T(8,128)(2,1)S(1)}, u32[]{:S(2)}, u32[]{:S(2)}) %collective-permute-start.24) | collective-permute-done | bytes 786464 | tf_op jit(solution)/shard_map/ppermute | solution.py:1177
  297.3 8.4 collective-permute-done.22.refs_0_
  328.7 8.9 finish.1
  337.7 52.6 %feed.1 = (bf16[3,256,1024]{2,1,0:T(8,128)(2,1)}, f32[3,256,1024]{2,1,0:T(8,128)}, bf16[1024,2816]{1,0:T(8,128)(2,1)}, bf16[1024,2816]{1,0:T(8,128)(2,1)}, bf16[2816,1024]{1,0:T(8,128)(2,1)}) custom-call(bf16[3,256,1024]{2,1,0:T(8,128)(2,1)} %get-tuple-element.172.normed, bf16[3,256,1024]{2,1,0:T(8,128)(2,1)} %bitcast.77, ...), custom_call_target="tpu_custom_call" | custom-call | flops 39862665216 | bytes 50000000 | tf_op jit(solution)/shard_map/feed/pallas_call | solution.py:582
  390.4 11.6 %prepare.1 = (bf16[3,272,512]{2,1,0:T(8,128)(2,1)}, bf16[3,272,512]{2,1,0:T(8,128)(2,1)}, f32[3,256,1024]{2,1,0:T(8,128)}, bf16[3,256,1024]{2,1,0:T(8,128)(2,1)}, f32[3,8,1024]{2,1,0:T(8,128)}) custom-call(f32[3,256,1024]{2,1,0:T(8,128)} %get-tuple-element.175.back_normed, f32[3,256,1024]{2,1,0:T(8,128)} %get-tuple-element.173.middle, ...), custom_call_target="tpu_custom_call" | custom-call | flops 1610612736 | bytes 22000000 | tf_op jit(solution)/shard_map/prepare/pallas_call | solution.py:639
  410.8 12.8 %collective-permute-done.28.da.refs_6_ = bf16[3,272,512]{2,1,0:T(8,128)(2,1)S(1)} collective-permute-done((bf16[3,272,512]{2,1,0:T(8,128)(2,1)}, bf16[3,272,512]{2,1,0:T(8,128)(2,1)S(1)}, u32[]{:S(2)}, u32[]{:S(2)}) %collective-permute-start.28) | collective-permute-done | bytes 835616 | tf_op jit(solution)/shard_map/ppermute | solution.py:1211
  429.4 18.8 %collective-permute-done.32.da.refs_10_ = bf16[3,272,512]{2,1,0:T(8,128)(2,1)} collective-permute-done((bf16[3,272,512]{2,1,0:T(8,128)(2,1)}, bf16[3,272,512]{2,1,0:T(8,128)(2,1)}, u32[]{:S(2)}, u32[]{:S(2)}) %collective-permute-start.32) | collective-permute-done | bytes 835616 | tf_op jit(solution)/shard_map/ppermute | solution.py:1211
  455.0 10.2 %unattend.8 = (bf16[3,256,512]{2,1,0:T(8,128)(2,1)S(1)}, bf16[3,256,512]{2,1,0:T(8,128)(2,1)S(1)}) custom-call(s32[1601]{0:T(1024)S(1)} %copy-done.51, bf16[3,256,512]{2,1,0:T(8,128)(2,1)S(1)} %copy-done.12, bf16[3,256,512]{2,1,0:T(8,128)(2,1)S(1)} %copy-done.15, bf16[3,272,512]{2,1,0:T(8,128)(2,1)S(1)} %copy-done.57, bf16[3,272,512]{2,1,0:T(8,128)(2,1)S(1)} %copy-done.60, ...), custom_call_target="tpu_custom_call" | custom-call | flops 8000000000 | bytes 12000000 | tf_op jit(solution)/shard_map/unattend/pallas_call | solution.py:741
  471.2 10.7 %unattend.9 = (bf16[3,256,512]{2,1,0:T(8,128)(2,1)S(1)}, bf16[3,256,512]{2,1,0:T(8,128)(2,1)S(1)}) custom-call(s32[1601]{0:T(1024)S(1)} %copy-done.51, bf16[3,256,512]{2,1,0:T(8,128)(2,1)S(1)} %copy-done.18, bf16[3,256,512]{2,1,0:T(8,128)(2,1)S(1)} %copy-done.21, bf16[3,272,512]{2,1,0:T(8,128)(2,1)} %collective-permute-done.32.da.refs_10_, ...), custom_call_target="tpu_custom_call" | custom-call | flops 8000000000 | bytes 12000000 | tf_op jit(solution)/shard_map/unattend/pallas_call | solution.py:741
  492.6 10.8 %unattend.10 = (bf16[3,256,512]{2,1,0:T(8,128)(2,1)S(1)}, bf16[3,256,512]{2,1,0:T(8,128)(2,1)S(1)}) custom-call(s32[1601]{0:T(1024)S(1)} %copy-done.51, bf16[3,256,512]{2,1,0:T(8,128)(2,1)S(1)} %copy-done.27, bf16[3,256,512]{2,1,0:T(8,128)(2,1)S(1)} %copy-done.33, bf16[3,272,512]{2,1,0:T(8,128)(2,1)} %collective-permute-done.36.da.refs_14_, ...), custom_call_target="tpu_custom_call" | custom-call | flops 8000000000 | bytes 12000000 | tf_op jit(solution)/shard_map/unattend/pallas_call | solution.py:741
  512.2 14.9 %collective-permute-done.40.da.refs_2_ = bf16[3,272,512]{2,1,0:T(8,128)(2,1)} collective-permute-done((bf16[3,272,512]{2,1,0:T(8,128)(2,1)}, bf16[3,272,512]{2,1,0:T(8,128)(2,1)}, u32[]{:S(2)}, u32[]{:S(2)}) %collective-permute-start.40) | collective-permute-done | bytes 835616 | tf_op jit(solution)/shard_map/ppermute | solution.py:1211
  529.3 10.7 %unattend.11 = (bf16[3,256,512]{2,1,0:T(8,128)(2,1)S(1)}, bf16[3,256,512]{2,1,0:T(8,128)(2,1)S(1)}) custom-call(s32[1601]{0:T(1024)S(1)} %copy-done.51, bf16[3,256,512]{2,1,0:T(8,128)(2,1)S(1)} %copy-done.24, bf16[3,256,512]{2,1,0:T(8,128)(2,1)S(1)} %copy-done.30, bf16[3,272,512]{2,1,0:T(8,128)(2,1)} %collective-permute-done.40.da.refs_2_, ...), custom_call_target="tpu_custom_call" | custom-call | flops 8000000000 | bytes 12000000 | tf_op jit(solution)/shard_map/unattend/pallas_call | solution.py:741
  548.0 13.9 %collective-permute-done.44.da.refs_6_ = bf16[3,272,512]{2,1,0:T(8,128)(2,1)} collective-permute-done((bf16[3,272,512]{2,1,0:T(8,128)(2,1)}, bf16[3,272,512]{2,1,0:T(8,128)(2,1)}, u32[]{:S(2)}, u32[]{:S(2)}) %collective-permute-start.44) | collective-permute-done | bytes 835616 | tf_op jit(solution)/shard_map/ppermute | solution.py:1211
  566.3 10.7 %unattend.12 = (bf16[3,256,512]{2,1,0:T(8,128)(2,1)S(1)}, bf16[3,256,512]{2,1,0:T(8,128)(2,1)S(1)}) custom-call(s32[1601]{0:T(1024)S(1)} %copy-done.51, bf16[3,256,512]{2,1,0:T(8,128)(2,1)S(1)} %copy-done.36, bf16[3,256,512]{2,1,0:T(8,128)(2,1)S(1)} %copy-done.39, bf16[3,272,512]{2,1,0:T(8,128)(2,1)} %collective-permute-done.44.da.refs_6_, ...), custom_call_target="tpu_custom_call" | custom-call | flops 8000000000 | bytes 12000000 | tf_op jit(solution)/shard_map/unattend/pallas_call | solution.py:741
  584.4 8.8 unattend.15
  599.2 11.0 %unattend.13 = (bf16[3,256,512]{2,1,0:T(8,128)(2,1)S(1)}, bf16[3,256,512]{2,1,0:T(8,128)(2,1)S(1)}) custom-call(s32[1601]{0:T(1024)S(1)} %copy-done.51, bf16[3,256,512]{2,1,0:T(8,128)(2,1)S(1)} %copy-done.42, bf16[3,256,512]{2,1,0:T(8,128)(2,1)S(1)} %copy-done.45, bf16[3,272,512]{2,1,0:T(8,128)(2,1)} %collective-permute-done.48.da.refs_10_, ...), custom_call_target="tpu_custom_call" | custom-call | flops 8000000000 | bytes 12000000 | tf_op jit(solution)/shard_map/unattend/pallas_call | solution.py:741
  618.1 18.5 %key_gradients.2 = (f32[3,256,1024]{2,1,0:T(8,128)}, f32[3,256,1024]{2,1,0:T(8,128)}) custom-call(s32[1601]{0:T(1024)S(1)} %copy-done.51, bf16[3,256,1024]{2,1,0:T(8,128)(2,1)S(1)} %copy-done.1, bf16[3,256,1024]{2,1,0:T(8,128)(2,1)} %get-tuple-element.123.v, bf16[3,256,512]{2,1,0:T(8,128)(2,1)S(1)} %copy-done.7, bf16[3,256,512]{2,1,0:T(8,128)(2,1)S(1)} %copy-done.10, ...), custom_call_target="tpu_custom_call" | custom-call | flops 12000000000 | bytes 20000000 | tf_op jit(solution)/shard_map/key_gradients/pallas_call | solution.py:836
  636.7 12.5 %collective-permute-done.52.da.refs_14_ = bf16[3,272,512]{2,1,0:T(8,128)(2,1)S(1)} collective-permute-done((bf16[3,272,512]{2,1,0:T(8,128)(2,1)}, bf16[3,272,512]{2,1,0:T(8,128)(2,1)S(1)}, u32[]{:S(2)}, u32[]{:S(2)}) %collective-permute-start.52) | collective-permute-done | bytes 835616 | tf_op jit(solution)/shard_map/ppermute | solution.py:1211
  649.2 9.3 %unattend.14 = (bf16[3,256,512]{2,1,0:T(8,128)(2,1)S(1)}, bf16[3,256,512]{2,1,0:T(8,128)(2,1)S(1)}) custom-call(s32[1601]{0:T(1024)S(1)} %copy-done.51, bf16[3,256,512]{2,1,0:T(8,128)(2,1)S(1)} %copy-done.48, bf16[3,256,512]{2,1,0:T(8,128)(2,1)S(1)} %copy-done.50, bf16[3,272,512]{2,1,0:T(8,128)(2,1)S(1)} %collective-permute-done.52.da.refs_14_, ...), custom_call_target="tpu_custom_call" | custom-call | flops 8000000000 | bytes 12000000 | tf_op jit(solution)/shard_map/unattend/pallas_call | solution.py:741
  662.9 17.5 %key_gradients.3 = (f32[3,256,1024]{2,1,0:T(8,128)}, f32[3,256,1024]{2,1,0:T(8,128)}) custom-call(s32[1601]{0:T(1024)S(1)} %copy-done.51, bf16[3,256,1024]{2,1,0:T(8,128)(2,1)S(1)} %copy-done.1, bf16[3,256,1024]{2,1,0:T(8,128)(2,1)} %get-tuple-element.123.v, bf16[3,256,512]{2,1,0:T(8,128)(2,1)S(1)} %copy-done.25, bf16[3,256,512]{2,1,0:T(8,128)(2,1)S(1)} %copy-done.31, ...), custom_call_target="tpu_custom_call" | custom-call | flops 12000000000 | bytes 20000000 | tf_op jit(solution)/shard_map/key_gradients/pallas_call | solution.py:836
  681.6 9.7 %unturn.1 = bf16[3,256,3072]{2,1,0:T(8,128)(2,1)} custom-call(bf16[3,256,512]{2,1,0:T(8,128)(2,1)} %copy-done.72, bf16[3,256,512]{2,1,0:T(8,128)(2,1)} %copy-done.73, bf16[3,256,512]{2,1,0:T(8,128)(2,1)} %copy-done.62, bf16[3,256,512]{2,1,0:T(8,128)(2,1)} %copy-done.63, f32[3,256,1024]{2,1,0:T(8,128)} %get-tuple-element.215.dk, ...), custom_call_target="tpu_custom_call" | custom-call | flops 10000000 | bytes 16000000 | tf_op jit(solution)/shard_map/unturn/pallas_call | solution.py:876
  716.4 174.7 %sums.1 = (bf16[16,16,9472]{2,1,0:T(8,128)(2,1)}, bf16[16,16,3072]{2,1,0:T(8,128)(2,1)S(1)}, f32[8,1024]{1,0:T(8,128)S(1)}) custom-call(bf16[16,16,9472]{2,1,0:T(8,128)(2,1)} %pad_maximum_fusion.early, bf16[4,16,16,3072]{3,2,1,0:T(8,128)(2,1)} %bitcast.70, f32[8,1024]{1,0:T(8,128)S(1)} %maximum_maximum_fusion.gains), custom_call_target="tpu_custom_call" | custom-call | flops 50000000 | bytes 400000000 | tf_op jit(solution)/shard_map/sums/pallas_call | solution.py:1065
  (380 shorter events, 290.8 us)
Async XLA Ops:
  7.2 45.9 %all-gather.8.cloned.1.call-start = ((), (), s32[]{:S(2)}) async-start(), calls=%async_computation.4 | async-start | bytes 2621440 | tf_op jit(solution)/shard_map/all_gather | solution.py:1146
  7.9 80.3 %all-gather.10.cloned.1.call-start = ((), (), s32[]{:S(2)}) async-start(), calls=%async_computation.5 | async-start | bytes 2621440 | tf_op jit(solution)/shard_map/all_gather | solution.py:1146
  8.7 79.6 %all-gather.12.cloned.1.call-start = ((), (), s32[]{:S(2)}) async-start(), calls=%async_computation.6 | async-start | bytes 2621440 | tf_op jit(solution)/shard_map/all_gather | solution.py:1146
  9.4 312.0 %all-gather.14.cloned.1.call-start = ((), (), s32[]{:S(2)}) async-start(), calls=%async_computation.7 | async-start | bytes 2621440 | tf_op jit(solution)/shard_map/all_gather | solution.py:1146
  10.0 327.6 %all-gather.16.cloned.1.call-start = ((), (), s32[]{:S(2)}) async-start(), calls=%async_computation.8 | async-start | bytes 7208960 | tf_op jit(solution)/shard_map/all_gather | solution.py:1146
  10.6 327.1 %all-gather.18.cloned.1.call-start = ((), (), s32[]{:S(2)}) async-start(), calls=%async_computation.9 | async-start | bytes 7208960 | tf_op jit(solution)/shard_map/all_gather | solution.py:1146
  11.2 326.5 %all-gather.20.cloned.1.call-start = ((), (), s32[]{:S(2)}) async-start(), calls=%async_computation.10 | async-start | bytes 7208960 | tf_op jit(solution)/shard_map/all_gather | solution.py:1146
  11.9 697.2 %reduce-scatter.5.cloned.1.call-start = ((), (), s32[]{:S(2)}) async-start(), calls=%async_computation.11 | async-start | bytes 7208960 | tf_op jit(solution)/shard_map/reduce_scatter | solution.py:1244
  58.9 36.6 %collective-permute-start = (bf16[3,256,512]{2,1,0:T(8,128)(2,1)}, bf16[3,256,512]{2,1,0:T(8,128)(2,1)S(1)}, u32[]{:S(2)}, u32[]{:S(2)}) collective-permute-start(bf16[3,256,512]{2,1,0:T(8,128)(2,1)} %get-tuple-element.119.qa.refs_0_), channel_id=1, source_target_pairs={{0,8},{8,16},{16,24},{24,28},{28,20},{20,12},{12,4},{4,0},{1,9},{9... | collective-permute-start | bytes 2359304 | tf_op jit(solution)/shard_map/ppermute | solution.py:1177
  58.9 40.3 %collective-permute-start.1 = (bf16[3,256,512]{2,1,0:T(8,128)(2,1)}, bf16[3,256,512]{2,1,0:T(8,128)(2,1)S(1)}, u32[]{:S(2)}, u32[]{:S(2)}) collective-permute-start(bf16[3,256,512]{2,1,0:T(8,128)(2,1)} %get-tuple-element.120.qb.refs_1_), channel_id=1, source_target_pairs={{8,0},{16,8},{24,16},{28,24},{20,28},{12,20},{4,12},{0,4},{9,1},{1... | collective-permute-start | bytes 2359304 | tf_op jit(solution)/shard_map/ppermute | solution.py:1177
  116.2 35.0 %collective-permute-start.9 = (bf16[3,256,512]{2,1,0:T(8,128)(2,1)S(1)}, bf16[3,256,512]{2,1,0:T(8,128)(2,1)S(1)}, u32[]{:S(2)}, u32[]{:S(2)}) collective-permute-start(bf16[3,256,512]{2,1,0:T(8,128)(2,1)S(1)} %collective-permute-done.5.qb.refs_9_), channel_id=1, source_target_pairs={{8,0},{16,8},{24,16},{28,24},{20,28},{12,20},{4,12},{0,4},{9,1},{1... | collective-permute-start | bytes 2359304 | tf_op jit(solution)/shard_map/ppermute | solution.py:1177
  148.7 34.8 %collective-permute-start.12 = (bf16[3,256,512]{2,1,0:T(8,128)(2,1)S(1)}, bf16[3,256,512]{2,1,0:T(8,128)(2,1)S(1)}, u32[]{:S(2)}, u32[]{:S(2)}) collective-permute-start(bf16[3,256,512]{2,1,0:T(8,128)(2,1)S(1)} %collective-permute-done.8.qa.refs_12_), channel_id=1, source_target_pairs={{0,8},{8,16},{16,24},{24,28},{28,20},{20,12},{12,4},{4,0},{1,9},{9... | collective-permute-start | bytes 2359304 | tf_op jit(solution)/shard_map/ppermute | solution.py:1177
  151.2 34.8 %collective-permute-start.13 = (bf16[3,256,512]{2,1,0:T(8,128)(2,1)S(1)}, bf16[3,256,512]{2,1,0:T(8,128)(2,1)S(1)}, u32[]{:S(2)}, u32[]{:S(2)}) collective-permute-start(bf16[3,256,512]{2,1,0:T(8,128)(2,1)S(1)} %collective-permute-done.9.qb.refs_13_), channel_id=1, source_target_pairs={{8,0},{16,8},{24,16},{28,24},{20,28},{12,20},{4,12},{0,4},{9,1},{1... | collective-permute-start | bytes 2359304 | tf_op jit(solution)/shard_map/ppermute | solution.py:1177
  183.5 34.8 %collective-permute-start.16 = (bf16[3,256,512]{2,1,0:T(8,128)(2,1)S(1)}, bf16[3,256,512]{2,1,0:T(8,128)(2,1)S(1)}, u32[]{:S(2)}, u32[]{:S(2)}) collective-permute-start(bf16[3,256,512]{2,1,0:T(8,128)(2,1)S(1)} %collective-permute-done.12.qa.refs_0_), channel_id=1, source_target_pairs={{0,8},{8,16},{16,24},{24,28},{28,20},{20,12},{12,4},{4,0},{1,9},{9... | collective-permute-start | bytes 2359304 | tf_op jit(solution)/shard_map/ppermute | solution.py:1177
  186.0 34.8 %collective-permute-start.17 = (bf16[3,256,512]{2,1,0:T(8,128)(2,1)S(1)}, bf16[3,256,512]{2,1,0:T(8,128)(2,1)S(1)}, u32[]{:S(2)}, u32[]{:S(2)}) collective-permute-start(bf16[3,256,512]{2,1,0:T(8,128)(2,1)S(1)} %collective-permute-done.13.qb.refs_1_), channel_id=1, source_target_pairs={{8,0},{16,8},{24,16},{28,24},{20,28},{12,20},{4,12},{0,4},{9,1},{1... | collective-permute-start | bytes 2359304 | tf_op jit(solution)/shard_map/ppermute | solution.py:1177
  218.3 34.8 %collective-permute-start.20 = (bf16[3,256,512]{2,1,0:T(8,128)(2,1)S(1)}, bf16[3,256,512]{2,1,0:T(8,128)(2,1)S(1)}, u32[]{:S(2)}, u32[]{:S(2)}) collective-permute-start(bf16[3,256,512]{2,1,0:T(8,128)(2,1)S(1)} %collective-permute-done.16.qa.refs_4_), channel_id=1, source_target_pairs={{0,8},{8,16},{16,24},{24,28},{28,20},{20,12},{12,4},{4,0},{1,9},{9... | collective-permute-start | bytes 2359304 | tf_op jit(solution)/shard_map/ppermute | solution.py:1177
  220.8 34.8 %collective-permute-start.21 = (bf16[3,256,512]{2,1,0:T(8,128)(2,1)S(1)}, bf16[3,256,512]{2,1,0:T(8,128)(2,1)S(1)}, u32[]{:S(2)}, u32[]{:S(2)}) collective-permute-start(bf16[3,256,512]{2,1,0:T(8,128)(2,1)S(1)} %collective-permute-done.17.qb.refs_5_), channel_id=1, source_target_pairs={{8,0},{16,8},{24,16},{28,24},{20,28},{12,20},{4,12},{0,4},{9,1},{1... | collective-permute-start | bytes 2359304 | tf_op jit(solution)/shard_map/ppermute | solution.py:1177
  253.0 34.8 %collective-permute-start.24 = (bf16[3,256,512]{2,1,0:T(8,128)(2,1)S(1)}, bf16[3,256,512]{2,1,0:T(8,128)(2,1)S(1)}, u32[]{:S(2)}, u32[]{:S(2)}) collective-permute-start(bf16[3,256,512]{2,1,0:T(8,128)(2,1)S(1)} %collective-permute-done.20.qa.refs_8_), channel_id=1, source_target_pairs={{0,8},{8,16},{16,24},{24,28},{28,20},{20,12},{12,4},{4,0},{1,9},{9... | collective-permute-start | bytes 2359304 | tf_op jit(solution)/shard_map/ppermute | solution.py:1177
  255.5 34.8 %collective-permute-start.25 = (bf16[3,256,512]{2,1,0:T(8,128)(2,1)S(1)}, bf16[3,256,512]{2,1,0:T(8,128)(2,1)S(1)}, u32[]{:S(2)}, u32[]{:S(2)}) collective-permute-start(bf16[3,256,512]{2,1,0:T(8,128)(2,1)S(1)} %collective-permute-done.21.qb.refs_9_), channel_id=1, source_target_pairs={{8,0},{16,8},{24,16},{28,24},{20,28},{12,20},{4,12},{0,4},{9,1},{1... | collective-permute-start | bytes 2359304 | tf_op jit(solution)/shard_map/ppermute | solution.py:1177
  390.3 322.1 %reduce-scatter.11.cloned.1.call-start = ((), (), s32[]{:S(2)}) async-start(), calls=%async_computation.14 | async-start | bytes 2621440 | tf_op jit(solution)/shard_map/reduce_scatter | solution.py:1244
  426.7 285.8 %reduce-scatter.9.cloned.1.call-start = ((), (), s32[]{:S(2)}) async-start(), calls=%async_computation.13 | async-start | bytes 7208960 | tf_op jit(solution)/shard_map/reduce_scatter | solution.py:1244
  427.3 285.2 %reduce-scatter.7.cloned.1.call-start = ((), (), s32[]{:S(2)}) async-start(), calls=%async_computation.12 | async-start | bytes 7208960 | tf_op jit(solution)/shard_map/reduce_scatter | solution.py:1244
  448.2 42.4 %collective-permute-start.36 = (bf16[3,272,512]{2,1,0:T(8,128)(2,1)}, bf16[3,272,512]{2,1,0:T(8,128)(2,1)}, u32[]{:S(2)}, u32[]{:S(2)}) collective-permute-start(bf16[3,272,512]{2,1,0:T(8,128)(2,1)} %collective-permute-done.32.da.refs_10_), channel_id=1, source_target_pairs={{0,8},{8,16},{16,24},{24,28},{28,20},{20,12},{12,4},{4,0},{1,9},{9... | collective-permute-start | bytes 2506760 | tf_op jit(solution)/shard_map/ppermute | solution.py:1211
  448.2 42.6 %collective-permute-start.37 = (bf16[3,272,512]{2,1,0:T(8,128)(2,1)}, bf16[3,272,512]{2,1,0:T(8,128)(2,1)}, u32[]{:S(2)}, u32[]{:S(2)}) collective-permute-start(bf16[3,272,512]{2,1,0:T(8,128)(2,1)} %collective-permute-done.33.db.refs_11_), channel_id=1, source_target_pairs={{8,0},{16,8},{24,16},{28,24},{20,28},{12,20},{4,12},{0,4},{9,1},{1... | collective-permute-start | bytes 2506760 | tf_op jit(solution)/shard_map/ppermute | solution.py:1211
  490.6 36.5 %collective-permute-start.40 = (bf16[3,272,512]{2,1,0:T(8,128)(2,1)}, bf16[3,272,512]{2,1,0:T(8,128)(2,1)}, u32[]{:S(2)}, u32[]{:S(2)}) collective-permute-start(bf16[3,272,512]{2,1,0:T(8,128)(2,1)} %collective-permute-done.36.da.refs_14_), channel_id=1, source_target_pairs={{0,8},{8,16},{16,24},{24,28},{28,20},{20,12},{12,4},{4,0},{1,9},{9... | collective-permute-start | bytes 2506760 | tf_op jit(solution)/shard_map/ppermute | solution.py:1211
  490.9 36.5 %collective-permute-start.41 = (bf16[3,272,512]{2,1,0:T(8,128)(2,1)}, bf16[3,272,512]{2,1,0:T(8,128)(2,1)}, u32[]{:S(2)}, u32[]{:S(2)}) collective-permute-start(bf16[3,272,512]{2,1,0:T(8,128)(2,1)} %collective-permute-done.37.db.refs_15_), channel_id=1, source_target_pairs={{8,0},{16,8},{24,16},{28,24},{20,28},{12,20},{4,12},{0,4},{9,1},{1... | collective-permute-start | bytes 2506760 | tf_op jit(solution)/shard_map/ppermute | solution.py:1211
  527.1 34.8 %collective-permute-start.44 = (bf16[3,272,512]{2,1,0:T(8,128)(2,1)}, bf16[3,272,512]{2,1,0:T(8,128)(2,1)}, u32[]{:S(2)}, u32[]{:S(2)}) collective-permute-start(bf16[3,272,512]{2,1,0:T(8,128)(2,1)} %collective-permute-done.40.da.refs_2_), channel_id=1, source_target_pairs={{0,8},{8,16},{16,24},{24,28},{28,20},{20,12},{12,4},{4,0},{1,9},{9... | collective-permute-start | bytes 2506760 | tf_op jit(solution)/shard_map/ppermute | solution.py:1211
  527.4 34.8 %collective-permute-start.45 = (bf16[3,272,512]{2,1,0:T(8,128)(2,1)}, bf16[3,272,512]{2,1,0:T(8,128)(2,1)}, u32[]{:S(2)}, u32[]{:S(2)}) collective-permute-start(bf16[3,272,512]{2,1,0:T(8,128)(2,1)} %collective-permute-done.41.db.refs_3_), channel_id=1, source_target_pairs={{8,0},{16,8},{24,16},{28,24},{20,28},{12,20},{4,12},{0,4},{9,1},{1... | collective-permute-start | bytes 2506760 | tf_op jit(solution)/shard_map/ppermute | solution.py:1211
  561.8 34.8 %collective-permute-start.48 = (bf16[3,272,512]{2,1,0:T(8,128)(2,1)}, bf16[3,272,512]{2,1,0:T(8,128)(2,1)}, u32[]{:S(2)}, u32[]{:S(2)}) collective-permute-start(bf16[3,272,512]{2,1,0:T(8,128)(2,1)} %collective-permute-done.44.da.refs_6_), channel_id=1, source_target_pairs={{0,8},{8,16},{16,24},{24,28},{28,20},{20,12},{12,4},{4,0},{1,9},{9... | collective-permute-start | bytes 2506760 | tf_op jit(solution)/shard_map/ppermute | solution.py:1211
  562.1 34.8 %collective-permute-start.49 = (bf16[3,272,512]{2,1,0:T(8,128)(2,1)}, bf16[3,272,512]{2,1,0:T(8,128)(2,1)}, u32[]{:S(2)}, u32[]{:S(2)}) collective-permute-start(bf16[3,272,512]{2,1,0:T(8,128)(2,1)} %collective-permute-done.45.db.refs_7_), channel_id=1, source_target_pairs={{8,0},{16,8},{24,16},{28,24},{20,28},{12,20},{4,12},{0,4},{9,1},{1... | collective-permute-start | bytes 2506760 | tf_op jit(solution)/shard_map/ppermute | solution.py:1211
  613.5 45.0 %collective-permute-start.50 = (bf16[3,256,512]{2,1,0:T(8,128)(2,1)S(1)}, bf16[3,256,512]{2,1,0:T(8,128)(2,1)S(1)}, u32[]{:S(2)}, u32[]{:S(2)}) collective-permute-start(bf16[3,256,512]{2,1,0:T(8,128)(2,1)S(1)} %get-tuple-element.207), channel_id=1, source_target_pairs={{0,8},{8,16},{16,24},{24,28},{28,20},{20,12},{12,4},{4,0},{1,9},{9... | collective-permute-start | bytes 2359304 | tf_op jit(solution)/shard_map/ppermute | solution.py:1223
  614.7 43.8 %collective-permute-start.51 = (bf16[3,256,512]{2,1,0:T(8,128)(2,1)S(1)}, bf16[3,256,512]{2,1,0:T(8,128)(2,1)S(1)}, u32[]{:S(2)}, u32[]{:S(2)}) collective-permute-start(bf16[3,256,512]{2,1,0:T(8,128)(2,1)S(1)} %get-tuple-element.208), channel_id=1, source_target_pairs={{8,0},{16,8},{24,16},{28,24},{20,28},{12,20},{4,12},{0,4},{9,1},{1... | collective-permute-start | bytes 2359304 | tf_op jit(solution)/shard_map/ppermute | solution.py:1223
  (120 other events, 1739.4 us)
Sparse Core Ops, SparseCore 0:
  9.6 25.2 all-gather.7
  36.5 22.6 all-gather.9
  60.7 22.5 all-gather.11
  84.7 22.5 all-gather.13
  108.8 43.4 all-gather.15
  153.6 43.4 all-gather.17
  198.6 43.3 all-gather.19
  390.5 57.7 reduce-scatter.4
  451.5 31.4 reduce-scatter.10
  485.4 54.8 reduce-scatter.8
  543.0 54.8 reduce-scatter.6

commit v3 on v2

--- a/solution.py
+++ b/solution.py
@@ -116,6 +116,54 @@
     return jnp.concatenate([here.reshape(1), owners.reshape(-1), lists]).astype(jnp.int32), cap
 
 
+def share_kernel(indices, gains, all_indices, all_gains, send_sem, recv_sem, *, count, shards):
+    here, shard = lax.axis_index("ctx"), lax.axis_index("fsdp")
+    groups = (("ctx", here, count, indices, all_indices), ("fsdp", shard, shards, gains, all_gains))
+    barrier = pltpu.get_barrier_semaphore()
+    for axis, index, size, _, _ in groups:
+        for k in range(1, size):
+            pl.semaphore_signal(
+                barrier, inc=1, device_id={axis: (index + k) % size}, device_id_type=pl.DeviceIdType.MESH
+            )
+    pl.semaphore_wait(barrier, count + shards - 2)
+    copies = []
+    for number, (axis, index, size, source, target) in enumerate(groups):
+        for k in range(1, size):
+            copy = pltpu.make_async_remote_copy(
+                source,
+                target.at[index],
+                send_sem.at[number, k],
+                recv_sem.at[number, k],
+                device_id={axis: (index + k) % size},
+                device_id_type=pl.DeviceIdType.MESH,
+            )
+            copy.start()
+            copies.append(copy)
+        target[index] = source[...]
+    for copy in copies:
+        copy.wait()
+
+
+def share(indices, gains, count, shards):
+    vmem = pl.BlockSpec(memory_space=pltpu.VMEM)
+    most = max(count, shards)
+    return pl.pallas_call(
+        functools.partial(share_kernel, count=count, shards=shards),
+        in_specs=[vmem, vmem],
+        out_specs=[vmem, vmem],
+        out_shape=[
+            jax.ShapeDtypeStruct((count,) + indices.shape, indices.dtype),
+            jax.ShapeDtypeStruct((shards,) + gains.shape, gains.dtype),
+        ],
+        scratch_shapes=[pltpu.SemaphoreType.DMA((2, most)), pltpu.SemaphoreType.DMA((2, most))],
+        compiler_params=pltpu.CompilerParams(
+            vmem_limit_bytes=8 * 2**20, collective_id=1, has_side_effects=True
+        ),
+        name="share",
+        cost_estimate=pl.CostEstimate(flops=0, bytes_accessed=20_000_000, transcendentals=0),
+    )(indices, gains)
+
+
 def collect_kernel(meta, ck, cv, mk, mv, sem_k, sem_v, *, micros, count, cap):
     owner = pl.program_id(0)
 
@@ -205,13 +253,14 @@
         out[0, :, place] = turn(product[:, cols], cosine[...], sine[...]).astype(BF16)
 
 
-def second_kernel(normed, key_weight, value_weight, cosine, sine, keys, values):
+def second_kernel(normed, weights, cosine, sine, keys, values, turned):
     low = normed[0]
-    product = nn(low, key_weight[...])
+    turned[...] = low.T
+    product = nn(low, weights[0])
     for h in range(HEADS):
         cols = slice(h * HEAD_DIM, (h + 1) * HEAD_DIM)
         keys[0, :, cols] = turn(product[:, cols], cosine[...], sine[...]).astype(BF16)
-    values[0] = nn(low, value_weight[...]).astype(BF16)
+    values[0] = nn(low, weights[1]).astype(BF16)
 
 
 def seq_spec(*shape):
@@ -246,24 +295,27 @@
     )(x, gain, weight, cosine, sine)
 
 
-def project_pairs(normed, key_weight, value_weight, cosine, sine):
+def project_pairs(normed, weights, cosine, sine):
     micros = normed.shape[0]
     return pl.pallas_call(
         second_kernel,
         grid=(micros,),
         in_specs=[
             seq_spec(ROWS, D),
-            full_spec(D, D),
-            full_spec(D, D),
+            full_spec(2, D, D),
             full_spec(ROWS, HEAD_DIM),
             full_spec(ROWS, HEAD_DIM),
         ],
-        out_specs=[seq_spec(ROWS, D), seq_spec(ROWS, D)],
-        out_shape=[seq_shape(micros, ROWS, D), seq_shape(micros, ROWS, D)],
+        out_specs=[seq_spec(ROWS, D), seq_spec(ROWS, D), pl.BlockSpec((D, ROWS), lambda m: (0, m))],
+        out_shape=[
+            seq_shape(micros, ROWS, D),
+            seq_shape(micros, ROWS, D),
+            jax.ShapeDtypeStruct((D, micros * ROWS), BF16),
+        ],
         compiler_params=params(),
         name="project_pairs",
         cost_estimate=pl.CostEstimate(flops=4 * micros * ROWS * D * D, bytes_accessed=10_000_000, transcendentals=0),
-    )(normed, key_weight, value_weight, cosine, sine)
+    )(normed, weights, cosine, sine)
 
 
 def causal_mask(turned=False):
@@ -755,9 +807,13 @@
     )(meta, qa, qb, da, db, keys, values, memory_keys, memory_values)
 
 
-def key_kernel(meta, k, v, *refs, steps, micros):
+def key_kernel(meta, k, v, *refs, steps, micros, last):
     number = len(steps)
-    sources, (dk, dv, qbuf, dbuf, sem) = refs[: 4 * number], refs[4 * number :]
+    sources, refs = refs[: 4 * number], refs[4 * number :]
+    if last:
+        dk_first, dv_first, cosine, sine, back_key, back_value, dk, dv, qbuf, dbuf, sem = refs
+    else:
+        dk, dv, qbuf, dbuf, sem = refs
     micro = pl.program_id(0)
     here = meta[0]
 
@@ -777,8 +833,8 @@
 
     request_ahead(fetch, micro, micros)
     fetch(micro, "wait")
-    dk[0] = jnp.zeros((ROWS, D), F32)
-    dv[0] = jnp.zeros((ROWS, D), F32)
+    dk[0] = dk_first[0] if last else jnp.zeros((ROWS, D), F32)
+    dv[0] = dv_first[0] if last else jnp.zeros((ROWS, D), F32)
     slot = micro % 2
     for side in range(2):
         spots = tiles(side)
@@ -824,90 +880,156 @@
             return carry
 
         lax.fori_loop(first, number, loop, 0)
-
-
-def key_gradients(meta, keys, values, queries, slopes, steps):
+    if last:
+        for h in range(HEADS):
+            cols = slice(h * HEAD_DIM, (h + 1) * HEAD_DIM)
+            back_key[0, :, cols] = turn(dk[0, :, cols] * SCALE, cosine[...], -sine[...]).astype(BF16)
+        back_value[0] = dv[0].astype(BF16)
+
+
+def key_gradients(meta, keys, values, queries, slopes, steps, first=(), angle=()):
     micros = keys.shape[0]
     whole = seq_spec(ROWS, D)
     anywhere = pl.BlockSpec(memory_space=pl.ANY)
     sources = []
     for step in steps:
         sources += [*queries[step], *slopes[step]]
+    last = bool(first)
+    sum_scratch = [pltpu.VMEM((1, ROWS, D), F32)] * 2 if last else []
     return pl.pallas_call(
-        functools.partial(key_kernel, steps=steps, micros=micros),
+        functools.partial(key_kernel, steps=steps, micros=micros, last=last),
         grid_spec=pltpu.PrefetchScalarGridSpec(
             num_scalar_prefetch=1,
             grid=(micros,),
-            in_specs=[whole, whole] + [anywhere] * len(sources),
+            in_specs=[whole, whole]
+            + [anywhere] * len(sources)
+            + [whole] * len(first)
+            + [full_spec(ROWS, HEAD_DIM)] * len(angle),
             out_specs=[whole, whole],
-            scratch_shapes=[
+            scratch_shapes=sum_scratch
+            + [
                 pltpu.VMEM((2, 2, len(steps), ROWS, SW), BF16),
                 pltpu.VMEM((2, 2, len(steps), SENT, SW), BF16),
                 pltpu.SemaphoreType.DMA((2,)),
             ],
         ),
-        out_shape=[
-            seq_shape(micros, ROWS, D, dtype=F32),
-            seq_shape(micros, ROWS, D, dtype=F32),
-        ],
+        out_shape=[seq_shape(micros, ROWS, D, dtype=BF16 if last else F32)] * 2,
         compiler_params=params(40),
         name="key_gradients",
         cost_estimate=pl.CostEstimate(
             flops=3_000_000_000 * len(steps), bytes_accessed=20_000_000, transcendentals=0
         ),
-    )(meta, keys, values, *sources)
-
-
-def unturn_kernel(acc_a, acc_b, pa, pb, dk, dv, dk_more, dv_more, cosine, sine, back):
-    for h in range(HEADS):
-        acc, part = (acc_a, pa) if h < SIDE else (acc_b, pb)
-        cols = slice(h % SIDE * HEAD_DIM, (h % SIDE + 1) * HEAD_DIM)
-        place = slice(h * HEAD_DIM, (h + 1) * HEAD_DIM)
-        value = (acc[0, :, cols].astype(F32) + part[0, :, cols].astype(F32)) * SCALE
-        key_place = slice(D + h * HEAD_DIM, D + (h + 1) * HEAD_DIM)
-        back[0, :, place] = turn(value, cosine[...], -sine[...]).astype(BF16)
-        back[0, :, key_place] = turn((dk[0, :, place] + dk_more[0, :, place]) * SCALE, cosine[...], -sine[...]).astype(BF16)
-    back[0, :, 2 * D :] = (dv[0] + dv_more[0]).astype(BF16)
-
-
-def unturn(acc_a, acc_b, pa, pb, key_parts, cosine, sine):
-    micros = acc_a.shape[0]
-    half, whole, angle = seq_spec(ROWS, SW), seq_spec(ROWS, D), full_spec(ROWS, HEAD_DIM)
-    return pl.pallas_call(
-        unturn_kernel,
-        grid=(micros,),
-        in_specs=[half, half, half, half, whole, whole, whole, whole, angle, angle],
-        out_specs=seq_spec(ROWS, 3 * D),
-        out_shape=seq_shape(micros, ROWS, 3 * D),
-        compiler_params=params(),
-        name="unturn",
-        cost_estimate=pl.CostEstimate(flops=10_000_000, bytes_accessed=16_000_000, transcendentals=0),
-    )(acc_a, acc_b, pa, pb, *key_parts, cosine, sine)
+    )(meta, keys, values, *sources, *first, *angle)
 
 
 def bits(size):
     return [1 << i for i in range(size.bit_length() - 1)]
 
 
-def sums_kernel(
-    early,
-    late,
-    gains,
+def by_rows(rows, chunks):
+    return rows % (16 * chunks) == 0
+
+
+PIECE = 512
+
+
+def tail_kernel(
+    acc_a,
+    acc_b,
+    part_a,
+    part_b,
+    cosine,
+    sine,
+    gain,
+    second,
+    *rest,
+    count,
+    shards,
+    parts,
+):
+    early_far, rest = rest[:parts], rest[parts:]
+    tail_work(
+        acc_a, acc_b, part_a, part_b, cosine, sine, gain, second, early_far, *rest, count=count, shards=shards
+    )
+
+
+def tail_work(
+    acc_a,
+    acc_b,
+    part_a,
+    part_b,
+    cosine,
+    sine,
+    gain,
+    second,
+    early_far,
+    back_key_far,
+    back_value_far,
+    turned_far,
+    query_far,
+    pairs_far,
+    x_far,
+    middle_far,
     early_out,
     late_out,
     gains_out,
+    input_out,
     *scratch,
     count,
     shards,
 ):
     scratch = list(scratch)
     halves = [scratch.pop(0) for _ in bits(shards)]
-    early_slots, late_slots, gain_in, gain_sum = (scratch.pop(0) for _ in range(4))
-    ring_send, ring_recv, half_send, half_recv, gain_send, gain_recv = scratch
+    (
+        back_query,
+        back_key,
+        back_value,
+        turned,
+        weight,
+        x,
+        middle,
+        early,
+        given,
+        early_slots,
+        late_slots,
+        gain_in,
+        gain_sum,
+        ring_send,
+        ring_recv,
+        half_send,
+        half_recv,
+        gain_send,
+        gain_recv,
+        near,
+    ) = scratch
+    micros = x.shape[0]
+    chunks = 2 * count
+    shard_rows = D // shards
     here, shard = lax.axis_index("ctx"), lax.axis_index("fsdp")
     place = ring_place(count)
     neighbour = (ring_index(place + 1, count), ring_index(place + count - 1, count))
     partners = [("fsdp", shard, bit) for bit in bits(shards)] + [("ctx", here, bit) for bit in bits(count)]
+
+    copies = {}
+    column = 0
+    pieces = []
+    for i, part in enumerate(early_far):
+        pieces.append((f"early{i}", part, early.at[:, :, column : column + part.shape[2]]))
+        column += part.shape[2]
+    for number, (name, source, target) in enumerate(
+        (
+            *pieces,
+            ("turned", turned_far, turned),
+            ("back_key", back_key_far, back_key),
+            ("back_value", back_value_far, back_value),
+            ("query", query_far, weight.at[0]),
+            ("pairs", pairs_far, weight.at[1:]),
+            ("x", x_far, x),
+            ("middle", middle_far, middle),
+        )
+    ):
+        copies[name] = pltpu.make_async_copy(source, target, near.at[number])
+        copies[name].start()
 
     def partner(axis, index, bit):
         return {axis: index + bit * (1 - 2 * ((index // bit) % 2))}
@@ -928,12 +1050,110 @@
         sent.append(copy)
         return copy
 
+    def flow(number, first_source, source, slots, out):
+        def home(side, hop):
+            sign = 1 - 2 * side
+            return side * count + (place - sign * hop + 2 * count) % count
+
+        def start(hop):
+            result = []
+            for side in range(2):
+                if hop == 1:
+                    pair = first_source(home(side, 1)), slots(side, 0)
+                elif hop < count:
+                    pair = slots(side, hop - 2), slots(side, hop - 1)
+                else:
+                    chunk = home(side, hop - count)
+                    pair = out(chunk), out(chunk)
+                result.append(
+                    send(
+                        *pair,
+                        ring_send.at[number, side, hop - 1],
+                        ring_recv.at[number, side, hop - 1],
+                        {"ctx": neighbour[side]},
+                    )
+                )
+            return result
+
+        def finish(hop, pending):
+            for side in range(2):
+                pending[side].wait_recv()
+                if hop < count:
+                    got = slots(side, hop - 1)
+                    total = got[...].astype(F32) + source(home(side, 1 + hop))[...].astype(F32)
+                    target = out(home(side, 0)) if hop == count - 1 else got
+                    target[...] = total.astype(BF16)
+
+        return start, finish
+
+    class Run:
+        def __init__(self, *arguments):
+            self.start, self.finish = flow(*arguments)
+            self.hop, self.pending = 0, None
+
+        def advance(self):
+            if self.hop:
+                self.finish(self.hop, self.pending)
+            self.hop += 1
+            if self.hop <= 2 * count - 2:
+                self.pending = self.start(self.hop)
+
+        def done(self):
+            return self.hop > 2 * count - 2
+
+    width = early.shape[2]
+    middle_column = width // HEAD_DIM // 2 * HEAD_DIM
+    runs = []
+    for number, cols in enumerate((slice(0, middle_column), slice(middle_column, width))):
+        runs.append(
+            Run(
+                number,
+                lambda c, cols=cols: early.at[c, :, cols],
+                lambda c, cols=cols: early.at[c, :, cols],
+                lambda side, slot, cols=cols: early_slots.at[side, slot, :, cols],
+                lambda c, cols=cols: early_out.at[c, :, cols],
+            )
+        )
+
+    sources = (back_query, back_key, back_value)
+
+    def product(s, target, add):
+        rows = turned[pl.ds(pl.multiple_of(s * shard_rows, shard_rows), shard_rows), :]
+        for start in range(0, 3 * D, PIECE):
+            column = start % D
+            right = sources[start // D][:, :, column : column + PIECE].reshape(micros * ROWS, PIECE)
+            value = nn(rows, right)
+            if by_rows(shard_rows, chunks):
+                value = value.reshape(chunks, shard_rows // chunks, PIECE)
+                spots = [((slice(None), slice(None), slice(start, start + PIECE)), value)]
+            else:
+                step = target.shape[2]
+                spots = [
+                    (((start + c) // step,), value[:, c : c + step]) for c in range(0, PIECE, step)
+                ]
+            for spot, piece in spots:
+                if add:
+                    piece = target[spot].astype(F32) + piece.astype(BF16).astype(F32)
+                target[spot] = piece.astype(BF16)
+
+    if not by_rows(shard_rows, chunks):
+        used = 3 * D // halves[0].shape[3]
+        for c in range(used, chunks):
+            given[:, c] = jnp.zeros_like(given[:, c])
+
+    def bit_of(i):
+        return (shard // (1 << i)) % 2
+
+    def give(j):
+        product(2 * j + 1 - bit_of(0), given.at[j], False)
+        return send(
+            given.at[j], halves[0].at[j], half_send.at[0, j], half_recv.at[0, j], partner("fsdp", shard, 1)
+        )
+
     def halve_start(i):
-        held = late if i == 0 else halves[i - 1]
-        bit = (shard // (1 << i)) % 2
         return [
             send(
-                held.at[2 * j + 1 - bit],
+                halves[i - 1].at[2 * j + 1 - bit_of(i)],
                 halves[i].at[j],
                 half_send.at[i, j],
                 half_recv.at[i, j],
@@ -942,19 +1162,44 @@
             for j in range(shards >> (i + 1))
         ]
 
-    def halve_finish(i, copies):
-        held = late if i == 0 else halves[i - 1]
-        bit = (shard // (1 << i)) % 2
-        for j, copy in enumerate(copies):
-            copy.wait_recv()
-
-            def add(c, carry):
-                halves[i][j, c] = (
-                    halves[i][j, c].astype(F32) + held[2 * j + bit, c].astype(F32)
+    def halve_finish(i, j, copy):
+        copy.wait_recv()
+        if i == 0:
+            product(2 * j + bit_of(0), halves[0].at[j], True)
+            return
+
+        def add(c, carry):
+            halves[i][j, c] = (
+                halves[i][j, c].astype(F32) + halves[i - 1][2 * j + bit_of(i), c].astype(F32)
+            ).astype(BF16)
+            return carry
+
+        lax.fori_loop(0, chunks, add, 0)
+
+    def unturn():
+        for m in range(micros):
+            for h in range(HEADS):
+                acc, part = (acc_a, part_a) if h < SIDE else (acc_b, part_b)
+                cols = slice(h % SIDE * HEAD_DIM, (h % SIDE + 1) * HEAD_DIM)
+                value = (acc[m, :, cols].astype(F32) + part[m, :, cols].astype(F32)) * SCALE
+                back_query[m, :, h * HEAD_DIM : (h + 1) * HEAD_DIM] = turn(
+                    value, cosine[...], -sine[...]
                 ).astype(BF16)
-                return carry
-
-            lax.fori_loop(0, 2 * count, add, 0)
+
+    def input_back(m):
+        slope = nt(back_query[m], weight[0]) + nt(back_key[m], weight[1]) + nt(back_value[m], weight[2])
+        value = x[m].astype(F32)
+        scale = lax.rsqrt(jnp.mean(value * value, axis=-1, keepdims=True) + EPS)
+        hat = value * scale
+        first = jnp.sum((slope * hat).reshape(ROWS // 8, 8, D), axis=0)
+        slope = slope * gain[...]
+        input_out[m] = middle[m] + scale * (slope - hat * jnp.mean(slope * hat, axis=-1, keepdims=True))
+        gain_sum[1] = first if m == 0 else gain_sum[1] + first
+
+    def gains_ready():
+        first = jnp.sum(gain_sum[1], axis=0, keepdims=True)
+        other = jnp.sum(jnp.sum(second[...], axis=0), axis=0, keepdims=True)
+        gain_sum[0] = jnp.concatenate([first, other, jnp.zeros((6, D), F32)], axis=0)
 
     def gain_start(i):
         return send(gain_sum.at[i], gain_in.at[i], gain_send.at[i], gain_recv.at[i], partner(*partners[i]))
@@ -963,160 +1208,143 @@
         copy.wait_recv()
         gain_sum[i + 1] = gain_sum[i] + gain_in[i]
 
-    def flow(number, source, slots, out):
-        def home(side, hop):
-            sign = 1 - 2 * side
-            return side * count + (place - sign * hop + 2 * count) % count
-
-        def sum_start(hop):
-            copies = []
-            for side in range(2):
-                held = source.at[home(side, 1)] if hop == 1 else slots.at[side, hop - 2]
-                copies.append(
-                    send(
-                        held,
-                        slots.at[side, hop - 1],
-                        ring_send.at[number, side, hop - 1],
-                        ring_recv.at[number, side, hop - 1],
-                        {"ctx": neighbour[side]},
-                    )
+    stages = len(halves)
+    late = []
+
+    def advance():
+        for run in runs:
+            for each in (run, *late):
+                if not each.done():
+                    each.advance()
+
+    for i in range(len(early_far)):
+        copies[f"early{i}"].wait()
+    advance()
+    unturn()
+    for name in ("turned", "back_key", "back_value"):
+        copies[name].wait()
+    half = []
+    for j in range(shards // 2):
+        half.append(give(j))
+        advance()
+    for j in range(shards // 2):
+        halve_finish(0, j, half[j])
+        advance()
+    for i in range(1, stages):
+        half = halve_start(i)
+        if i < stages - 1:
+            for j, copy in enumerate(half):
+                halve_finish(i, j, copy)
+            advance()
+    for name in ("query", "pairs", "x", "middle"):
+        copies[name].wait()
+    for m in range(micros):
+        input_back(m)
+        advance()
+    gains_ready()
+    for i in range(len(partners)):
+        copy = gain_start(i)
+        advance()
+        if i == 0:
+            if stages > 1:
+                halve_finish(stages - 1, 0, half[0])
+            late.append(
+                Run(
+                    2,
+                    lambda c: halves[-1].at[0, c],
+                    lambda c: halves[-1].at[0, c],
+                    lambda side, slot: late_slots.at[side, slot],
+                    lambda c: late_out.at[c],
                 )
-            return copies
-
-        def sum_finish(hop, copies):
-            for side in range(2):
-                copies[side].wait_recv()
-                total = slots[side, hop - 1].astype(F32) + source[home(side, 1 + hop)].astype(F32)
-                if hop == count - 1:
-                    out[home(side, 0)] = total.astype(BF16)
-                else:
-                    slots[side, hop - 1] = total.astype(BF16)
-
-        def copy_start(hop):
-            copies = []
-            for side in range(2):
-                chunk = home(side, hop - 1)
-                copies.append(
-                    send(
-                        out.at[chunk],
-                        out.at[chunk],
-                        ring_send.at[number, side, count - 2 + hop],
-                        ring_recv.at[number, side, count - 2 + hop],
-                        {"ctx": neighbour[side]},
-                    )
-                )
-            return copies
-
-        def copy_finish(copies):
-            for copy in copies:
-                copy.wait_recv()
-
-        return sum_start, sum_finish, copy_start, copy_finish
-
-    early_flow = flow(0, early, early_slots, early_out)
-    late_flow = flow(1, halves[-1].at[0], late_slots, late_out)
-    gain_sum[0] = gains[...]
-    stages, exchanges = len(halves), len(partners)
-    half = halve_start(0)
-    gain = gain_start(0)
-    stage, exchange = 0, 0
-    ring = early_flow[0](1)
-    for hop in range(1, count):
-        early_flow[1](hop, ring)
-        if hop < count - 1:
-            ring = early_flow[0](hop + 1)
-        if stage < stages - 1:
-            halve_finish(stage, half)
-            stage += 1
-            half = halve_start(stage)
-        if exchange < exchanges:
-            gain_finish(exchange, gain)
-            exchange += 1
-            if exchange < exchanges:
-                gain = gain_start(exchange)
-    ring = early_flow[2](1)
-    halve_finish(stage, half)
-    late_ring = late_flow[0](1)
-    for hop in range(1, count):
-        early_flow[3](ring)
-        if hop < count - 1:
-            ring = early_flow[2](hop + 1)
-        late_flow[1](hop, late_ring)
-        if hop < count - 1:
-            late_ring = late_flow[0](hop + 1)
-        if exchange < exchanges:
-            gain_finish(exchange, gain)
-            exchange += 1
-            if exchange < exchanges:
-                gain = gain_start(exchange)
-    for hop in range(1, count):
-        late_flow[3](late_flow[2](hop))
-    gains_out[...] = gain_sum[exchanges]
+            )
+        gain_finish(i, copy)
+    while not all(run.done() for run in runs + late):
+        advance()
+    gains_out[...] = gain_sum[len(partners)]
     for copy in sent:
         copy.wait_send()
 
 
-def sums(early, late, gains):
-    shards, chunks, rows, width = late.shape
-    count = chunks // 2
-    more = early.shape[-1]
+def tail(received, own, angle, gain, second, early, back_key, back_value, turned, weights, x, middle, count, shards):
+    micros = x.shape[0]
+    chunks = 2 * count
+    shard_rows = D // shards
+    if by_rows(shard_rows, chunks):
+        late = (chunks, shard_rows // chunks, 3 * D)
+    else:
+        late = (chunks, shard_rows, -(-3 * D // (chunks * HEAD_DIM)) * HEAD_DIM)
     exchanges = len(bits(shards)) + len(bits(count))
+    early_shape = early[0].shape[:2] + (sum(part.shape[2] for part in early),)
     vmem = pl.BlockSpec(memory_space=pltpu.VMEM)
+    anywhere = pl.BlockSpec(memory_space=pl.ANY)
     return pl.pallas_call(
-        functools.partial(sums_kernel, count=count, shards=shards),
-        in_specs=[vmem] * 3,
-        out_specs=[vmem] * 3,
+        functools.partial(tail_kernel, count=count, shards=shards, parts=len(early)),
+        in_specs=[vmem] * 8 + [anywhere] * (7 + len(early)),
+        out_specs=[vmem] * 4,
         out_shape=[
-            jax.ShapeDtypeStruct(early.shape, BF16),
-            jax.ShapeDtypeStruct(late.shape[1:], BF16),
-            jax.ShapeDtypeStruct(gains.shape, F32),
+            jax.ShapeDtypeStruct(early_shape, BF16),
+            jax.ShapeDtypeStruct(late, BF16),
+            jax.ShapeDtypeStruct((8, D), F32),
+            seq_shape(micros, ROWS, D, dtype=F32),
         ],
-        scratch_shapes=[pltpu.VMEM((bit and shards // (2 * bit), chunks, rows, width), BF16) for bit in bits(shards)]
+        scratch_shapes=[pltpu.VMEM((shards // (2 * bit),) + late, BF16) for bit in bits(shards)]
+        + [pltpu.VMEM((micros, ROWS, D), BF16)] * 3
         + [
-            pltpu.VMEM((2, count - 1, early.shape[1], more), BF16),
-            pltpu.VMEM((2, count - 1, rows, width), BF16),
-            pltpu.VMEM((exchanges,) + gains.shape, F32),
-            pltpu.VMEM((exchanges + 1,) + gains.shape, F32),
-            pltpu.SemaphoreType.DMA((2, 2, 2 * count - 2)),
-            pltpu.SemaphoreType.DMA((2, 2, 2 * count - 2)),
+            pltpu.VMEM(turned.shape, BF16),
+            pltpu.VMEM((3, D, D), BF16),
+            pltpu.VMEM((micros, ROWS, D), BF16),
+            pltpu.VMEM((micros, ROWS, D), F32),
+            pltpu.VMEM(early_shape, BF16),
+            pltpu.VMEM((shards // 2,) + late, BF16),
+            pltpu.VMEM((2, count - 1) + early_shape[1:], BF16),
+            pltpu.VMEM((2, count - 1) + late[1:], BF16),
+            pltpu.VMEM((exchanges, 8, D), F32),
+            pltpu.VMEM((exchanges + 1, 8, D), F32),
+            pltpu.SemaphoreType.DMA((3, 2, 2 * count - 2)),
+            pltpu.SemaphoreType.DMA((3, 2, 2 * count - 2)),
             pltpu.SemaphoreType.DMA((len(bits(shards)), shards // 2)),
             pltpu.SemaphoreType.DMA((len(bits(shards)), shards // 2)),
             pltpu.SemaphoreType.DMA((exchanges,)),
             pltpu.SemaphoreType.DMA((exchanges,)),
+            pltpu.SemaphoreType.DMA((7 + len(early),)),
         ],
         compiler_params=pltpu.CompilerParams(
-            vmem_limit_bytes=48 * 2**20, collective_id=0, has_side_effects=True
+            vmem_limit_bytes=60 * 2**20, collective_id=0, has_side_effects=True
         ),
-        name="sums",
-        cost_estimate=pl.CostEstimate(flops=50_000_000, bytes_accessed=400_000_000, transcendentals=0),
-    )(early, late, gains)
-
-
-def to_chunks(value, count):
-    rows, width = value.shape[-2:]
-    lead = value.shape[:-2]
+        name="tail",
+        cost_estimate=pl.CostEstimate(flops=12_000_000_000, bytes_accessed=300_000_000, transcendentals=0),
+    )(
+        *received,
+        *own,
+        *angle,
+        gain,
+        second,
+        *early,
+        back_key,
+        back_value,
+        turned,
+        *weights,
+        x,
+        middle,
+    )
+
+
+def to_chunks(parts, count):
+    rows = parts[0].shape[0]
     chunks = 2 * count
-    if rows % (16 * chunks) == 0:
-        return value.reshape(lead + (chunks, rows // chunks, width))
+    if by_rows(rows, chunks):
+        return [part.reshape(chunks, rows // chunks, -1) for part in parts]
+    value = jnp.concatenate(parts, axis=1)
+    width = value.shape[1]
     step = -(-width // (chunks * HEAD_DIM)) * HEAD_DIM
-    value = jnp.pad(value, [(0, 0)] * len(lead) + [(0, 0), (0, step * chunks - width)])
-    return jnp.moveaxis(value.reshape(lead + (rows, chunks, step)), -2, -3)
+    value = jnp.pad(value, [(0, 0), (0, step * chunks - width)])
+    return [jnp.moveaxis(value.reshape(rows, chunks, step), 1, 0)]
 
 
 def from_chunks(value, rows, width):
-    if value.shape[0] * value.shape[1] == rows:
+    if by_rows(rows, value.shape[0]):
         return value.reshape(rows, width)
     return jnp.moveaxis(value, 0, 1).reshape(rows, -1)[:, :width]
-
-
-def norm_parts(value):
-    scale = lax.rsqrt(jnp.mean(value * value, axis=-1, keepdims=True) + EPS)
-    return value * scale, scale
-
-
-def norm_back(hat, scale, back, gain):
-    slope = back * gain
-    return scale * (slope - hat * jnp.mean(slope * hat, axis=-1, keepdims=True))
 
 
 def body(
@@ -1145,17 +1373,27 @@
     def gather(value):
         return lax.all_gather(value, "fsdp", axis=0, tiled=True)
 
-    indices = lax.all_gather(block_indices, "ctx", axis=1, tiled=True)
-    gains = lax.all_gather(jnp.stack([first_gain, second_gain]), "fsdp", axis=1, tiled=True)
+    shards = lax.axis_size("fsdp")
+    requested = block_indices.reshape(micros, -1)
+    own_rows = D // shards
+    indices, gains = share(
+        jnp.pad(requested, ((0, -micros % 8), (0, 0))),
+        jnp.pad(
+            jnp.stack([first_gain, second_gain]).astype(F32), ((0, 6), (0, -own_rows % HEAD_DIM))
+        ),
+        count,
+        shards,
+    )
+    indices = jnp.moveaxis(indices[:, :micros], 0, 1)
+    gains = jnp.moveaxis(gains[:, :2, :own_rows], 0, 1).reshape(2, D)
     full_query = gather(query_weight)
-    full_key = gather(key_weight)
-    full_value = gather(value_weight)
+    pair_weights = lax.all_gather(jnp.stack([key_weight, value_weight]), "fsdp", axis=1, tiled=True)
     full_output = gather(output_weight)
     full_gate = gather(gate_weight)
     full_up = gather(up_weight)
     full_down = gather(down_weight)
-    gain_one = gains[0:1].astype(F32)
-    gain_two = gains[1:2].astype(F32)
+    gain_one = gains[0:1]
+    gain_two = gains[1:2]
 
     pieces_at = jnp.stack([here, 2 * count - 1 - here])
     positions = (pieces_at[:, None] * HALF + jnp.arange(HALF, dtype=jnp.int32)[None, :]).reshape(ROWS)
@@ -1166,16 +1404,19 @@
     sine = jnp.concatenate([-sine, sine], axis=1)
 
     meta, cap = make_meta(indices, partner, cache_keys.shape[1] // BLOCK, count)
-    memory_keys, memory_values = collect(meta, cache_keys, cache_values, count, cap)
-
     x = tokens.reshape(micros, ROWS, D)
     normed_low, qa, qb = project_query(x, gain_one, full_query, cosine, sine)
-    keys, values = project_pairs(normed_low, full_key, full_value, cosine, sine)
-
+    meta, qa, qb = lax.optimization_barrier((meta, qa, qb))
     queries = [(qa, qb)]
     for _ in range(count - 1):
         qa, qb = lax.ppermute(qa, "ctx", onward), lax.ppermute(qb, "ctx", backward)
         queries.append((qa, qb))
+    memory_keys, memory_values = collect(meta, cache_keys, cache_values, count, cap)
+    queries[1], normed_low, memory_keys = lax.optimization_barrier((queries[1], normed_low, memory_keys))
+    keys, values, normed_turned = project_pairs(normed_low, pair_weights, cosine, sine)
+    for step in range(1, count - 1):
+        queries[step], queries[step + 1] = lax.optimization_barrier((queries[step], queries[step + 1]))
+
 
     acc = ()
     for step in list(range(1, count)) + [0]:
@@ -1198,19 +1439,26 @@
     da, db, back_middle, back_attn, gain_part = prepare(
         back_mid_normed, middle, incoming, gain_two, full_output, mixed, total
     )
-    gradient_second = jnp.sum(gain_part, axis=(0, 1))
-    gradient_output = jnp.einsum(
-        "tc,td->cd", mixed_low.reshape(rows, D), back_attn.reshape(rows, D), preferred_element_type=F32
-    ).astype(BF16)
-    back_middle = back_middle.reshape(rows, D)
-    inputs = tokens.reshape(rows, D).astype(F32)
+
+    def scatter(part):
+        return lax.psum_scatter(part, "fsdp", scatter_dimension=0, tiled=True)
 
     slopes = [(da, db)]
     for _ in range(count - 1):
         da, db = slopes[-1]
         slopes.append((lax.ppermute(da, "ctx", onward), lax.ppermute(db, "ctx", backward)))
-    slopes[1], gradient_output = lax.optimization_barrier((slopes[1], gradient_output))
-
+
+    slopes[1], back_attn = lax.optimization_barrier((slopes[1], back_attn))
+    gradient_output = jnp.einsum(
+        "tc,td->cd", mixed_low.reshape(rows, D), back_attn.reshape(rows, D), preferred_element_type=F32
+    ).astype(BF16)
+    early = [
+        scatter(part).reshape(own_rows, -1)
+        for part in (gradient_down, gradient_gate, gradient_up, gradient_output)
+    ]
+    early_width = sum(part.shape[1] for part in early)
+    for step in range(1, count - 1):
+        slopes[step], slopes[step + 1] = lax.optimization_barrier((slopes[step], slopes[step + 1]))
     acc = ()
     for step in range(count):
         part = unattend(
@@ -1222,44 +1470,31 @@
         if acc:
             acc = (lax.ppermute(acc[0], "ctx", onward), lax.ppermute(acc[1], "ctx", backward))
         acc = combine(acc, part)
-    key_parts = [
-        part
-        for steps in (range(count // 2), range(count // 2, count))
-        for part in key_gradients(meta, keys, values, queries, slopes, steps)
-    ]
+    middle_step = count // 2
+    first_sums = key_gradients(meta, keys, values, queries, slopes, range(middle_step))
+    back_key, back_value = key_gradients(
+        meta, keys, values, queries, slopes, range(middle_step, count), first_sums, (cosine, sine)
+    )
     ra, rb = lax.ppermute(acc[0], "ctx", onward), lax.ppermute(acc[1], "ctx", backward)
-    back = unturn(ra, rb, *own, key_parts, cosine, sine).reshape(rows, 3 * D)
-    normed_low = normed_low.reshape(rows, D)
-    late = jnp.einsum("tc,td->cd", normed_low, back, preferred_element_type=F32).astype(BF16)
-    back_in_normed = (
-        jnp.einsum("td,cd->tc", back[:, :D], full_query, preferred_element_type=F32)
-        + jnp.einsum("td,cd->tc", back[:, D : 2 * D], full_key, preferred_element_type=F32)
-        + jnp.einsum("td,cd->tc", back[:, 2 * D :], full_value, preferred_element_type=F32)
+    early_sum, late_sum, gain_changes, input_gradient = tail(
+        (ra, rb),
+        own,
+        (cosine, sine),
+        gain_one,
+        gain_part,
+        to_chunks(early, count),
+        back_key,
+        back_value,
+        normed_turned,
+        (full_query, pair_weights),
+        x,
+        back_middle,
+        count,
+        shards,
     )
-    in_hat, in_scale = norm_parts(inputs)
-    gradient_first = jnp.sum(back_in_normed * in_hat, axis=0)
-    input_gradient = back_middle + norm_back(in_hat, in_scale, back_in_normed, gain_one)
-
-    def scatter(part):
-        return lax.psum_scatter(part, "fsdp", scatter_dimension=0, tiled=True)
-
-    early = jnp.concatenate(
-        [
-            scatter(part).reshape(D // lax.axis_size("fsdp"), -1)
-            for part in (gradient_down, gradient_gate, gradient_up, gradient_output)
-        ],
-        axis=1,
-    )
-    shards = lax.axis_size("fsdp")
-    late = late.reshape(shards, D // shards, 3 * D)
-    gains_part = jnp.concatenate(
-        [gradient_first[None], gradient_second[None], jnp.zeros((6, D), F32)], axis=0
-    )
-    early_sum, late_sum, gain_changes = sums(to_chunks(early, count), to_chunks(late, count), gains_part)
-    early = from_chunks(early_sum, *early.shape).astype(F32)
-    three = from_chunks(late_sum, *late.shape[1:]).astype(F32)
+    early = from_chunks(early_sum, own_rows, early_width).astype(F32)
+    three = from_chunks(late_sum, D // shards, 3 * D).astype(F32)
     units = gate_weight.shape[1]
-    own_rows = D // lax.axis_size("fsdp")
     gain_changes = lax.dynamic_slice_in_dim(
         gain_changes, lax.axis_index("fsdp") * own_rows, own_rows, axis=1
     )

time: 919 us -> 846 us (0.921)
  blocking collectives: 37.5 us -> 0 us
  Pallas kernels: 488 us -> 465 us
  waiting for transfers between devices: 228 us -> 244 us
  matrix products: 19.6 us -> 4.73 us
  starting transfers between devices: 70.9 us -> 61.7 us
    all_gather x2 -> x0, blocking collectives: 37.5 us -> none  [the longest x1 32.4 us: body(): indices = lax.all_gather(block_indices, 'ctx', axis=1, tiled=True)]
    pallas_call x4, Pallas kernels: 221 us -> 187 us  [the longest x1 140 us: tail(): pl.pallas_call(functools.partial(tail_kernel, count=count, shards=shards,...]
    dot_general x4 -> x0, matrix products: 14.9 us -> none  [the longest x1 7.16 us: body(): jnp.einsum('tc,td->cd', normed_low, back, preferred_element_type=F32)]
    ppermute x7, waiting for transfers between devices: 60.8 us -> 74.9 us  [body(): lax.ppermute(qa, 'ctx', onward)]
    ppermute x14, waiting for transfers between devices: 65.4 us -> 78.4 us  [body(): lax.ppermute(acc[0], 'ctx', onward)]
    ppermute x14, starting transfers between devices: 19.4 us -> 9.37 us  [body(): lax.ppermute(acc[1], 'ctx', backward)]
    ppermute x14, starting transfers between devices: 12.2 us -> 21.7 us  [body(): lax.ppermute(acc[0], 'ctx', onward)]
    unnamed x170 -> x146, local copies, waits for them, and re-layouts: 22 us -> 15.5 us
  transfers between devices with their start and end apart: 67 -> 66, of which waited for: 39 -> 38; matrix products, arithmetic and copies ran while one was open for 4% -> 2% of each run, Pallas kernels for 29% -> 33%
where the time goes in v3:
time: 846 us; the launch traced here: 833 us
  Pallas kernels  465 us (55%)
  waiting for transfers between devices  244 us (29%)
  starting transfers between devices  61.7 us (7%)
  local copies, waits for them, and re-layouts  32.3 us (4%)
  between operations  15.6 us (2%)
  other arithmetic  10.1 us (1%)
    pallas_call x1, Pallas kernels, tail(): pl.pallas_call(functools.partial(tail_kernel, count=count, shards=shards,...  140 us
    pallas_call x8, Pallas kernels, unattend(): pl.pallas_call(functools.partial(backward_kernel, step=step, count=count,...  86.9 us
    ppermute x14, waiting for transfers between devices, body(): lax.ppermute(acc[0], 'ctx', onward)  78.4 us
    ppermute x7, waiting for transfers between devices, body(): lax.ppermute(qa, 'ctx', onward)  74.9 us
    ppermute x7, waiting for transfers between devices, body(): lax.ppermute(da, 'ctx', onward)  67.6 us
    pallas_call x8, Pallas kernels, attend(): pl.pallas_call(functools.partial(forward_kernel, step=step, count=count,...  66.5 us
    pallas_call x1, Pallas kernels, feed(): pl.pallas_call(feed_kernel, grid=(units // TILE,), in_specs=[whole, whole...  52.6 us
    pallas_call x2, Pallas kernels, key_gradients(): pl.pallas_call(functools.partial(key_kernel, steps=steps, micros=micros,...  37.8 us
  transfers between devices with their start and end apart: 66, of which 38 were waited for; matrix products, arithmetic and copies ran while one was open for 2% of the time, Pallas kernels for 33%

profile of v3, /device:TPU:0, one launch (start us, length us, event | category | flops | bytes accessed | tf_op | source)
XLA Modules:
  0.0 833.2 jit_solution(7200873015817763731)
XLA Ops:
  13.1 9.5 %share.1 = (s32[8,8,128]{2,1,0:T(8,128)S(1)}, f32[4,8,256]{2,1,0:T(8,128)S(1)}) custom-call(s32[8,128]{1,0:T(8,128)S(1)} %pad.10.indices, f32[8,256]{1,0:T(8,128)S(1)} %fusion.20.gains), custom_call_target="tpu_custom_call" | custom-call | bytes 20000000 | tf_op jit(solution)/shard_map/share/pallas_call | solution.py:150
  42.9 17.9 %collective-permute-done.qa.refs_4_ = bf16[3,256,512]{2,1,0:T(8,128)(2,1)S(1)} collective-permute-done((bf16[3,256,512]{2,1,0:T(8,128)(2,1)}, bf16[3,256,512]{2,1,0:T(8,128)(2,1)S(1)}, u32[]{:S(2)}, u32[]{:S(2)}) %collective-permute-start) | collective-permute-done | bytes 786464 | tf_op jit(solution)/shard_map/ppermute | solution.py:1412
  62.8 28.1 %collect.1 = (bf16[3,8,2,32,64,128]{5,4,3,2,1,0:T(8,128)(2,1)}, bf16[3,8,2,32,64,128]{5,4,3,2,1,0:T(8,128)(2,1)}) custom-call(s32[1601]{0:T(1024)} %concatenate.14.meta, bf16[6144,1024]{1,0:T(8,128)(2,1)} %bitcast.53, bf16[6144,1024]{1,0:T(8,128)(2,1)} %bitcast.54), custom_call_target="tpu_custom_call" | custom-call | bytes 90000000 | tf_op jit(solution)/shard_map/collect/pallas_call | solution.py:223
  103.3 8.2 attend.8
  115.8 8.0 attend.9
  123.8 9.4 %collective-permute-done.4.refs_0_ = bf16[3,272,512]{2,1,0:T(8,128)(2,1)S(1)} collective-permute-done((bf16[3,272,512]{2,1,0:T(8,128)(2,1)S(1)}, bf16[3,272,512]{2,1,0:T(8,128)(2,1)S(1)}, u32[]{:S(2)}, u32[]{:S(2)}) %collective-permute-start.4) | collective-permute-done | bytes 835616 | tf_op jit(solution)/shard_map/ppermute | solution.py:1427
  135.9 14.2 %collective-permute-done.10.qa.refs_0_ = bf16[3,256,512]{2,1,0:T(8,128)(2,1)S(1)} collective-permute-done((bf16[3,256,512]{2,1,0:T(8,128)(2,1)}, bf16[3,256,512]{2,1,0:T(8,128)(2,1)S(1)}, u32[]{:S(2)}, u32[]{:S(2)}) %collective-permute-start.10) | collective-permute-done | bytes 786464 | tf_op jit(solution)/shard_map/ppermute | solution.py:1412
  152.4 10.2 %attend.10 = (bf16[3,256,512]{2,1,0:T(8,128)(2,1)S(1)}, bf16[3,256,512]{2,1,0:T(8,128)(2,1)S(1)}, f32[3,8,256]{2,1,0:T(8,128)S(1)}, f32[3,8,256]{2,1,0:T(8,128)S(1)}) custom-call(s32[1601]{0:T(1024)S(1)} %copy-done.41, bf16[3,256,512]{2,1,0:T(8,128)(2,1)} %collective-permute-done.6.qa.refs_12_, bf16[3,256,512]{2,1,0:T(8,128)(2,1)} %collective-permute-done.7.qb.refs_13_, ...), custom_call_target="tpu_custom_call" | custom-call | flops 6000000000 | bytes 10000000 | tf_op jit(solution)/shard_map/attend/pallas_call | solution.py:495
  170.6 14.2 %collective-permute-done.14.qa.refs_4_ = bf16[3,256,512]{2,1,0:T(8,128)(2,1)S(1)} collective-permute-done((bf16[3,256,512]{2,1,0:T(8,128)(2,1)S(1)}, bf16[3,256,512]{2,1,0:T(8,128)(2,1)S(1)}, u32[]{:S(2)}, u32[]{:S(2)}) %collective-permute-start.14) | collective-permute-done | bytes 786464 | tf_op jit(solution)/shard_map/ppermute | solution.py:1412
  194.5 8.3 collective-permute-done.12.refs_0_
  205.4 14.2 %collective-permute-done.18.qa.refs_8_ = bf16[3,256,512]{2,1,0:T(8,128)(2,1)S(1)} collective-permute-done((bf16[3,256,512]{2,1,0:T(8,128)(2,1)S(1)}, bf16[3,256,512]{2,1,0:T(8,128)(2,1)S(1)}, u32[]{:S(2)}, u32[]{:S(2)}) %collective-permute-start.18) | collective-permute-done | bytes 786464 | tf_op jit(solution)/shard_map/ppermute | solution.py:1412
  240.2 14.2 %collective-permute-done.22.qa.refs_12_ = bf16[3,256,512]{2,1,0:T(8,128)(2,1)S(1)} collective-permute-done((bf16[3,256,512]{2,1,0:T(8,128)(2,1)S(1)}, bf16[3,256,512]{2,1,0:T(8,128)(2,1)S(1)}, u32[]{:S(2)}, u32[]{:S(2)}) %collective-permute-start.22) | collective-permute-done | bytes 786464 | tf_op jit(solution)/shard_map/ppermute | solution.py:1412
  254.5 9.2 %attend.13 = (bf16[3,256,512]{2,1,0:T(8,128)(2,1)S(1)}, bf16[3,256,512]{2,1,0:T(8,128)(2,1)S(1)}, f32[3,8,256]{2,1,0:T(8,128)S(1)}, f32[3,8,256]{2,1,0:T(8,128)S(1)}) custom-call(s32[1601]{0:T(1024)S(1)} %copy-done.41, bf16[3,256,512]{2,1,0:T(8,128)(2,1)S(1)} %collective-permute-done.18.qa.refs_8_, ...), custom_call_target="tpu_custom_call" | custom-call | flops 6000000000 | bytes 10000000 | tf_op jit(solution)/shard_map/attend/pallas_call | solution.py:495
  312.1 8.9 %finish.1 = (f32[3,256,1024]{2,1,0:T(8,128)}, bf16[3,256,1024]{2,1,0:T(8,128)(2,1)}, f32[3,2,8,256]{3,2,1,0:T(8,128)}, f32[3,256,1024]{2,1,0:T(8,128)}, bf16[3,256,1024]{2,1,0:T(8,128)(2,1)}) custom-call(bf16[3,272,512]{2,1,0:T(8,128)(2,1)} %collective-permute-done.26.acc_a, bf16[3,272,512]{2,1,0:T(8,128)(2,1)} %collective-permute-done.27.acc_b, ...), custom_call_target="tpu_custom_call" | custom-call | flops 1610612736 | bytes 16000000 | tf_op jit(solution)/shard_map/finish/pallas_call | solution.py:572
  321.0 52.6 %feed.1 = (bf16[3,256,1024]{2,1,0:T(8,128)(2,1)}, f32[3,256,1024]{2,1,0:T(8,128)}, bf16[1024,2816]{1,0:T(8,128)(2,1)}, bf16[1024,2816]{1,0:T(8,128)(2,1)}, bf16[2816,1024]{1,0:T(8,128)(2,1)}) custom-call(bf16[3,256,1024]{2,1,0:T(8,128)(2,1)} %get-tuple-element.264.normed, bf16[3,256,1024]{2,1,0:T(8,128)(2,1)} %bitcast.58, ...), custom_call_target="tpu_custom_call" | custom-call | flops 39862665216 | bytes 50000000 | tf_op jit(solution)/shard_map/feed/pallas_call | solution.py:634
  373.8 12.0 %prepare.1 = (bf16[3,272,512]{2,1,0:T(8,128)(2,1)}, bf16[3,272,512]{2,1,0:T(8,128)(2,1)}, f32[3,256,1024]{2,1,0:T(8,128)}, bf16[3,256,1024]{2,1,0:T(8,128)(2,1)}, f32[3,8,1024]{2,1,0:T(8,128)}) custom-call(f32[3,256,1024]{2,1,0:T(8,128)} %get-tuple-element.267.back_normed, f32[3,256,1024]{2,1,0:T(8,128)} %get-tuple-element.265.middle, ...), custom_call_target="tpu_custom_call" | custom-call | flops 1610612736 | bytes 22000000 | tf_op jit(solution)/shard_map/prepare/pallas_call | solution.py:691
  388.0 17.5 %collective-permute-done.28.da.refs_6_ = bf16[3,272,512]{2,1,0:T(8,128)(2,1)} collective-permute-done((bf16[3,272,512]{2,1,0:T(8,128)(2,1)}, bf16[3,272,512]{2,1,0:T(8,128)(2,1)}, u32[]{:S(2)}, u32[]{:S(2)}) %collective-permute-start.28) | collective-permute-done | bytes 835616 | tf_op jit(solution)/shard_map/ppermute | solution.py:1449
  415.1 16.5 %collective-permute-done.30.da.refs_10_ = bf16[3,272,512]{2,1,0:T(8,128)(2,1)S(1)} collective-permute-done((bf16[3,272,512]{2,1,0:T(8,128)(2,1)}, bf16[3,272,512]{2,1,0:T(8,128)(2,1)S(1)}, u32[]{:S(2)}, u32[]{:S(2)}) %collective-permute-start.30) | collective-permute-done | bytes 835616 | tf_op jit(solution)/shard_map/ppermute | solution.py:1449
  433.9 16.3 %collective-permute-done.34.da.refs_14_ = bf16[3,272,512]{2,1,0:T(8,128)(2,1)S(1)} collective-permute-done((bf16[3,272,512]{2,1,0:T(8,128)(2,1)S(1)}, bf16[3,272,512]{2,1,0:T(8,128)(2,1)S(1)}, u32[]{:S(2)}, u32[]{:S(2)}) %collective-permute-start.34) | collective-permute-done | bytes 835616 | tf_op jit(solution)/shard_map/ppermute | solution.py:1449
  452.3 16.7 %collective-permute-done.38.da.refs_2_ = bf16[3,272,512]{2,1,0:T(8,128)(2,1)S(1)} collective-permute-done((bf16[3,272,512]{2,1,0:T(8,128)(2,1)S(1)}, bf16[3,272,512]{2,1,0:T(8,128)(2,1)S(1)}, u32[]{:S(2)}, u32[]{:S(2)}) %collective-permute-start.38) | collective-permute-done | bytes 835616 | tf_op jit(solution)/shard_map/ppermute | solution.py:1449
  473.7 11.4 %unattend.8 = (bf16[3,256,512]{2,1,0:T(8,128)(2,1)S(1)}, bf16[3,256,512]{2,1,0:T(8,128)(2,1)S(1)}) custom-call(s32[1601]{0:T(1024)S(1)} %copy-done.41, bf16[3,256,512]{2,1,0:T(8,128)(2,1)S(1)} %copy-done.10, bf16[3,256,512]{2,1,0:T(8,128)(2,1)S(1)} %copy-done.13, bf16[3,272,512]{2,1,0:T(8,128)(2,1)} %collective-permute-done.28.da.refs_6_, ...), custom_call_target="tpu_custom_call" | custom-call | flops 8000000000 | bytes 12000000 | tf_op jit(solution)/shard_map/unattend/pallas_call | solution.py:793
  487.4 10.2 %unattend.9 = (bf16[3,256,512]{2,1,0:T(8,128)(2,1)S(1)}, bf16[3,256,512]{2,1,0:T(8,128)(2,1)S(1)}) custom-call(s32[1601]{0:T(1024)S(1)} %copy-done.41, bf16[3,256,512]{2,1,0:T(8,128)(2,1)S(1)} %copy-done.16, bf16[3,256,512]{2,1,0:T(8,128)(2,1)S(1)} %copy-done.19, bf16[3,272,512]{2,1,0:T(8,128)(2,1)S(1)} %collective-permute-done.30.da.refs_10_, ...), custom_call_target="tpu_custom_call" | custom-call | flops 8000000000 | bytes 12000000 | tf_op jit(solution)/shard_map/unattend/pallas_call | solution.py:793
  508.1 12.4 %unattend.10 = (bf16[3,256,512]{2,1,0:T(8,128)(2,1)S(1)}, bf16[3,256,512]{2,1,0:T(8,128)(2,1)S(1)}) custom-call(s32[1601]{0:T(1024)S(1)} %copy-done.41, bf16[3,256,512]{2,1,0:T(8,128)(2,1)} %collective-permute-done.6.qa.refs_12_, bf16[3,256,512]{2,1,0:T(8,128)(2,1)} %collective-permute-done.7.qb.refs_13_, ...), custom_call_target="tpu_custom_call" | custom-call | flops 8000000000 | bytes 12000000 | tf_op jit(solution)/shard_map/unattend/pallas_call | solution.py:793
  527.7 9.8 %unattend.11 = (bf16[3,256,512]{2,1,0:T(8,128)(2,1)S(1)}, bf16[3,256,512]{2,1,0:T(8,128)(2,1)S(1)}) custom-call(s32[1601]{0:T(1024)S(1)} %copy-done.41, bf16[3,256,512]{2,1,0:T(8,128)(2,1)S(1)} %copy-done.22, bf16[3,256,512]{2,1,0:T(8,128)(2,1)S(1)} %copy-done.25, bf16[3,272,512]{2,1,0:T(8,128)(2,1)S(1)} %collective-permute-done.38.da.refs_2_, ...), custom_call_target="tpu_custom_call" | custom-call | flops 8000000000 | bytes 12000000 | tf_op jit(solution)/shard_map/unattend/pallas_call | solution.py:793
  537.5 16.7 %collective-permute-done.40.refs_0_ = bf16[3,256,512]{2,1,0:T(8,128)(2,1)S(1)} collective-permute-done((bf16[3,256,512]{2,1,0:T(8,128)(2,1)S(1)}, bf16[3,256,512]{2,1,0:T(8,128)(2,1)S(1)}, u32[]{:S(2)}, u32[]{:S(2)}) %collective-permute-start.40) | collective-permute-done | bytes 786464 | tf_op jit(solution)/shard_map/ppermute | solution.py:1471
  563.0 11.2 %unattend.12 = (bf16[3,256,512]{2,1,0:T(8,128)(2,1)S(1)}, bf16[3,256,512]{2,1,0:T(8,128)(2,1)S(1)}) custom-call(s32[1601]{0:T(1024)S(1)} %copy-done.41, bf16[3,256,512]{2,1,0:T(8,128)(2,1)S(1)} %copy-done.28, bf16[3,256,512]{2,1,0:T(8,128)(2,1)S(1)} %copy-done.31, bf16[3,272,512]{2,1,0:T(8,128)(2,1)} %collective-permute-done.42.da.refs_6_, ...), custom_call_target="tpu_custom_call" | custom-call | flops 8000000000 | bytes 12000000 | tf_op jit(solution)/shard_map/unattend/pallas_call | solution.py:793
  583.8 8.8 %unattend.15 = (bf16[3,256,512]{2,1,0:T(8,128)(2,1)S(1)}, bf16[3,256,512]{2,1,0:T(8,128)(2,1)S(1)}) custom-call(s32[1601]{0:T(1024)S(1)} %copy-done.41, bf16[3,256,512]{2,1,0:T(8,128)(2,1)S(1)} %copy-done.6, bf16[3,256,512]{2,1,0:T(8,128)(2,1)S(1)} %copy-done.8, bf16[3,272,512]{2,1,0:T(8,128)(2,1)S(1)} %copy-done.42, bf16[3,272,512]{2,1,0:T(8,128)(2,1)S(1)} %copy-done.43, ...), custom_call_target="tpu_custom_call" | custom-call | flops 8000000000 | bytes 12000000 | tf_op jit(solution)/shard_map/unattend/pallas_call | solution.py:793
  597.1 12.8 %unattend.13 = (bf16[3,256,512]{2,1,0:T(8,128)(2,1)S(1)}, bf16[3,256,512]{2,1,0:T(8,128)(2,1)S(1)}) custom-call(s32[1601]{0:T(1024)S(1)} %copy-done.41, bf16[3,256,512]{2,1,0:T(8,128)(2,1)S(1)} %copy-done.34, bf16[3,256,512]{2,1,0:T(8,128)(2,1)S(1)} %copy-done.36, bf16[3,272,512]{2,1,0:T(8,128)(2,1)} %collective-permute-done.46.da.refs_10_, ...), custom_call_target="tpu_custom_call" | custom-call | flops 8000000000 | bytes 12000000 | tf_op jit(solution)/shard_map/unattend/pallas_call | solution.py:793
  614.0 18.6 %key_gradients.2 = (f32[3,256,1024]{2,1,0:T(8,128)}, f32[3,256,1024]{2,1,0:T(8,128)}) custom-call(s32[1601]{0:T(1024)S(1)} %copy-done.41, bf16[3,256,1024]{2,1,0:T(8,128)(2,1)S(1)} %copy-done.1, bf16[3,256,1024]{2,1,0:T(8,128)(2,1)} %get-tuple-element.193.v, bf16[3,256,512]{2,1,0:T(8,128)(2,1)S(1)} %copy-done.6, bf16[3,256,512]{2,1,0:T(8,128)(2,1)S(1)} %copy-done.8, ...), custom_call_target="tpu_custom_call" | custom-call | flops 12000000000 | bytes 20000000 | tf_op jit(solution)/shard_map/key_gradients/pallas_call | solution.py:899
  632.6 10.2 %unattend.14 = (bf16[3,256,512]{2,1,0:T(8,128)(2,1)S(1)}, bf16[3,256,512]{2,1,0:T(8,128)(2,1)S(1)}) custom-call(s32[1601]{0:T(1024)S(1)} %copy-done.41, bf16[3,256,512]{2,1,0:T(8,128)(2,1)S(1)} %copy-done.38, bf16[3,256,512]{2,1,0:T(8,128)(2,1)S(1)} %copy-done.40, bf16[3,272,512]{2,1,0:T(8,128)(2,1)S(1)} %collective-permute-done.50.da.refs_14_, ...), custom_call_target="tpu_custom_call" | custom-call | flops 8000000000 | bytes 12000000 | tf_op jit(solution)/shard_map/unattend/pallas_call | solution.py:793
  645.5 19.2 %key_gradients.3 = (bf16[3,256,1024]{2,1,0:T(8,128)(2,1)}, bf16[3,256,1024]{2,1,0:T(8,128)(2,1)}) custom-call(s32[1601]{0:T(1024)S(1)} %copy-done.41, bf16[3,256,1024]{2,1,0:T(8,128)(2,1)} %get-tuple-element.192.k, bf16[3,256,1024]{2,1,0:T(8,128)(2,1)} %get-tuple-element.193.v, bf16[3,256,512]{2,1,0:T(8,128)(2,1)S(1)} %copy-done.23, ...), custom_call_target="tpu_custom_call" | custom-call | flops 12000000000 | bytes 20000000 | tf_op jit(solution)/shard_map/key_gradients/pallas_call | solution.py:899
  670.1 139.9 %tail.1 = (bf16[16,16,9472]{2,1,0:T(8,128)(2,1)}, bf16[16,16,3072]{2,1,0:T(8,128)(2,1)}, f32[8,1024]{1,0:T(8,128)}, f32[3,256,1024]{2,1,0:T(8,128)}) custom-call(bf16[3,256,512]{2,1,0:T(8,128)(2,1)} %copy-done.68, bf16[3,256,512]{2,1,0:T(8,128)(2,1)} %copy-done.69, bf16[3,256,512]{2,1,0:T(8,128)(2,1)} %copy-done.62, bf16[3,256,512]{2,1,0:T(8,128)(2,1)} %copy-done.63, ...), custom_call_target="tpu_custom_call" | custom-call | flops 12000000000 | bytes 300000000 | tf_op jit(solution)/shard_map/tail/pallas_call | solution.py:1280
  (342 shorter events, 230.1 us)
Async XLA Ops:
  7.9 85.1 %all-gather.9.cloned.1.call-start = ((), (), s32[]{:S(2)}) async-start(), calls=%async_computation.5 | async-start | bytes 5242880 | tf_op jit(solution)/shard_map/all_gather | solution.py:1390
  10.3 293.7 %all-gather.11.cloned.1.call-start = ((), (), s32[]{:S(2)}) async-start(), calls=%async_computation.6 | async-start | bytes 2621440 | tf_op jit(solution)/shard_map/all_gather | solution.py:1374
  11.0 310.0 %all-gather.13.cloned.1.call-start = ((), (), s32[]{:S(2)}) async-start(), calls=%async_computation.7 | async-start | bytes 7208960 | tf_op jit(solution)/shard_map/all_gather | solution.py:1374
  11.6 309.4 %all-gather.15.cloned.1.call-start = ((), (), s32[]{:S(2)}) async-start(), calls=%async_computation.8 | async-start | bytes 7208960 | tf_op jit(solution)/shard_map/all_gather | solution.py:1374
  12.2 308.9 %all-gather.17.cloned.1.call-start = ((), (), s32[]{:S(2)}) async-start(), calls=%async_computation.9 | async-start | bytes 7208960 | tf_op jit(solution)/shard_map/all_gather | solution.py:1374
  12.7 652.0 %reduce-scatter.5.cloned.1.call-start = ((), (), s32[]{:S(2)}) async-start(), calls=%async_computation.10 | async-start | bytes 7208960 | tf_op jit(solution)/shard_map/reduce_scatter | solution.py:1444
  60.7 30.1 %collective-permute-start.2 = (bf16[3,256,512]{2,1,0:T(8,128)(2,1)S(1)}, bf16[3,256,512]{2,1,0:T(8,128)(2,1)S(1)}, u32[]{:S(2)}, u32[]{:S(2)}) collective-permute-start(bf16[3,256,512]{2,1,0:T(8,128)(2,1)S(1)} %collective-permute-done.qa.refs_4_), channel_id=1, source_target_pairs={{0,8},{8,16},{16,24},{24,28},{28,20},{20,12},{12,4},{4,0},{1,9},{9... | collective-permute-start | bytes 2359304 | tf_op jit(solution)/shard_map/ppermute | solution.py:1412
  113.8 36.4 %collective-permute-start.10 = (bf16[3,256,512]{2,1,0:T(8,128)(2,1)}, bf16[3,256,512]{2,1,0:T(8,128)(2,1)S(1)}, u32[]{:S(2)}, u32[]{:S(2)}) collective-permute-start(bf16[3,256,512]{2,1,0:T(8,128)(2,1)} %collective-permute-done.6.qa.refs_12_), channel_id=1, source_target_pairs={{0,8},{8,16},{16,24},{24,28},{28,20},{20,12},{12,4},{4,0},{1,9},{9... | collective-permute-start | bytes 2359304 | tf_op jit(solution)/shard_map/ppermute | solution.py:1412
  113.8 36.4 %collective-permute-start.11 = (bf16[3,256,512]{2,1,0:T(8,128)(2,1)}, bf16[3,256,512]{2,1,0:T(8,128)(2,1)S(1)}, u32[]{:S(2)}, u32[]{:S(2)}) collective-permute-start(bf16[3,256,512]{2,1,0:T(8,128)(2,1)} %collective-permute-done.7.qb.refs_13_), channel_id=1, source_target_pairs={{8,0},{16,8},{24,16},{28,24},{20,28},{12,20},{4,12},{0,4},{9,1},{1... | collective-permute-start | bytes 2359304 | tf_op jit(solution)/shard_map/ppermute | solution.py:1412
  133.8 34.3 %collective-permute-start.8 = (bf16[3,272,512]{2,1,0:T(8,128)(2,1)S(1)}, bf16[3,272,512]{2,1,0:T(8,128)(2,1)S(1)}, u32[]{:S(2)}, u32[]{:S(2)}) collective-permute-start(bf16[3,272,512]{2,1,0:T(8,128)(2,1)S(1)} %get-tuple-element.210), channel_id=1, source_target_pairs={{0,8},{8,16},{16,24},{24,28},{28,20},{20,12},{12,4},{4,0},{1,9},{9... | collective-permute-start | bytes 2506760 | tf_op jit(solution)/shard_map/ppermute | solution.py:1427
  135.9 32.2 %collective-permute-start.9 = (bf16[3,272,512]{2,1,0:T(8,128)(2,1)S(1)}, bf16[3,272,512]{2,1,0:T(8,128)(2,1)S(1)}, u32[]{:S(2)}, u32[]{:S(2)}) collective-permute-start(bf16[3,272,512]{2,1,0:T(8,128)(2,1)S(1)} %get-tuple-element.211), channel_id=1, source_target_pairs={{8,0},{16,8},{24,16},{28,24},{20,28},{12,20},{4,12},{0,4},{9,1},{1... | collective-permute-start | bytes 2506760 | tf_op jit(solution)/shard_map/ppermute | solution.py:1427
  150.2 34.7 %collective-permute-start.14 = (bf16[3,256,512]{2,1,0:T(8,128)(2,1)S(1)}, bf16[3,256,512]{2,1,0:T(8,128)(2,1)S(1)}, u32[]{:S(2)}, u32[]{:S(2)}) collective-permute-start(bf16[3,256,512]{2,1,0:T(8,128)(2,1)S(1)} %collective-permute-done.10.qa.refs_0_), channel_id=1, source_target_pairs={{0,8},{8,16},{16,24},{24,28},{28,20},{20,12},{12,4},{4,0},{1,9},{9... | collective-permute-start | bytes 2359304 | tf_op jit(solution)/shard_map/ppermute | solution.py:1412
  152.2 32.7 %collective-permute-start.15 = (bf16[3,256,512]{2,1,0:T(8,128)(2,1)S(1)}, bf16[3,256,512]{2,1,0:T(8,128)(2,1)S(1)}, u32[]{:S(2)}, u32[]{:S(2)}) collective-permute-start(bf16[3,256,512]{2,1,0:T(8,128)(2,1)S(1)} %collective-permute-done.11.qb.refs_1_), channel_id=1, source_target_pairs={{8,0},{16,8},{24,16},{28,24},{20,28},{12,20},{4,12},{0,4},{9,1},{1... | collective-permute-start | bytes 2359304 | tf_op jit(solution)/shard_map/ppermute | solution.py:1412
  168.5 34.3 %collective-permute-start.12 = (bf16[3,272,512]{2,1,0:T(8,128)(2,1)S(1)}, bf16[3,272,512]{2,1,0:T(8,128)(2,1)S(1)}, u32[]{:S(2)}, u32[]{:S(2)}) collective-permute-start(bf16[3,272,512]{2,1,0:T(8,128)(2,1)S(1)} %get-tuple-element.220), channel_id=1, source_target_pairs={{0,8},{8,16},{16,24},{24,28},{28,20},{20,12},{12,4},{4,0},{1,9},{9... | collective-permute-start | bytes 2506760 | tf_op jit(solution)/shard_map/ppermute | solution.py:1427
  170.6 32.2 %collective-permute-start.13 = (bf16[3,272,512]{2,1,0:T(8,128)(2,1)S(1)}, bf16[3,272,512]{2,1,0:T(8,128)(2,1)S(1)}, u32[]{:S(2)}, u32[]{:S(2)}) collective-permute-start(bf16[3,272,512]{2,1,0:T(8,128)(2,1)S(1)} %get-tuple-element.221), channel_id=1, source_target_pairs={{8,0},{16,8},{24,16},{28,24},{20,28},{12,20},{4,12},{0,4},{9,1},{1... | collective-permute-start | bytes 2506760 | tf_op jit(solution)/shard_map/ppermute | solution.py:1427
  185.0 34.7 %collective-permute-start.18 = (bf16[3,256,512]{2,1,0:T(8,128)(2,1)S(1)}, bf16[3,256,512]{2,1,0:T(8,128)(2,1)S(1)}, u32[]{:S(2)}, u32[]{:S(2)}) collective-permute-start(bf16[3,256,512]{2,1,0:T(8,128)(2,1)S(1)} %collective-permute-done.14.qa.refs_4_), channel_id=1, source_target_pairs={{0,8},{8,16},{16,24},{24,28},{28,20},{20,12},{12,4},{4,0},{1,9},{9... | collective-permute-start | bytes 2359304 | tf_op jit(solution)/shard_map/ppermute | solution.py:1412
  187.0 32.7 %collective-permute-start.19 = (bf16[3,256,512]{2,1,0:T(8,128)(2,1)S(1)}, bf16[3,256,512]{2,1,0:T(8,128)(2,1)S(1)}, u32[]{:S(2)}, u32[]{:S(2)}) collective-permute-start(bf16[3,256,512]{2,1,0:T(8,128)(2,1)S(1)} %collective-permute-done.15.qb.refs_5_), channel_id=1, source_target_pairs={{8,0},{16,8},{24,16},{28,24},{20,28},{12,20},{4,12},{0,4},{9,1},{1... | collective-permute-start | bytes 2359304 | tf_op jit(solution)/shard_map/ppermute | solution.py:1412
  203.3 34.3 %collective-permute-start.16 = (bf16[3,272,512]{2,1,0:T(8,128)(2,1)S(1)}, bf16[3,272,512]{2,1,0:T(8,128)(2,1)S(1)}, u32[]{:S(2)}, u32[]{:S(2)}) collective-permute-start(bf16[3,272,512]{2,1,0:T(8,128)(2,1)S(1)} %get-tuple-element.230), channel_id=1, source_target_pairs={{0,8},{8,16},{16,24},{24,28},{28,20},{20,12},{12,4},{4,0},{1,9},{9... | collective-permute-start | bytes 2506760 | tf_op jit(solution)/shard_map/ppermute | solution.py:1427
  205.4 32.2 %collective-permute-start.17 = (bf16[3,272,512]{2,1,0:T(8,128)(2,1)S(1)}, bf16[3,272,512]{2,1,0:T(8,128)(2,1)S(1)}, u32[]{:S(2)}, u32[]{:S(2)}) collective-permute-start(bf16[3,272,512]{2,1,0:T(8,128)(2,1)S(1)} %get-tuple-element.231), channel_id=1, source_target_pairs={{8,0},{16,8},{24,16},{28,24},{20,28},{12,20},{4,12},{0,4},{9,1},{1... | collective-permute-start | bytes 2506760 | tf_op jit(solution)/shard_map/ppermute | solution.py:1427
  219.7 34.7 %collective-permute-start.22 = (bf16[3,256,512]{2,1,0:T(8,128)(2,1)S(1)}, bf16[3,256,512]{2,1,0:T(8,128)(2,1)S(1)}, u32[]{:S(2)}, u32[]{:S(2)}) collective-permute-start(bf16[3,256,512]{2,1,0:T(8,128)(2,1)S(1)} %collective-permute-done.18.qa.refs_8_), channel_id=1, source_target_pairs={{0,8},{8,16},{16,24},{24,28},{28,20},{20,12},{12,4},{4,0},{1,9},{9... | collective-permute-start | bytes 2359304 | tf_op jit(solution)/shard_map/ppermute | solution.py:1412
  221.8 32.7 %collective-permute-start.23 = (bf16[3,256,512]{2,1,0:T(8,128)(2,1)S(1)}, bf16[3,256,512]{2,1,0:T(8,128)(2,1)S(1)}, u32[]{:S(2)}, u32[]{:S(2)}) collective-permute-start(bf16[3,256,512]{2,1,0:T(8,128)(2,1)S(1)} %collective-permute-done.19.qb.refs_9_), channel_id=1, source_target_pairs={{8,0},{16,8},{24,16},{28,24},{20,28},{12,20},{4,12},{0,4},{9,1},{1... | collective-permute-start | bytes 2359304 | tf_op jit(solution)/shard_map/ppermute | solution.py:1412
  373.7 295.3 %reduce-scatter.11.cloned.1.call-start = ((), (), s32[]{:S(2)}) async-start(), calls=%async_computation.13 | async-start | bytes 2621440 | tf_op jit(solution)/shard_map/reduce_scatter | solution.py:1444
  411.1 257.9 %reduce-scatter.7.cloned.1.call-start = ((), (), s32[]{:S(2)}) async-start(), calls=%async_computation.11 | async-start | bytes 7208960 | tf_op jit(solution)/shard_map/reduce_scatter | solution.py:1444
  411.8 257.2 %reduce-scatter.9.cloned.1.call-start = ((), (), s32[]{:S(2)}) async-start(), calls=%async_computation.12 | async-start | bytes 7208960 | tf_op jit(solution)/shard_map/reduce_scatter | solution.py:1444
  469.0 37.0 %collective-permute-start.42 = (bf16[3,272,512]{2,1,0:T(8,128)(2,1)S(1)}, bf16[3,272,512]{2,1,0:T(8,128)(2,1)}, u32[]{:S(2)}, u32[]{:S(2)}) collective-permute-start(bf16[3,272,512]{2,1,0:T(8,128)(2,1)S(1)} %collective-permute-done.38.da.refs_2_), channel_id=1, source_target_pairs={{0,8},{8,16},{16,24},{24,28},{28,20},{20,12},{12,4},{4,0},{1,9},{9... | collective-permute-start | bytes 2506760 | tf_op jit(solution)/shard_map/ppermute | solution.py:1449
  470.6 36.1 %collective-permute-start.43 = (bf16[3,272,512]{2,1,0:T(8,128)(2,1)S(1)}, bf16[3,272,512]{2,1,0:T(8,128)(2,1)}, u32[]{:S(2)}, u32[]{:S(2)}) collective-permute-start(bf16[3,272,512]{2,1,0:T(8,128)(2,1)S(1)} %collective-permute-done.39.db.refs_3_), channel_id=1, source_target_pairs={{8,0},{16,8},{24,16},{28,24},{20,28},{12,20},{4,12},{0,4},{9,1},{1... | collective-permute-start | bytes 2506760 | tf_op jit(solution)/shard_map/ppermute | solution.py:1449
  506.1 52.4 %collective-permute-start.46 = (bf16[3,272,512]{2,1,0:T(8,128)(2,1)}, bf16[3,272,512]{2,1,0:T(8,128)(2,1)}, u32[]{:S(2)}, u32[]{:S(2)}) collective-permute-start(bf16[3,272,512]{2,1,0:T(8,128)(2,1)} %collective-permute-done.42.da.refs_6_), channel_id=1, source_target_pairs={{0,8},{8,16},{16,24},{24,28},{28,20},{20,12},{12,4},{4,0},{1,9},{9... | collective-permute-start | bytes 2506760 | tf_op jit(solution)/shard_map/ppermute | solution.py:1449
  506.7 51.7 %collective-permute-start.47 = (bf16[3,272,512]{2,1,0:T(8,128)(2,1)}, bf16[3,272,512]{2,1,0:T(8,128)(2,1)}, u32[]{:S(2)}, u32[]{:S(2)}) collective-permute-start(bf16[3,272,512]{2,1,0:T(8,128)(2,1)} %collective-permute-done.43.db.refs_7_), channel_id=1, source_target_pairs={{8,0},{16,8},{24,16},{28,24},{20,28},{12,20},{4,12},{0,4},{9,1},{1... | collective-permute-start | bytes 2506760 | tf_op jit(solution)/shard_map/ppermute | solution.py:1449
  558.5 36.5 %collective-permute-start.50 = (bf16[3,272,512]{2,1,0:T(8,128)(2,1)}, bf16[3,272,512]{2,1,0:T(8,128)(2,1)S(1)}, u32[]{:S(2)}, u32[]{:S(2)}) collective-permute-start(bf16[3,272,512]{2,1,0:T(8,128)(2,1)} %collective-permute-done.46.da.refs_10_), channel_id=1, source_target_pairs={{0,8},{8,16},{16,24},{24,28},{28,20},{20,12},{12,4},{4,0},{1,9},{9... | collective-permute-start | bytes 2506760 | tf_op jit(solution)/shard_map/ppermute | solution.py:1449
  560.6 36.5 %collective-permute-start.51 = (bf16[3,272,512]{2,1,0:T(8,128)(2,1)}, bf16[3,272,512]{2,1,0:T(8,128)(2,1)S(1)}, u32[]{:S(2)}, u32[]{:S(2)}) collective-permute-start(bf16[3,272,512]{2,1,0:T(8,128)(2,1)} %collective-permute-done.47.db.refs_11_), channel_id=1, source_target_pairs={{8,0},{16,8},{24,16},{28,24},{20,28},{12,20},{4,12},{0,4},{9,1},{1... | collective-permute-start | bytes 2506760 | tf_op jit(solution)/shard_map/ppermute | solution.py:1449
  611.5 31.4 %collective-permute-start.52 = (bf16[3,256,512]{2,1,0:T(8,128)(2,1)}, bf16[3,256,512]{2,1,0:T(8,128)(2,1)S(1)}, u32[]{:S(2)}, u32[]{:S(2)}) collective-permute-start(bf16[3,256,512]{2,1,0:T(8,128)(2,1)} %get-tuple-element.319), channel_id=1, source_target_pairs={{0,8},{8,16},{16,24},{24,28},{28,20},{20,12},{12,4},{4,0},{1,9},{9... | collective-permute-start | bytes 2359304 | tf_op jit(solution)/shard_map/ppermute | solution.py:1471
  612.2 30.7 %collective-permute-start.53 = (bf16[3,256,512]{2,1,0:T(8,128)(2,1)S(1)}, bf16[3,256,512]{2,1,0:T(8,128)(2,1)S(1)}, u32[]{:S(2)}, u32[]{:S(2)}) collective-permute-start(bf16[3,256,512]{2,1,0:T(8,128)(2,1)S(1)} %get-tuple-element.320), channel_id=1, source_target_pairs={{8,0},{16,8},{24,16},{28,24},{20,28},{12,20},{4,12},{0,4},{9,1},{1... | collective-permute-start | bytes 2359304 | tf_op jit(solution)/shard_map/ppermute | solution.py:1471
  (106 other events, 1972.5 us)
Sparse Core Ops, SparseCore 0:
  9.6 25.4 all-gather.6
  37.2 34.2 all-gather.8
  73.1 22.5 all-gather.10
  97.2 43.3 all-gather.12
  142.0 43.4 all-gather.14
  186.9 43.3 all-gather.16
  373.8 55.7 reduce-scatter.4
  432.8 31.4 reduce-scatter.10
  466.9 54.8 reduce-scatter.6
  524.3 54.8 reduce-scatter.8

commit v4 on v3

--- a/solution.py
+++ b/solution.py
@@ -164,8 +164,9 @@
     )(indices, gains)
 
 
-def collect_kernel(meta, ck, cv, mk, mv, sem_k, sem_v, *, micros, count, cap):
-    owner = pl.program_id(0)
+def collect_kernel(meta, ck, cv, *refs, micros, count, cap, first):
+    mk, mv, sem_k, sem_v = refs[-4:]
+    owner = pl.program_id(0) + first
 
     def list_of(i):
         base = list_base(count) + (owner * 2 * micros + i) * (cap + 1)
@@ -215,25 +216,28 @@
     lax.fori_loop(0, 2 * micros, finish, 0)
 
 
-def collect(meta, cache_keys, cache_values, count, cap):
+def collect(meta, cache_keys, cache_values, count, cap, owners, into=()):
     micros = cache_keys.shape[0]
     shape = jax.ShapeDtypeStruct((micros, count, 2, cap, BLOCK, HEAD_DIM), BF16)
     anywhere = pl.BlockSpec(memory_space=pl.ANY)
-    block = pl.BlockSpec((micros, 1, 2, cap, BLOCK, HEAD_DIM), lambda o, meta: (0, o, 0, 0, 0, 0))
+    block = pl.BlockSpec((micros, 1, 2, cap, BLOCK, HEAD_DIM), lambda o, meta: (0, o + owners.start, 0, 0, 0, 0))
     return pl.pallas_call(
-        functools.partial(collect_kernel, micros=micros, count=count, cap=cap),
+        functools.partial(collect_kernel, micros=micros, count=count, cap=cap, first=owners.start),
         grid_spec=pltpu.PrefetchScalarGridSpec(
             num_scalar_prefetch=1,
-            grid=(count,),
-            in_specs=[anywhere, anywhere],
+            grid=(len(owners),),
+            in_specs=[anywhere, anywhere] + [anywhere] * len(into),
             out_specs=[block, block],
             scratch_shapes=[pltpu.SemaphoreType.DMA, pltpu.SemaphoreType.DMA],
         ),
         out_shape=[shape, shape],
+        input_output_aliases={3: 0, 4: 1} if into else {},
         compiler_params=params(),
         name="collect",
-        cost_estimate=pl.CostEstimate(flops=0, bytes_accessed=90_000_000, transcendentals=0),
-    )(meta, cache_keys.reshape(-1, D), cache_values.reshape(-1, D))
+        cost_estimate=pl.CostEstimate(
+            flops=0, bytes_accessed=11_000_000 * len(owners), transcendentals=0
+        ),
+    )(meta, cache_keys.reshape(-1, D), cache_values.reshape(-1, D), *into)
 
 
 def turn(value, cosine, sine):
@@ -1223,29 +1227,32 @@
     unturn()
     for name in ("turned", "back_key", "back_value"):
         copies[name].wait()
-    half = []
-    for j in range(shards // 2):
-        half.append(give(j))
+    order = [list(range(shards // 2))]
+    if stages > 1:
+        order = [
+            [2 * j + 1 - bit_of(1) for j in range(shards // 4)],
+            [2 * j + bit_of(1) for j in range(shards // 4)],
+        ]
+    half = None
+    for numbers in order:
+        given_now = []
+        for j in numbers:
+            given_now.append(give(j))
+            advance()
+        for j, copy in zip(numbers, given_now):
+            halve_finish(0, j, copy)
+            advance()
+        if half is None and stages > 1:
+            half = halve_start(1)
+    for i in range(1, stages - 1):
+        for j, copy in enumerate(half):
+            halve_finish(i, j, copy)
+        half = halve_start(i + 1)
         advance()
-    for j in range(shards // 2):
-        halve_finish(0, j, half[j])
-        advance()
-    for i in range(1, stages):
-        half = halve_start(i)
-        if i < stages - 1:
-            for j, copy in enumerate(half):
-                halve_finish(i, j, copy)
-            advance()
     for name in ("query", "pairs", "x", "middle"):
         copies[name].wait()
     for m in range(micros):
-        input_back(m)
-        advance()
-    gains_ready()
-    for i in range(len(partners)):
-        copy = gain_start(i)
-        advance()
-        if i == 0:
+        if m == micros - 1:
             if stages > 1:
                 halve_finish(stages - 1, 0, half[0])
             late.append(
@@ -1257,6 +1264,13 @@
                     lambda c: late_out.at[c],
                 )
             )
+            advance()
+        input_back(m)
+        advance()
+    gains_ready()
+    for i in range(len(partners)):
+        copy = gain_start(i)
+        advance()
         gain_finish(i, copy)
     while not all(run.done() for run in runs + late):
         advance()
@@ -1405,14 +1419,19 @@
 
     meta, cap = make_meta(indices, partner, cache_keys.shape[1] // BLOCK, count)
     x = tokens.reshape(micros, ROWS, D)
+    some = count * 3 // 8
+    memory = collect(meta, cache_keys, cache_values, count, cap, range(some))
+    x, memory = lax.optimization_barrier((x, memory))
     normed_low, qa, qb = project_query(x, gain_one, full_query, cosine, sine)
     meta, qa, qb = lax.optimization_barrier((meta, qa, qb))
     queries = [(qa, qb)]
     for _ in range(count - 1):
         qa, qb = lax.ppermute(qa, "ctx", onward), lax.ppermute(qb, "ctx", backward)
         queries.append((qa, qb))
-    memory_keys, memory_values = collect(meta, cache_keys, cache_values, count, cap)
-    queries[1], normed_low, memory_keys = lax.optimization_barrier((queries[1], normed_low, memory_keys))
+    memory_keys, memory_values = collect(
+        meta, cache_keys, cache_values, count, cap, range(some, count), memory
+    )
+    queries[1], normed_low = lax.optimization_barrier((queries[1], normed_low))
     keys, values, normed_turned = project_pairs(normed_low, pair_weights, cosine, sine)
     for step in range(1, count - 1):
         queries[step], queries[step + 1] = lax.optimization_barrier((queries[step], queries[step + 1]))
@@ -1459,6 +1478,9 @@
     early_width = sum(part.shape[1] for part in early)
     for step in range(1, count - 1):
         slopes[step], slopes[step + 1] = lax.optimization_barrier((slopes[step], slopes[step + 1]))
+    middle_step = count // 2 + 1
+    first_sums = key_gradients(meta, keys, values, queries, slopes, range(middle_step))
+    slopes[middle_step - 2], first_sums = lax.optimization_barrier((slopes[middle_step - 2], first_sums))
     acc = ()
     for step in range(count):
         part = unattend(
@@ -1470,8 +1492,6 @@
         if acc:
             acc = (lax.ppermute(acc[0], "ctx", onward), lax.ppermute(acc[1], "ctx", backward))
         acc = combine(acc, part)
-    middle_step = count // 2
-    first_sums = key_gradients(meta, keys, values, queries, slopes, range(middle_step))
     back_key, back_value = key_gradients(
         meta, keys, values, queries, slopes, range(middle_step, count), first_sums, (cosine, sine)
     )

time: 846 us -> 834 us (0.986)
    ppermute x14, starting transfers between devices: 21.7 us -> 11.9 us  [body(): lax.ppermute(acc[0], 'ctx', onward)]
    ppermute x14, starting transfers between devices: 9.37 us -> 18.2 us  [body(): lax.ppermute(acc[1], 'ctx', backward)]
    pallas_call x1 -> x2, Pallas kernels: 28.1 us -> 29.9 us  [collect(): pl.pallas_call(functools.partial(collect_kernel, micros=micros, count=cou...]
  transfers between devices with their start and end apart: 66 -> 66, of which waited for: 38 -> 28; matrix products, arithmetic and copies ran while one was open for 2% -> 2% of each run, Pallas kernels for 33% -> 33%
where the time goes in v4:
time: 834 us; the launch traced here: 821 us
  Pallas kernels  459 us (55%)
  waiting for transfers between devices  238 us (29%)
  starting transfers between devices  61.6 us (7%)
  local copies, waits for them, and re-layouts  32.5 us (4%)
  between operations  15.6 us (2%)
  other arithmetic  10.1 us (1%)
    pallas_call x1, Pallas kernels, tail(): pl.pallas_call(functools.partial(tail_kernel, count=count, shards=shards,...  133 us
    pallas_call x8, Pallas kernels, unattend(): pl.pallas_call(functools.partial(backward_kernel, step=step, count=count,...  86.9 us
    ppermute x14, waiting for transfers between devices, body(): lax.ppermute(acc[0], 'ctx', onward)  86.2 us
    ppermute x7, waiting for transfers between devices, body(): lax.ppermute(qa, 'ctx', onward)  73.7 us
    ppermute x7, waiting for transfers between devices, body(): lax.ppermute(da, 'ctx', onward)  65.3 us
    pallas_call x8, Pallas kernels, attend(): pl.pallas_call(functools.partial(forward_kernel, step=step, count=count,...  64.9 us
    pallas_call x1, Pallas kernels, feed(): pl.pallas_call(feed_kernel, grid=(units // TILE,), in_specs=[whole, whole...  52.6 us
    pallas_call x2, Pallas kernels, key_gradients(): pl.pallas_call(functools.partial(key_kernel, steps=steps, micros=micros,...  37.2 us
  transfers between devices with their start and end apart: 66, of which 28 were waited for; matrix products, arithmetic and copies ran while one was open for 2% of the time, Pallas kernels for 33%

profile of v4, /device:TPU:0, one launch (start us, length us, event | category | flops | bytes accessed | tf_op | source)
XLA Modules:
  0.0 821.2 jit_solution(14108396441718954444)
XLA Ops:
  13.1 9.5 %share.1 = (s32[8,8,128]{2,1,0:T(8,128)S(1)}, f32[4,8,256]{2,1,0:T(8,128)S(1)}) custom-call(s32[8,128]{1,0:T(8,128)S(1)} %pad.10.indices, f32[8,256]{1,0:T(8,128)S(1)} %fusion.20.gains), custom_call_target="tpu_custom_call" | custom-call | bytes 20000000 | tf_op jit(solution)/shard_map/share/pallas_call | solution.py:150
  28.0 11.8 %collect.2 = (bf16[3,8,2,32,64,128]{5,4,3,2,1,0:T(8,128)(2,1)}, bf16[3,8,2,32,64,128]{5,4,3,2,1,0:T(8,128)(2,1)}) custom-call(s32[1601]{0:T(1024)} %concatenate.14.meta, bf16[6144,1024]{1,0:T(8,128)(2,1)} %bitcast.53, bf16[6144,1024]{1,0:T(8,128)(2,1)} %bitcast.55), custom_call_target="tpu_custom_call" | custom-call | bytes 33000000 | tf_op jit(solution)/shard_map/collect/pallas_call | solution.py:224
  48.5 16.4 %collective-permute-done.qa.refs_4_ = bf16[3,256,512]{2,1,0:T(8,128)(2,1)S(1)} collective-permute-done((bf16[3,256,512]{2,1,0:T(8,128)(2,1)}, bf16[3,256,512]{2,1,0:T(8,128)(2,1)S(1)}, u32[]{:S(2)}, u32[]{:S(2)}) %collective-permute-start) | collective-permute-done | bytes 786464 | tf_op jit(solution)/shard_map/ppermute | solution.py:1429
  68.5 18.2 %collect.3 = (bf16[3,8,2,32,64,128]{5,4,3,2,1,0:T(8,128)(2,1)}, bf16[3,8,2,32,64,128]{5,4,3,2,1,0:T(8,128)(2,1)}) custom-call(s32[1601]{0:T(1024)} %concatenate.14.meta, bf16[6144,1024]{1,0:T(8,128)(2,1)} %bitcast.54, bf16[6144,1024]{1,0:T(8,128)(2,1)} %bitcast.56, ...), custom_call_target="tpu_custom_call", output_to_operand_aliasing={{0}: (3, {}), {1}: (4, {})} | custom-call | bytes 55000000 | tf_op jit(solution)/shard_map/collect/pallas_call | solution.py:224
  119.3 9.7 %collective-permute-done.4.refs_0_ = bf16[3,272,512]{2,1,0:T(8,128)(2,1)S(1)} collective-permute-done((bf16[3,272,512]{2,1,0:T(8,128)(2,1)S(1)}, bf16[3,272,512]{2,1,0:T(8,128)(2,1)S(1)}, u32[]{:S(2)}, u32[]{:S(2)}) %collective-permute-start.4) | collective-permute-done | bytes 835616 | tf_op jit(solution)/shard_map/ppermute | solution.py:1446
  131.5 14.3 %collective-permute-done.10.qa.refs_16_ = bf16[3,256,512]{2,1,0:T(8,128)(2,1)S(1)} collective-permute-done((bf16[3,256,512]{2,1,0:T(8,128)(2,1)}, bf16[3,256,512]{2,1,0:T(8,128)(2,1)S(1)}, u32[]{:S(2)}, u32[]{:S(2)}) %collective-permute-start.10) | collective-permute-done | bytes 786464 | tf_op jit(solution)/shard_map/ppermute | solution.py:1429
  148.0 8.8 %attend.10 = (bf16[3,256,512]{2,1,0:T(8,128)(2,1)S(1)}, bf16[3,256,512]{2,1,0:T(8,128)(2,1)S(1)}, f32[3,8,256]{2,1,0:T(8,128)S(1)}, f32[3,8,256]{2,1,0:T(8,128)S(1)}) custom-call(s32[1601]{0:T(1024)S(1)} %copy-done.42, bf16[3,256,512]{2,1,0:T(8,128)(2,1)} %collective-permute-done.6.qa.refs_12_, bf16[3,256,512]{2,1,0:T(8,128)(2,1)} %collective-permute-done.7.qb.refs_13_, ...), custom_call_target="tpu_custom_call" | custom-call | flops 6000000000 | bytes 10000000 | tf_op jit(solution)/shard_map/attend/pallas_call | solution.py:499
  166.2 14.3 %collective-permute-done.14.qa.refs_0_ = bf16[3,256,512]{2,1,0:T(8,128)(2,1)S(1)} collective-permute-done((bf16[3,256,512]{2,1,0:T(8,128)(2,1)S(1)}, bf16[3,256,512]{2,1,0:T(8,128)(2,1)S(1)}, u32[]{:S(2)}, u32[]{:S(2)}) %collective-permute-start.14) | collective-permute-done | bytes 786464 | tf_op jit(solution)/shard_map/ppermute | solution.py:1429
  201.0 14.3 %collective-permute-done.18.qa.refs_4_ = bf16[3,256,512]{2,1,0:T(8,128)(2,1)S(1)} collective-permute-done((bf16[3,256,512]{2,1,0:T(8,128)(2,1)S(1)}, bf16[3,256,512]{2,1,0:T(8,128)(2,1)S(1)}, u32[]{:S(2)}, u32[]{:S(2)}) %collective-permute-start.18) | collective-permute-done | bytes 786464 | tf_op jit(solution)/shard_map/ppermute | solution.py:1429
  235.7 14.3 %collective-permute-done.22.qa.refs_8_ = bf16[3,256,512]{2,1,0:T(8,128)(2,1)S(1)} collective-permute-done((bf16[3,256,512]{2,1,0:T(8,128)(2,1)S(1)}, bf16[3,256,512]{2,1,0:T(8,128)(2,1)S(1)}, u32[]{:S(2)}, u32[]{:S(2)}) %collective-permute-start.22) | collective-permute-done | bytes 786464 | tf_op jit(solution)/shard_map/ppermute | solution.py:1429
  257.9 10.1 %collective-permute-done.20.refs_0_ = bf16[3,272,512]{2,1,0:T(8,128)(2,1)S(1)} collective-permute-done((bf16[3,272,512]{2,1,0:T(8,128)(2,1)S(1)}, bf16[3,272,512]{2,1,0:T(8,128)(2,1)S(1)}, u32[]{:S(2)}, u32[]{:S(2)}) %collective-permute-start.20) | collective-permute-done | bytes 835616 | tf_op jit(solution)/shard_map/ppermute | solution.py:1446
  278.4 10.7 %collective-permute-done.24.refs_0_ = bf16[3,272,512]{2,1,0:T(8,128)(2,1)S(1)} collective-permute-done((bf16[3,272,512]{2,1,0:T(8,128)(2,1)S(1)}, bf16[3,272,512]{2,1,0:T(8,128)(2,1)S(1)}, u32[]{:S(2)}, u32[]{:S(2)}) %collective-permute-start.24) | collective-permute-done | bytes 835616 | tf_op jit(solution)/shard_map/ppermute | solution.py:1446
  293.6 8.7 %attend.15 = (bf16[3,256,512]{2,1,0:T(8,128)(2,1)S(1)}, bf16[3,256,512]{2,1,0:T(8,128)(2,1)S(1)}, f32[3,8,256]{2,1,0:T(8,128)S(1)}, f32[3,8,256]{2,1,0:T(8,128)S(1)}) custom-call(s32[1601]{0:T(1024)S(1)} %copy-done.42, bf16[3,256,512]{2,1,0:T(8,128)(2,1)S(1)} %copy-done.6, bf16[3,256,512]{2,1,0:T(8,128)(2,1)S(1)} %copy-done.9, ...), custom_call_target="tpu_custom_call" | custom-call | flops 6000000000 | bytes 10000000 | tf_op jit(solution)/shard_map/attend/pallas_call | solution.py:499
  312.3 8.9 %finish.1 = (f32[3,256,1024]{2,1,0:T(8,128)}, bf16[3,256,1024]{2,1,0:T(8,128)(2,1)}, f32[3,2,8,256]{3,2,1,0:T(8,128)}, f32[3,256,1024]{2,1,0:T(8,128)}, bf16[3,256,1024]{2,1,0:T(8,128)(2,1)}) custom-call(bf16[3,272,512]{2,1,0:T(8,128)(2,1)} %collective-permute-done.26.acc_a, bf16[3,272,512]{2,1,0:T(8,128)(2,1)} %collective-permute-done.27.acc_b, ...), custom_call_target="tpu_custom_call" | custom-call | flops 1610612736 | bytes 16000000 | tf_op jit(solution)/shard_map/finish/pallas_call | solution.py:576
  321.3 52.6 %feed.1 = (bf16[3,256,1024]{2,1,0:T(8,128)(2,1)}, f32[3,256,1024]{2,1,0:T(8,128)}, bf16[1024,2816]{1,0:T(8,128)(2,1)}, bf16[1024,2816]{1,0:T(8,128)(2,1)}, bf16[2816,1024]{1,0:T(8,128)(2,1)}) custom-call(bf16[3,256,1024]{2,1,0:T(8,128)(2,1)} %get-tuple-element.276.normed, bf16[3,256,1024]{2,1,0:T(8,128)(2,1)} %bitcast.60, ...), custom_call_target="tpu_custom_call" | custom-call | flops 39862665216 | bytes 50000000 | tf_op jit(solution)/shard_map/feed/pallas_call | solution.py:638
  374.0 12.8 %prepare.1 = (bf16[3,272,512]{2,1,0:T(8,128)(2,1)}, bf16[3,272,512]{2,1,0:T(8,128)(2,1)}, f32[3,256,1024]{2,1,0:T(8,128)}, bf16[3,256,1024]{2,1,0:T(8,128)(2,1)}, f32[3,8,1024]{2,1,0:T(8,128)}) custom-call(f32[3,256,1024]{2,1,0:T(8,128)} %get-tuple-element.279.back_normed, f32[3,256,1024]{2,1,0:T(8,128)} %get-tuple-element.277.middle, ...), custom_call_target="tpu_custom_call" | custom-call | flops 1610612736 | bytes 22000000 | tf_op jit(solution)/shard_map/prepare/pallas_call | solution.py:695
  388.9 16.6 %collective-permute-done.28.da.refs_6_ = bf16[3,272,512]{2,1,0:T(8,128)(2,1)} collective-permute-done((bf16[3,272,512]{2,1,0:T(8,128)(2,1)}, bf16[3,272,512]{2,1,0:T(8,128)(2,1)}, u32[]{:S(2)}, u32[]{:S(2)}) %collective-permute-start.28) | collective-permute-done | bytes 835616 | tf_op jit(solution)/shard_map/ppermute | solution.py:1468
  414.3 16.6 %collective-permute-done.30.da.refs_10_ = bf16[3,272,512]{2,1,0:T(8,128)(2,1)S(1)} collective-permute-done((bf16[3,272,512]{2,1,0:T(8,128)(2,1)}, bf16[3,272,512]{2,1,0:T(8,128)(2,1)S(1)}, u32[]{:S(2)}, u32[]{:S(2)}) %collective-permute-start.30) | collective-permute-done | bytes 835616 | tf_op jit(solution)/shard_map/ppermute | solution.py:1468
  433.0 16.4 %collective-permute-done.34.refs_14_.da = bf16[3,272,512]{2,1,0:T(8,128)(2,1)S(1)} collective-permute-done((bf16[3,272,512]{2,1,0:T(8,128)(2,1)S(1)}, bf16[3,272,512]{2,1,0:T(8,128)(2,1)S(1)}, u32[]{:S(2)}, u32[]{:S(2)}) %collective-permute-start.34) | collective-permute-done | bytes 835616 | tf_op jit(solution)/shard_map/ppermute | solution.py:1468
  451.4 15.7 %collective-permute-done.38.refs_18_.da = bf16[3,272,512]{2,1,0:T(8,128)(2,1)S(1)} collective-permute-done((bf16[3,272,512]{2,1,0:T(8,128)(2,1)S(1)}, bf16[3,272,512]{2,1,0:T(8,128)(2,1)S(1)}, u32[]{:S(2)}, u32[]{:S(2)}) %collective-permute-start.38) | collective-permute-done | bytes 835616 | tf_op jit(solution)/shard_map/ppermute | solution.py:1468
  472.1 11.7 %unattend.8 = (bf16[3,256,512]{2,1,0:T(8,128)(2,1)S(1)}, bf16[3,256,512]{2,1,0:T(8,128)(2,1)S(1)}) custom-call(s32[1601]{0:T(1024)S(1)} %copy-done.42, bf16[3,256,512]{2,1,0:T(8,128)(2,1)S(1)} %copy-done.25, bf16[3,256,512]{2,1,0:T(8,128)(2,1)S(1)} %copy-done.28, bf16[3,272,512]{2,1,0:T(8,128)(2,1)} %collective-permute-done.28.da.refs_6_, ...), custom_call_target="tpu_custom_call" | custom-call | flops 8000000000 | bytes 12000000 | tf_op jit(solution)/shard_map/unattend/pallas_call | solution.py:797
  486.1 10.2 %unattend.9 = (bf16[3,256,512]{2,1,0:T(8,128)(2,1)S(1)}, bf16[3,256,512]{2,1,0:T(8,128)(2,1)S(1)}) custom-call(s32[1601]{0:T(1024)S(1)} %copy-done.42, bf16[3,256,512]{2,1,0:T(8,128)(2,1)S(1)} %copy-done.35, bf16[3,256,512]{2,1,0:T(8,128)(2,1)S(1)} %copy-done.37, bf16[3,272,512]{2,1,0:T(8,128)(2,1)S(1)} %collective-permute-done.30.da.refs_10_, ...), custom_call_target="tpu_custom_call" | custom-call | flops 8000000000 | bytes 12000000 | tf_op jit(solution)/shard_map/unattend/pallas_call | solution.py:797
  508.2 22.0 %key_gradients.2 = (f32[3,256,1024]{2,1,0:T(8,128)}, f32[3,256,1024]{2,1,0:T(8,128)}) custom-call(s32[1601]{0:T(1024)S(1)} %copy-done.42, bf16[3,256,1024]{2,1,0:T(8,128)(2,1)} %get-tuple-element.202.k, bf16[3,256,1024]{2,1,0:T(8,128)(2,1)} %get-tuple-element.203.v, bf16[3,256,512]{2,1,0:T(8,128)(2,1)S(1)} %copy-done.7, bf16[3,256,512]{2,1,0:T(8,128)(2,1)S(1)} %copy-done.10, ...), custom_call_target="tpu_custom_call" | custom-call | flops 15000000512 | bytes 20000000 | tf_op jit(solution)/shard_map/key_gradients/pallas_call | solution.py:903
  530.3 11.2 %unattend.10 = (bf16[3,256,512]{2,1,0:T(8,128)(2,1)S(1)}, bf16[3,256,512]{2,1,0:T(8,128)(2,1)S(1)}) custom-call(s32[1601]{0:T(1024)S(1)} %copy-done.42, bf16[3,256,512]{2,1,0:T(8,128)(2,1)} %collective-permute-done.6.qa.refs_12_, bf16[3,256,512]{2,1,0:T(8,128)(2,1)} %collective-permute-done.7.qb.refs_13_, ...), custom_call_target="tpu_custom_call" | custom-call | flops 8000000000 | bytes 12000000 | tf_op jit(solution)/shard_map/unattend/pallas_call | solution.py:797
  546.2 10.7 %unattend.11 = (bf16[3,256,512]{2,1,0:T(8,128)(2,1)S(1)}, bf16[3,256,512]{2,1,0:T(8,128)(2,1)S(1)}) custom-call(s32[1601]{0:T(1024)S(1)} %copy-done.42, bf16[3,256,512]{2,1,0:T(8,128)(2,1)S(1)} %copy-done.39, bf16[3,256,512]{2,1,0:T(8,128)(2,1)S(1)} %copy-done.41, bf16[3,272,512]{2,1,0:T(8,128)(2,1)S(1)} %copy-done.52, bf16[3,272,512]{2,1,0:T(8,128)(2,1)S(1)} %copy-done.54, ...), custom_call_target="tpu_custom_call" | custom-call | flops 8000000000 | bytes 12000000 | tf_op jit(solution)/shard_map/unattend/pallas_call | solution.py:797
  567.0 10.2 %unattend.12 = (bf16[3,256,512]{2,1,0:T(8,128)(2,1)S(1)}, bf16[3,256,512]{2,1,0:T(8,128)(2,1)S(1)}) custom-call(s32[1601]{0:T(1024)S(1)} %copy-done.42, bf16[3,256,512]{2,1,0:T(8,128)(2,1)S(1)} %copy-done.13, bf16[3,256,512]{2,1,0:T(8,128)(2,1)S(1)} %copy-done.16, bf16[3,272,512]{2,1,0:T(8,128)(2,1)S(1)} %collective-permute-done.40.da.refs_2_, ...), custom_call_target="tpu_custom_call" | custom-call | flops 8000000000 | bytes 12000000 | tf_op jit(solution)/shard_map/unattend/pallas_call | solution.py:797
  577.2 15.6 %collective-permute-done.44.refs_0_ = bf16[3,256,512]{2,1,0:T(8,128)(2,1)S(1)} collective-permute-done((bf16[3,256,512]{2,1,0:T(8,128)(2,1)S(1)}, bf16[3,256,512]{2,1,0:T(8,128)(2,1)S(1)}, u32[]{:S(2)}, u32[]{:S(2)}) %collective-permute-start.44) | collective-permute-done | bytes 786464 | tf_op jit(solution)/shard_map/ppermute | solution.py:1493
  601.0 11.1 %unattend.13 = (bf16[3,256,512]{2,1,0:T(8,128)(2,1)S(1)}, bf16[3,256,512]{2,1,0:T(8,128)(2,1)S(1)}) custom-call(s32[1601]{0:T(1024)S(1)} %copy-done.42, bf16[3,256,512]{2,1,0:T(8,128)(2,1)S(1)} %copy-done.19, bf16[3,256,512]{2,1,0:T(8,128)(2,1)S(1)} %copy-done.22, bf16[3,272,512]{2,1,0:T(8,128)(2,1)} %collective-permute-done.46.da.refs_6_, ...), custom_call_target="tpu_custom_call" | custom-call | flops 8000000000 | bytes 12000000 | tf_op jit(solution)/shard_map/unattend/pallas_call | solution.py:797
  618.2 10.1 %unattend.15 = (bf16[3,256,512]{2,1,0:T(8,128)(2,1)S(1)}, bf16[3,256,512]{2,1,0:T(8,128)(2,1)S(1)}) custom-call(s32[1601]{0:T(1024)S(1)} %copy-done.42, bf16[3,256,512]{2,1,0:T(8,128)(2,1)S(1)} %copy-done.8, bf16[3,256,512]{2,1,0:T(8,128)(2,1)S(1)} %copy-done.11, bf16[3,272,512]{2,1,0:T(8,128)(2,1)S(1)} %copy-done.44, bf16[3,272,512]{2,1,0:T(8,128)(2,1)S(1)} %copy-done.46, ...), custom_call_target="tpu_custom_call" | custom-call | flops 8000000000 | bytes 12000000 | tf_op jit(solution)/shard_map/unattend/pallas_call | solution.py:797
  628.4 11.6 %unattend.14 = (bf16[3,256,512]{2,1,0:T(8,128)(2,1)S(1)}, bf16[3,256,512]{2,1,0:T(8,128)(2,1)S(1)}) custom-call(s32[1601]{0:T(1024)S(1)} %copy-done.42, bf16[3,256,512]{2,1,0:T(8,128)(2,1)S(1)} %copy-done.31, bf16[3,256,512]{2,1,0:T(8,128)(2,1)S(1)} %copy-done.33, bf16[3,272,512]{2,1,0:T(8,128)(2,1)} %collective-permute-done.50.da.refs_10_, ...), custom_call_target="tpu_custom_call" | custom-call | flops 8000000000 | bytes 12000000 | tf_op jit(solution)/shard_map/unattend/pallas_call | solution.py:797
  642.8 15.1 %key_gradients.3 = (bf16[3,256,1024]{2,1,0:T(8,128)(2,1)S(1)}, bf16[3,256,1024]{2,1,0:T(8,128)(2,1)S(1)}) custom-call(s32[1601]{0:T(1024)S(1)} %copy-done.42, bf16[3,256,1024]{2,1,0:T(8,128)(2,1)} %get-tuple-element.202.k, bf16[3,256,1024]{2,1,0:T(8,128)(2,1)} %get-tuple-element.203.v, bf16[3,256,512]{2,1,0:T(8,128)(2,1)S(1)} %copy-done.14, ...), custom_call_target="tpu_custom_call" | custom-call | flops 8999999488 | bytes 20000000 | tf_op jit(solution)/shard_map/key_gradients/pallas_call | solution.py:903
  665.4 132.5 %tail.1 = (bf16[16,16,9472]{2,1,0:T(8,128)(2,1)}, bf16[16,16,3072]{2,1,0:T(8,128)(2,1)}, f32[8,1024]{1,0:T(8,128)}, f32[3,256,1024]{2,1,0:T(8,128)}) custom-call(bf16[3,256,512]{2,1,0:T(8,128)(2,1)} %copy-done.69, bf16[3,256,512]{2,1,0:T(8,128)(2,1)} %copy-done.70, bf16[3,256,512]{2,1,0:T(8,128)(2,1)} %copy-done.61, bf16[3,256,512]{2,1,0:T(8,128)(2,1)} %copy-done.62, ...), custom_call_target="tpu_custom_call" | custom-call | flops 12000000000 | bytes 300000000 | tf_op jit(solution)/shard_map/tail/pallas_call | solution.py:1294
  (345 shorter events, 232.6 us)
Async XLA Ops:
  7.2 33.4 %all-gather.7.cloned.1.call-start = ((), (), s32[]{:S(2)}) async-start(), calls=%async_computation.4 | async-start | bytes 2621440 | tf_op jit(solution)/shard_map/all_gather | solution.py:1388
  7.9 80.9 %all-gather.9.cloned.1.call-start = ((), (), s32[]{:S(2)}) async-start(), calls=%async_computation.5 | async-start | bytes 5242880 | tf_op jit(solution)/shard_map/all_gather | solution.py:1404
  10.3 295.0 %all-gather.11.cloned.1.call-start = ((), (), s32[]{:S(2)}) async-start(), calls=%async_computation.6 | async-start | bytes 2621440 | tf_op jit(solution)/shard_map/all_gather | solution.py:1388
  11.0 310.2 %all-gather.13.cloned.1.call-start = ((), (), s32[]{:S(2)}) async-start(), calls=%async_computation.7 | async-start | bytes 7208960 | tf_op jit(solution)/shard_map/all_gather | solution.py:1388
  11.6 309.7 %all-gather.15.cloned.1.call-start = ((), (), s32[]{:S(2)}) async-start(), calls=%async_computation.8 | async-start | bytes 7208960 | tf_op jit(solution)/shard_map/all_gather | solution.py:1388
  12.2 309.1 %all-gather.17.cloned.1.call-start = ((), (), s32[]{:S(2)}) async-start(), calls=%async_computation.9 | async-start | bytes 7208960 | tf_op jit(solution)/shard_map/all_gather | solution.py:1388
  12.7 647.5 %reduce-scatter.5.cloned.1.call-start = ((), (), s32[]{:S(2)}) async-start(), calls=%async_computation.10 | async-start | bytes 7208960 | tf_op jit(solution)/shard_map/reduce_scatter | solution.py:1463
  109.5 36.3 %collective-permute-start.10 = (bf16[3,256,512]{2,1,0:T(8,128)(2,1)}, bf16[3,256,512]{2,1,0:T(8,128)(2,1)S(1)}, u32[]{:S(2)}, u32[]{:S(2)}) collective-permute-start(bf16[3,256,512]{2,1,0:T(8,128)(2,1)} %collective-permute-done.6.qa.refs_12_), channel_id=1, source_target_pairs={{0,8},{8,16},{16,24},{24,28},{28,20},{20,12},{12,4},{4,0},{1,9},{9... | collective-permute-start | bytes 2359304 | tf_op jit(solution)/shard_map/ppermute | solution.py:1429
  109.9 35.9 %collective-permute-start.11 = (bf16[3,256,512]{2,1,0:T(8,128)(2,1)}, bf16[3,256,512]{2,1,0:T(8,128)(2,1)S(1)}, u32[]{:S(2)}, u32[]{:S(2)}) collective-permute-start(bf16[3,256,512]{2,1,0:T(8,128)(2,1)} %collective-permute-done.7.qb.refs_13_), channel_id=1, source_target_pairs={{8,0},{16,8},{24,16},{28,24},{20,28},{12,20},{4,12},{0,4},{9,1},{1... | collective-permute-start | bytes 2359304 | tf_op jit(solution)/shard_map/ppermute | solution.py:1429
  129.4 34.3 %collective-permute-start.8 = (bf16[3,272,512]{2,1,0:T(8,128)(2,1)S(1)}, bf16[3,272,512]{2,1,0:T(8,128)(2,1)S(1)}, u32[]{:S(2)}, u32[]{:S(2)}) collective-permute-start(bf16[3,272,512]{2,1,0:T(8,128)(2,1)S(1)} %get-tuple-element.222), channel_id=1, source_target_pairs={{0,8},{8,16},{16,24},{24,28},{28,20},{20,12},{12,4},{4,0},{1,9},{9... | collective-permute-start | bytes 2506760 | tf_op jit(solution)/shard_map/ppermute | solution.py:1446
  130.3 33.4 %collective-permute-start.9 = (bf16[3,272,512]{2,1,0:T(8,128)(2,1)S(1)}, bf16[3,272,512]{2,1,0:T(8,128)(2,1)S(1)}, u32[]{:S(2)}, u32[]{:S(2)}) collective-permute-start(bf16[3,272,512]{2,1,0:T(8,128)(2,1)S(1)} %get-tuple-element.223), channel_id=1, source_target_pairs={{8,0},{16,8},{24,16},{28,24},{20,28},{12,20},{4,12},{0,4},{9,1},{1... | collective-permute-start | bytes 2506760 | tf_op jit(solution)/shard_map/ppermute | solution.py:1446
  145.8 34.8 %collective-permute-start.14 = (bf16[3,256,512]{2,1,0:T(8,128)(2,1)S(1)}, bf16[3,256,512]{2,1,0:T(8,128)(2,1)S(1)}, u32[]{:S(2)}, u32[]{:S(2)}) collective-permute-start(bf16[3,256,512]{2,1,0:T(8,128)(2,1)S(1)} %collective-permute-done.10.qa.refs_16_), channel_id=1, source_target_pairs={{0,8},{8,16},{16,24},{24,28},{28,20},{20,12},{12,4},{4,0},{1,9},{9... | collective-permute-start | bytes 2359304 | tf_op jit(solution)/shard_map/ppermute | solution.py:1429
  146.7 33.9 %collective-permute-start.15 = (bf16[3,256,512]{2,1,0:T(8,128)(2,1)S(1)}, bf16[3,256,512]{2,1,0:T(8,128)(2,1)S(1)}, u32[]{:S(2)}, u32[]{:S(2)}) collective-permute-start(bf16[3,256,512]{2,1,0:T(8,128)(2,1)S(1)} %collective-permute-done.11.qb.refs_17_), channel_id=1, source_target_pairs={{8,0},{16,8},{24,16},{28,24},{20,28},{12,20},{4,12},{0,4},{9,1},{1... | collective-permute-start | bytes 2359304 | tf_op jit(solution)/shard_map/ppermute | solution.py:1429
  164.1 34.3 %collective-permute-start.12 = (bf16[3,272,512]{2,1,0:T(8,128)(2,1)S(1)}, bf16[3,272,512]{2,1,0:T(8,128)(2,1)S(1)}, u32[]{:S(2)}, u32[]{:S(2)}) collective-permute-start(bf16[3,272,512]{2,1,0:T(8,128)(2,1)S(1)} %get-tuple-element.232), channel_id=1, source_target_pairs={{0,8},{8,16},{16,24},{24,28},{28,20},{20,12},{12,4},{4,0},{1,9},{9... | collective-permute-start | bytes 2506760 | tf_op jit(solution)/shard_map/ppermute | solution.py:1446
  165.1 33.4 %collective-permute-start.13 = (bf16[3,272,512]{2,1,0:T(8,128)(2,1)S(1)}, bf16[3,272,512]{2,1,0:T(8,128)(2,1)S(1)}, u32[]{:S(2)}, u32[]{:S(2)}) collective-permute-start(bf16[3,272,512]{2,1,0:T(8,128)(2,1)S(1)} %get-tuple-element.233), channel_id=1, source_target_pairs={{8,0},{16,8},{24,16},{28,24},{20,28},{12,20},{4,12},{0,4},{9,1},{1... | collective-permute-start | bytes 2506760 | tf_op jit(solution)/shard_map/ppermute | solution.py:1446
  180.6 34.8 %collective-permute-start.18 = (bf16[3,256,512]{2,1,0:T(8,128)(2,1)S(1)}, bf16[3,256,512]{2,1,0:T(8,128)(2,1)S(1)}, u32[]{:S(2)}, u32[]{:S(2)}) collective-permute-start(bf16[3,256,512]{2,1,0:T(8,128)(2,1)S(1)} %collective-permute-done.14.qa.refs_0_), channel_id=1, source_target_pairs={{0,8},{8,16},{16,24},{24,28},{28,20},{20,12},{12,4},{4,0},{1,9},{9... | collective-permute-start | bytes 2359304 | tf_op jit(solution)/shard_map/ppermute | solution.py:1429
  181.5 33.9 %collective-permute-start.19 = (bf16[3,256,512]{2,1,0:T(8,128)(2,1)S(1)}, bf16[3,256,512]{2,1,0:T(8,128)(2,1)S(1)}, u32[]{:S(2)}, u32[]{:S(2)}) collective-permute-start(bf16[3,256,512]{2,1,0:T(8,128)(2,1)S(1)} %collective-permute-done.15.qb.refs_1_), channel_id=1, source_target_pairs={{8,0},{16,8},{24,16},{28,24},{20,28},{12,20},{4,12},{0,4},{9,1},{1... | collective-permute-start | bytes 2359304 | tf_op jit(solution)/shard_map/ppermute | solution.py:1429
  198.9 34.3 %collective-permute-start.16 = (bf16[3,272,512]{2,1,0:T(8,128)(2,1)S(1)}, bf16[3,272,512]{2,1,0:T(8,128)(2,1)S(1)}, u32[]{:S(2)}, u32[]{:S(2)}) collective-permute-start(bf16[3,272,512]{2,1,0:T(8,128)(2,1)S(1)} %get-tuple-element.242), channel_id=1, source_target_pairs={{0,8},{8,16},{16,24},{24,28},{28,20},{20,12},{12,4},{4,0},{1,9},{9... | collective-permute-start | bytes 2506760 | tf_op jit(solution)/shard_map/ppermute | solution.py:1446
  215.3 34.8 %collective-permute-start.22 = (bf16[3,256,512]{2,1,0:T(8,128)(2,1)S(1)}, bf16[3,256,512]{2,1,0:T(8,128)(2,1)S(1)}, u32[]{:S(2)}, u32[]{:S(2)}) collective-permute-start(bf16[3,256,512]{2,1,0:T(8,128)(2,1)S(1)} %collective-permute-done.18.qa.refs_4_), channel_id=1, source_target_pairs={{0,8},{8,16},{16,24},{24,28},{28,20},{20,12},{12,4},{4,0},{1,9},{9... | collective-permute-start | bytes 2359304 | tf_op jit(solution)/shard_map/ppermute | solution.py:1429
  216.2 33.9 %collective-permute-start.23 = (bf16[3,256,512]{2,1,0:T(8,128)(2,1)S(1)}, bf16[3,256,512]{2,1,0:T(8,128)(2,1)S(1)}, u32[]{:S(2)}, u32[]{:S(2)}) collective-permute-start(bf16[3,256,512]{2,1,0:T(8,128)(2,1)S(1)} %collective-permute-done.19.qb.refs_5_), channel_id=1, source_target_pairs={{8,0},{16,8},{24,16},{28,24},{20,28},{12,20},{4,12},{0,4},{9,1},{1... | collective-permute-start | bytes 2359304 | tf_op jit(solution)/shard_map/ppermute | solution.py:1429
  233.7 34.3 %collective-permute-start.20 = (bf16[3,272,512]{2,1,0:T(8,128)(2,1)S(1)}, bf16[3,272,512]{2,1,0:T(8,128)(2,1)S(1)}, u32[]{:S(2)}, u32[]{:S(2)}) collective-permute-start(bf16[3,272,512]{2,1,0:T(8,128)(2,1)S(1)} %get-tuple-element.252), channel_id=1, source_target_pairs={{0,8},{8,16},{16,24},{24,28},{28,20},{20,12},{12,4},{4,0},{1,9},{9... | collective-permute-start | bytes 2506760 | tf_op jit(solution)/shard_map/ppermute | solution.py:1446
  374.0 290.3 %reduce-scatter.11.cloned.1.call-start = ((), (), s32[]{:S(2)}) async-start(), calls=%async_computation.13 | async-start | bytes 2621440 | tf_op jit(solution)/shard_map/reduce_scatter | solution.py:1463
  410.9 253.4 %reduce-scatter.7.cloned.1.call-start = ((), (), s32[]{:S(2)}) async-start(), calls=%async_computation.11 | async-start | bytes 7208960 | tf_op jit(solution)/shard_map/reduce_scatter | solution.py:1463
  411.7 252.7 %reduce-scatter.9.cloned.1.call-start = ((), (), s32[]{:S(2)}) async-start(), calls=%async_computation.12 | async-start | bytes 7208960 | tf_op jit(solution)/shard_map/reduce_scatter | solution.py:1463
  467.1 38.9 %collective-permute-start.40 = (bf16[3,272,512]{2,1,0:T(8,128)(2,1)S(1)}, bf16[3,272,512]{2,1,0:T(8,128)(2,1)S(1)}, u32[]{:S(2)}, u32[]{:S(2)}) collective-permute-start(bf16[3,272,512]{2,1,0:T(8,128)(2,1)S(1)} %collective-permute-done.38.refs_18_.da), channel_id=1, source_target_pairs={{0,8},{8,16},{16,24},{24,28},{28,20},{20,12},{12,4},{4,0},{1,9},{9... | collective-permute-start | bytes 2506760 | tf_op jit(solution)/shard_map/ppermute | solution.py:1468
  468.9 37.1 %collective-permute-start.41 = (bf16[3,272,512]{2,1,0:T(8,128)(2,1)S(1)}, bf16[3,272,512]{2,1,0:T(8,128)(2,1)S(1)}, u32[]{:S(2)}, u32[]{:S(2)}) collective-permute-start(bf16[3,272,512]{2,1,0:T(8,128)(2,1)S(1)} %collective-permute-done.39.refs_19_.db), channel_id=1, source_target_pairs={{8,0},{16,8},{24,16},{28,24},{20,28},{12,20},{4,12},{0,4},{9,1},{1... | collective-permute-start | bytes 2506760 | tf_op jit(solution)/shard_map/ppermute | solution.py:1468
  503.8 37.7 %collective-permute-start.36 = (bf16[3,256,512]{2,1,0:T(8,128)(2,1)}, bf16[3,256,512]{2,1,0:T(8,128)(2,1)S(1)}, u32[]{:S(2)}, u32[]{:S(2)}) collective-permute-start(bf16[3,256,512]{2,1,0:T(8,128)(2,1)} %get-tuple-element.299), channel_id=1, source_target_pairs={{0,8},{8,16},{16,24},{24,28},{28,20},{20,12},{12,4},{4,0},{1,9},{9... | collective-permute-start | bytes 2359304 | tf_op jit(solution)/shard_map/ppermute | solution.py:1493
  506.0 35.5 %collective-permute-start.37 = (bf16[3,256,512]{2,1,0:T(8,128)(2,1)}, bf16[3,256,512]{2,1,0:T(8,128)(2,1)S(1)}, u32[]{:S(2)}, u32[]{:S(2)}) collective-permute-start(bf16[3,256,512]{2,1,0:T(8,128)(2,1)} %get-tuple-element.300), channel_id=1, source_target_pairs={{8,0},{16,8},{24,16},{28,24},{20,28},{12,20},{4,12},{0,4},{9,1},{1... | collective-permute-start | bytes 2359304 | tf_op jit(solution)/shard_map/ppermute | solution.py:1493
  506.1 38.0 %collective-permute-start.46 = (bf16[3,272,512]{2,1,0:T(8,128)(2,1)S(1)}, bf16[3,272,512]{2,1,0:T(8,128)(2,1)}, u32[]{:S(2)}, u32[]{:S(2)}) collective-permute-start(bf16[3,272,512]{2,1,0:T(8,128)(2,1)S(1)} %collective-permute-done.40.da.refs_2_), channel_id=1, source_target_pairs={{0,8},{8,16},{16,24},{24,28},{28,20},{20,12},{12,4},{4,0},{1,9},{9... | collective-permute-start | bytes 2506760 | tf_op jit(solution)/shard_map/ppermute | solution.py:1468
  508.1 37.5 %collective-permute-start.47 = (bf16[3,272,512]{2,1,0:T(8,128)(2,1)S(1)}, bf16[3,272,512]{2,1,0:T(8,128)(2,1)}, u32[]{:S(2)}, u32[]{:S(2)}) collective-permute-start(bf16[3,272,512]{2,1,0:T(8,128)(2,1)S(1)} %collective-permute-done.41.db.refs_3_), channel_id=1, source_target_pairs={{8,0},{16,8},{24,16},{28,24},{20,28},{12,20},{4,12},{0,4},{9,1},{1... | collective-permute-start | bytes 2506760 | tf_op jit(solution)/shard_map/ppermute | solution.py:1468
  544.0 54.7 %collective-permute-start.50 = (bf16[3,272,512]{2,1,0:T(8,128)(2,1)}, bf16[3,272,512]{2,1,0:T(8,128)(2,1)}, u32[]{:S(2)}, u32[]{:S(2)}) collective-permute-start(bf16[3,272,512]{2,1,0:T(8,128)(2,1)} %collective-permute-done.46.da.refs_6_), channel_id=1, source_target_pairs={{0,8},{8,16},{16,24},{24,28},{28,20},{20,12},{12,4},{4,0},{1,9},{9... | collective-permute-start | bytes 2506760 | tf_op jit(solution)/shard_map/ppermute | solution.py:1468
  545.6 53.1 %collective-permute-start.51 = (bf16[3,272,512]{2,1,0:T(8,128)(2,1)}, bf16[3,272,512]{2,1,0:T(8,128)(2,1)}, u32[]{:S(2)}, u32[]{:S(2)}) collective-permute-start(bf16[3,272,512]{2,1,0:T(8,128)(2,1)} %collective-permute-done.47.db.refs_7_), channel_id=1, source_target_pairs={{8,0},{16,8},{24,16},{28,24},{20,28},{12,20},{4,12},{0,4},{9,1},{1... | collective-permute-start | bytes 2506760 | tf_op jit(solution)/shard_map/ppermute | solution.py:1468
  (107 other events, 1827.5 us)
Sparse Core Ops, SparseCore 0:
  9.6 25.4 all-gather.6
  37.2 34.2 all-gather.8
  73.1 22.5 all-gather.10
  97.2 43.4 all-gather.12
  142.0 43.3 all-gather.14
  186.9 43.4 all-gather.16
  374.1 54.1 reduce-scatter.4
  431.5 31.4 reduce-scatter.10
  465.6 54.8 reduce-scatter.6
  523.0 54.8 reduce-scatter.8

commit v5 on v4

--- a/solution.py
+++ b/solution.py
@@ -1424,13 +1424,14 @@
     x, memory = lax.optimization_barrier((x, memory))
     normed_low, qa, qb = project_query(x, gain_one, full_query, cosine, sine)
     meta, qa, qb = lax.optimization_barrier((meta, qa, qb))
+    memory = collect(meta, cache_keys, cache_values, count, cap, range(some, count), memory)
     queries = [(qa, qb)]
-    for _ in range(count - 1):
+    for step in range(1, count):
         qa, qb = lax.ppermute(qa, "ctx", onward), lax.ppermute(qb, "ctx", backward)
+        if step == 1:
+            qa, qb, memory = lax.optimization_barrier((qa, qb, memory))
         queries.append((qa, qb))
-    memory_keys, memory_values = collect(
-        meta, cache_keys, cache_values, count, cap, range(some, count), memory
-    )
+    memory_keys, memory_values = memory
     queries[1], normed_low = lax.optimization_barrier((queries[1], normed_low))
     keys, values, normed_turned = project_pairs(normed_low, pair_weights, cosine, sine)
     for step in range(1, count - 1):
@@ -1476,6 +1477,7 @@
         for part in (gradient_down, gradient_gate, gradient_up, gradient_output)
     ]
     early_width = sum(part.shape[1] for part in early)
+    slopes[-1], early[0] = lax.optimization_barrier((slopes[-1], early[0]))
     for step in range(1, count - 1):
         slopes[step], slopes[step + 1] = lax.optimization_barrier((slopes[step], slopes[step + 1]))
     middle_step = count // 2 + 1

time: 834 us -> 827 us (level)
  waiting for transfers between devices: 238 us -> 211 us
  Pallas kernels: 459 us -> 485 us
    ppermute x14, waiting for transfers between devices: 86.2 us -> 62.2 us  [body(): lax.ppermute(acc[0], 'ctx', onward)]
    pallas_call x8, Pallas kernels: 64.9 us -> 75.6 us  [attend(): pl.pallas_call(functools.partial(forward_kernel, step=step, count=count,...]
    pallas_call x8, Pallas kernels: 86.9 us -> 97.2 us  [unattend(): pl.pallas_call(functools.partial(backward_kernel, step=step, count=count,...]
  transfers between devices with their start and end apart: 66 -> 66, of which waited for: 28 -> 35; matrix products, arithmetic and copies ran while one was open for 2% -> 2% of each run, Pallas kernels for 33% -> 37%
where the time goes in v5:
time: 827 us; the launch traced here: 818 us
  Pallas kernels  485 us (59%)
  waiting for transfers between devices  211 us (26%)
  starting transfers between devices  58.7 us (7%)
  local copies, waits for them, and re-layouts  32.6 us (4%)
  between operations  15.7 us (2%)
  other arithmetic  10.1 us (1%)
    pallas_call x1, Pallas kernels, tail(): pl.pallas_call(functools.partial(tail_kernel, count=count, shards=shards,...  133 us
    pallas_call x8, Pallas kernels, unattend(): pl.pallas_call(functools.partial(backward_kernel, step=step, count=count,...  97.2 us
    pallas_call x8, Pallas kernels, attend(): pl.pallas_call(functools.partial(forward_kernel, step=step, count=count,...  75.6 us
    ppermute x7, waiting for transfers between devices, body(): lax.ppermute(qa, 'ctx', onward)  71 us
    ppermute x7, waiting for transfers between devices, body(): lax.ppermute(da, 'ctx', onward)  67.1 us
    ppermute x14, waiting for transfers between devices, body(): lax.ppermute(acc[0], 'ctx', onward)  62.2 us
    pallas_call x1, Pallas kernels, feed(): pl.pallas_call(feed_kernel, grid=(units // TILE,), in_specs=[whole, whole...  52.6 us
    pallas_call x2, Pallas kernels, key_gradients(): pl.pallas_call(functools.partial(key_kernel, steps=steps, micros=micros,...  37.2 us
  transfers between devices with their start and end apart: 66, of which 35 were waited for; matrix products, arithmetic and copies ran while one was open for 2% of the time, Pallas kernels for 37%

profile of v5, /device:TPU:0, one launch (start us, length us, event | category | flops | bytes accessed | tf_op | source)
XLA Modules:
  0.0 817.6 jit_solution(7931964154021797383)
XLA Ops:
  13.1 9.5 %share.1 = (s32[8,8,128]{2,1,0:T(8,128)S(1)}, f32[4,8,256]{2,1,0:T(8,128)S(1)}) custom-call(s32[8,128]{1,0:T(8,128)S(1)} %pad.10.indices, f32[8,256]{1,0:T(8,128)S(1)} %fusion.20.gains), custom_call_target="tpu_custom_call" | custom-call | bytes 20000000 | tf_op jit(solution)/shard_map/share/pallas_call | solution.py:150
  28.0 13.5 %collect.2 = (bf16[3,8,2,32,64,128]{5,4,3,2,1,0:T(8,128)(2,1)}, bf16[3,8,2,32,64,128]{5,4,3,2,1,0:T(8,128)(2,1)}) custom-call(s32[1601]{0:T(1024)} %concatenate.14.meta, bf16[6144,1024]{1,0:T(8,128)(2,1)} %bitcast.54, bf16[6144,1024]{1,0:T(8,128)(2,1)} %bitcast.56), custom_call_target="tpu_custom_call" | custom-call | bytes 33000000 | tf_op jit(solution)/shard_map/collect/pallas_call | solution.py:224
  50.5 21.2 %collect.3 = (bf16[3,8,2,32,64,128]{5,4,3,2,1,0:T(8,128)(2,1)}, bf16[3,8,2,32,64,128]{5,4,3,2,1,0:T(8,128)(2,1)}) custom-call(s32[1601]{0:T(1024)} %concatenate.14.meta, bf16[6144,1024]{1,0:T(8,128)(2,1)} %bitcast.55, bf16[6144,1024]{1,0:T(8,128)(2,1)} %bitcast.57, ...), custom_call_target="tpu_custom_call", output_to_operand_aliasing={{0}: (3, {}), {1}: (4, {})} | custom-call | bytes 55000000 | tf_op jit(solution)/shard_map/collect/pallas_call | solution.py:224
  73.9 14.0 %collective-permute-done.2.qa.refs_8_ = bf16[3,256,512]{2,1,0:T(8,128)(2,1)S(1)} collective-permute-done((bf16[3,256,512]{2,1,0:T(8,128)(2,1)S(1)}, bf16[3,256,512]{2,1,0:T(8,128)(2,1)S(1)}, u32[]{:S(2)}, u32[]{:S(2)}) %collective-permute-start.2) | collective-permute-done | bytes 786464 | tf_op jit(solution)/shard_map/ppermute | solution.py:1430
  113.6 9.9 %attend.9 = (bf16[3,256,512]{2,1,0:T(8,128)(2,1)S(1)}, bf16[3,256,512]{2,1,0:T(8,128)(2,1)S(1)}, f32[3,8,256]{2,1,0:T(8,128)S(1)}, f32[3,8,256]{2,1,0:T(8,128)S(1)}) custom-call(s32[1601]{0:T(1024)S(1)} %copy-done.42, bf16[3,256,512]{2,1,0:T(8,128)(2,1)S(1)} %collective-permute-done.2.qa.refs_8_, bf16[3,256,512]{2,1,0:T(8,128)(2,1)S(1)} %collective-permute-done.3.qb.refs_9_, ...), custom_call_target="tpu_custom_call" | custom-call | flops 6000000000 | bytes 10000000 | tf_op jit(solution)/shard_map/attend/pallas_call | solution.py:499
  133.7 14.3 %collective-permute-done.10.qa.refs_16_ = bf16[3,256,512]{2,1,0:T(8,128)(2,1)S(1)} collective-permute-done((bf16[3,256,512]{2,1,0:T(8,128)(2,1)}, bf16[3,256,512]{2,1,0:T(8,128)(2,1)S(1)}, u32[]{:S(2)}, u32[]{:S(2)}) %collective-permute-start.10) | collective-permute-done | bytes 786464 | tf_op jit(solution)/shard_map/ppermute | solution.py:1430
  150.2 9.9 %attend.10 = (bf16[3,256,512]{2,1,0:T(8,128)(2,1)S(1)}, bf16[3,256,512]{2,1,0:T(8,128)(2,1)S(1)}, f32[3,8,256]{2,1,0:T(8,128)S(1)}, f32[3,8,256]{2,1,0:T(8,128)S(1)}) custom-call(s32[1601]{0:T(1024)S(1)} %copy-done.42, bf16[3,256,512]{2,1,0:T(8,128)(2,1)} %collective-permute-done.6.qa.refs_12_, bf16[3,256,512]{2,1,0:T(8,128)(2,1)} %collective-permute-done.7.qb.refs_13_, ...), custom_call_target="tpu_custom_call" | custom-call | flops 6000000000 | bytes 10000000 | tf_op jit(solution)/shard_map/attend/pallas_call | solution.py:499
  168.4 14.3 %collective-permute-done.14.qa.refs_0_ = bf16[3,256,512]{2,1,0:T(8,128)(2,1)S(1)} collective-permute-done((bf16[3,256,512]{2,1,0:T(8,128)(2,1)S(1)}, bf16[3,256,512]{2,1,0:T(8,128)(2,1)S(1)}, u32[]{:S(2)}, u32[]{:S(2)}) %collective-permute-start.14) | collective-permute-done | bytes 786464 | tf_op jit(solution)/shard_map/ppermute | solution.py:1430
  184.8 9.5 %attend.11 = (bf16[3,256,512]{2,1,0:T(8,128)(2,1)S(1)}, bf16[3,256,512]{2,1,0:T(8,128)(2,1)S(1)}, f32[3,8,256]{2,1,0:T(8,128)S(1)}, f32[3,8,256]{2,1,0:T(8,128)S(1)}) custom-call(s32[1601]{0:T(1024)S(1)} %copy-done.42, bf16[3,256,512]{2,1,0:T(8,128)(2,1)S(1)} %collective-permute-done.10.qa.refs_16_, ...), custom_call_target="tpu_custom_call" | custom-call | flops 6000000000 | bytes 10000000 | tf_op jit(solution)/shard_map/attend/pallas_call | solution.py:499
  203.2 14.3 %collective-permute-done.18.qa.refs_4_ = bf16[3,256,512]{2,1,0:T(8,128)(2,1)S(1)} collective-permute-done((bf16[3,256,512]{2,1,0:T(8,128)(2,1)S(1)}, bf16[3,256,512]{2,1,0:T(8,128)(2,1)S(1)}, u32[]{:S(2)}, u32[]{:S(2)}) %collective-permute-start.18) | collective-permute-done | bytes 786464 | tf_op jit(solution)/shard_map/ppermute | solution.py:1430
  219.5 9.5 %attend.12 = (bf16[3,256,512]{2,1,0:T(8,128)(2,1)S(1)}, bf16[3,256,512]{2,1,0:T(8,128)(2,1)S(1)}, f32[3,8,256]{2,1,0:T(8,128)S(1)}, f32[3,8,256]{2,1,0:T(8,128)S(1)}) custom-call(s32[1601]{0:T(1024)S(1)} %copy-done.42, bf16[3,256,512]{2,1,0:T(8,128)(2,1)S(1)} %collective-permute-done.14.qa.refs_0_, ...), custom_call_target="tpu_custom_call" | custom-call | flops 6000000000 | bytes 10000000 | tf_op jit(solution)/shard_map/attend/pallas_call | solution.py:499
  237.9 14.3 %collective-permute-done.22.qa.refs_8_ = bf16[3,256,512]{2,1,0:T(8,128)(2,1)S(1)} collective-permute-done((bf16[3,256,512]{2,1,0:T(8,128)(2,1)S(1)}, bf16[3,256,512]{2,1,0:T(8,128)(2,1)S(1)}, u32[]{:S(2)}, u32[]{:S(2)}) %collective-permute-start.22) | collective-permute-done | bytes 786464 | tf_op jit(solution)/shard_map/ppermute | solution.py:1430
  252.3 9.3 %attend.13 = (bf16[3,256,512]{2,1,0:T(8,128)(2,1)S(1)}, bf16[3,256,512]{2,1,0:T(8,128)(2,1)S(1)}, f32[3,8,256]{2,1,0:T(8,128)S(1)}, f32[3,8,256]{2,1,0:T(8,128)S(1)}) custom-call(s32[1601]{0:T(1024)S(1)} %copy-done.42, bf16[3,256,512]{2,1,0:T(8,128)(2,1)S(1)} %collective-permute-done.18.qa.refs_4_, ...), custom_call_target="tpu_custom_call" | custom-call | flops 6000000000 | bytes 10000000 | tf_op jit(solution)/shard_map/attend/pallas_call | solution.py:499
  271.1 9.5 %attend.14 = (bf16[3,256,512]{2,1,0:T(8,128)(2,1)S(1)}, bf16[3,256,512]{2,1,0:T(8,128)(2,1)S(1)}, f32[3,8,256]{2,1,0:T(8,128)S(1)}, f32[3,8,256]{2,1,0:T(8,128)S(1)}) custom-call(s32[1601]{0:T(1024)S(1)} %copy-done.42, bf16[3,256,512]{2,1,0:T(8,128)(2,1)S(1)} %collective-permute-done.22.qa.refs_8_, ...), custom_call_target="tpu_custom_call" | custom-call | flops 6000000000 | bytes 10000000 | tf_op jit(solution)/shard_map/attend/pallas_call | solution.py:499
  319.8 52.6 %feed.1 = (bf16[3,256,1024]{2,1,0:T(8,128)(2,1)}, f32[3,256,1024]{2,1,0:T(8,128)}, bf16[1024,2816]{1,0:T(8,128)(2,1)}, bf16[1024,2816]{1,0:T(8,128)(2,1)}, bf16[2816,1024]{1,0:T(8,128)(2,1)}) custom-call(bf16[3,256,1024]{2,1,0:T(8,128)(2,1)} %get-tuple-element.287.normed, bf16[3,256,1024]{2,1,0:T(8,128)(2,1)} %bitcast.61, ...), custom_call_target="tpu_custom_call" | custom-call | flops 39862665216 | bytes 50000000 | tf_op jit(solution)/shard_map/feed/pallas_call | solution.py:638
  372.5 12.8 %prepare.1 = (bf16[3,272,512]{2,1,0:T(8,128)(2,1)}, bf16[3,272,512]{2,1,0:T(8,128)(2,1)}, f32[3,256,1024]{2,1,0:T(8,128)}, bf16[3,256,1024]{2,1,0:T(8,128)(2,1)}, f32[3,8,1024]{2,1,0:T(8,128)}) custom-call(f32[3,256,1024]{2,1,0:T(8,128)} %get-tuple-element.290.back_normed, f32[3,256,1024]{2,1,0:T(8,128)} %get-tuple-element.288.middle, ...), custom_call_target="tpu_custom_call" | custom-call | flops 1610612736 | bytes 22000000 | tf_op jit(solution)/shard_map/prepare/pallas_call | solution.py:695
  387.4 16.8 %collective-permute-done.28.da.refs_6_ = bf16[3,272,512]{2,1,0:T(8,128)(2,1)} collective-permute-done((bf16[3,272,512]{2,1,0:T(8,128)(2,1)}, bf16[3,272,512]{2,1,0:T(8,128)(2,1)}, u32[]{:S(2)}, u32[]{:S(2)}) %collective-permute-start.28) | collective-permute-done | bytes 835616 | tf_op jit(solution)/shard_map/ppermute | solution.py:1469
  412.2 16.9 %collective-permute-done.30.da.refs_10_ = bf16[3,272,512]{2,1,0:T(8,128)(2,1)S(1)} collective-permute-done((bf16[3,272,512]{2,1,0:T(8,128)(2,1)}, bf16[3,272,512]{2,1,0:T(8,128)(2,1)S(1)}, u32[]{:S(2)}, u32[]{:S(2)}) %collective-permute-start.30) | collective-permute-done | bytes 835616 | tf_op jit(solution)/shard_map/ppermute | solution.py:1469
  431.2 16.7 %collective-permute-done.34.refs_14_.da = bf16[3,272,512]{2,1,0:T(8,128)(2,1)S(1)} collective-permute-done((bf16[3,272,512]{2,1,0:T(8,128)(2,1)S(1)}, bf16[3,272,512]{2,1,0:T(8,128)(2,1)S(1)}, u32[]{:S(2)}, u32[]{:S(2)}) %collective-permute-start.34) | collective-permute-done | bytes 835616 | tf_op jit(solution)/shard_map/ppermute | solution.py:1469
  450.0 16.6 %collective-permute-done.38.refs_18_.da = bf16[3,272,512]{2,1,0:T(8,128)(2,1)S(1)} collective-permute-done((bf16[3,272,512]{2,1,0:T(8,128)(2,1)S(1)}, bf16[3,272,512]{2,1,0:T(8,128)(2,1)S(1)}, u32[]{:S(2)}, u32[]{:S(2)}) %collective-permute-start.38) | collective-permute-done | bytes 835616 | tf_op jit(solution)/shard_map/ppermute | solution.py:1469
  471.2 12.7 %unattend.8 = (bf16[3,256,512]{2,1,0:T(8,128)(2,1)S(1)}, bf16[3,256,512]{2,1,0:T(8,128)(2,1)S(1)}) custom-call(s32[1601]{0:T(1024)S(1)} %copy-done.42, bf16[3,256,512]{2,1,0:T(8,128)(2,1)S(1)} %copy-done.27, bf16[3,256,512]{2,1,0:T(8,128)(2,1)S(1)} %copy-done.32, bf16[3,272,512]{2,1,0:T(8,128)(2,1)} %collective-permute-done.28.da.refs_6_, ...), custom_call_target="tpu_custom_call" | custom-call | flops 8000000000 | bytes 12000000 | tf_op jit(solution)/shard_map/unattend/pallas_call | solution.py:797
  486.3 12.4 %unattend.9 = (bf16[3,256,512]{2,1,0:T(8,128)(2,1)S(1)}, bf16[3,256,512]{2,1,0:T(8,128)(2,1)S(1)}) custom-call(s32[1601]{0:T(1024)S(1)} %copy-done.42, bf16[3,256,512]{2,1,0:T(8,128)(2,1)S(1)} %copy-done.35, bf16[3,256,512]{2,1,0:T(8,128)(2,1)S(1)} %copy-done.37, bf16[3,272,512]{2,1,0:T(8,128)(2,1)S(1)} %collective-permute-done.30.da.refs_10_, ...), custom_call_target="tpu_custom_call" | custom-call | flops 8000000000 | bytes 12000000 | tf_op jit(solution)/shard_map/unattend/pallas_call | solution.py:797
  505.3 22.0 %key_gradients.2 = (f32[3,256,1024]{2,1,0:T(8,128)}, f32[3,256,1024]{2,1,0:T(8,128)}) custom-call(s32[1601]{0:T(1024)S(1)} %copy-done.42, bf16[3,256,1024]{2,1,0:T(8,128)(2,1)} %get-tuple-element.215.k, bf16[3,256,1024]{2,1,0:T(8,128)(2,1)} %get-tuple-element.216.v, bf16[3,256,512]{2,1,0:T(8,128)(2,1)S(1)} %copy-done.7, bf16[3,256,512]{2,1,0:T(8,128)(2,1)S(1)} %copy-done.10, ...), custom_call_target="tpu_custom_call" | custom-call | flops 15000000512 | bytes 20000000 | tf_op jit(solution)/shard_map/key_gradients/pallas_call | solution.py:903
  527.3 12.1 %unattend.10 = (bf16[3,256,512]{2,1,0:T(8,128)(2,1)S(1)}, bf16[3,256,512]{2,1,0:T(8,128)(2,1)S(1)}) custom-call(s32[1601]{0:T(1024)S(1)} %copy-done.42, bf16[3,256,512]{2,1,0:T(8,128)(2,1)} %collective-permute-done.6.qa.refs_12_, bf16[3,256,512]{2,1,0:T(8,128)(2,1)} %collective-permute-done.7.qb.refs_13_, ...), custom_call_target="tpu_custom_call" | custom-call | flops 8000000000 | bytes 12000000 | tf_op jit(solution)/shard_map/unattend/pallas_call | solution.py:797
  544.1 12.0 %unattend.11 = (bf16[3,256,512]{2,1,0:T(8,128)(2,1)S(1)}, bf16[3,256,512]{2,1,0:T(8,128)(2,1)S(1)}) custom-call(s32[1601]{0:T(1024)S(1)} %copy-done.42, bf16[3,256,512]{2,1,0:T(8,128)(2,1)S(1)} %copy-done.39, bf16[3,256,512]{2,1,0:T(8,128)(2,1)S(1)} %copy-done.41, bf16[3,272,512]{2,1,0:T(8,128)(2,1)S(1)} %copy-done.52, bf16[3,272,512]{2,1,0:T(8,128)(2,1)S(1)} %copy-done.54, ...), custom_call_target="tpu_custom_call" | custom-call | flops 8000000000 | bytes 12000000 | tf_op jit(solution)/shard_map/unattend/pallas_call | solution.py:797
  563.4 12.0 %unattend.12 = (bf16[3,256,512]{2,1,0:T(8,128)(2,1)S(1)}, bf16[3,256,512]{2,1,0:T(8,128)(2,1)S(1)}) custom-call(s32[1601]{0:T(1024)S(1)} %copy-done.42, bf16[3,256,512]{2,1,0:T(8,128)(2,1)S(1)} %copy-done.13, bf16[3,256,512]{2,1,0:T(8,128)(2,1)S(1)} %copy-done.16, bf16[3,272,512]{2,1,0:T(8,128)(2,1)S(1)} %collective-permute-done.40.da.refs_2_, ...), custom_call_target="tpu_custom_call" | custom-call | flops 8000000000 | bytes 12000000 | tf_op jit(solution)/shard_map/unattend/pallas_call | solution.py:797
  575.4 14.0 %collective-permute-done.44.refs_0_ = bf16[3,256,512]{2,1,0:T(8,128)(2,1)S(1)} collective-permute-done((bf16[3,256,512]{2,1,0:T(8,128)(2,1)S(1)}, bf16[3,256,512]{2,1,0:T(8,128)(2,1)S(1)}, u32[]{:S(2)}, u32[]{:S(2)}) %collective-permute-start.44) | collective-permute-done | bytes 786464 | tf_op jit(solution)/shard_map/ppermute | solution.py:1495
  599.7 12.4 %unattend.13 = (bf16[3,256,512]{2,1,0:T(8,128)(2,1)S(1)}, bf16[3,256,512]{2,1,0:T(8,128)(2,1)S(1)}) custom-call(s32[1601]{0:T(1024)S(1)} %copy-done.42, bf16[3,256,512]{2,1,0:T(8,128)(2,1)S(1)} %copy-done.19, bf16[3,256,512]{2,1,0:T(8,128)(2,1)S(1)} %copy-done.22, bf16[3,272,512]{2,1,0:T(8,128)(2,1)} %collective-permute-done.46.da.refs_6_, ...), custom_call_target="tpu_custom_call" | custom-call | flops 8000000000 | bytes 12000000 | tf_op jit(solution)/shard_map/unattend/pallas_call | solution.py:797
  616.9 10.2 %unattend.15 = (bf16[3,256,512]{2,1,0:T(8,128)(2,1)S(1)}, bf16[3,256,512]{2,1,0:T(8,128)(2,1)S(1)}) custom-call(s32[1601]{0:T(1024)S(1)} %copy-done.42, bf16[3,256,512]{2,1,0:T(8,128)(2,1)S(1)} %copy-done.8, bf16[3,256,512]{2,1,0:T(8,128)(2,1)S(1)} %copy-done.11, bf16[3,272,512]{2,1,0:T(8,128)(2,1)S(1)} %copy-done.44, bf16[3,272,512]{2,1,0:T(8,128)(2,1)S(1)} %copy-done.46, ...), custom_call_target="tpu_custom_call" | custom-call | flops 8000000000 | bytes 12000000 | tf_op jit(solution)/shard_map/unattend/pallas_call | solution.py:797
  627.1 13.3 %unattend.14 = (bf16[3,256,512]{2,1,0:T(8,128)(2,1)S(1)}, bf16[3,256,512]{2,1,0:T(8,128)(2,1)S(1)}) custom-call(s32[1601]{0:T(1024)S(1)} %copy-done.42, bf16[3,256,512]{2,1,0:T(8,128)(2,1)S(1)} %copy-done.25, bf16[3,256,512]{2,1,0:T(8,128)(2,1)S(1)} %copy-done.30, bf16[3,272,512]{2,1,0:T(8,128)(2,1)} %collective-permute-done.50.da.refs_10_, ...), custom_call_target="tpu_custom_call" | custom-call | flops 8000000000 | bytes 12000000 | tf_op jit(solution)/shard_map/unattend/pallas_call | solution.py:797
  643.3 15.1 %key_gradients.3 = (bf16[3,256,1024]{2,1,0:T(8,128)(2,1)S(1)}, bf16[3,256,1024]{2,1,0:T(8,128)(2,1)S(1)}) custom-call(s32[1601]{0:T(1024)S(1)} %copy-done.42, bf16[3,256,1024]{2,1,0:T(8,128)(2,1)} %get-tuple-element.215.k, bf16[3,256,1024]{2,1,0:T(8,128)(2,1)} %get-tuple-element.216.v, bf16[3,256,512]{2,1,0:T(8,128)(2,1)S(1)} %copy-done.14, ...), custom_call_target="tpu_custom_call" | custom-call | flops 8999999488 | bytes 20000000 | tf_op jit(solution)/shard_map/key_gradients/pallas_call | solution.py:903
  661.8 132.5 %tail.1 = (bf16[16,16,9472]{2,1,0:T(8,128)(2,1)}, bf16[16,16,3072]{2,1,0:T(8,128)(2,1)}, f32[8,1024]{1,0:T(8,128)}, f32[3,256,1024]{2,1,0:T(8,128)}) custom-call(bf16[3,256,512]{2,1,0:T(8,128)(2,1)} %copy-done.69, bf16[3,256,512]{2,1,0:T(8,128)(2,1)} %copy-done.70, bf16[3,256,512]{2,1,0:T(8,128)(2,1)} %copy-done.61, bf16[3,256,512]{2,1,0:T(8,128)(2,1)} %copy-done.62, ...), custom_call_target="tpu_custom_call" | custom-call | flops 12000000000 | bytes 300000000 | tf_op jit(solution)/shard_map/tail/pallas_call | solution.py:1294
  (345 shorter events, 215.7 us)
Async XLA Ops:
  7.2 35.2 %all-gather.7.cloned.1.call-start = ((), (), s32[]{:S(2)}) async-start(), calls=%async_computation.4 | async-start | bytes 2621440 | tf_op jit(solution)/shard_map/all_gather | solution.py:1388
  7.9 82.0 %all-gather.9.cloned.1.call-start = ((), (), s32[]{:S(2)}) async-start(), calls=%async_computation.5 | async-start | bytes 5242880 | tf_op jit(solution)/shard_map/all_gather | solution.py:1404
  10.3 293.9 %all-gather.11.cloned.1.call-start = ((), (), s32[]{:S(2)}) async-start(), calls=%async_computation.6 | async-start | bytes 2621440 | tf_op jit(solution)/shard_map/all_gather | solution.py:1388
  11.0 308.7 %all-gather.13.cloned.1.call-start = ((), (), s32[]{:S(2)}) async-start(), calls=%async_computation.7 | async-start | bytes 7208960 | tf_op jit(solution)/shard_map/all_gather | solution.py:1388
  11.6 308.2 %all-gather.15.cloned.1.call-start = ((), (), s32[]{:S(2)}) async-start(), calls=%async_computation.8 | async-start | bytes 7208960 | tf_op jit(solution)/shard_map/all_gather | solution.py:1388
  12.2 307.6 %all-gather.17.cloned.1.call-start = ((), (), s32[]{:S(2)}) async-start(), calls=%async_computation.9 | async-start | bytes 7208960 | tf_op jit(solution)/shard_map/all_gather | solution.py:1388
  12.7 580.6 %reduce-scatter.5.cloned.1.call-start = ((), (), s32[]{:S(2)}) async-start(), calls=%async_computation.10 | async-start | bytes 7208960 | tf_op jit(solution)/shard_map/reduce_scatter | solution.py:1464
  111.6 36.4 %collective-permute-start.10 = (bf16[3,256,512]{2,1,0:T(8,128)(2,1)}, bf16[3,256,512]{2,1,0:T(8,128)(2,1)S(1)}, u32[]{:S(2)}, u32[]{:S(2)}) collective-permute-start(bf16[3,256,512]{2,1,0:T(8,128)(2,1)} %collective-permute-done.6.qa.refs_12_), channel_id=1, source_target_pairs={{0,8},{8,16},{16,24},{24,28},{28,20},{20,12},{12,4},{4,0},{1,9},{9... | collective-permute-start | bytes 2359304 | tf_op jit(solution)/shard_map/ppermute | solution.py:1430
  111.6 36.4 %collective-permute-start.11 = (bf16[3,256,512]{2,1,0:T(8,128)(2,1)}, bf16[3,256,512]{2,1,0:T(8,128)(2,1)S(1)}, u32[]{:S(2)}, u32[]{:S(2)}) collective-permute-start(bf16[3,256,512]{2,1,0:T(8,128)(2,1)} %collective-permute-done.7.qb.refs_13_), channel_id=1, source_target_pairs={{8,0},{16,8},{24,16},{28,24},{20,28},{12,20},{4,12},{0,4},{9,1},{1... | collective-permute-start | bytes 2359304 | tf_op jit(solution)/shard_map/ppermute | solution.py:1430
  131.6 34.3 %collective-permute-start.8 = (bf16[3,272,512]{2,1,0:T(8,128)(2,1)S(1)}, bf16[3,272,512]{2,1,0:T(8,128)(2,1)S(1)}, u32[]{:S(2)}, u32[]{:S(2)}) collective-permute-start(bf16[3,272,512]{2,1,0:T(8,128)(2,1)S(1)} %get-tuple-element.233), channel_id=1, source_target_pairs={{0,8},{8,16},{16,24},{24,28},{28,20},{20,12},{12,4},{4,0},{1,9},{9... | collective-permute-start | bytes 2506760 | tf_op jit(solution)/shard_map/ppermute | solution.py:1447
  131.6 34.3 %collective-permute-start.9 = (bf16[3,272,512]{2,1,0:T(8,128)(2,1)S(1)}, bf16[3,272,512]{2,1,0:T(8,128)(2,1)S(1)}, u32[]{:S(2)}, u32[]{:S(2)}) collective-permute-start(bf16[3,272,512]{2,1,0:T(8,128)(2,1)S(1)} %get-tuple-element.234), channel_id=1, source_target_pairs={{8,0},{16,8},{24,16},{28,24},{20,28},{12,20},{4,12},{0,4},{9,1},{1... | collective-permute-start | bytes 2506760 | tf_op jit(solution)/shard_map/ppermute | solution.py:1447
  148.0 34.7 %collective-permute-start.14 = (bf16[3,256,512]{2,1,0:T(8,128)(2,1)S(1)}, bf16[3,256,512]{2,1,0:T(8,128)(2,1)S(1)}, u32[]{:S(2)}, u32[]{:S(2)}) collective-permute-start(bf16[3,256,512]{2,1,0:T(8,128)(2,1)S(1)} %collective-permute-done.10.qa.refs_16_), channel_id=1, source_target_pairs={{0,8},{8,16},{16,24},{24,28},{28,20},{20,12},{12,4},{4,0},{1,9},{9... | collective-permute-start | bytes 2359304 | tf_op jit(solution)/shard_map/ppermute | solution.py:1430
  148.0 34.8 %collective-permute-start.15 = (bf16[3,256,512]{2,1,0:T(8,128)(2,1)S(1)}, bf16[3,256,512]{2,1,0:T(8,128)(2,1)S(1)}, u32[]{:S(2)}, u32[]{:S(2)}) collective-permute-start(bf16[3,256,512]{2,1,0:T(8,128)(2,1)S(1)} %collective-permute-done.11.qb.refs_17_), channel_id=1, source_target_pairs={{8,0},{16,8},{24,16},{28,24},{20,28},{12,20},{4,12},{0,4},{9,1},{1... | collective-permute-start | bytes 2359304 | tf_op jit(solution)/shard_map/ppermute | solution.py:1430
  166.3 34.3 %collective-permute-start.12 = (bf16[3,272,512]{2,1,0:T(8,128)(2,1)S(1)}, bf16[3,272,512]{2,1,0:T(8,128)(2,1)S(1)}, u32[]{:S(2)}, u32[]{:S(2)}) collective-permute-start(bf16[3,272,512]{2,1,0:T(8,128)(2,1)S(1)} %get-tuple-element.243), channel_id=1, source_target_pairs={{0,8},{8,16},{16,24},{24,28},{28,20},{20,12},{12,4},{4,0},{1,9},{9... | collective-permute-start | bytes 2506760 | tf_op jit(solution)/shard_map/ppermute | solution.py:1447
  166.4 34.3 %collective-permute-start.13 = (bf16[3,272,512]{2,1,0:T(8,128)(2,1)S(1)}, bf16[3,272,512]{2,1,0:T(8,128)(2,1)S(1)}, u32[]{:S(2)}, u32[]{:S(2)}) collective-permute-start(bf16[3,272,512]{2,1,0:T(8,128)(2,1)S(1)} %get-tuple-element.244), channel_id=1, source_target_pairs={{8,0},{16,8},{24,16},{28,24},{20,28},{12,20},{4,12},{0,4},{9,1},{1... | collective-permute-start | bytes 2506760 | tf_op jit(solution)/shard_map/ppermute | solution.py:1447
  182.7 34.7 %collective-permute-start.18 = (bf16[3,256,512]{2,1,0:T(8,128)(2,1)S(1)}, bf16[3,256,512]{2,1,0:T(8,128)(2,1)S(1)}, u32[]{:S(2)}, u32[]{:S(2)}) collective-permute-start(bf16[3,256,512]{2,1,0:T(8,128)(2,1)S(1)} %collective-permute-done.14.qa.refs_0_), channel_id=1, source_target_pairs={{0,8},{8,16},{16,24},{24,28},{28,20},{20,12},{12,4},{4,0},{1,9},{9... | collective-permute-start | bytes 2359304 | tf_op jit(solution)/shard_map/ppermute | solution.py:1430
  182.7 34.8 %collective-permute-start.19 = (bf16[3,256,512]{2,1,0:T(8,128)(2,1)S(1)}, bf16[3,256,512]{2,1,0:T(8,128)(2,1)S(1)}, u32[]{:S(2)}, u32[]{:S(2)}) collective-permute-start(bf16[3,256,512]{2,1,0:T(8,128)(2,1)S(1)} %collective-permute-done.15.qb.refs_1_), channel_id=1, source_target_pairs={{8,0},{16,8},{24,16},{28,24},{20,28},{12,20},{4,12},{0,4},{9,1},{1... | collective-permute-start | bytes 2359304 | tf_op jit(solution)/shard_map/ppermute | solution.py:1430
  201.1 34.3 %collective-permute-start.16 = (bf16[3,272,512]{2,1,0:T(8,128)(2,1)S(1)}, bf16[3,272,512]{2,1,0:T(8,128)(2,1)S(1)}, u32[]{:S(2)}, u32[]{:S(2)}) collective-permute-start(bf16[3,272,512]{2,1,0:T(8,128)(2,1)S(1)} %get-tuple-element.253), channel_id=1, source_target_pairs={{0,8},{8,16},{16,24},{24,28},{28,20},{20,12},{12,4},{4,0},{1,9},{9... | collective-permute-start | bytes 2506760 | tf_op jit(solution)/shard_map/ppermute | solution.py:1447
  201.2 34.3 %collective-permute-start.17 = (bf16[3,272,512]{2,1,0:T(8,128)(2,1)S(1)}, bf16[3,272,512]{2,1,0:T(8,128)(2,1)S(1)}, u32[]{:S(2)}, u32[]{:S(2)}) collective-permute-start(bf16[3,272,512]{2,1,0:T(8,128)(2,1)S(1)} %get-tuple-element.254), channel_id=1, source_target_pairs={{8,0},{16,8},{24,16},{28,24},{20,28},{12,20},{4,12},{0,4},{9,1},{1... | collective-permute-start | bytes 2506760 | tf_op jit(solution)/shard_map/ppermute | solution.py:1447
  217.5 34.7 %collective-permute-start.22 = (bf16[3,256,512]{2,1,0:T(8,128)(2,1)S(1)}, bf16[3,256,512]{2,1,0:T(8,128)(2,1)S(1)}, u32[]{:S(2)}, u32[]{:S(2)}) collective-permute-start(bf16[3,256,512]{2,1,0:T(8,128)(2,1)S(1)} %collective-permute-done.18.qa.refs_4_), channel_id=1, source_target_pairs={{0,8},{8,16},{16,24},{24,28},{28,20},{20,12},{12,4},{4,0},{1,9},{9... | collective-permute-start | bytes 2359304 | tf_op jit(solution)/shard_map/ppermute | solution.py:1430
  217.5 34.8 %collective-permute-start.23 = (bf16[3,256,512]{2,1,0:T(8,128)(2,1)S(1)}, bf16[3,256,512]{2,1,0:T(8,128)(2,1)S(1)}, u32[]{:S(2)}, u32[]{:S(2)}) collective-permute-start(bf16[3,256,512]{2,1,0:T(8,128)(2,1)S(1)} %collective-permute-done.19.qb.refs_5_), channel_id=1, source_target_pairs={{8,0},{16,8},{24,16},{28,24},{20,28},{12,20},{4,12},{0,4},{9,1},{1... | collective-permute-start | bytes 2359304 | tf_op jit(solution)/shard_map/ppermute | solution.py:1430
  372.5 288.2 %reduce-scatter.11.cloned.1.call-start = ((), (), s32[]{:S(2)}) async-start(), calls=%async_computation.13 | async-start | bytes 2621440 | tf_op jit(solution)/shard_map/reduce_scatter | solution.py:1464
  408.8 251.8 %reduce-scatter.7.cloned.1.call-start = ((), (), s32[]{:S(2)}) async-start(), calls=%async_computation.11 | async-start | bytes 7208960 | tf_op jit(solution)/shard_map/reduce_scatter | solution.py:1464
  409.6 251.1 %reduce-scatter.9.cloned.1.call-start = ((), (), s32[]{:S(2)}) async-start(), calls=%async_computation.12 | async-start | bytes 7208960 | tf_op jit(solution)/shard_map/reduce_scatter | solution.py:1464
  466.6 36.5 %collective-permute-start.40 = (bf16[3,272,512]{2,1,0:T(8,128)(2,1)S(1)}, bf16[3,272,512]{2,1,0:T(8,128)(2,1)S(1)}, u32[]{:S(2)}, u32[]{:S(2)}) collective-permute-start(bf16[3,272,512]{2,1,0:T(8,128)(2,1)S(1)} %collective-permute-done.38.refs_18_.da), channel_id=1, source_target_pairs={{0,8},{8,16},{16,24},{24,28},{28,20},{20,12},{12,4},{4,0},{1,9},{9... | collective-permute-start | bytes 2506760 | tf_op jit(solution)/shard_map/ppermute | solution.py:1469
  467.0 36.2 %collective-permute-start.41 = (bf16[3,272,512]{2,1,0:T(8,128)(2,1)S(1)}, bf16[3,272,512]{2,1,0:T(8,128)(2,1)S(1)}, u32[]{:S(2)}, u32[]{:S(2)}) collective-permute-start(bf16[3,272,512]{2,1,0:T(8,128)(2,1)S(1)} %collective-permute-done.39.refs_19_.db), channel_id=1, source_target_pairs={{8,0},{16,8},{24,16},{28,24},{20,28},{12,20},{4,12},{0,4},{9,1},{1... | collective-permute-start | bytes 2506760 | tf_op jit(solution)/shard_map/ppermute | solution.py:1469
  500.9 38.6 %collective-permute-start.36 = (bf16[3,256,512]{2,1,0:T(8,128)(2,1)}, bf16[3,256,512]{2,1,0:T(8,128)(2,1)S(1)}, u32[]{:S(2)}, u32[]{:S(2)}) collective-permute-start(bf16[3,256,512]{2,1,0:T(8,128)(2,1)} %get-tuple-element.310), channel_id=1, source_target_pairs={{0,8},{8,16},{16,24},{24,28},{28,20},{20,12},{12,4},{4,0},{1,9},{9... | collective-permute-start | bytes 2359304 | tf_op jit(solution)/shard_map/ppermute | solution.py:1495
  502.7 36.8 %collective-permute-start.37 = (bf16[3,256,512]{2,1,0:T(8,128)(2,1)}, bf16[3,256,512]{2,1,0:T(8,128)(2,1)S(1)}, u32[]{:S(2)}, u32[]{:S(2)}) collective-permute-start(bf16[3,256,512]{2,1,0:T(8,128)(2,1)} %get-tuple-element.311), channel_id=1, source_target_pairs={{8,0},{16,8},{24,16},{28,24},{20,28},{12,20},{4,12},{0,4},{9,1},{1... | collective-permute-start | bytes 2359304 | tf_op jit(solution)/shard_map/ppermute | solution.py:1495
  503.1 38.9 %collective-permute-start.46 = (bf16[3,272,512]{2,1,0:T(8,128)(2,1)S(1)}, bf16[3,272,512]{2,1,0:T(8,128)(2,1)}, u32[]{:S(2)}, u32[]{:S(2)}) collective-permute-start(bf16[3,272,512]{2,1,0:T(8,128)(2,1)S(1)} %collective-permute-done.40.da.refs_2_), channel_id=1, source_target_pairs={{0,8},{8,16},{16,24},{24,28},{28,20},{20,12},{12,4},{4,0},{1,9},{9... | collective-permute-start | bytes 2506760 | tf_op jit(solution)/shard_map/ppermute | solution.py:1469
  504.8 37.3 %collective-permute-start.47 = (bf16[3,272,512]{2,1,0:T(8,128)(2,1)S(1)}, bf16[3,272,512]{2,1,0:T(8,128)(2,1)}, u32[]{:S(2)}, u32[]{:S(2)}) collective-permute-start(bf16[3,272,512]{2,1,0:T(8,128)(2,1)S(1)} %collective-permute-done.41.db.refs_3_), channel_id=1, source_target_pairs={{8,0},{16,8},{24,16},{28,24},{20,28},{12,20},{4,12},{0,4},{9,1},{1... | collective-permute-start | bytes 2506760 | tf_op jit(solution)/shard_map/ppermute | solution.py:1469
  542.0 55.4 %collective-permute-start.50 = (bf16[3,272,512]{2,1,0:T(8,128)(2,1)}, bf16[3,272,512]{2,1,0:T(8,128)(2,1)}, u32[]{:S(2)}, u32[]{:S(2)}) collective-permute-start(bf16[3,272,512]{2,1,0:T(8,128)(2,1)} %collective-permute-done.46.da.refs_6_), channel_id=1, source_target_pairs={{0,8},{8,16},{16,24},{24,28},{28,20},{20,12},{12,4},{4,0},{1,9},{9... | collective-permute-start | bytes 2506760 | tf_op jit(solution)/shard_map/ppermute | solution.py:1469
  542.1 55.3 %collective-permute-start.51 = (bf16[3,272,512]{2,1,0:T(8,128)(2,1)}, bf16[3,272,512]{2,1,0:T(8,128)(2,1)}, u32[]{:S(2)}, u32[]{:S(2)}) collective-permute-start(bf16[3,272,512]{2,1,0:T(8,128)(2,1)} %collective-permute-done.47.db.refs_7_), channel_id=1, source_target_pairs={{8,0},{16,8},{24,16},{28,24},{20,28},{12,20},{4,12},{0,4},{9,1},{1... | collective-permute-start | bytes 2506760 | tf_op jit(solution)/shard_map/ppermute | solution.py:1469
  (107 other events, 1780.6 us)
Sparse Core Ops, SparseCore 0:
  9.6 25.4 all-gather.6
  37.2 34.2 all-gather.8
  73.1 22.5 all-gather.10
  97.2 43.4 all-gather.12
  142.0 43.3 all-gather.14
  186.9 43.4 all-gather.16
  372.6 52.1 reduce-scatter.4
  428.0 31.3 reduce-scatter.10
  462.0 54.8 reduce-scatter.6
  519.5 54.8 reduce-scatter.8

commit v6 on v5

--- a/solution.py
+++ b/solution.py
@@ -1430,11 +1430,12 @@
         qa, qb = lax.ppermute(qa, "ctx", onward), lax.ppermute(qb, "ctx", backward)
         if step == 1:
             qa, qb, memory = lax.optimization_barrier((qa, qb, memory))
+            keys, values, normed_turned = project_pairs(normed_low, pair_weights, cosine, sine)
+        if step == 2:
+            qa, qb, keys, values = lax.optimization_barrier((qa, qb, keys, values))
         queries.append((qa, qb))
     memory_keys, memory_values = memory
-    queries[1], normed_low = lax.optimization_barrier((queries[1], normed_low))
-    keys, values, normed_turned = project_pairs(normed_low, pair_weights, cosine, sine)
-    for step in range(1, count - 1):
+    for step in range(2, count - 1):
         queries[step], queries[step + 1] = lax.optimization_barrier((queries[step], queries[step + 1]))
 
 

time: 827 us -> 816 us (0.987)
  Pallas kernels: 485 us -> 441 us
  waiting for transfers between devices: 211 us -> 240 us
    ppermute x14, waiting for transfers between devices: 62.2 us -> 87.5 us  [body(): lax.ppermute(acc[0], 'ctx', onward)]
    pallas_call x8, Pallas kernels: 97.2 us -> 77.6 us  [unattend(): pl.pallas_call(functools.partial(backward_kernel, step=step, count=count,...]
    pallas_call x8, Pallas kernels: 75.6 us -> 56.1 us  [attend(): pl.pallas_call(functools.partial(forward_kernel, step=step, count=count,...]
    ppermute x14, starting transfers between devices: 22.8 us -> 11.1 us  [body(): lax.ppermute(acc[1], 'ctx', backward)]
    ppermute x14, starting transfers between devices: 7.45 us -> 18.9 us  [body(): lax.ppermute(acc[0], 'ctx', onward)]
    ppermute x7, starting transfers between devices: 0.19 us -> 9.09 us  [body(): lax.ppermute(qa, 'ctx', onward)]
    ppermute x7, starting transfers between devices: 14.2 us -> 5.33 us  [body(): lax.ppermute(qb, 'ctx', backward)]
    pallas_call x2, Pallas kernels: 34.7 us -> 25.9 us  [collect(): pl.pallas_call(functools.partial(collect_kernel, micros=micros, count=cou...]
  transfers between devices with their start and end apart: 66 -> 66, of which waited for: 35 -> 37; matrix products, arithmetic and copies ran while one was open for 2% -> 2% of each run, Pallas kernels for 37% -> 31%
where the time goes in v6:
time: 816 us; the launch traced here: 803 us
  Pallas kernels  441 us (54%)
  waiting for transfers between devices  240 us (29%)
  starting transfers between devices  59.3 us (7%)
  local copies, waits for them, and re-layouts  32.5 us (4%)
  between operations  15.7 us (2%)
  other arithmetic  10.1 us (1%)
    pallas_call x1, Pallas kernels, tail(): pl.pallas_call(functools.partial(tail_kernel, count=count, shards=shards,...  138 us
    ppermute x14, waiting for transfers between devices, body(): lax.ppermute(acc[0], 'ctx', onward)  87.5 us
    pallas_call x8, Pallas kernels, unattend(): pl.pallas_call(functools.partial(backward_kernel, step=step, count=count,...  77.6 us
    ppermute x7, waiting for transfers between devices, body(): lax.ppermute(qa, 'ctx', onward)  71.5 us
    ppermute x7, waiting for transfers between devices, body(): lax.ppermute(da, 'ctx', onward)  64.2 us
    pallas_call x8, Pallas kernels, attend(): pl.pallas_call(functools.partial(forward_kernel, step=step, count=count,...  56.1 us
    pallas_call x1, Pallas kernels, feed(): pl.pallas_call(feed_kernel, grid=(units // TILE,), in_specs=[whole, whole...  52.7 us
    pallas_call x2, Pallas kernels, key_gradients(): pl.pallas_call(functools.partial(key_kernel, steps=steps, micros=micros,...  37.1 us
  transfers between devices with their start and end apart: 66, of which 37 were waited for; matrix products, arithmetic and copies ran while one was open for 2% of the time, Pallas kernels for 31%

profile of v6, /device:TPU:0, one launch (start us, length us, event | category | flops | bytes accessed | tf_op | source)
XLA Modules:
  0.0 803.1 jit_solution(14959743201600273515)
XLA Ops:
  13.1 9.5 %share.1 = (s32[8,8,128]{2,1,0:T(8,128)S(1)}, f32[4,8,256]{2,1,0:T(8,128)S(1)}) custom-call(s32[8,128]{1,0:T(8,128)S(1)} %pad.10.indices, f32[8,256]{1,0:T(8,128)S(1)} %fusion.20.gains), custom_call_target="tpu_custom_call" | custom-call | bytes 20000000 | tf_op jit(solution)/shard_map/share/pallas_call | solution.py:150
  26.6 10.3 %collect.2 = (bf16[3,8,2,32,64,128]{5,4,3,2,1,0:T(8,128)(2,1)}, bf16[3,8,2,32,64,128]{5,4,3,2,1,0:T(8,128)(2,1)}) custom-call(s32[1601]{0:T(1024)} %concatenate.14.meta, bf16[6144,1024]{1,0:T(8,128)(2,1)} %bitcast.54, bf16[6144,1024]{1,0:T(8,128)(2,1)} %bitcast.56), custom_call_target="tpu_custom_call" | custom-call | bytes 33000000 | tf_op jit(solution)/shard_map/collect/pallas_call | solution.py:224
  47.0 15.5 %collect.3 = (bf16[3,8,2,32,64,128]{5,4,3,2,1,0:T(8,128)(2,1)}, bf16[3,8,2,32,64,128]{5,4,3,2,1,0:T(8,128)(2,1)}) custom-call(s32[1601]{0:T(1024)} %concatenate.14.meta, bf16[6144,1024]{1,0:T(8,128)(2,1)} %bitcast.55, bf16[6144,1024]{1,0:T(8,128)(2,1)} %bitcast.57, ...), custom_call_target="tpu_custom_call", output_to_operand_aliasing={{0}: (3, {}), {1}: (4, {})} | custom-call | bytes 55000000 | tf_op jit(solution)/shard_map/collect/pallas_call | solution.py:224
  115.1 8.6 %collective-permute-done.4.refs_0_ = bf16[3,272,512]{2,1,0:T(8,128)(2,1)S(1)} collective-permute-done((bf16[3,272,512]{2,1,0:T(8,128)(2,1)S(1)}, bf16[3,272,512]{2,1,0:T(8,128)(2,1)S(1)}, u32[]{:S(2)}, u32[]{:S(2)}) %collective-permute-start.4) | collective-permute-done | bytes 835616 | tf_op jit(solution)/shard_map/ppermute | solution.py:1448
  126.6 14.0 %collective-permute-done.10.qa.refs_16_ = bf16[3,256,512]{2,1,0:T(8,128)(2,1)S(1)} collective-permute-done((bf16[3,256,512]{2,1,0:T(8,128)(2,1)S(1)}, bf16[3,256,512]{2,1,0:T(8,128)(2,1)S(1)}, u32[]{:S(2)}, u32[]{:S(2)}) %collective-permute-start.10) | collective-permute-done | bytes 786464 | tf_op jit(solution)/shard_map/ppermute | solution.py:1430
  143.1 7.9 attend.10
  161.3 14.0 %collective-permute-done.14.qa.refs_0_ = bf16[3,256,512]{2,1,0:T(8,128)(2,1)S(1)} collective-permute-done((bf16[3,256,512]{2,1,0:T(8,128)(2,1)S(1)}, bf16[3,256,512]{2,1,0:T(8,128)(2,1)S(1)}, u32[]{:S(2)}, u32[]{:S(2)}) %collective-permute-start.14) | collective-permute-done | bytes 786464 | tf_op jit(solution)/shard_map/ppermute | solution.py:1430
  184.2 9.0 %collective-permute-done.12.refs_0_ = bf16[3,272,512]{2,1,0:T(8,128)(2,1)S(1)} collective-permute-done((bf16[3,272,512]{2,1,0:T(8,128)(2,1)S(1)}, bf16[3,272,512]{2,1,0:T(8,128)(2,1)S(1)}, u32[]{:S(2)}, u32[]{:S(2)}) %collective-permute-start.12) | collective-permute-done | bytes 835616 | tf_op jit(solution)/shard_map/ppermute | solution.py:1448
  196.1 14.0 %collective-permute-done.18.qa.refs_4_ = bf16[3,256,512]{2,1,0:T(8,128)(2,1)S(1)} collective-permute-done((bf16[3,256,512]{2,1,0:T(8,128)(2,1)S(1)}, bf16[3,256,512]{2,1,0:T(8,128)(2,1)S(1)}, u32[]{:S(2)}, u32[]{:S(2)}) %collective-permute-start.18) | collective-permute-done | bytes 786464 | tf_op jit(solution)/shard_map/ppermute | solution.py:1430
  220.2 7.8 collective-permute-done.16.refs_0_
  230.8 14.0 %collective-permute-done.22.qa.refs_8_ = bf16[3,256,512]{2,1,0:T(8,128)(2,1)S(1)} collective-permute-done((bf16[3,256,512]{2,1,0:T(8,128)(2,1)S(1)}, bf16[3,256,512]{2,1,0:T(8,128)(2,1)S(1)}, u32[]{:S(2)}, u32[]{:S(2)}) %collective-permute-start.22) | collective-permute-done | bytes 786464 | tf_op jit(solution)/shard_map/ppermute | solution.py:1430
  251.8 9.6 %collective-permute-done.20.refs_0_ = bf16[3,272,512]{2,1,0:T(8,128)(2,1)S(1)} collective-permute-done((bf16[3,272,512]{2,1,0:T(8,128)(2,1)S(1)}, bf16[3,272,512]{2,1,0:T(8,128)(2,1)S(1)}, u32[]{:S(2)}, u32[]{:S(2)}) %collective-permute-start.20) | collective-permute-done | bytes 835616 | tf_op jit(solution)/shard_map/ppermute | solution.py:1448
  270.5 10.6 %collective-permute-done.24.refs_0_ = bf16[3,272,512]{2,1,0:T(8,128)(2,1)S(1)} collective-permute-done((bf16[3,272,512]{2,1,0:T(8,128)(2,1)S(1)}, bf16[3,272,512]{2,1,0:T(8,128)(2,1)S(1)}, u32[]{:S(2)}, u32[]{:S(2)}) %collective-permute-start.24) | collective-permute-done | bytes 835616 | tf_op jit(solution)/shard_map/ppermute | solution.py:1448
  301.1 8.9 %finish.1 = (f32[3,256,1024]{2,1,0:T(8,128)}, bf16[3,256,1024]{2,1,0:T(8,128)(2,1)}, f32[3,2,8,256]{3,2,1,0:T(8,128)}, f32[3,256,1024]{2,1,0:T(8,128)}, bf16[3,256,1024]{2,1,0:T(8,128)(2,1)}) custom-call(bf16[3,272,512]{2,1,0:T(8,128)(2,1)} %collective-permute-done.26.acc_a, bf16[3,272,512]{2,1,0:T(8,128)(2,1)} %collective-permute-done.27.acc_b, ...), custom_call_target="tpu_custom_call" | custom-call | flops 1610612736 | bytes 16000000 | tf_op jit(solution)/shard_map/finish/pallas_call | solution.py:576
  310.1 52.7 %feed.1 = (bf16[3,256,1024]{2,1,0:T(8,128)(2,1)}, f32[3,256,1024]{2,1,0:T(8,128)}, bf16[1024,2816]{1,0:T(8,128)(2,1)}, bf16[1024,2816]{1,0:T(8,128)(2,1)}, bf16[2816,1024]{1,0:T(8,128)(2,1)}) custom-call(bf16[3,256,1024]{2,1,0:T(8,128)(2,1)} %get-tuple-element.281.normed, bf16[3,256,1024]{2,1,0:T(8,128)(2,1)} %bitcast.61, ...), custom_call_target="tpu_custom_call" | custom-call | flops 39862665216 | bytes 50000000 | tf_op jit(solution)/shard_map/feed/pallas_call | solution.py:638
  362.8 12.7 %prepare.1 = (bf16[3,272,512]{2,1,0:T(8,128)(2,1)}, bf16[3,272,512]{2,1,0:T(8,128)(2,1)}, f32[3,256,1024]{2,1,0:T(8,128)}, bf16[3,256,1024]{2,1,0:T(8,128)(2,1)}, f32[3,8,1024]{2,1,0:T(8,128)}) custom-call(f32[3,256,1024]{2,1,0:T(8,128)} %get-tuple-element.284.back_normed, f32[3,256,1024]{2,1,0:T(8,128)} %get-tuple-element.282.middle, ...), custom_call_target="tpu_custom_call" | custom-call | flops 1610612736 | bytes 22000000 | tf_op jit(solution)/shard_map/prepare/pallas_call | solution.py:695
  377.6 14.0 %collective-permute-done.28.da.refs_6_ = bf16[3,272,512]{2,1,0:T(8,128)(2,1)} collective-permute-done((bf16[3,272,512]{2,1,0:T(8,128)(2,1)}, bf16[3,272,512]{2,1,0:T(8,128)(2,1)}, u32[]{:S(2)}, u32[]{:S(2)}) %collective-permute-start.28) | collective-permute-done | bytes 835616 | tf_op jit(solution)/shard_map/ppermute | solution.py:1470
  399.6 16.8 %collective-permute-done.30.da.refs_10_ = bf16[3,272,512]{2,1,0:T(8,128)(2,1)S(1)} collective-permute-done((bf16[3,272,512]{2,1,0:T(8,128)(2,1)}, bf16[3,272,512]{2,1,0:T(8,128)(2,1)S(1)}, u32[]{:S(2)}, u32[]{:S(2)}) %collective-permute-start.30) | collective-permute-done | bytes 835616 | tf_op jit(solution)/shard_map/ppermute | solution.py:1470
  418.5 16.7 %collective-permute-done.34.refs_14_.da = bf16[3,272,512]{2,1,0:T(8,128)(2,1)S(1)} collective-permute-done((bf16[3,272,512]{2,1,0:T(8,128)(2,1)S(1)}, bf16[3,272,512]{2,1,0:T(8,128)(2,1)S(1)}, u32[]{:S(2)}, u32[]{:S(2)}) %collective-permute-start.34) | collective-permute-done | bytes 835616 | tf_op jit(solution)/shard_map/ppermute | solution.py:1470
  437.3 16.6 %collective-permute-done.38.refs_18_.da = bf16[3,272,512]{2,1,0:T(8,128)(2,1)S(1)} collective-permute-done((bf16[3,272,512]{2,1,0:T(8,128)(2,1)S(1)}, bf16[3,272,512]{2,1,0:T(8,128)(2,1)S(1)}, u32[]{:S(2)}, u32[]{:S(2)}) %collective-permute-start.38) | collective-permute-done | bytes 835616 | tf_op jit(solution)/shard_map/ppermute | solution.py:1470
  458.4 10.4 %unattend.8 = (bf16[3,256,512]{2,1,0:T(8,128)(2,1)S(1)}, bf16[3,256,512]{2,1,0:T(8,128)(2,1)S(1)}) custom-call(s32[1601]{0:T(1024)S(1)} %copy-done.46, bf16[3,256,512]{2,1,0:T(8,128)(2,1)S(1)} %copy-done.27, bf16[3,256,512]{2,1,0:T(8,128)(2,1)S(1)} %copy-done.32, bf16[3,272,512]{2,1,0:T(8,128)(2,1)} %collective-permute-done.28.da.refs_6_, ...), custom_call_target="tpu_custom_call" | custom-call | flops 8000000000 | bytes 12000000 | tf_op jit(solution)/shard_map/unattend/pallas_call | solution.py:797
  471.1 9.3 %unattend.9 = (bf16[3,256,512]{2,1,0:T(8,128)(2,1)S(1)}, bf16[3,256,512]{2,1,0:T(8,128)(2,1)S(1)}) custom-call(s32[1601]{0:T(1024)S(1)} %copy-done.46, bf16[3,256,512]{2,1,0:T(8,128)(2,1)S(1)} %copy-done.35, bf16[3,256,512]{2,1,0:T(8,128)(2,1)S(1)} %copy-done.37, bf16[3,272,512]{2,1,0:T(8,128)(2,1)S(1)} %collective-permute-done.30.da.refs_10_, ...), custom_call_target="tpu_custom_call" | custom-call | flops 8000000000 | bytes 12000000 | tf_op jit(solution)/shard_map/unattend/pallas_call | solution.py:797
  493.9 22.0 %key_gradients.2 = (f32[3,256,1024]{2,1,0:T(8,128)}, f32[3,256,1024]{2,1,0:T(8,128)}) custom-call(s32[1601]{0:T(1024)S(1)} %copy-done.46, bf16[3,256,1024]{2,1,0:T(8,128)(2,1)} %get-tuple-element.209.k, bf16[3,256,1024]{2,1,0:T(8,128)(2,1)} %get-tuple-element.210.v, bf16[3,256,512]{2,1,0:T(8,128)(2,1)S(1)} %copy-done.7, bf16[3,256,512]{2,1,0:T(8,128)(2,1)S(1)} %copy-done.10, ...), custom_call_target="tpu_custom_call" | custom-call | flops 15000000512 | bytes 20000000 | tf_op jit(solution)/shard_map/key_gradients/pallas_call | solution.py:903
  515.9 10.2 %unattend.10 = (bf16[3,256,512]{2,1,0:T(8,128)(2,1)S(1)}, bf16[3,256,512]{2,1,0:T(8,128)(2,1)S(1)}) custom-call(s32[1601]{0:T(1024)S(1)} %copy-done.46, bf16[3,256,512]{2,1,0:T(8,128)(2,1)S(1)} %copy-done.43, bf16[3,256,512]{2,1,0:T(8,128)(2,1)S(1)} %copy-done.45, bf16[3,272,512]{2,1,0:T(8,128)(2,1)S(1)} %collective-permute-done.34.refs_14_.da, ...), custom_call_target="tpu_custom_call" | custom-call | flops 8000000000 | bytes 12000000 | tf_op jit(solution)/shard_map/unattend/pallas_call | solution.py:797
  530.7 8.9 %unattend.11 = (bf16[3,256,512]{2,1,0:T(8,128)(2,1)S(1)}, bf16[3,256,512]{2,1,0:T(8,128)(2,1)S(1)}) custom-call(s32[1601]{0:T(1024)S(1)} %copy-done.46, bf16[3,256,512]{2,1,0:T(8,128)(2,1)S(1)} %copy-done.39, bf16[3,256,512]{2,1,0:T(8,128)(2,1)S(1)} %copy-done.41, bf16[3,272,512]{2,1,0:T(8,128)(2,1)S(1)} %copy-done.56, bf16[3,272,512]{2,1,0:T(8,128)(2,1)S(1)} %copy-done.58, ...), custom_call_target="tpu_custom_call" | custom-call | flops 8000000000 | bytes 12000000 | tf_op jit(solution)/shard_map/unattend/pallas_call | solution.py:797
  550.5 10.2 %unattend.12 = (bf16[3,256,512]{2,1,0:T(8,128)(2,1)S(1)}, bf16[3,256,512]{2,1,0:T(8,128)(2,1)S(1)}) custom-call(s32[1601]{0:T(1024)S(1)} %copy-done.46, bf16[3,256,512]{2,1,0:T(8,128)(2,1)S(1)} %copy-done.13, bf16[3,256,512]{2,1,0:T(8,128)(2,1)S(1)} %copy-done.16, bf16[3,272,512]{2,1,0:T(8,128)(2,1)S(1)} %collective-permute-done.40.da.refs_2_, ...), custom_call_target="tpu_custom_call" | custom-call | flops 8000000000 | bytes 12000000 | tf_op jit(solution)/shard_map/unattend/pallas_call | solution.py:797
  560.7 14.2 %collective-permute-done.44.refs_0_ = bf16[3,256,512]{2,1,0:T(8,128)(2,1)S(1)} collective-permute-done((bf16[3,256,512]{2,1,0:T(8,128)(2,1)S(1)}, bf16[3,256,512]{2,1,0:T(8,128)(2,1)S(1)}, u32[]{:S(2)}, u32[]{:S(2)}) %collective-permute-start.44) | collective-permute-done | bytes 786464 | tf_op jit(solution)/shard_map/ppermute | solution.py:1496
  586.7 9.9 %unattend.13 = (bf16[3,256,512]{2,1,0:T(8,128)(2,1)S(1)}, bf16[3,256,512]{2,1,0:T(8,128)(2,1)S(1)}) custom-call(s32[1601]{0:T(1024)S(1)} %copy-done.46, bf16[3,256,512]{2,1,0:T(8,128)(2,1)S(1)} %copy-done.19, bf16[3,256,512]{2,1,0:T(8,128)(2,1)S(1)} %copy-done.22, bf16[3,272,512]{2,1,0:T(8,128)(2,1)} %collective-permute-done.46.da.refs_6_, ...), custom_call_target="tpu_custom_call" | custom-call | flops 8000000000 | bytes 12000000 | tf_op jit(solution)/shard_map/unattend/pallas_call | solution.py:797
  601.4 8.4 %unattend.15 = (bf16[3,256,512]{2,1,0:T(8,128)(2,1)S(1)}, bf16[3,256,512]{2,1,0:T(8,128)(2,1)S(1)}) custom-call(s32[1601]{0:T(1024)S(1)} %copy-done.46, bf16[3,256,512]{2,1,0:T(8,128)(2,1)S(1)} %copy-done.8, bf16[3,256,512]{2,1,0:T(8,128)(2,1)S(1)} %copy-done.11, bf16[3,272,512]{2,1,0:T(8,128)(2,1)S(1)} %copy-done.48, bf16[3,272,512]{2,1,0:T(8,128)(2,1)S(1)} %copy-done.50, ...), custom_call_target="tpu_custom_call" | custom-call | flops 8000000000 | bytes 12000000 | tf_op jit(solution)/shard_map/unattend/pallas_call | solution.py:797
  609.9 10.3 %unattend.14 = (bf16[3,256,512]{2,1,0:T(8,128)(2,1)S(1)}, bf16[3,256,512]{2,1,0:T(8,128)(2,1)S(1)}) custom-call(s32[1601]{0:T(1024)S(1)} %copy-done.46, bf16[3,256,512]{2,1,0:T(8,128)(2,1)S(1)} %copy-done.25, bf16[3,256,512]{2,1,0:T(8,128)(2,1)S(1)} %copy-done.30, bf16[3,272,512]{2,1,0:T(8,128)(2,1)} %collective-permute-done.50.da.refs_10_, ...), custom_call_target="tpu_custom_call" | custom-call | flops 8000000000 | bytes 12000000 | tf_op jit(solution)/shard_map/unattend/pallas_call | solution.py:797
  623.0 15.1 %key_gradients.3 = (bf16[3,256,1024]{2,1,0:T(8,128)(2,1)S(1)}, bf16[3,256,1024]{2,1,0:T(8,128)(2,1)S(1)}) custom-call(s32[1601]{0:T(1024)S(1)} %copy-done.46, bf16[3,256,1024]{2,1,0:T(8,128)(2,1)} %get-tuple-element.209.k, bf16[3,256,1024]{2,1,0:T(8,128)(2,1)} %get-tuple-element.210.v, bf16[3,256,512]{2,1,0:T(8,128)(2,1)S(1)} %copy-done.14, ...), custom_call_target="tpu_custom_call" | custom-call | flops 8999999488 | bytes 20000000 | tf_op jit(solution)/shard_map/key_gradients/pallas_call | solution.py:903
  641.5 138.4 %tail.1 = (bf16[16,16,9472]{2,1,0:T(8,128)(2,1)}, bf16[16,16,3072]{2,1,0:T(8,128)(2,1)}, f32[8,1024]{1,0:T(8,128)}, f32[3,256,1024]{2,1,0:T(8,128)}) custom-call(bf16[3,256,512]{2,1,0:T(8,128)(2,1)} %copy-done.73, bf16[3,256,512]{2,1,0:T(8,128)(2,1)} %copy-done.74, bf16[3,256,512]{2,1,0:T(8,128)(2,1)} %copy-done.65, bf16[3,256,512]{2,1,0:T(8,128)(2,1)} %copy-done.66, ...), custom_call_target="tpu_custom_call" | custom-call | flops 12000000000 | bytes 300000000 | tf_op jit(solution)/shard_map/tail/pallas_call | solution.py:1294
  (353 shorter events, 236.8 us)
Async XLA Ops:
  7.9 63.6 %all-gather.9.cloned.1.call-start = ((), (), s32[]{:S(2)}) async-start(), calls=%async_computation.5 | async-start | bytes 5242880 | tf_op jit(solution)/shard_map/all_gather | solution.py:1404
  10.3 284.1 %all-gather.11.cloned.1.call-start = ((), (), s32[]{:S(2)}) async-start(), calls=%async_computation.6 | async-start | bytes 2621440 | tf_op jit(solution)/shard_map/all_gather | solution.py:1388
  11.0 299.0 %all-gather.13.cloned.1.call-start = ((), (), s32[]{:S(2)}) async-start(), calls=%async_computation.7 | async-start | bytes 7208960 | tf_op jit(solution)/shard_map/all_gather | solution.py:1388
  11.6 298.5 %all-gather.15.cloned.1.call-start = ((), (), s32[]{:S(2)}) async-start(), calls=%async_computation.8 | async-start | bytes 7208960 | tf_op jit(solution)/shard_map/all_gather | solution.py:1388
  12.2 297.9 %all-gather.17.cloned.1.call-start = ((), (), s32[]{:S(2)}) async-start(), calls=%async_computation.9 | async-start | bytes 7208960 | tf_op jit(solution)/shard_map/all_gather | solution.py:1388
  12.7 567.7 %reduce-scatter.5.cloned.1.call-start = ((), (), s32[]{:S(2)}) async-start(), calls=%async_computation.10 | async-start | bytes 7208960 | tf_op jit(solution)/shard_map/reduce_scatter | solution.py:1465
  106.1 34.4 %collective-permute-start.10 = (bf16[3,256,512]{2,1,0:T(8,128)(2,1)S(1)}, bf16[3,256,512]{2,1,0:T(8,128)(2,1)S(1)}, u32[]{:S(2)}, u32[]{:S(2)}) collective-permute-start(bf16[3,256,512]{2,1,0:T(8,128)(2,1)S(1)} %collective-permute-done.6.qa.refs_12_), channel_id=1, source_target_pairs={{0,8},{8,16},{16,24},{24,28},{28,20},{20,12},{12,4},{4,0},{1,9},{9... | collective-permute-start | bytes 2359304 | tf_op jit(solution)/shard_map/ppermute | solution.py:1430
  108.2 32.7 %collective-permute-start.11 = (bf16[3,256,512]{2,1,0:T(8,128)(2,1)S(1)}, bf16[3,256,512]{2,1,0:T(8,128)(2,1)S(1)}, u32[]{:S(2)}, u32[]{:S(2)}) collective-permute-start(bf16[3,256,512]{2,1,0:T(8,128)(2,1)S(1)} %collective-permute-done.7.qb.refs_13_), channel_id=1, source_target_pairs={{8,0},{16,8},{24,16},{28,24},{20,28},{12,20},{4,12},{0,4},{9,1},{1... | collective-permute-start | bytes 2359304 | tf_op jit(solution)/shard_map/ppermute | solution.py:1430
  124.5 34.0 %collective-permute-start.8 = (bf16[3,272,512]{2,1,0:T(8,128)(2,1)S(1)}, bf16[3,272,512]{2,1,0:T(8,128)(2,1)S(1)}, u32[]{:S(2)}, u32[]{:S(2)}) collective-permute-start(bf16[3,272,512]{2,1,0:T(8,128)(2,1)S(1)} %get-tuple-element.227), channel_id=1, source_target_pairs={{0,8},{8,16},{16,24},{24,28},{28,20},{20,12},{12,4},{4,0},{1,9},{9... | collective-permute-start | bytes 2506760 | tf_op jit(solution)/shard_map/ppermute | solution.py:1448
  126.6 32.2 %collective-permute-start.9 = (bf16[3,272,512]{2,1,0:T(8,128)(2,1)S(1)}, bf16[3,272,512]{2,1,0:T(8,128)(2,1)S(1)}, u32[]{:S(2)}, u32[]{:S(2)}) collective-permute-start(bf16[3,272,512]{2,1,0:T(8,128)(2,1)S(1)} %get-tuple-element.228), channel_id=1, source_target_pairs={{8,0},{16,8},{24,16},{28,24},{20,28},{12,20},{4,12},{0,4},{9,1},{1... | collective-permute-start | bytes 2506760 | tf_op jit(solution)/shard_map/ppermute | solution.py:1448
  140.9 34.4 %collective-permute-start.14 = (bf16[3,256,512]{2,1,0:T(8,128)(2,1)S(1)}, bf16[3,256,512]{2,1,0:T(8,128)(2,1)S(1)}, u32[]{:S(2)}, u32[]{:S(2)}) collective-permute-start(bf16[3,256,512]{2,1,0:T(8,128)(2,1)S(1)} %collective-permute-done.10.qa.refs_16_), channel_id=1, source_target_pairs={{0,8},{8,16},{16,24},{24,28},{28,20},{20,12},{12,4},{4,0},{1,9},{9... | collective-permute-start | bytes 2359304 | tf_op jit(solution)/shard_map/ppermute | solution.py:1430
  142.9 32.7 %collective-permute-start.15 = (bf16[3,256,512]{2,1,0:T(8,128)(2,1)S(1)}, bf16[3,256,512]{2,1,0:T(8,128)(2,1)S(1)}, u32[]{:S(2)}, u32[]{:S(2)}) collective-permute-start(bf16[3,256,512]{2,1,0:T(8,128)(2,1)S(1)} %collective-permute-done.11.qb.refs_17_), channel_id=1, source_target_pairs={{8,0},{16,8},{24,16},{28,24},{20,28},{12,20},{4,12},{0,4},{9,1},{1... | collective-permute-start | bytes 2359304 | tf_op jit(solution)/shard_map/ppermute | solution.py:1430
  159.2 34.0 %collective-permute-start.12 = (bf16[3,272,512]{2,1,0:T(8,128)(2,1)S(1)}, bf16[3,272,512]{2,1,0:T(8,128)(2,1)S(1)}, u32[]{:S(2)}, u32[]{:S(2)}) collective-permute-start(bf16[3,272,512]{2,1,0:T(8,128)(2,1)S(1)} %get-tuple-element.237), channel_id=1, source_target_pairs={{0,8},{8,16},{16,24},{24,28},{28,20},{20,12},{12,4},{4,0},{1,9},{9... | collective-permute-start | bytes 2506760 | tf_op jit(solution)/shard_map/ppermute | solution.py:1448
  161.3 32.2 %collective-permute-start.13 = (bf16[3,272,512]{2,1,0:T(8,128)(2,1)S(1)}, bf16[3,272,512]{2,1,0:T(8,128)(2,1)S(1)}, u32[]{:S(2)}, u32[]{:S(2)}) collective-permute-start(bf16[3,272,512]{2,1,0:T(8,128)(2,1)S(1)} %get-tuple-element.238), channel_id=1, source_target_pairs={{8,0},{16,8},{24,16},{28,24},{20,28},{12,20},{4,12},{0,4},{9,1},{1... | collective-permute-start | bytes 2506760 | tf_op jit(solution)/shard_map/ppermute | solution.py:1448
  175.7 34.4 %collective-permute-start.18 = (bf16[3,256,512]{2,1,0:T(8,128)(2,1)S(1)}, bf16[3,256,512]{2,1,0:T(8,128)(2,1)S(1)}, u32[]{:S(2)}, u32[]{:S(2)}) collective-permute-start(bf16[3,256,512]{2,1,0:T(8,128)(2,1)S(1)} %collective-permute-done.14.qa.refs_0_), channel_id=1, source_target_pairs={{0,8},{8,16},{16,24},{24,28},{28,20},{20,12},{12,4},{4,0},{1,9},{9... | collective-permute-start | bytes 2359304 | tf_op jit(solution)/shard_map/ppermute | solution.py:1430
  177.7 32.7 %collective-permute-start.19 = (bf16[3,256,512]{2,1,0:T(8,128)(2,1)S(1)}, bf16[3,256,512]{2,1,0:T(8,128)(2,1)S(1)}, u32[]{:S(2)}, u32[]{:S(2)}) collective-permute-start(bf16[3,256,512]{2,1,0:T(8,128)(2,1)S(1)} %collective-permute-done.15.qb.refs_1_), channel_id=1, source_target_pairs={{8,0},{16,8},{24,16},{28,24},{20,28},{12,20},{4,12},{0,4},{9,1},{1... | collective-permute-start | bytes 2359304 | tf_op jit(solution)/shard_map/ppermute | solution.py:1430
  194.0 34.0 %collective-permute-start.16 = (bf16[3,272,512]{2,1,0:T(8,128)(2,1)S(1)}, bf16[3,272,512]{2,1,0:T(8,128)(2,1)S(1)}, u32[]{:S(2)}, u32[]{:S(2)}) collective-permute-start(bf16[3,272,512]{2,1,0:T(8,128)(2,1)S(1)} %get-tuple-element.247), channel_id=1, source_target_pairs={{0,8},{8,16},{16,24},{24,28},{28,20},{20,12},{12,4},{4,0},{1,9},{9... | collective-permute-start | bytes 2506760 | tf_op jit(solution)/shard_map/ppermute | solution.py:1448
  196.1 32.2 %collective-permute-start.17 = (bf16[3,272,512]{2,1,0:T(8,128)(2,1)S(1)}, bf16[3,272,512]{2,1,0:T(8,128)(2,1)S(1)}, u32[]{:S(2)}, u32[]{:S(2)}) collective-permute-start(bf16[3,272,512]{2,1,0:T(8,128)(2,1)S(1)} %get-tuple-element.248), channel_id=1, source_target_pairs={{8,0},{16,8},{24,16},{28,24},{20,28},{12,20},{4,12},{0,4},{9,1},{1... | collective-permute-start | bytes 2506760 | tf_op jit(solution)/shard_map/ppermute | solution.py:1448
  210.4 34.4 %collective-permute-start.22 = (bf16[3,256,512]{2,1,0:T(8,128)(2,1)S(1)}, bf16[3,256,512]{2,1,0:T(8,128)(2,1)S(1)}, u32[]{:S(2)}, u32[]{:S(2)}) collective-permute-start(bf16[3,256,512]{2,1,0:T(8,128)(2,1)S(1)} %collective-permute-done.18.qa.refs_4_), channel_id=1, source_target_pairs={{0,8},{8,16},{16,24},{24,28},{28,20},{20,12},{12,4},{4,0},{1,9},{9... | collective-permute-start | bytes 2359304 | tf_op jit(solution)/shard_map/ppermute | solution.py:1430
  212.4 32.7 %collective-permute-start.23 = (bf16[3,256,512]{2,1,0:T(8,128)(2,1)S(1)}, bf16[3,256,512]{2,1,0:T(8,128)(2,1)S(1)}, u32[]{:S(2)}, u32[]{:S(2)}) collective-permute-start(bf16[3,256,512]{2,1,0:T(8,128)(2,1)S(1)} %collective-permute-done.19.qb.refs_5_), channel_id=1, source_target_pairs={{8,0},{16,8},{24,16},{28,24},{20,28},{12,20},{4,12},{0,4},{9,1},{1... | collective-permute-start | bytes 2359304 | tf_op jit(solution)/shard_map/ppermute | solution.py:1430
  228.8 32.6 %collective-permute-start.20 = (bf16[3,272,512]{2,1,0:T(8,128)(2,1)S(1)}, bf16[3,272,512]{2,1,0:T(8,128)(2,1)S(1)}, u32[]{:S(2)}, u32[]{:S(2)}) collective-permute-start(bf16[3,272,512]{2,1,0:T(8,128)(2,1)S(1)} %get-tuple-element.257), channel_id=1, source_target_pairs={{0,8},{8,16},{16,24},{24,28},{28,20},{20,12},{12,4},{4,0},{1,9},{9... | collective-permute-start | bytes 2506760 | tf_op jit(solution)/shard_map/ppermute | solution.py:1448
  362.8 277.6 %reduce-scatter.11.cloned.1.call-start = ((), (), s32[]{:S(2)}) async-start(), calls=%async_computation.13 | async-start | bytes 2621440 | tf_op jit(solution)/shard_map/reduce_scatter | solution.py:1465
  396.2 244.1 %reduce-scatter.7.cloned.1.call-start = ((), (), s32[]{:S(2)}) async-start(), calls=%async_computation.11 | async-start | bytes 7208960 | tf_op jit(solution)/shard_map/reduce_scatter | solution.py:1465
  397.0 243.4 %reduce-scatter.9.cloned.1.call-start = ((), (), s32[]{:S(2)}) async-start(), calls=%async_computation.12 | async-start | bytes 7208960 | tf_op jit(solution)/shard_map/reduce_scatter | solution.py:1465
  453.9 37.8 %collective-permute-start.40 = (bf16[3,272,512]{2,1,0:T(8,128)(2,1)S(1)}, bf16[3,272,512]{2,1,0:T(8,128)(2,1)S(1)}, u32[]{:S(2)}, u32[]{:S(2)}) collective-permute-start(bf16[3,272,512]{2,1,0:T(8,128)(2,1)S(1)} %collective-permute-done.38.refs_18_.da), channel_id=1, source_target_pairs={{0,8},{8,16},{16,24},{24,28},{28,20},{20,12},{12,4},{4,0},{1,9},{9... | collective-permute-start | bytes 2506760 | tf_op jit(solution)/shard_map/ppermute | solution.py:1470
  455.5 36.2 %collective-permute-start.41 = (bf16[3,272,512]{2,1,0:T(8,128)(2,1)S(1)}, bf16[3,272,512]{2,1,0:T(8,128)(2,1)S(1)}, u32[]{:S(2)}, u32[]{:S(2)}) collective-permute-start(bf16[3,272,512]{2,1,0:T(8,128)(2,1)S(1)} %collective-permute-done.39.refs_19_.db), channel_id=1, source_target_pairs={{8,0},{16,8},{24,16},{28,24},{20,28},{12,20},{4,12},{0,4},{9,1},{1... | collective-permute-start | bytes 2506760 | tf_op jit(solution)/shard_map/ppermute | solution.py:1470
  489.6 36.6 %collective-permute-start.36 = (bf16[3,256,512]{2,1,0:T(8,128)(2,1)S(1)}, bf16[3,256,512]{2,1,0:T(8,128)(2,1)S(1)}, u32[]{:S(2)}, u32[]{:S(2)}) collective-permute-start(bf16[3,256,512]{2,1,0:T(8,128)(2,1)S(1)} %get-tuple-element.304), channel_id=1, source_target_pairs={{0,8},{8,16},{16,24},{24,28},{28,20},{20,12},{12,4},{4,0},{1,9},{9... | collective-permute-start | bytes 2359304 | tf_op jit(solution)/shard_map/ppermute | solution.py:1496
  490.7 35.5 %collective-permute-start.37 = (bf16[3,256,512]{2,1,0:T(8,128)(2,1)S(1)}, bf16[3,256,512]{2,1,0:T(8,128)(2,1)S(1)}, u32[]{:S(2)}, u32[]{:S(2)}) collective-permute-start(bf16[3,256,512]{2,1,0:T(8,128)(2,1)S(1)} %get-tuple-element.305), channel_id=1, source_target_pairs={{8,0},{16,8},{24,16},{28,24},{20,28},{12,20},{4,12},{0,4},{9,1},{1... | collective-permute-start | bytes 2359304 | tf_op jit(solution)/shard_map/ppermute | solution.py:1496
  491.7 37.0 %collective-permute-start.46 = (bf16[3,272,512]{2,1,0:T(8,128)(2,1)S(1)}, bf16[3,272,512]{2,1,0:T(8,128)(2,1)}, u32[]{:S(2)}, u32[]{:S(2)}) collective-permute-start(bf16[3,272,512]{2,1,0:T(8,128)(2,1)S(1)} %collective-permute-done.40.da.refs_2_), channel_id=1, source_target_pairs={{0,8},{8,16},{16,24},{24,28},{28,20},{20,12},{12,4},{4,0},{1,9},{9... | collective-permute-start | bytes 2506760 | tf_op jit(solution)/shard_map/ppermute | solution.py:1470
  492.8 36.4 %collective-permute-start.47 = (bf16[3,272,512]{2,1,0:T(8,128)(2,1)S(1)}, bf16[3,272,512]{2,1,0:T(8,128)(2,1)}, u32[]{:S(2)}, u32[]{:S(2)}) collective-permute-start(bf16[3,272,512]{2,1,0:T(8,128)(2,1)S(1)} %collective-permute-done.41.db.refs_3_), channel_id=1, source_target_pairs={{8,0},{16,8},{24,16},{28,24},{20,28},{12,20},{4,12},{0,4},{9,1},{1... | collective-permute-start | bytes 2506760 | tf_op jit(solution)/shard_map/ppermute | solution.py:1470
  528.7 55.8 %collective-permute-start.50 = (bf16[3,272,512]{2,1,0:T(8,128)(2,1)}, bf16[3,272,512]{2,1,0:T(8,128)(2,1)}, u32[]{:S(2)}, u32[]{:S(2)}) collective-permute-start(bf16[3,272,512]{2,1,0:T(8,128)(2,1)} %collective-permute-done.46.da.refs_6_), channel_id=1, source_target_pairs={{0,8},{8,16},{16,24},{24,28},{28,20},{20,12},{12,4},{4,0},{1,9},{9... | collective-permute-start | bytes 2506760 | tf_op jit(solution)/shard_map/ppermute | solution.py:1470
  529.2 55.3 %collective-permute-start.51 = (bf16[3,272,512]{2,1,0:T(8,128)(2,1)}, bf16[3,272,512]{2,1,0:T(8,128)(2,1)}, u32[]{:S(2)}, u32[]{:S(2)}) collective-permute-start(bf16[3,272,512]{2,1,0:T(8,128)(2,1)} %collective-permute-done.47.db.refs_7_), channel_id=1, source_target_pairs={{8,0},{16,8},{24,16},{28,24},{20,28},{12,20},{4,12},{0,4},{9,1},{1... | collective-permute-start | bytes 2506760 | tf_op jit(solution)/shard_map/ppermute | solution.py:1470
  (111 other events, 1877.7 us)
Sparse Core Ops, SparseCore 0:
  9.6 25.4 all-gather.6
  37.2 34.2 all-gather.8
  73.1 22.5 all-gather.10
  97.2 43.3 all-gather.12
  142.0 43.3 all-gather.14
  186.9 43.4 all-gather.16
  362.9 54.3 reduce-scatter.4
  420.6 31.3 reduce-scatter.10
  454.5 54.8 reduce-scatter.6
  512.0 54.8 reduce-scatter.8
